TPU v7x, 32 devices: a whole 2x2x4 slice. The times are simulated.
32 devices in a mesh: tok: 4 (over y, x), vocab: 8 (over z, core).
Axes of the slice: x: 2, y: 2, z: 4, core: 2. Of those that a mesh axis runs over, the one named last changes fastest.
Arguments:
- teacher_logits: bfloat16 [512, 32768], P('tok', 'vocab'), may hold values from -18 to 240
- hidden: bfloat16 [512, 4608], P('tok'), may hold values from -6 to 6
- new_head: bfloat16 [4608, 32768], P(None, ('tok', 'vocab')), may hold values from -0.26516504 to 0.26516504
- labels: int32 [512], replicated, may hold values from 0 to 32767
- map_target: int32 [256, 4], P('vocab'), may hold values from 0 to 255, as said below
- map_weight: bfloat16 [256, 4, 128, 128], P('vocab'), may hold values from 0 to 0.017578125, as said below
Outputs:
- loss: float32 [512], P('tok')
- head_grad: bfloat16 [4608, 32768], P(None, ('tok', 'vocab'))
Inputs may be any that keep to these rules, and one draw needn't show every extreme that they name: `map_target`: values are ids of new blocks; new block b belongs to the device at index b // 8 of tok and vocab together, tok first. Of the 128 entries of one vocab index, at most 8 belong to one device, and some device gets exactly 8. `map_weight`: entries are non-negative.
All inputs are finite; a program needn't handle non-finite values.
Results may differ from a plain program's by a relative error of at most 0.001.
The roundings to bfloat16 on the way count: a program that leaves them out, or rounds other values in their place, can miss the bound.
Values may be sent and summed in bfloat16 or wider, within the bound.
No kernel may reach another device: no remote copies, remote signals or barrier semaphores. Data moves between devices by JAX's collectives and lax.ppermute only.
A program may use at most 128 MiB of HBM per device.

v0:
```python
import functools

import jax
import jax.numpy as jnp
from jax import lax
from jax.experimental import pallas as pl
from jax.experimental.pallas import tpu as pltpu
from jax.sharding import PartitionSpec as P

F32 = jnp.float32
BF16 = jnp.bfloat16
LANES = 128
BATCH = 8
COST = pl.CostEstimate(flops=1024, bytes_accessed=1024, transcendentals=0)
SLOT_BITS = 10
SLOT_BASE = 1 << SLOT_BITS
SMEM_SPEC = pl.BlockSpec(memory_space=pltpu.SMEM)
VMEM_SPEC = pl.BlockSpec(memory_space=pltpu.VMEM)


def params(mebibytes):
    return pltpu.CompilerParams(vmem_limit_bytes=mebibytes * 1024 * 1024)


def in_hbm(x):
    return pltpu.with_memory_space_constraint(x, pltpu.HBM)


def tree(op, items):
    while len(items) > 1:
        items = [op(items[i], items[i + 1]) if i + 1 < len(items) else items[i] for i in range(0, len(items), 2)]
    return items[0]


def total_at(rows_of, top_row, total_row):
    top = tree(jnp.maximum, [r[top_row] for r in rows_of])
    total = tree(jnp.add, [r[total_row] * jnp.exp(r[top_row] - top) for r in rows_of])
    return top, total


def split_rows(refs):
    return [[ref[k : k + 1, :] for k in range(8)] for ref in refs]


def rows_from_columns(columns):
    n = columns[0].shape[0]
    lane = lax.broadcasted_iota(jnp.int32, (n, LANES), 1)
    tile = jnp.zeros((n, LANES), F32)
    for place, column in enumerate(columns):
        tile = jnp.where(lane == place, column, tile)
    return tile.T[0:8, :]


def columns_from_rows(rows):
    n = rows[0].shape[1]
    return jnp.concatenate(rows + [jnp.zeros((LANES - len(rows), n), F32)], axis=0).T


def teacher_kernel(x_ref, stat_ref):
    rows, cols = x_ref.shape
    places = range(0, cols, LANES)
    read = lambda place: x_ref[:, place : place + LANES].astype(F32)
    top = jnp.full((rows, LANES), -jnp.inf, F32)
    for place in places:
        top = jnp.maximum(top, read(place))
    top = jnp.max(top, axis=1, keepdims=True)
    total = jnp.zeros((rows, LANES), F32)
    for place in places:
        total = total + jnp.exp(read(place) - top)
    stat_ref[...] = rows_from_columns([top, jnp.sum(total, axis=1, keepdims=True)])


def teacher_stats(x):
    return pl.pallas_call(
        teacher_kernel,
        in_specs=[VMEM_SPEC],
        out_specs=VMEM_SPEC,
        out_shape=jax.ShapeDtypeStruct((8, x.shape[0]), F32),
        compiler_params=params(6),
        cost_estimate=COST,
        name="teacher_stats",
    )(x)


def divide(x, n):
    return lax.shift_right_logical(x, n.bit_length() - 1) if n & (n - 1) == 0 else x // n


def plan_kernel(own_ref, peer_ref, list_ref, count_ref):
    lists = count_ref.shape[0]
    entries = own_ref.shape[0]
    for p in range(lists):
        count_ref[p] = 0

    def visit(i, carry):
        for side, ref in enumerate((own_ref, peer_ref)):
            code = ref[i]
            row = lax.shift_right_logical(code, SLOT_BITS)
            n = count_ref[row]
            list_ref[row, n] = (side * entries + i) * SLOT_BASE + (code & (SLOT_BASE - 1))
            count_ref[row] = n + 1
        return carry

    lax.fori_loop(0, entries, visit, 0, unroll=8)
    for p in range(lists):
        n = count_ref[p]
        for k in range(BATCH - 1):
            list_ref[p, n + k] = SLOT_BASE - 1


def plan(own_code, peer_code, lists):
    room = 2 * own_code.size + BATCH
    return pl.pallas_call(
        plan_kernel,
        in_specs=[SMEM_SPEC] * 2,
        out_specs=[SMEM_SPEC] * 2,
        out_shape=[jax.ShapeDtypeStruct((lists, room), jnp.int32), jax.ShapeDtypeStruct((lists,), jnp.int32)],
        compiler_params=params(1),
        cost_estimate=COST,
        name="entry_lists",
    )(own_code, peer_code)


def probs_kernel(x_own, x_peer, *refs):
    stats, (probs, columns) = refs[:-2], refs[-2:]

    @pl.when(pl.program_id(0) == 0)
    def _():
        top, total = total_at(split_rows(stats), 0, 1)
        columns[...] = columns_from_rows([top, 1.0 / total])

    top, scale = columns[:, 0:1], columns[:, 1:2]
    for side, x in enumerate((x_own, x_peer)):
        for j in range(x.shape[1] // LANES):
            raised = jnp.exp(x[:, j * LANES : (j + 1) * LANES].astype(F32) - top)
            probs[side, j] = (raised * scale).astype(BF16)


def sums_kernel(spot_ref, list_ref, count_ref, probs, w_own, w_peer, *refs, first, fan, pieces):
    outs, mass_ref, acc = refs[:-2], refs[-2], refs[-1]
    step = pl.program_id(0)
    slots, rows, _ = outs[0].shape
    side = w_own.shape[0] * fan
    mass = jnp.zeros((rows, LANES), F32)
    for k, out in enumerate(outs):
        piece = spot_ref[0] * pieces + first + k + step
        acc[...] = jnp.zeros_like(acc)

        def add(i, carry):
            parts = []
            for u in range(BATCH):
                item = list_ref[piece, i * BATCH + u]
                slot = item & (SLOT_BASE - 1)
                entry = lax.shift_right_logical(item, SLOT_BITS)
                weight = jnp.where(entry < side, 0, 1)
                parts.append((entry, slot, weight))
            for entry, slot, peer in parts:
                j = divide(entry, fan)
                f = entry - j * fan
                local_j = j - peer * (side // fan)
                weight = jnp.where(peer == 1, w_peer[local_j, f], w_own[local_j, f])
                part = jnp.dot(probs[j], weight, preferred_element_type=F32)
                acc[jnp.minimum(slot, slots)] += part.astype(BF16).astype(F32)
            return carry

        lax.fori_loop(0, divide(count_ref[piece] + BATCH - 1, BATCH), add, 0)

        def drain(i, mass):
            block = acc[i]
            out[i] = block.astype(BF16)
            return mass + block

        mass = lax.fori_loop(0, slots, drain, mass, unroll=4)
    part = rows_from_columns([jnp.sum(mass, axis=1, keepdims=True)])

    @pl.when(step == 0)
    def _():
        mass_ref[...] = part

    @pl.when(step > 0)
    def _():
        mass_ref[...] += part


def teacher_probs(x_own, x_peer, stats):
    rows, cols = x_own.shape
    steps = 4
    blocks = cols // LANES
    part = pl.BlockSpec((rows, cols // steps), lambda i: (0, i))
    probs = pl.pallas_call(
        probs_kernel,
        grid=(steps,),
        in_specs=[part, part] + [pl.BlockSpec(s.shape, lambda i: (0, 0)) for s in stats],
        out_specs=pl.BlockSpec((2, blocks // steps, rows, LANES), lambda i: (0, i, 0, 0)),
        out_shape=jax.ShapeDtypeStruct((2, blocks, rows, LANES), BF16),
        scratch_shapes=[pltpu.VMEM((rows, LANES), F32)],
        compiler_params=params(8),
        cost_estimate=COST,
        name="teacher_probs",
    )(in_hbm(x_own), in_hbm(x_peer), *stats)
    return probs.reshape(2 * blocks, rows, LANES)


def chip_sums(spot, lists, counts, probs, w_own, w_peer, first, n_out, steps, slots):
    rows = probs.shape[1]
    fan = w_own.shape[1]
    whole = lambda shape: pl.BlockSpec(shape, lambda s: (0,) * len(shape))
    out = pltpu.HBM((steps * slots, rows, LANES), BF16)
    return pl.pallas_call(
        functools.partial(sums_kernel, first=first, fan=fan, pieces=counts.shape[0] // 2),
        grid=(steps,),
        in_specs=[SMEM_SPEC] * 3 + [VMEM_SPEC] * 3,
        out_specs=[pl.BlockSpec((slots, rows, LANES), lambda s: (s, 0, 0))] * n_out + [whole((8, rows))],
        out_shape=[out] * n_out + [jax.ShapeDtypeStruct((8, rows), F32)],
        scratch_shapes=[pltpu.VMEM((slots + 1, rows, LANES), F32)],
        compiler_params=params(24),
        cost_estimate=COST,
        name="chip_sums",
    )(spot, lists, counts, probs, w_own, w_peer)


def logits_kernel(spot_ref, after_ref, near_ref, far_ref, head_ref, *refs):
    out_ref, turned_ref, everyone = refs
    n_tok = out_ref.shape[0]
    half = near_ref.shape[0] // n_tok
    del after_ref

    @pl.when(pl.program_id(0) == 0)
    def _():
        core = spot_ref[0]
        for r in range(n_tok):
            source = slice(r * half, (r + 1) * half)
            for side, ref in ((core, near_ref), (1 - core, far_ref)):
                start = pl.multiple_of((2 * r + side) * half, half)
                everyone[pl.ds(start, half), :] = ref[source, :]

    result = jnp.dot(everyone[...], head_ref[...], preferred_element_type=F32)
    for r in range(n_tok):
        out_ref[r] = result[2 * r * half : 2 * (r + 1) * half, :]
    part = turned_ref.shape[0]
    start = pl.multiple_of(pl.program_id(0) * part, part)
    turned_ref[...] = everyone[:, pl.ds(start, part)].T


def student_logits(spot, after, near, far, head, n_tok):
    every, depth = 2 * near.shape[0], near.shape[1]
    rows = every // n_tok
    cols = head.shape[1]
    tile = 256
    whole = lambda shape: pl.BlockSpec(shape, lambda i: (0, 0))
    return pl.pallas_call(
        logits_kernel,
        grid=(cols // tile,),
        in_specs=[SMEM_SPEC, pl.BlockSpec(memory_space=pl.ANY), whole(near.shape), whole(far.shape)]
        + [pl.BlockSpec((depth, tile), lambda i: (0, i))],
        out_specs=[pl.BlockSpec((n_tok, rows, tile), lambda i: (0, 0, i))]
        + [pl.BlockSpec((depth * tile // cols, every), lambda i: (i, 0))],
        out_shape=[pltpu.HBM((n_tok, rows, cols), F32), pltpu.HBM((depth, every), BF16)],
        scratch_shapes=[pltpu.VMEM((every, depth), BF16)],
        compiler_params=params(30),
        cost_estimate=COST,
        name="student_logits",
    )(spot, after, near, far, in_hbm(head))


def student_kernel(base_ref, labels_ref, mass_ref, logits_ref, stat_ref):
    n_tok, rows, cols = logits_ref.shape
    lane = lax.broadcasted_iota(jnp.int32, (rows, LANES), 1)
    label = labels_ref[...]
    top = jnp.full((rows, LANES), -jnp.inf, F32)
    hit = jnp.zeros((rows, LANES), F32)
    for t in range(n_tok):
        for b in range(0, cols, LANES):
            block = logits_ref[t, :, b : b + LANES]
            top = jnp.maximum(top, block)
            hit = hit + jnp.where(lane == label - (base_ref[t] + b), block, 0.0)
    top = jnp.max(top, axis=1, keepdims=True)
    total = jnp.zeros((rows, LANES), F32)
    for t in range(n_tok):
        for b in range(0, cols, LANES):
            total = total + jnp.exp(logits_ref[t, :, b : b + LANES] - top)
    total = jnp.sum(total, axis=1, keepdims=True)
    hit = jnp.sum(hit, axis=1, keepdims=True)
    stat_ref[...] = rows_from_columns([jnp.zeros_like(hit), top, total, hit])
    stat_ref[0:1, :] = mass_ref[0:1, :]


def student_stats(base, label_column, mass, logits):
    return pl.pallas_call(
        student_kernel,
        in_specs=[SMEM_SPEC] + [VMEM_SPEC] * 3,
        out_specs=VMEM_SPEC,
        out_shape=jax.ShapeDtypeStruct(mass.shape, F32),
        compiler_params=params(10),
        cost_estimate=COST,
        name="student_stats",
    )(base, label_column, mass, logits)


def merge_kernel(*refs):
    stats, out = refs[:-1], refs[-1]
    parts = split_rows(stats)
    mass = tree(jnp.add, [r[0] for r in parts])
    top, total = total_at(parts, 1, 2)
    hit = tree(jnp.add, [r[3] for r in parts])
    out[...] = jnp.concatenate([mass, top, total, hit, jnp.zeros((4, top.shape[1]), F32)], axis=0)


def merge_stats(stats):
    return pl.pallas_call(
        merge_kernel,
        in_specs=[VMEM_SPEC] * len(stats),
        out_specs=VMEM_SPEC,
        out_shape=jax.ShapeDtypeStruct(stats[0].shape, F32),
        compiler_params=params(1),
        cost_estimate=COST,
        name="merge_stats",
    )(*stats)


def totals_kernel(*refs):
    stats, (columns, loss_ref) = refs[:-2], refs[-2:]
    parts = split_rows(stats)
    mass = tree(jnp.add, [r[0] for r in parts])
    top, total = total_at(parts, 1, 2)
    log_total = top + jnp.log(total)
    label_logit = tree(jnp.add, [r[3] for r in parts])
    columns[...] = columns_from_rows([mass + 1.0, log_total])
    loss_ref[...] = mass * log_total + log_total - label_logit


def token_totals(stats):
    rows = stats[0].shape[1]
    return pl.pallas_call(
        totals_kernel,
        in_specs=[VMEM_SPEC] * len(stats),
        out_specs=[VMEM_SPEC] * 2,
        out_shape=[jax.ShapeDtypeStruct((rows, LANES), F32), jax.ShapeDtypeStruct((1, rows), F32)],
        compiler_params=params(2),
        cost_estimate=COST,
        name="token_totals",
    )(*stats)


def grad_kernel(tok_ref, base_ref, labels_ref, columns, *refs, n_sums):
    sums = refs[:n_sums]
    logits_ref, *grads, inner_ref, inner = refs[n_sums:]
    step = pl.program_id(0)
    _, rows, cols = logits_ref.shape

    @pl.when(step == 0)
    def _():
        inner[...] = jnp.zeros_like(inner)

    lane = lax.broadcasted_iota(jnp.int32, (rows, LANES), 1)
    lift, log_total = columns[:, 0:1], columns[:, 1:2]
    label = labels_ref[...] - base_ref[token_group(step, tok_ref, len(grads))]
    for r in range(len(grads)):

        @pl.when(step == r)
        def _():
            running = inner[...]
            for b in range(cols // LANES):
                place = slice(b * LANES, (b + 1) * LANES)
                target = functools.reduce(
                    jnp.add, [ref[z, b].astype(F32) for ref in sums for z in range(ref.shape[0])]
                )
                score = logits_ref[0, :, place]
                running = running + target * score
                hit = jnp.where(lane == label - b * LANES, 1.0, 0.0)
                grads[r][:, place] = (lift * jnp.exp(score - log_total) - target - hit).astype(BF16)
            inner[...] = running

    @pl.when(step == pl.num_programs(0) - 1)
    def _():
        inner_ref[...] = rows_from_columns([jnp.sum(inner[...], axis=1, keepdims=True)])[0:1, :]


def token_group(step, tok_ref, n_tok):
    return tok_ref[0] ^ (n_tok - 1 - step)


def grad_logits(tok, base, label_column, columns, sums, logits):
    n_tok, rows, cols = logits.shape
    per = cols // LANES
    whole = lambda shape: pl.BlockSpec(shape, lambda t, tok_ref: (0,) * len(shape))
    group = lambda t, tok_ref: token_group(t, tok_ref, n_tok)
    return pl.pallas_call(
        functools.partial(grad_kernel, n_sums=len(sums)),
        grid_spec=pltpu.PrefetchScalarGridSpec(
            num_scalar_prefetch=1,
            grid=(n_tok,),
            in_specs=[SMEM_SPEC, whole(label_column.shape), whole(columns.shape)]
            + [pl.BlockSpec((s.shape[0], per, rows, LANES), lambda t, r: (0, group(t, r), 0, 0)) for s in sums]
            + [pl.BlockSpec((1, rows, cols), lambda t, r: (group(t, r), 0, 0))],
            out_specs=[whole((rows, cols))] * n_tok + [whole((1, rows))],
            scratch_shapes=[pltpu.VMEM((rows, LANES), F32)],
        ),
        out_shape=[pltpu.HBM((rows, cols), BF16)] * n_tok + [jax.ShapeDtypeStruct((1, rows), F32)],
        compiler_params=params(14),
        cost_estimate=COST,
        name="grad_logits",
    )(tok, base, label_column, columns, *sums, logits)


def product_kernel(tok_ref, a_ref, *refs):
    pieces, o_ref, b_ref = refs[:-2], refs[-2], refs[-1]
    rows = pieces[0].shape[0]

    @pl.when(pl.program_id(0) == 0)
    def _():
        for r, piece in enumerate(pieces):
            start = pl.multiple_of(token_group(r, tok_ref, len(pieces)) * rows, rows)
            b_ref[pl.ds(start, rows), :] = piece[...]

    o_ref[...] = jnp.dot(a_ref[...], b_ref[...], preferred_element_type=F32).astype(o_ref.dtype)


def head_product(tok, a, pieces):
    m, k = a.shape
    rows, n = pieces[0].shape
    tile = m // 6
    return pl.pallas_call(
        product_kernel,
        grid=(m // tile,),
        in_specs=[SMEM_SPEC, pl.BlockSpec((tile, k), lambda i: (i, 0))]
        + [pl.BlockSpec((rows, n), lambda i: (0, 0))] * len(pieces),
        out_specs=pl.BlockSpec((tile, n), lambda i: (i, 0)),
        out_shape=jax.ShapeDtypeStruct((m, n), BF16),
        scratch_shapes=[pltpu.VMEM((k, n), BF16)],
        compiler_params=params(20),
        cost_estimate=COST,
        name="head_product",
    )(tok, in_hbm(a), *pieces[:-1], in_hbm(pieces[-1]))


def swap(x, axis, mask):
    return lax.ppermute(x, axis, [(i, i ^ mask) for i in range(lax.axis_size(axis))])


def gather_chips(x):
    n = lax.axis_size("vocab")
    if n > 8:
        lines = [[2 * z + c for z in range(n // 2)] for c in range(2)]
        everything = lax.all_gather(x, "vocab", axis=0, axis_index_groups=lines)
        return [everything[z] for z in range(n // 2)]
    return [x] + [swap(x, "vocab", r) for r in range(2, n, 2)]


def gather_cores(x):
    chips = gather_chips(x)
    return chips + [swap(chip, "vocab", 1) for chip in chips]


def half_rows(hidden, spot, n_tok):
    half = hidden.shape[0] // 2
    own = lax.dynamic_slice_in_dim(hidden, spot[0] * half, half)
    return jnp.broadcast_to(own, (n_tok,) + own.shape)


def plus(a, b):
    return (a.astype(F32) + b.astype(F32)).astype(BF16)


def exchange_tok(x):
    return lax.all_to_all(x, "tok", split_axis=0, concat_axis=0, tiled=True)


def send(x, hops):
    return lax.ppermute(x, "vocab", [(2 * a + c, 2 * b + c) for a, b in hops for c in range(2)])


def local(teacher_logits, hidden, new_head, labels, map_target, map_weight):
    rows = teacher_logits.shape[0]
    block = map_weight.shape[2]
    n_tok = lax.axis_size("tok")
    n_vocab = lax.axis_size("vocab")
    n_z = n_vocab // 2
    new_cols = new_head.shape[1]
    per = new_cols // block
    tok = lax.axis_index("tok")
    vocab = lax.axis_index("vocab")
    spot = jnp.stack([vocab % 2, vocab // 2]).astype(jnp.int32)
    slots = n_tok * per
    in_line = n_z == 4

    owner = map_target // per
    owner_vocab = owner % n_vocab
    owner_z = owner_vocab // 2
    if in_line:
        z = vocab // 2
        outer = (owner_z == 0) | (owner_z == n_z - 1)
        near_place = jnp.where(owner_z == z, 3, 2)
        place = jnp.where((owner_z // 2) == (z // 2), near_place, jnp.where(outer, 0, 1))
    else:
        place = owner_z
    slot = (owner // n_vocab) * per + map_target % per
    code = (((owner_vocab % 2) * n_z + place) * SLOT_BASE + slot).astype(jnp.int32).reshape(-1)

    peer_logits = swap(teacher_logits, "vocab", 1)
    peer_code = swap(code, "vocab", 1)
    peer_weight = swap(map_weight, "vocab", 1)
    teacher = teacher_stats(teacher_logits)
    totals = gather_cores(teacher)
    lists, counts = plan(code, peer_code, 2 * n_z)
    probs = teacher_probs(teacher_logits, peer_logits, totals)

    if in_line:
        inward, across, beyond = [(0, 1), (3, 2)], [(1, 2), (2, 1)], [(1, 3), (2, 0)]
        far_outer, mass_a = chip_sums(spot, lists, counts, probs, map_weight, peer_weight, 0, 1, 1, slots)
        first = send(far_outer, inward)
        rows_in, mass_a = lax.optimization_barrier((hidden, mass_a))
        copies, probs = lax.optimization_barrier((half_rows(rows_in, spot, n_tok), probs))
        near = exchange_tok(copies)
        far_inner, beside, own, mass_b = chip_sums(
            spot, lists, counts, probs, map_weight, peer_weight, 1, 3, 1, slots
        )
        second = send(far_inner, inward)
        first, mass = lax.optimization_barrier((first, mass_a + mass_b))
        merged = plus(far_outer, first)
        arrived = send(merged, beyond)
        near, waited, merged = lax.optimization_barrier((near, beside, merged))
        third = swap(waited, "vocab", 2)
    else:
        sums, mass = chip_sums(spot, lists, counts, probs, map_weight, peer_weight, 0, 1, n_z, slots)
        lines = [[2 * z + c for z in range(n_z)] for c in range(2)]
        sums = lax.all_to_all(
            sums.reshape(n_z, slots, rows, block),
            "vocab",
            split_axis=0,
            concat_axis=0,
            axis_index_groups=lines,
            tiled=True,
        )
        sums = [sums]
        near = exchange_tok(half_rows(hidden, spot, n_tok))

    near = near.reshape(n_tok * (rows // 2), -1)
    far = swap(near, "vocab", 1)
    scores, turned = student_logits(spot, mass, near, far, new_head, n_tok)
    base = (jnp.arange(n_tok, dtype=jnp.int32) * n_vocab + vocab) * new_cols
    label_column = lax.dynamic_slice_in_dim(labels, tok * rows, rows).reshape(rows, 1)
    scores = exchange_tok(scores)
    if in_line:
        second, arrived, turned = lax.optimization_barrier((second, arrived, turned))
        merged_inner = plus(far_inner, second)
        crossed = send(merged_inner, across)
        scores, merged_inner = lax.optimization_barrier((scores, merged_inner))
        sums = [x[None] for x in (own, third, crossed, arrived)]
    student = student_stats(base, label_column, mass, scores)
    student = merge_stats([student, swap(student, "vocab", 1)])
    stats = gather_chips(student)

    group = tok.astype(jnp.int32).reshape(1)
    columns, base_loss = token_totals(stats)
    *grads, inner = grad_logits(group, base, label_column, columns, sums, scores)
    grads = [swap(x, "tok", n_tok - 1 - r) for r, x in enumerate(grads[:-1])] + [grads[-1]]
    mask = 1
    while mask < n_vocab:
        inner = inner + swap(inner, "vocab", mask)
        mask *= 2
    return ((base_loss - inner).reshape(rows), head_product(group, turned, grads))


def solution(mesh):
    return jax.shard_map(
        local,
        mesh=mesh,
        in_specs=(
            P("tok", "vocab"),
            P("tok", None),
            P(None, ("tok", "vocab")),
            P(),
            P("vocab", None),
            P("vocab", None, None, None),
        ),
        out_specs=(P("tok"), P(None, ("tok", "vocab"))),
        check_vma=False,
    )
```

profile of v0, /device:TPU:0, one launch (start us, length us, event | category | flops | bytes accessed | tf_op | source)
XLA Modules:
  0.0 150.5 jit_solution(16990120261236589880)
XLA Ops:
  3.1 3.0 %collective-permute-start.2 = (f32[8,128]{1,0:T(8,128)S(1)}, f32[8,128]{1,0:T(8,128)S(1)}, u32[]{:S(2)}, u32[]{:S(2)}) collective-permute-start(f32[8,128]{1,0:T(8,128)S(1)} %teacher_stats.1.refs_0_), channel_id=1, source_target_pairs={{0,2},{1,3},{2,0},{3,1},{4,6},{5,7},{6,4},{7,5},{8,10},{9,11},{10,... | collective-permute-start | bytes 12296 | tf_op jit(solution)/shard_map/ppermute | solution.py:438
  7.1 2.7 %collective-permute-start.3 = (f32[8,128]{1,0:T(8,128)S(1)}, f32[8,128]{1,0:T(8,128)S(1)}, u32[]{:S(2)}, u32[]{:S(2)}) collective-permute-start(f32[8,128]{1,0:T(8,128)S(1)} %teacher_stats.1.refs_0_), channel_id=1, source_target_pairs={{0,4},{1,5},{2,6},{3,7},{4,0},{5,1},{6,2},{7,3},{8,12},{9,13},{10,... | collective-permute-start | bytes 12296 | tf_op jit(solution)/shard_map/ppermute | solution.py:438
  9.7 3.1 %collective-permute-start.4 = (f32[8,128]{1,0:T(8,128)S(1)}, f32[8,128]{1,0:T(8,128)S(1)}, u32[]{:S(2)}, u32[]{:S(2)}) collective-permute-start(f32[8,128]{1,0:T(8,128)S(1)} %teacher_stats.1.refs_0_), channel_id=1, source_target_pairs={{0,6},{1,7},{2,4},{3,5},{4,2},{5,3},{6,0},{7,1},{8,14},{9,15},{10,... | collective-permute-start | bytes 12296 | tf_op jit(solution)/shard_map/ppermute | solution.py:438
  13.4 1.8 %collective-permute-done.4.refs_3_ = f32[8,128]{1,0:T(8,128)S(1)} collective-permute-done((f32[8,128]{1,0:T(8,128)S(1)}, f32[8,128]{1,0:T(8,128)S(1)}, u32[]{:S(2)}, u32[]{:S(2)}) %collective-permute-start.4) | collective-permute-done | bytes 4128 | tf_op jit(solution)/shard_map/ppermute | solution.py:438
  15.7 3.0 %entry_lists.1 = (s32[8,264]{1,0:T(8,128)S(1)}, s32[8]{0:T(128)S(1)}) custom-call(s32[128]{0:T(128)S(1)} %reshape.23.own_ref, s32[128]{0:T(128)S(1)} %collective-permute-done.peer_ref), custom_call_target="tpu_custom_call" | custom-call | flops 1024 | bytes 1024 | tf_op jit(solution)/shard_map/entry_lists/pallas_call | solution.py:113
  18.8 3.4 %teacher_probs.1 = bf16[2,32,128,128]{3,2,1,0:T(8,128)(2,1)S(1)} custom-call(bf16[128,4096]{1,0:T(8,128)(2,1)} %x_own.1, bf16[128,4096]{1,0:T(8,128)(2,1)} %collective-permute-done.1.x_peer, f32[8,128]{1,0:T(8,128)S(1)} %teacher_stats.1.refs_0_, f32[8,128]{1,0:T(8,128)S(1)} %collective-permute-done.2.refs_1_, f32[8,128]{1,0:T(8,128)S(1)} %collective-permute-done.3.refs_2_, ...), custom_call_target="tpu_custom_call" | custom-call | flops 1024 | bytes 1024 | tf_op jit(solution)/shard_map/teacher_probs/pallas_call | solution.py:190
  22.2 4.5 %chip_sums.2 = (bf16[32,128,128]{2,1,0:T(8,128)(2,1)}, f32[8,128]{1,0:T(8,128)S(1)}) custom-call(s32[2]{0:T(128)S(1)} %pad_add_fusion.spot_ref, s32[8,264]{1,0:T(8,128)S(1)} %get-tuple-element.31.list_ref, s32[8]{0:T(128)S(1)} %get-tuple-element.32.count_ref, bf16[64,128,128]{2,1,0:T(8,128)(2,1)S(1)} %bitcast.13, bf16[32,4,128,128]{3,2,1,0:T(8,128)(2,1)S(1)} %copy-done.1, ...), custom_call_target="tpu_custom_call" | custom-call | flops 1024 | bytes 1024 | tf_op jit(solution)/shard_map/chip_sums/pallas_call | solution.py:209
  26.8 1.6 %broadcast_in_dim.21 = bf16[4,64,4608]{2,1,0:T(8,128)(2,1)} broadcast(bf16[64,4608]{1,0:T(8,128)(2,1)S(1)} %constant_dynamic-slice_fusion), dimensions={1,2} | broadcast | bytes 2949120 | tf_op jit(solution)/shard_map/broadcast_in_dim | solution.py:458
  28.4 4.5 %all-to-all-start = ((bf16[4,64,4608]{2,1,0:T(8,128)(2,1)}), bf16[4,64,4608]{2,1,0:T(8,128)(2,1)}, u32[]{:S(2)}, u32[]{:S(2)}) async-start(bf16[4,64,4608]{2,1,0:T(8,128)(2,1)} %broadcast_in_dim.21), calls=%async_computation | async-start | bytes 4718592 | tf_op jit(solution)/shard_map/all_to_all | solution.py:466
  32.9 1.5 %collective-permute-start.10 = (bf16[32,128,128]{2,1,0:T(8,128)(2,1)}, bf16[32,128,128]{2,1,0:T(8,128)(2,1)S(1)}, u32[]{:S(2)}, u32[]{:S(2)}) collective-permute-start(bf16[32,128,128]{2,1,0:T(8,128)(2,1)} %get-tuple-element.33), channel_id=1, source_target_pairs={{0,2},{1,3},{6,4},{7,5},{8,10},{9,11},{14,12},{15,13},{16,18},{17,... | collective-permute-start | bytes 3145736 | tf_op jit(solution)/shard_map/ppermute | solution.py:470
  34.5 2.2 %copy-done.2 = bf16[32,4,128,128]{3,2,1,0:T(8,128)(2,1)S(1)} copy-done((bf16[32,4,128,128]{3,2,1,0:T(8,128)(2,1)S(1)}, bf16[32,4,128,128]{3,2,1,0:T(8,128)(2,1)}, u32[]{:S(2)}) %copy-start.2) | copy-done | bytes 4194328
  36.6 8.1 %chip_sums.3 = (bf16[32,128,128]{2,1,0:T(8,128)(2,1)}, bf16[32,128,128]{2,1,0:T(8,128)(2,1)}, bf16[32,128,128]{2,1,0:T(8,128)(2,1)}, f32[8,128]{1,0:T(8,128)S(1)}) custom-call(s32[2]{0:T(128)S(1)} %pad_add_fusion.spot_ref, s32[8,264]{1,0:T(8,128)S(1)} %get-tuple-element.31.list_ref, s32[8]{0:T(128)S(1)} %get-tuple-element.32.count_ref, ...), custom_call_target="tpu_custom_call" | custom-call | flops 1024 | bytes 1024 | tf_op jit(solution)/shard_map/chip_sums/pallas_call | solution.py:209
  44.8 12.6 %collective-permute-done.10 = bf16[32,128,128]{2,1,0:T(8,128)(2,1)S(1)} collective-permute-done((bf16[32,128,128]{2,1,0:T(8,128)(2,1)}, bf16[32,128,128]{2,1,0:T(8,128)(2,1)S(1)}, u32[]{:S(2)}, u32[]{:S(2)}) %collective-permute-start.10) | collective-permute-done | bytes 1048608 | tf_op jit(solution)/shard_map/ppermute | solution.py:470
  57.4 1.5 add_convert_fusion.1
  58.9 2.2 %all-to-all-done = bf16[4,64,4608]{2,1,0:T(8,128)(2,1)} async-done(((bf16[4,64,4608]{2,1,0:T(8,128)(2,1)}), bf16[4,64,4608]{2,1,0:T(8,128)(2,1)}, u32[]{:S(2)}, u32[]{:S(2)}) %all-to-all-start) | async-done | bytes 2359328 | tf_op jit(solution)/shard_map/all_to_all | solution.py:466
  61.1 3.1 %collective-permute-start.12 = (bf16[32,128,128]{2,1,0:T(8,128)(2,1)}, bf16[32,128,128]{2,1,0:T(8,128)(2,1)}, u32[]{:S(2)}, u32[]{:S(2)}) collective-permute-start(bf16[32,128,128]{2,1,0:T(8,128)(2,1)} %get-tuple-element.45), channel_id=1, source_target_pairs={{0,2},{1,3},{6,4},{7,5},{8,10},{9,11},{14,12},{15,13},{16,18},{17,... | collective-permute-start | bytes 3145736 | tf_op jit(solution)/shard_map/ppermute | solution.py:470
  65.8 10.4 %student_logits.1 = (f32[4,128,1024]{2,1,0:T(8,128)}, bf16[4608,512]{1,0:T(8,128)(2,1)}) custom-call(s32[2]{0:T(128)S(1)} %pad_add_fusion.spot_ref, f32[8,128]{1,0:T(8,128)S(1)} %add.74.after_ref.mass_ref, bf16[256,4608]{1,0:T(8,128)(2,1)} %bitcast.4.near_ref, bf16[256,4608]{1,0:T(8,128)(2,1)S(1)} %collective-permute-done.11.far_ref, bf16[4608,1024]{1,0:T(8,128)(2,1)} %head_ref.1), custom_call_target="tpu_custom_call" | custom-call | flops 1024 | bytes 1024 | tf_op jit(solution)/shard_map/student_logits/pallas_call | solution.py:251
  76.2 3.6 %all-to-all-start.1 = ((f32[4,128,1024]{2,1,0:T(8,128)}), f32[4,128,1024]{2,1,0:T(8,128)S(1)}, u32[]{:S(2)}, u32[]{:S(2)}) async-start(f32[4,128,1024]{2,1,0:T(8,128)} %get-tuple-element.44), calls=%async_computation.1 | async-start | bytes 4194304 | tf_op jit(solution)/shard_map/all_to_all | solution.py:466
  79.8 5.4 %collective-permute-start.18 = (bf16[32,128,128]{2,1,0:T(8,128)(2,1)}, bf16[32,128,128]{2,1,0:T(8,128)(2,1)}, u32[]{:S(2)}, u32[]{:S(2)}) collective-permute-start(bf16[32,128,128]{2,1,0:T(8,128)(2,1)} %get-tuple-element.52), channel_id=1, source_target_pairs={{0,2},{1,3},{2,0},{3,1},{4,6},{5,7},{6,4},{7,5},{8,10},{9,11},{10,... | collective-permute-start | bytes 3145736 | tf_op jit(solution)/shard_map/ppermute | solution.py:438
  85.2 1.7 %collective-permute-done.12 = bf16[32,128,128]{2,1,0:T(8,128)(2,1)} collective-permute-done((bf16[32,128,128]{2,1,0:T(8,128)(2,1)}, bf16[32,128,128]{2,1,0:T(8,128)(2,1)}, u32[]{:S(2)}, u32[]{:S(2)}) %collective-permute-start.12) | collective-permute-done | bytes 1048608 | tf_op jit(solution)/shard_map/ppermute | solution.py:470
  86.9 5.7 %collective-permute-done.13 = bf16[32,128,128]{2,1,0:T(8,128)(2,1)} collective-permute-done((bf16[32,128,128]{2,1,0:T(8,128)(2,1)}, bf16[32,128,128]{2,1,0:T(8,128)(2,1)}, u32[]{:S(2)}, u32[]{:S(2)}) %collective-permute-start.13) | collective-permute-done | bytes 1048608 | tf_op jit(solution)/shard_map/ppermute | solution.py:470
  92.7 3.0 %add_convert_fusion = bf16[32,128,128]{2,1,0:T(8,128)(2,1)} fusion(bf16[32,128,128]{2,1,0:T(8,128)(2,1)} %collective-permute-done.12, bf16[32,128,128]{2,1,0:T(8,128)(2,1)} %get-tuple-element.45), kind=kLoop, calls=%fused_computation | loop fusion | flops 2097152 | bytes 3145728 | tf_op jit(solution)/shard_map/convert_element_type | solution.py:462
  95.7 1.6 %collective-permute-start.19 = (bf16[32,128,128]{2,1,0:T(8,128)(2,1)}, bf16[32,128,128]{2,1,0:T(8,128)(2,1)}, u32[]{:S(2)}, u32[]{:S(2)}) collective-permute-start(bf16[32,128,128]{2,1,0:T(8,128)(2,1)} %add_convert_fusion), channel_id=1, source_target_pairs={{2,4},{3,5},{4,2},{5,3},{10,12},{11,13},{12,10},{13,11},{18,20},{1... | collective-permute-start | bytes 3145736 | tf_op jit(solution)/shard_map/ppermute | solution.py:470
  98.2 7.0 %all-to-all-done.1.logits_ref.refs_4_ = f32[4,128,1024]{2,1,0:T(8,128)S(1)} async-done(((f32[4,128,1024]{2,1,0:T(8,128)}), f32[4,128,1024]{2,1,0:T(8,128)S(1)}, u32[]{:S(2)}, u32[]{:S(2)}) %all-to-all-start.1) | async-done | bytes 2097184 | tf_op jit(solution)/shard_map/all_to_all | solution.py:466
  107.9 5.0 %collective-permute-start.15 = (f32[8,128]{1,0:T(8,128)S(1)}, f32[8,128]{1,0:T(8,128)S(1)}, u32[]{:S(2)}, u32[]{:S(2)}) collective-permute-start(f32[8,128]{1,0:T(8,128)S(1)} %merge_stats.1.refs_0_), channel_id=1, source_target_pairs={{0,2},{1,3},{2,0},{3,1},{4,6},{5,7},{6,4},{7,5},{8,10},{9,11},{10,... | collective-permute-start | bytes 12296 | tf_op jit(solution)/shard_map/ppermute | solution.py:438
  112.9 2.4 %collective-permute-start.17 = (f32[8,128]{1,0:T(8,128)S(1)}, f32[8,128]{1,0:T(8,128)S(1)}, u32[]{:S(2)}, u32[]{:S(2)}) collective-permute-start(f32[8,128]{1,0:T(8,128)S(1)} %merge_stats.1.refs_0_), channel_id=1, source_target_pairs={{0,6},{1,7},{2,4},{3,5},{4,2},{5,3},{6,0},{7,1},{8,14},{9,15},{10,... | collective-permute-start | bytes 12296 | tf_op jit(solution)/shard_map/ppermute | solution.py:438
  115.3 7.2 %collective-permute-done.16.refs_2_ = f32[8,128]{1,0:T(8,128)S(1)} collective-permute-done((f32[8,128]{1,0:T(8,128)S(1)}, f32[8,128]{1,0:T(8,128)S(1)}, u32[]{:S(2)}, u32[]{:S(2)}) %collective-permute-start.16) | collective-permute-done | bytes 4128 | tf_op jit(solution)/shard_map/ppermute | solution.py:438
  122.7 4.6 %grad_logits.1 = (bf16[128,1024]{1,0:T(8,128)(2,1)}, bf16[128,1024]{1,0:T(8,128)(2,1)}, bf16[128,1024]{1,0:T(8,128)(2,1)}, bf16[128,1024]{1,0:T(8,128)(2,1)}, f32[1,128]{1,0:T(1,128)S(1)}) custom-call(s32[1]{0:T(128)} %bitcast.5.tok_ref, s32[4]{0:T(128)S(1)} %add_multiply_fusion.base_ref, s32[128,1]{1,0:T(8,128)S(1)} %copy.12.labels_ref, ...), custom_call_target="tpu_custom_call" | custom-call | flops 1024 | bytes 1024 | tf_op jit(solution)/shard_map/grad_logits/pallas_call | solution.py:388
  127.3 2.6 %collective-permute-start.23 = (bf16[128,1024]{1,0:T(8,128)(2,1)}, bf16[128,1024]{1,0:T(8,128)(2,1)S(1)}, u32[]{:S(2)}, u32[]{:S(2)}) collective-permute-start(bf16[128,1024]{1,0:T(8,128)(2,1)} %get-tuple-element.56), channel_id=1, source_target_pairs={{0,24},{8,16},{16,8},{24,0},{1,25},{9,17},{17,9},{25,1},{2,26},{10... | collective-permute-start | bytes 786440 | tf_op jit(solution)/shard_map/ppermute | solution.py:438
  132.5 2.9 %collective-permute-done.21 = f32[1,128]{1,0:T(1,128)S(1)} collective-permute-done((f32[1,128]{1,0:T(1,128)S(1)}, f32[1,128]{1,0:T(1,128)S(1)}, u32[]{:S(2)}, u32[]{:S(2)}) %collective-permute-start.21) | collective-permute-done | bytes 544 | tf_op jit(solution)/shard_map/ppermute | solution.py:438
  135.8 4.1 %collective-permute-done.22 = f32[1,128]{1,0:T(1,128)S(1)} collective-permute-done((f32[1,128]{1,0:T(1,128)S(1)}, f32[1,128]{1,0:T(1,128)S(1)}, u32[]{:S(2)}, u32[]{:S(2)}) %collective-permute-start.22) | collective-permute-done | bytes 544 | tf_op jit(solution)/shard_map/ppermute | solution.py:438
  140.6 9.9 %head_product.1 = bf16[4608,1024]{1,0:T(8,128)(2,1)} custom-call(s32[1]{0:T(128)} %bitcast.5.tok_ref, bf16[4608,512]{1,0:T(8,128)(2,1)} %get-tuple-element.55.a_ref, bf16[128,1024]{1,0:T(8,128)(2,1)S(1)} %collective-permute-done.23.refs_0_, bf16[128,1024]{1,0:T(8,128)(2,1)S(1)} %collective-permute-done.24.refs_1_, ...), custom_call_target="tpu_custom_call" | custom-call | flops 1024 | bytes 1024 | tf_op jit(solution)/shard_map/head_product/pallas_call | solution.py:423
  (62 shorter events, 13.6 us)
Async XLA Ops:
  0.6 26.1 %copy-start = (bf16[128,4608]{1,0:T(8,128)(2,1)S(1)}, bf16[128,4608]{1,0:T(8,128)(2,1)}, u32[]{:S(2)}) copy-start(bf16[128,4608]{1,0:T(8,128)(2,1)} %param.7) | copy-start | bytes 3538948
  0.6 21.6 %collective-permute-start.9 = (bf16[32,4,128,128]{3,2,1,0:T(8,128)(2,1)}, bf16[32,4,128,128]{3,2,1,0:T(8,128)(2,1)}, u32[]{:S(2)}, u32[]{:S(2)}) collective-permute-start(bf16[32,4,128,128]{3,2,1,0:T(8,128)(2,1)} %w_own.3), channel_id=1, source_target_pairs={{0,1},{1,0},{2,3},{3,2},{4,5},{5,4},{6,7},{7,6},{8,9},{9,8},{10,11... | collective-permute-start | bytes 12582920 | tf_op jit(solution)/shard_map/ppermute | solution.py:438
  1.2 17.6 %collective-permute-start.1 = (bf16[128,4096]{1,0:T(8,128)(2,1)}, bf16[128,4096]{1,0:T(8,128)(2,1)}, u32[]{:S(2)}, u32[]{:S(2)}) collective-permute-start(bf16[128,4096]{1,0:T(8,128)(2,1)} %x_own.1), channel_id=1, source_target_pairs={{0,1},{1,0},{2,3},{3,2},{4,5},{5,4},{6,7},{7,6},{8,9},{9,8},{10,11... | collective-permute-start | bytes 3145736 | tf_op jit(solution)/shard_map/ppermute | solution.py:438
  3.1 9.8 %collective-permute-start.2 = (f32[8,128]{1,0:T(8,128)S(1)}, f32[8,128]{1,0:T(8,128)S(1)}, u32[]{:S(2)}, u32[]{:S(2)}) collective-permute-start(f32[8,128]{1,0:T(8,128)S(1)} %teacher_stats.1.refs_0_), channel_id=1, source_target_pairs={{0,2},{1,3},{2,0},{3,1},{4,6},{5,7},{6,4},{7,5},{8,10},{9,11},{10,... | collective-permute-start | bytes 12296 | tf_op jit(solution)/shard_map/ppermute | solution.py:438
  7.0 2.7 %collective-permute-start = (s32[128]{0:T(128)S(1)}, s32[128]{0:T(128)S(1)}, u32[]{:S(2)}, u32[]{:S(2)}) collective-permute-start(s32[128]{0:T(128)S(1)} %reshape.23.own_ref), channel_id=1, source_target_pairs={{0,1},{1,0},{2,3},{3,2},{4,5},{5,4},{6,7},{7,6},{8,9},{9,8},{10,11... | collective-permute-start | bytes 1544 | tf_op jit(solution)/shard_map/ppermute | solution.py:438
  7.1 5.8 %collective-permute-start.3 = (f32[8,128]{1,0:T(8,128)S(1)}, f32[8,128]{1,0:T(8,128)S(1)}, u32[]{:S(2)}, u32[]{:S(2)}) collective-permute-start(f32[8,128]{1,0:T(8,128)S(1)} %teacher_stats.1.refs_0_), channel_id=1, source_target_pairs={{0,4},{1,5},{2,6},{3,7},{4,0},{5,1},{6,2},{7,3},{8,12},{9,13},{10,... | collective-permute-start | bytes 12296 | tf_op jit(solution)/shard_map/ppermute | solution.py:438
  9.7 5.4 %collective-permute-start.4 = (f32[8,128]{1,0:T(8,128)S(1)}, f32[8,128]{1,0:T(8,128)S(1)}, u32[]{:S(2)}, u32[]{:S(2)}) collective-permute-start(f32[8,128]{1,0:T(8,128)S(1)} %teacher_stats.1.refs_0_), channel_id=1, source_target_pairs={{0,6},{1,7},{2,4},{3,5},{4,2},{5,3},{6,0},{7,1},{8,14},{9,15},{10,... | collective-permute-start | bytes 12296 | tf_op jit(solution)/shard_map/ppermute | solution.py:438
  12.9 2.3 %collective-permute-start.5 = (f32[8,128]{1,0:T(8,128)S(1)}, f32[8,128]{1,0:T(8,128)S(1)}, u32[]{:S(2)}, u32[]{:S(2)}) collective-permute-start(f32[8,128]{1,0:T(8,128)S(1)} %teacher_stats.1.refs_0_), channel_id=1, source_target_pairs={{0,1},{1,0},{2,3},{3,2},{4,5},{5,4},{6,7},{7,6},{8,9},{9,8},{10,11... | collective-permute-start | bytes 12296 | tf_op jit(solution)/shard_map/ppermute | solution.py:438
  12.9 5.9 %collective-permute-start.6 = (f32[8,128]{1,0:T(8,128)S(1)}, f32[8,128]{1,0:T(8,128)S(1)}, u32[]{:S(2)}, u32[]{:S(2)}) collective-permute-start(f32[8,128]{1,0:T(8,128)S(1)} %collective-permute-done.2.refs_1_), channel_id=1, source_target_pairs={{0,1},{1,0},{2,3},{3,2},{4,5},{5,4},{6,7},{7,6},{8,9},{9,8},{10,11... | collective-permute-start | bytes 12296 | tf_op jit(solution)/shard_map/ppermute | solution.py:438
  15.2 3.6 %collective-permute-start.7 = (f32[8,128]{1,0:T(8,128)S(1)}, f32[8,128]{1,0:T(8,128)S(1)}, u32[]{:S(2)}, u32[]{:S(2)}) collective-permute-start(f32[8,128]{1,0:T(8,128)S(1)} %collective-permute-done.3.refs_2_), channel_id=1, source_target_pairs={{0,1},{1,0},{2,3},{3,2},{4,5},{5,4},{6,7},{7,6},{8,9},{9,8},{10,11... | collective-permute-start | bytes 12296 | tf_op jit(solution)/shard_map/ppermute | solution.py:438
  15.2 3.6 %collective-permute-start.8 = (f32[8,128]{1,0:T(8,128)S(1)}, f32[8,128]{1,0:T(8,128)S(1)}, u32[]{:S(2)}, u32[]{:S(2)}) collective-permute-start(f32[8,128]{1,0:T(8,128)S(1)} %collective-permute-done.4.refs_3_), channel_id=1, source_target_pairs={{0,1},{1,0},{2,3},{3,2},{4,5},{5,4},{6,7},{7,6},{8,9},{9,8},{10,11... | collective-permute-start | bytes 12296 | tf_op jit(solution)/shard_map/ppermute | solution.py:438
  18.7 3.5 %copy-start.1 = (bf16[32,4,128,128]{3,2,1,0:T(8,128)(2,1)S(1)}, bf16[32,4,128,128]{3,2,1,0:T(8,128)(2,1)}, u32[]{:S(2)}) copy-start(bf16[32,4,128,128]{3,2,1,0:T(8,128)(2,1)} %w_own.3) | copy-start | bytes 12582916
  28.4 32.7 %all-to-all-start = ((bf16[4,64,4608]{2,1,0:T(8,128)(2,1)}), bf16[4,64,4608]{2,1,0:T(8,128)(2,1)}, u32[]{:S(2)}, u32[]{:S(2)}) async-start(bf16[4,64,4608]{2,1,0:T(8,128)(2,1)} %broadcast_in_dim.21), calls=%async_computation | async-start | bytes 4718592 | tf_op jit(solution)/shard_map/all_to_all | solution.py:466
  32.9 24.5 %collective-permute-start.10 = (bf16[32,128,128]{2,1,0:T(8,128)(2,1)}, bf16[32,128,128]{2,1,0:T(8,128)(2,1)S(1)}, u32[]{:S(2)}, u32[]{:S(2)}) collective-permute-start(bf16[32,128,128]{2,1,0:T(8,128)(2,1)} %get-tuple-element.33), channel_id=1, source_target_pairs={{0,2},{1,3},{6,4},{7,5},{8,10},{9,11},{14,12},{15,13},{16,18},{17,... | collective-permute-start | bytes 3145736 | tf_op jit(solution)/shard_map/ppermute | solution.py:470
  36.6 20.7 %copy-start.5 = (bf16[32,128,128]{2,1,0:T(8,128)(2,1)S(1)}, bf16[32,128,128]{2,1,0:T(8,128)(2,1)}, u32[]{:S(2)}) copy-start(bf16[32,128,128]{2,1,0:T(8,128)(2,1)} %get-tuple-element.33) | copy-start | bytes 3145732
  61.1 4.7 %collective-permute-start.11 = (bf16[256,4608]{1,0:T(8,128)(2,1)}, bf16[256,4608]{1,0:T(8,128)(2,1)S(1)}, u32[]{:S(2)}, u32[]{:S(2)}) collective-permute-start(bf16[256,4608]{1,0:T(8,128)(2,1)} %bitcast.4.near_ref), channel_id=1, source_target_pairs={{0,1},{1,0},{2,3},{3,2},{4,5},{5,4},{6,7},{7,6},{8,9},{9,8},{10,11... | collective-permute-start | bytes 7077896 | tf_op jit(solution)/shard_map/ppermute | solution.py:438
  61.1 25.8 %collective-permute-start.12 = (bf16[32,128,128]{2,1,0:T(8,128)(2,1)}, bf16[32,128,128]{2,1,0:T(8,128)(2,1)}, u32[]{:S(2)}, u32[]{:S(2)}) collective-permute-start(bf16[32,128,128]{2,1,0:T(8,128)(2,1)} %get-tuple-element.45), channel_id=1, source_target_pairs={{0,2},{1,3},{6,4},{7,5},{8,10},{9,11},{14,12},{15,13},{16,18},{17,... | collective-permute-start | bytes 3145736 | tf_op jit(solution)/shard_map/ppermute | solution.py:470
  64.2 28.5 %collective-permute-start.13 = (bf16[32,128,128]{2,1,0:T(8,128)(2,1)}, bf16[32,128,128]{2,1,0:T(8,128)(2,1)}, u32[]{:S(2)}, u32[]{:S(2)}) collective-permute-start(bf16[32,128,128]{2,1,0:T(8,128)(2,1)} %add_convert_fusion.1), channel_id=1, source_target_pairs={{2,6},{3,7},{4,0},{5,1},{10,14},{11,15},{12,8},{13,9},{18,22},{19,... | collective-permute-start | bytes 3145736 | tf_op jit(solution)/shard_map/ppermute | solution.py:470
  76.2 29.0 %all-to-all-start.1 = ((f32[4,128,1024]{2,1,0:T(8,128)}), f32[4,128,1024]{2,1,0:T(8,128)S(1)}, u32[]{:S(2)}, u32[]{:S(2)}) async-start(f32[4,128,1024]{2,1,0:T(8,128)} %get-tuple-element.44), calls=%async_computation.1 | async-start | bytes 4194304 | tf_op jit(solution)/shard_map/all_to_all | solution.py:466
  79.8 42.8 %collective-permute-start.18 = (bf16[32,128,128]{2,1,0:T(8,128)(2,1)}, bf16[32,128,128]{2,1,0:T(8,128)(2,1)}, u32[]{:S(2)}, u32[]{:S(2)}) collective-permute-start(bf16[32,128,128]{2,1,0:T(8,128)(2,1)} %get-tuple-element.52), channel_id=1, source_target_pairs={{0,2},{1,3},{2,0},{3,1},{4,6},{5,7},{6,4},{7,5},{8,10},{9,11},{10,... | collective-permute-start | bytes 3145736 | tf_op jit(solution)/shard_map/ppermute | solution.py:438
  95.7 27.0 %collective-permute-start.19 = (bf16[32,128,128]{2,1,0:T(8,128)(2,1)}, bf16[32,128,128]{2,1,0:T(8,128)(2,1)}, u32[]{:S(2)}, u32[]{:S(2)}) collective-permute-start(bf16[32,128,128]{2,1,0:T(8,128)(2,1)} %add_convert_fusion), channel_id=1, source_target_pairs={{2,4},{3,5},{4,2},{5,3},{10,12},{11,13},{12,10},{13,11},{18,20},{1... | collective-permute-start | bytes 3145736 | tf_op jit(solution)/shard_map/ppermute | solution.py:470
  105.2 17.4 %copy-start.4 = (bf16[32,128,128]{2,1,0:T(8,128)(2,1)S(1)}, bf16[32,128,128]{2,1,0:T(8,128)(2,1)}, u32[]{:S(2)}) copy-start(bf16[32,128,128]{2,1,0:T(8,128)(2,1)} %get-tuple-element.51) | copy-start | bytes 3145732
  106.6 1.2 collective-permute-start.14
  107.9 7.5 %collective-permute-start.15 = (f32[8,128]{1,0:T(8,128)S(1)}, f32[8,128]{1,0:T(8,128)S(1)}, u32[]{:S(2)}, u32[]{:S(2)}) collective-permute-start(f32[8,128]{1,0:T(8,128)S(1)} %merge_stats.1.refs_0_), channel_id=1, source_target_pairs={{0,2},{1,3},{2,0},{3,1},{4,6},{5,7},{6,4},{7,5},{8,10},{9,11},{10,... | collective-permute-start | bytes 12296 | tf_op jit(solution)/shard_map/ppermute | solution.py:438
  112.9 9.6 %collective-permute-start.16 = (f32[8,128]{1,0:T(8,128)S(1)}, f32[8,128]{1,0:T(8,128)S(1)}, u32[]{:S(2)}, u32[]{:S(2)}) collective-permute-start(f32[8,128]{1,0:T(8,128)S(1)} %merge_stats.1.refs_0_), channel_id=1, source_target_pairs={{0,4},{1,5},{2,6},{3,7},{4,0},{5,1},{6,2},{7,3},{8,12},{9,13},{10,... | collective-permute-start | bytes 12296 | tf_op jit(solution)/shard_map/ppermute | solution.py:438
  112.9 9.6 %collective-permute-start.17 = (f32[8,128]{1,0:T(8,128)S(1)}, f32[8,128]{1,0:T(8,128)S(1)}, u32[]{:S(2)}, u32[]{:S(2)}) collective-permute-start(f32[8,128]{1,0:T(8,128)S(1)} %merge_stats.1.refs_0_), channel_id=1, source_target_pairs={{0,6},{1,7},{2,4},{3,5},{4,2},{5,3},{6,0},{7,1},{8,14},{9,15},{10,... | collective-permute-start | bytes 12296 | tf_op jit(solution)/shard_map/ppermute | solution.py:438
  127.3 13.1 %collective-permute-start.23 = (bf16[128,1024]{1,0:T(8,128)(2,1)}, bf16[128,1024]{1,0:T(8,128)(2,1)S(1)}, u32[]{:S(2)}, u32[]{:S(2)}) collective-permute-start(bf16[128,1024]{1,0:T(8,128)(2,1)} %get-tuple-element.56), channel_id=1, source_target_pairs={{0,24},{8,16},{16,8},{24,0},{1,25},{9,17},{17,9},{25,1},{2,26},{10... | collective-permute-start | bytes 786440 | tf_op jit(solution)/shard_map/ppermute | solution.py:438
  129.9 10.5 %collective-permute-start.24 = (bf16[128,1024]{1,0:T(8,128)(2,1)}, bf16[128,1024]{1,0:T(8,128)(2,1)S(1)}, u32[]{:S(2)}, u32[]{:S(2)}) collective-permute-start(bf16[128,1024]{1,0:T(8,128)(2,1)} %get-tuple-element.57), channel_id=1, source_target_pairs={{0,16},{8,24},{16,0},{24,8},{1,17},{9,25},{17,1},{25,9},{2,18},{10... | collective-permute-start | bytes 786440 | tf_op jit(solution)/shard_map/ppermute | solution.py:438
  130.4 10.2 %collective-permute-start.25 = (bf16[128,1024]{1,0:T(8,128)(2,1)}, bf16[128,1024]{1,0:T(8,128)(2,1)S(1)}, u32[]{:S(2)}, u32[]{:S(2)}) collective-permute-start(bf16[128,1024]{1,0:T(8,128)(2,1)} %get-tuple-element.58), channel_id=1, source_target_pairs={{0,8},{8,0},{16,24},{24,16},{1,9},{9,1},{17,25},{25,17},{2,10},{10... | collective-permute-start | bytes 786440 | tf_op jit(solution)/shard_map/ppermute | solution.py:438
  130.8 1.1 collective-permute-start.20
  131.9 3.5 %collective-permute-start.21 = (f32[1,128]{1,0:T(1,128)S(1)}, f32[1,128]{1,0:T(1,128)S(1)}, u32[]{:S(2)}, u32[]{:S(2)}) collective-permute-start(f32[1,128]{1,0:T(1,128)S(1)} %add.77), channel_id=1, source_target_pairs={{0,2},{1,3},{2,0},{3,1},{4,6},{5,7},{6,4},{7,5},{8,10},{9,11},{10,... | collective-permute-start | bytes 1544 | tf_op jit(solution)/shard_map/ppermute | solution.py:438
  135.5 4.4 %collective-permute-start.22 = (f32[1,128]{1,0:T(1,128)S(1)}, f32[1,128]{1,0:T(1,128)S(1)}, u32[]{:S(2)}, u32[]{:S(2)}) collective-permute-start(f32[1,128]{1,0:T(1,128)S(1)} %add.78), channel_id=1, source_target_pairs={{0,4},{1,5},{2,6},{3,7},{4,0},{5,1},{6,2},{7,3},{8,12},{9,13},{10,... | collective-permute-start | bytes 1544 | tf_op jit(solution)/shard_map/ppermute | solution.py:438
  (2 other events, 3.4 us)
where the time goes:
time: 151 us
  waiting for transfers between devices  48.1 us (32%)
  Pallas kernels  46 us (30%)
  starting transfers between devices  43.5 us (29%)
  local copies, waits for them, and re-layouts  6.12 us (4%)
  other arithmetic  5.86 us (4%)
    ppermute x22, starting transfers between devices, swap(): lax.ppermute(x, axis, [(i, i ^ mask) for i in range(lax.axis_size(axis))])  27.9 us
    ppermute x4, waiting for transfers between devices, send(): lax.ppermute(x, 'vocab', [(2 * a + c, 2 * b + c) for a, b in hops for c i...  20 us
    ppermute x22, waiting for transfers between devices, swap(): lax.ppermute(x, axis, [(i, i ^ mask) for i in range(lax.axis_size(axis))])  18.9 us
    pallas_call x2, Pallas kernels, chip_sums(): pl.pallas_call(functools.partial(sums_kernel, first=first, fan=fan, piece...  12.6 us
    pallas_call x1, Pallas kernels, student_logits(): pl.pallas_call(logits_kernel, grid=(cols // tile,), in_specs=[SMEM_SPEC,...  10.4 us
    pallas_call x1, Pallas kernels, head_product(): pl.pallas_call(product_kernel, grid=(m // tile,), in_specs=[SMEM_SPEC, pl...  9.89 us
    all_to_all x2, waiting for transfers between devices, exchange_tok(): return lax.all_to_all(x, 'tok', split_axis=0, concat_axis=0, tiled=True)  9.23 us
    all_to_all x2, starting transfers between devices, exchange_tok(): return lax.all_to_all(x, 'tok', split_axis=0, concat_axis=0, tiled=True)  8.15 us
  transfers between devices with their start and end apart: 28, of which 13 were waited for; matrix products, arithmetic and copies ran while one was open for 5% of the time, Pallas kernels for 18%

commit v1 on v0

--- a/solution.py
+++ b/solution.py
@@ -219,48 +219,53 @@
     )(spot, lists, counts, probs, w_own, w_peer)
 
 
-def logits_kernel(spot_ref, after_ref, near_ref, far_ref, head_ref, *refs):
-    out_ref, turned_ref, everyone = refs
-    n_tok = out_ref.shape[0]
-    half = near_ref.shape[0] // n_tok
+def logits_kernel(place_ref, after_ref, own_ref, *refs):
+    n_other = (len(refs) - 4) // 2
+    near, far, (head_ref, out_ref, turned_ref, everyone) = refs[:n_other], refs[n_other : 2 * n_other], refs[-4:]
+    rows = own_ref.shape[0]
+    half = rows // 2
     del after_ref
 
     @pl.when(pl.program_id(0) == 0)
     def _():
-        core = spot_ref[0]
-        for r in range(n_tok):
-            source = slice(r * half, (r + 1) * half)
-            for side, ref in ((core, near_ref), (1 - core, far_ref)):
-                start = pl.multiple_of((2 * r + side) * half, half)
-                everyone[pl.ds(start, half), :] = ref[source, :]
+        core, tok = place_ref[0], place_ref[1]
+        everyone[pl.ds(pl.multiple_of(tok * rows, rows), rows), :] = own_ref[...]
+        for r in range(n_other):
+            start = (tok ^ (r + 1)) * rows
+            everyone[pl.ds(pl.multiple_of(start + core * half, half), half), :] = near[r][...]
+            everyone[pl.ds(pl.multiple_of(start + (1 - core) * half, half), half), :] = far[r][...]
 
     result = jnp.dot(everyone[...], head_ref[...], preferred_element_type=F32)
-    for r in range(n_tok):
-        out_ref[r] = result[2 * r * half : 2 * (r + 1) * half, :]
+    for t in range(out_ref.shape[0]):
+        out_ref[t] = result[t * rows : (t + 1) * rows, :]
     part = turned_ref.shape[0]
     start = pl.multiple_of(pl.program_id(0) * part, part)
     turned_ref[...] = everyone[:, pl.ds(start, part)].T
 
 
-def student_logits(spot, after, near, far, head, n_tok):
-    every, depth = 2 * near.shape[0], near.shape[1]
-    rows = every // n_tok
+def student_logits(place, after, own, near, far, head):
+    rows, depth = own.shape
+    n_tok = len(near) + 1
+    every = n_tok * rows
     cols = head.shape[1]
     tile = 256
     whole = lambda shape: pl.BlockSpec(shape, lambda i: (0, 0))
     return pl.pallas_call(
         logits_kernel,
         grid=(cols // tile,),
-        in_specs=[SMEM_SPEC, pl.BlockSpec(memory_space=pl.ANY), whole(near.shape), whole(far.shape)]
+        in_specs=[SMEM_SPEC, pl.BlockSpec(memory_space=pl.ANY), whole(own.shape)]
+        + [whole(x.shape) for x in near + far]
         + [pl.BlockSpec((depth, tile), lambda i: (0, i))],
-        out_specs=[pl.BlockSpec((n_tok, rows, tile), lambda i: (0, 0, i))]
-        + [pl.BlockSpec((depth * tile // cols, every), lambda i: (i, 0))],
+        out_specs=[
+            pl.BlockSpec((n_tok, rows, tile), lambda i: (0, 0, i)),
+            pl.BlockSpec((depth * tile // cols, every), lambda i: (i, 0)),
+        ],
         out_shape=[pltpu.HBM((n_tok, rows, cols), F32), pltpu.HBM((depth, every), BF16)],
         scratch_shapes=[pltpu.VMEM((every, depth), BF16)],
-        compiler_params=params(30),
+        compiler_params=params(32),
         cost_estimate=COST,
         name="student_logits",
-    )(spot, after, near, far, in_hbm(head))
+    )(place, after, own, *near, *far, in_hbm(head))
 
 
 def student_kernel(base_ref, labels_ref, mass_ref, logits_ref, stat_ref):
@@ -406,29 +411,31 @@
 def product_kernel(tok_ref, a_ref, *refs):
     pieces, o_ref, b_ref = refs[:-2], refs[-2], refs[-1]
     rows = pieces[0].shape[0]
-
-    @pl.when(pl.program_id(0) == 0)
+    m, n = pl.program_id(0), pl.program_id(1)
+
+    @pl.when((m == 0) & (n == 0))
     def _():
         for r, piece in enumerate(pieces):
             start = pl.multiple_of(token_group(r, tok_ref, len(pieces)) * rows, rows)
-            b_ref[pl.ds(start, rows), :] = piece[...]
-
-    o_ref[...] = jnp.dot(a_ref[...], b_ref[...], preferred_element_type=F32).astype(o_ref.dtype)
+            for part in range(b_ref.shape[0]):
+                b_ref[part, pl.ds(start, rows), :] = piece[:, part * b_ref.shape[2] : (part + 1) * b_ref.shape[2]]
+
+    o_ref[...] = jnp.dot(a_ref[...], b_ref[n], preferred_element_type=F32).astype(o_ref.dtype)
 
 
 def head_product(tok, a, pieces):
     m, k = a.shape
     rows, n = pieces[0].shape
-    tile = m // 6
+    steps = 2
     return pl.pallas_call(
         product_kernel,
-        grid=(m // tile,),
-        in_specs=[SMEM_SPEC, pl.BlockSpec((tile, k), lambda i: (i, 0))]
-        + [pl.BlockSpec((rows, n), lambda i: (0, 0))] * len(pieces),
-        out_specs=pl.BlockSpec((tile, n), lambda i: (i, 0)),
+        grid=(steps, steps),
+        in_specs=[SMEM_SPEC, pl.BlockSpec((m // steps, k), lambda i, j: (i, 0))]
+        + [pl.BlockSpec((rows, n), lambda i, j: (0, 0))] * len(pieces),
+        out_specs=pl.BlockSpec((m // steps, n // steps), lambda i, j: (i, j)),
         out_shape=jax.ShapeDtypeStruct((m, n), BF16),
-        scratch_shapes=[pltpu.VMEM((k, n), BF16)],
-        compiler_params=params(20),
+        scratch_shapes=[pltpu.VMEM((steps, k, n // steps), BF16)],
+        compiler_params=params(30),
         cost_estimate=COST,
         name="head_product",
     )(tok, in_hbm(a), *pieces[:-1], in_hbm(pieces[-1]))
@@ -450,12 +457,6 @@
 def gather_cores(x):
     chips = gather_chips(x)
     return chips + [swap(chip, "vocab", 1) for chip in chips]
-
-
-def half_rows(hidden, spot, n_tok):
-    half = hidden.shape[0] // 2
-    own = lax.dynamic_slice_in_dim(hidden, spot[0] * half, half)
-    return jnp.broadcast_to(own, (n_tok,) + own.shape)
 
 
 def plus(a, b):
@@ -505,13 +506,13 @@
     lists, counts = plan(code, peer_code, 2 * n_z)
     probs = teacher_probs(teacher_logits, peer_logits, totals)
 
+    half = lax.dynamic_slice_in_dim(hidden, spot[0] * (rows // 2), rows // 2)
     if in_line:
         inward, across, beyond = [(0, 1), (3, 2)], [(1, 2), (2, 1)], [(1, 3), (2, 0)]
         far_outer, mass_a = chip_sums(spot, lists, counts, probs, map_weight, peer_weight, 0, 1, 1, slots)
         first = send(far_outer, inward)
-        rows_in, mass_a = lax.optimization_barrier((hidden, mass_a))
-        copies, probs = lax.optimization_barrier((half_rows(rows_in, spot, n_tok), probs))
-        near = exchange_tok(copies)
+        half, probs, mass_a = lax.optimization_barrier((half, probs, mass_a))
+        near = [swap(half, "tok", r) for r in range(1, n_tok)]
         far_inner, beside, own, mass_b = chip_sums(
             spot, lists, counts, probs, map_weight, peer_weight, 1, 3, 1, slots
         )
@@ -519,7 +520,7 @@
         first, mass = lax.optimization_barrier((first, mass_a + mass_b))
         merged = plus(far_outer, first)
         arrived = send(merged, beyond)
-        near, waited, merged = lax.optimization_barrier((near, beside, merged))
+        *near, waited, merged = lax.optimization_barrier((*near, beside, merged))
         third = swap(waited, "vocab", 2)
     else:
         sums, mass = chip_sums(spot, lists, counts, probs, map_weight, peer_weight, 0, 1, n_z, slots)
@@ -533,11 +534,11 @@
             tiled=True,
         )
         sums = [sums]
-        near = exchange_tok(half_rows(hidden, spot, n_tok))
-
-    near = near.reshape(n_tok * (rows // 2), -1)
-    far = swap(near, "vocab", 1)
-    scores, turned = student_logits(spot, mass, near, far, new_head, n_tok)
+        near = [swap(half, "tok", r) for r in range(1, n_tok)]
+
+    far = [swap(x, "vocab", 1) for x in near]
+    where = jnp.stack([vocab % 2, tok]).astype(jnp.int32)
+    scores, turned = student_logits(where, mass, hidden, near, far, new_head)
     base = (jnp.arange(n_tok, dtype=jnp.int32) * n_vocab + vocab) * new_cols
     label_column = lax.dynamic_slice_in_dim(labels, tok * rows, rows).reshape(rows, 1)
     scores = exchange_tok(scores)

time: 151 us -> 145 us (0.960)
  starting transfers between devices: 43.5 us -> 38.3 us
  waiting for transfers between devices: 48.1 us -> 46 us
    ppermute x4, waiting for transfers between devices: 20 us -> 10.6 us  [send(): lax.ppermute(x, 'vocab', [(2 * a + c, 2 * b + c) for a, b in hops for c i...]
    all_to_all x2 -> x1, waiting for transfers between devices: 9.23 us -> 14.2 us  [exchange_tok(): return lax.all_to_all(x, 'tok', split_axis=0, concat_axis=0, tiled=True)]
    all_to_all x2 -> x1, starting transfers between devices: 8.15 us -> 3.61 us  [exchange_tok(): return lax.all_to_all(x, 'tok', split_axis=0, concat_axis=0, tiled=True)]
    ppermute x22 -> x27, waiting for transfers between devices: 18.9 us -> 21.3 us  [swap(): lax.ppermute(x, axis, [(i, i ^ mask) for i in range(lax.axis_size(axis))])]
    ppermute x22 -> x27, starting transfers between devices: 27.9 us -> 26.2 us  [swap(): lax.ppermute(x, axis, [(i, i ^ mask) for i in range(lax.axis_size(axis))])]
    broadcast_in_dim x1 -> x0, local copies, waits for them, and re-layouts: 1.59 us -> none  [half_rows(): return jnp.broadcast_to(own, (n_tok,) + own.shape)]
    unnamed x12 -> x16, local copies, waits for them, and re-layouts: 3.43 us -> 4.41 us
  transfers between devices with their start and end apart: 28 -> 32, of which waited for: 13 -> 15; matrix products, arithmetic and copies ran while one was open for 5% -> 5% of each run, Pallas kernels for 18% -> 19%
where the time goes in v1:
time: 145 us; the launch traced here: 144 us
  Pallas kernels  46.8 us (32%)
  waiting for transfers between devices  46 us (32%)
  starting transfers between devices  38.3 us (26%)
  other arithmetic  7.07 us (5%)
  local copies, waits for them, and re-layouts  4.83 us (3%)
    ppermute x27, starting transfers between devices, swap(): lax.ppermute(x, axis, [(i, i ^ mask) for i in range(lax.axis_size(axis))])  26.2 us
    ppermute x27, waiting for transfers between devices, swap(): lax.ppermute(x, axis, [(i, i ^ mask) for i in range(lax.axis_size(axis))])  21.3 us
    all_to_all x1, waiting for transfers between devices, exchange_tok(): return lax.all_to_all(x, 'tok', split_axis=0, concat_axis=0, tiled=True)  14.2 us
    pallas_call x2, Pallas kernels, chip_sums(): pl.pallas_call(functools.partial(sums_kernel, first=first, fan=fan, piece...  12.8 us
    ppermute x4, waiting for transfers between devices, send(): lax.ppermute(x, 'vocab', [(2 * a + c, 2 * b + c) for a, b in hops for c i...  10.6 us
    pallas_call x1, Pallas kernels, head_product(): pl.pallas_call(product_kernel, grid=(steps, steps), in_specs=[SMEM_SPEC,...  10.2 us
    pallas_call x1, Pallas kernels, student_logits(): pl.pallas_call(logits_kernel, grid=(cols // tile,), in_specs=[SMEM_SPEC,...  10.1 us
    ppermute x4, starting transfers between devices, send(): lax.ppermute(x, 'vocab', [(2 * a + c, 2 * b + c) for a, b in hops for c i...  8.54 us
  transfers between devices with their start and end apart: 32, of which 15 were waited for; matrix products, arithmetic and copies ran while one was open for 5% of the time, Pallas kernels for 19%

profile of v1, /device:TPU:0, one launch (start us, length us, event | category | flops | bytes accessed | tf_op | source)
XLA Modules:
  0.0 144.0 jit_solution(8834580945621533902)
XLA Ops:
  3.1 3.0 %collective-permute-start.2 = (f32[8,128]{1,0:T(8,128)S(1)}, f32[8,128]{1,0:T(8,128)S(1)}, u32[]{:S(2)}, u32[]{:S(2)}) collective-permute-start(f32[8,128]{1,0:T(8,128)S(1)} %teacher_stats.1.refs_0_), channel_id=1, source_target_pairs={{0,2},{1,3},{2,0},{3,1},{4,6},{5,7},{6,4},{7,5},{8,10},{9,11},{10,... | collective-permute-start | bytes 12296 | tf_op jit(solution)/shard_map/ppermute | solution.py:445
  7.1 2.7 %collective-permute-start.3 = (f32[8,128]{1,0:T(8,128)S(1)}, f32[8,128]{1,0:T(8,128)S(1)}, u32[]{:S(2)}, u32[]{:S(2)}) collective-permute-start(f32[8,128]{1,0:T(8,128)S(1)} %teacher_stats.1.refs_0_), channel_id=1, source_target_pairs={{0,4},{1,5},{2,6},{3,7},{4,0},{5,1},{6,2},{7,3},{8,12},{9,13},{10,... | collective-permute-start | bytes 12296 | tf_op jit(solution)/shard_map/ppermute | solution.py:445
  9.7 3.8 %collective-permute-start.4 = (f32[8,128]{1,0:T(8,128)S(1)}, f32[8,128]{1,0:T(8,128)S(1)}, u32[]{:S(2)}, u32[]{:S(2)}) collective-permute-start(f32[8,128]{1,0:T(8,128)S(1)} %teacher_stats.1.refs_0_), channel_id=1, source_target_pairs={{0,6},{1,7},{2,4},{3,5},{4,2},{5,3},{6,0},{7,1},{8,14},{9,15},{10,... | collective-permute-start | bytes 12296 | tf_op jit(solution)/shard_map/ppermute | solution.py:445
  15.7 3.0 %entry_lists.1 = (s32[8,264]{1,0:T(8,128)S(1)}, s32[8]{0:T(128)S(1)}) custom-call(s32[128]{0:T(128)S(1)} %reshape.18.own_ref, s32[128]{0:T(128)S(1)} %collective-permute-done.peer_ref), custom_call_target="tpu_custom_call" | custom-call | flops 1024 | bytes 1024 | tf_op jit(solution)/shard_map/entry_lists/pallas_call | solution.py:113
  19.8 3.9 %teacher_probs.1 = bf16[2,32,128,128]{3,2,1,0:T(8,128)(2,1)S(1)} custom-call(bf16[128,4096]{1,0:T(8,128)(2,1)} %x_own.1, bf16[128,4096]{1,0:T(8,128)(2,1)} %copy-done.7, f32[8,128]{1,0:T(8,128)S(1)} %teacher_stats.1.refs_0_, f32[8,128]{1,0:T(8,128)S(1)} %collective-permute-done.2.refs_1_, f32[8,128]{1,0:T(8,128)S(1)} %collective-permute-done.3.refs_2_, ...), custom_call_target="tpu_custom_call" | custom-call | flops 1024 | bytes 1024 | tf_op jit(solution)/shard_map/teacher_probs/pallas_call | solution.py:190
  23.7 4.8 %chip_sums.2 = (bf16[32,128,128]{2,1,0:T(8,128)(2,1)}, f32[8,128]{1,0:T(8,128)S(1)}) custom-call(s32[2]{0:T(128)S(1)} %pad_add_fusion.spot_ref, s32[8,264]{1,0:T(8,128)S(1)} %get-tuple-element.32.list_ref, s32[8]{0:T(128)S(1)} %get-tuple-element.33.count_ref, bf16[64,128,128]{2,1,0:T(8,128)(2,1)S(1)} %bitcast.12, bf16[32,4,128,128]{3,2,1,0:T(8,128)(2,1)S(1)} %copy-done.1, ...), custom_call_target="tpu_custom_call" | custom-call | flops 1024 | bytes 1024 | tf_op jit(solution)/shard_map/chip_sums/pallas_call | solution.py:209
  28.5 3.3 %collective-permute-start.10 = (bf16[32,128,128]{2,1,0:T(8,128)(2,1)}, bf16[32,128,128]{2,1,0:T(8,128)(2,1)}, u32[]{:S(2)}, u32[]{:S(2)}) collective-permute-start(bf16[32,128,128]{2,1,0:T(8,128)(2,1)} %get-tuple-element.34), channel_id=1, source_target_pairs={{0,2},{1,3},{6,4},{7,5},{8,10},{9,11},{14,12},{15,13},{16,18},{17,... | collective-permute-start | bytes 3145736 | tf_op jit(solution)/shard_map/ppermute | solution.py:471
  31.8 1.6 %collective-permute-start.11 = (bf16[64,4608]{1,0:T(8,128)(2,1)S(1)}, bf16[64,4608]{1,0:T(8,128)(2,1)}, u32[]{:S(2)}, u32[]{:S(2)}) collective-permute-start(bf16[64,4608]{1,0:T(8,128)(2,1)S(1)} %constant_dynamic-slice_fusion), channel_id=1, source_target_pairs={{0,8},{8,0},{16,24},{24,16},{1,9},{9,1},{17,25},{25,17},{2,10},{10... | collective-permute-start | bytes 1769480 | tf_op jit(solution)/shard_map/ppermute | solution.py:445
  33.4 1.5 %collective-permute-start.12 = (bf16[64,4608]{1,0:T(8,128)(2,1)S(1)}, bf16[64,4608]{1,0:T(8,128)(2,1)}, u32[]{:S(2)}, u32[]{:S(2)}) collective-permute-start(bf16[64,4608]{1,0:T(8,128)(2,1)S(1)} %constant_dynamic-slice_fusion), channel_id=1, source_target_pairs={{0,16},{8,24},{16,0},{24,8},{1,17},{9,25},{17,1},{25,9},{2,18},{10... | collective-permute-start | bytes 1769480 | tf_op jit(solution)/shard_map/ppermute | solution.py:445
  35.4 2.2 %copy-done.2 = bf16[32,4,128,128]{3,2,1,0:T(8,128)(2,1)S(1)} copy-done((bf16[32,4,128,128]{3,2,1,0:T(8,128)(2,1)S(1)}, bf16[32,4,128,128]{3,2,1,0:T(8,128)(2,1)}, u32[]{:S(2)}) %copy-start.2) | copy-done | bytes 4194328
  37.6 8.0 %chip_sums.3 = (bf16[32,128,128]{2,1,0:T(8,128)(2,1)}, bf16[32,128,128]{2,1,0:T(8,128)(2,1)}, bf16[32,128,128]{2,1,0:T(8,128)(2,1)}, f32[8,128]{1,0:T(8,128)S(1)}) custom-call(s32[2]{0:T(128)S(1)} %pad_add_fusion.spot_ref, s32[8,264]{1,0:T(8,128)S(1)} %get-tuple-element.32.list_ref, s32[8]{0:T(128)S(1)} %get-tuple-element.33.count_ref, ...), custom_call_target="tpu_custom_call" | custom-call | flops 1024 | bytes 1024 | tf_op jit(solution)/shard_map/chip_sums/pallas_call | solution.py:209
  45.5 2.3 %collective-permute-start.17 = (bf16[32,128,128]{2,1,0:T(8,128)(2,1)}, bf16[32,128,128]{2,1,0:T(8,128)(2,1)}, u32[]{:S(2)}, u32[]{:S(2)}) collective-permute-start(bf16[32,128,128]{2,1,0:T(8,128)(2,1)} %get-tuple-element.47), channel_id=1, source_target_pairs={{0,2},{1,3},{6,4},{7,5},{8,10},{9,11},{14,12},{15,13},{16,18},{17,... | collective-permute-start | bytes 3145736 | tf_op jit(solution)/shard_map/ppermute | solution.py:471
  47.8 6.8 %collective-permute-done.10 = bf16[32,128,128]{2,1,0:T(8,128)(2,1)} collective-permute-done((bf16[32,128,128]{2,1,0:T(8,128)(2,1)}, bf16[32,128,128]{2,1,0:T(8,128)(2,1)}, u32[]{:S(2)}, u32[]{:S(2)}) %collective-permute-start.10) | collective-permute-done | bytes 1048608 | tf_op jit(solution)/shard_map/ppermute | solution.py:471
  54.6 2.6 %add_convert_fusion.1 = bf16[32,128,128]{2,1,0:T(8,128)(2,1)} fusion(bf16[32,128,128]{2,1,0:T(8,128)(2,1)} %collective-permute-done.10, bf16[32,128,128]{2,1,0:T(8,128)(2,1)S(1)} %copy-done.6), kind=kLoop, calls=%fused_computation.1 | loop fusion | flops 2097152 | bytes 3145728 | tf_op jit(solution)/shard_map/convert_element_type | solution.py:463
  58.5 2.4 %collective-permute-done.12.refs_1_ = bf16[64,4608]{1,0:T(8,128)(2,1)} collective-permute-done((bf16[64,4608]{1,0:T(8,128)(2,1)S(1)}, bf16[64,4608]{1,0:T(8,128)(2,1)}, u32[]{:S(2)}, u32[]{:S(2)}) %collective-permute-start.12) | collective-permute-done | bytes 589856 | tf_op jit(solution)/shard_map/ppermute | solution.py:445
  61.5 1.6 %collective-permute-done.14.refs_3_ = bf16[64,4608]{1,0:T(8,128)(2,1)S(1)} collective-permute-done((bf16[64,4608]{1,0:T(8,128)(2,1)}, bf16[64,4608]{1,0:T(8,128)(2,1)S(1)}, u32[]{:S(2)}, u32[]{:S(2)}) %collective-permute-start.14) | collective-permute-done | bytes 589856 | tf_op jit(solution)/shard_map/ppermute | solution.py:445
  64.8 10.1 %student_logits.1 = (f32[4,128,1024]{2,1,0:T(8,128)}, bf16[4608,512]{1,0:T(8,128)(2,1)}) custom-call(s32[2]{0:T(128)S(1)} %pad_add_fusion.1.place_ref, f32[8,128]{1,0:T(8,128)S(1)} %add.75.after_ref.mass_ref, bf16[128,4608]{1,0:T(8,128)(2,1)S(1)} %copy-done.4, bf16[64,4608]{1,0:T(8,128)(2,1)} %collective-permute-done.11.refs_0_, ...), custom_call_target="tpu_custom_call" | custom-call | flops 1024 | bytes 1024 | tf_op jit(solution)/shard_map/student_logits/pallas_call | solution.py:253
  74.9 3.6 %all-to-all-start = ((f32[4,128,1024]{2,1,0:T(8,128)}), f32[4,128,1024]{2,1,0:T(8,128)S(1)}, u32[]{:S(2)}, u32[]{:S(2)}) async-start(f32[4,128,1024]{2,1,0:T(8,128)} %get-tuple-element.46), calls=%async_computation | async-start | bytes 4194304 | tf_op jit(solution)/shard_map/all_to_all | solution.py:467
  78.5 2.5 %collective-permute-start.23 = (bf16[32,128,128]{2,1,0:T(8,128)(2,1)}, bf16[32,128,128]{2,1,0:T(8,128)(2,1)}, u32[]{:S(2)}, u32[]{:S(2)}) collective-permute-start(bf16[32,128,128]{2,1,0:T(8,128)(2,1)} %get-tuple-element.54), channel_id=1, source_target_pairs={{0,2},{1,3},{2,0},{3,1},{4,6},{5,7},{6,4},{7,5},{8,10},{9,11},{10,... | collective-permute-start | bytes 3145736 | tf_op jit(solution)/shard_map/ppermute | solution.py:445
  81.0 3.7 %collective-permute-done.18 = bf16[32,128,128]{2,1,0:T(8,128)(2,1)} collective-permute-done((bf16[32,128,128]{2,1,0:T(8,128)(2,1)}, bf16[32,128,128]{2,1,0:T(8,128)(2,1)}, u32[]{:S(2)}, u32[]{:S(2)}) %collective-permute-start.18) | collective-permute-done | bytes 1048608 | tf_op jit(solution)/shard_map/ppermute | solution.py:471
  84.7 3.1 %add_convert_fusion = bf16[32,128,128]{2,1,0:T(8,128)(2,1)} fusion(bf16[32,128,128]{2,1,0:T(8,128)(2,1)} %collective-permute-done.17, bf16[32,128,128]{2,1,0:T(8,128)(2,1)} %get-tuple-element.47), kind=kLoop, calls=%fused_computation | loop fusion | flops 2097152 | bytes 3145728 | tf_op jit(solution)/shard_map/convert_element_type | solution.py:463
  87.8 1.7 %collective-permute-start.24 = (bf16[32,128,128]{2,1,0:T(8,128)(2,1)}, bf16[32,128,128]{2,1,0:T(8,128)(2,1)}, u32[]{:S(2)}, u32[]{:S(2)}) collective-permute-start(bf16[32,128,128]{2,1,0:T(8,128)(2,1)} %add_convert_fusion), channel_id=1, source_target_pairs={{2,4},{3,5},{4,2},{5,3},{10,12},{11,13},{12,10},{13,11},{18,20},{1... | collective-permute-start | bytes 3145736 | tf_op jit(solution)/shard_map/ppermute | solution.py:471
  89.8 14.2 %all-to-all-done.logits_ref.refs_4_ = f32[4,128,1024]{2,1,0:T(8,128)S(1)} async-done(((f32[4,128,1024]{2,1,0:T(8,128)}), f32[4,128,1024]{2,1,0:T(8,128)S(1)}, u32[]{:S(2)}, u32[]{:S(2)}) %all-to-all-start) | async-done | bytes 2097184 | tf_op jit(solution)/shard_map/all_to_all | solution.py:467
  104.0 1.4 student_stats.1.refs_0_
  106.6 2.4 %collective-permute-start.20 = (f32[8,128]{1,0:T(8,128)S(1)}, f32[8,128]{1,0:T(8,128)S(1)}, u32[]{:S(2)}, u32[]{:S(2)}) collective-permute-start(f32[8,128]{1,0:T(8,128)S(1)} %merge_stats.1.refs_0_), channel_id=1, source_target_pairs={{0,2},{1,3},{2,0},{3,1},{4,6},{5,7},{6,4},{7,5},{8,10},{9,11},{10,... | collective-permute-start | bytes 12296 | tf_op jit(solution)/shard_map/ppermute | solution.py:445
  111.5 2.1 %collective-permute-done.21.refs_2_ = f32[8,128]{1,0:T(8,128)S(1)} collective-permute-done((f32[8,128]{1,0:T(8,128)S(1)}, f32[8,128]{1,0:T(8,128)S(1)}, u32[]{:S(2)}, u32[]{:S(2)}) %collective-permute-start.21) | collective-permute-done | bytes 4128 | tf_op jit(solution)/shard_map/ppermute | solution.py:445
  113.6 1.9 %collective-permute-done.22.refs_3_ = f32[8,128]{1,0:T(8,128)S(1)} collective-permute-done((f32[8,128]{1,0:T(8,128)S(1)}, f32[8,128]{1,0:T(8,128)S(1)}, u32[]{:S(2)}, u32[]{:S(2)}) %collective-permute-start.22) | collective-permute-done | bytes 4128 | tf_op jit(solution)/shard_map/ppermute | solution.py:445
  115.6 4.7 %grad_logits.1 = (bf16[128,1024]{1,0:T(8,128)(2,1)}, bf16[128,1024]{1,0:T(8,128)(2,1)}, bf16[128,1024]{1,0:T(8,128)(2,1)}, bf16[128,1024]{1,0:T(8,128)(2,1)}, f32[1,128]{1,0:T(1,128)S(1)}) custom-call(s32[1]{0:T(128)} %bitcast.4.tok_ref, s32[4]{0:T(128)S(1)} %add_multiply_fusion.base_ref, s32[128,1]{1,0:T(8,128)S(1)} %copy.12.labels_ref, ...), custom_call_target="tpu_custom_call" | custom-call | flops 1024 | bytes 1024 | tf_op jit(solution)/shard_map/grad_logits/pallas_call | solution.py:393
  121.7 1.5 %collective-permute-start.29 = (bf16[128,1024]{1,0:T(8,128)(2,1)}, bf16[128,1024]{1,0:T(8,128)(2,1)S(1)}, u32[]{:S(2)}, u32[]{:S(2)}) collective-permute-start(bf16[128,1024]{1,0:T(8,128)(2,1)} %get-tuple-element.59), channel_id=1, source_target_pairs={{0,16},{8,24},{16,0},{24,8},{1,17},{9,25},{17,1},{25,9},{2,18},{10... | collective-permute-start | bytes 786440 | tf_op jit(solution)/shard_map/ppermute | solution.py:445
  124.9 3.5 %collective-permute-done.26 = f32[1,128]{1,0:T(1,128)S(1)} collective-permute-done((f32[1,128]{1,0:T(1,128)S(1)}, f32[1,128]{1,0:T(1,128)S(1)}, u32[]{:S(2)}, u32[]{:S(2)}) %collective-permute-start.26) | collective-permute-done | bytes 544 | tf_op jit(solution)/shard_map/ppermute | solution.py:445
  128.6 4.3 %collective-permute-done.27 = f32[1,128]{1,0:T(1,128)S(1)} collective-permute-done((f32[1,128]{1,0:T(1,128)S(1)}, f32[1,128]{1,0:T(1,128)S(1)}, u32[]{:S(2)}, u32[]{:S(2)}) %collective-permute-start.27) | collective-permute-done | bytes 544 | tf_op jit(solution)/shard_map/ppermute | solution.py:445
  133.8 10.2 %head_product.1 = bf16[4608,1024]{1,0:T(8,128)(2,1)} custom-call(s32[1]{0:T(128)} %bitcast.4.tok_ref, bf16[4608,512]{1,0:T(8,128)(2,1)} %get-tuple-element.57.a_ref, bf16[128,1024]{1,0:T(8,128)(2,1)S(1)} %collective-permute-done.28.refs_0_, bf16[128,1024]{1,0:T(8,128)(2,1)S(1)} %collective-permute-done.29.refs_1_, ...), custom_call_target="tpu_custom_call" | custom-call | flops 1024 | bytes 1024 | tf_op jit(solution)/shard_map/head_product/pallas_call | solution.py:430
  (74 shorter events, 18.7 us)
Async XLA Ops:
  0.6 23.0 %collective-permute-start.9 = (bf16[32,4,128,128]{3,2,1,0:T(8,128)(2,1)}, bf16[32,4,128,128]{3,2,1,0:T(8,128)(2,1)}, u32[]{:S(2)}, u32[]{:S(2)}) collective-permute-start(bf16[32,4,128,128]{3,2,1,0:T(8,128)(2,1)} %w_own.3), channel_id=1, source_target_pairs={{0,1},{1,0},{2,3},{3,2},{4,5},{5,4},{6,7},{7,6},{8,9},{9,8},{10,11... | collective-permute-start | bytes 12582920 | tf_op jit(solution)/shard_map/ppermute | solution.py:445
  1.2 17.6 %collective-permute-start.1 = (bf16[128,4096]{1,0:T(8,128)(2,1)}, bf16[128,4096]{1,0:T(8,128)(2,1)S(1)}, u32[]{:S(2)}, u32[]{:S(2)}) collective-permute-start(bf16[128,4096]{1,0:T(8,128)(2,1)} %x_own.1), channel_id=1, source_target_pairs={{0,1},{1,0},{2,3},{3,2},{4,5},{5,4},{6,7},{7,6},{8,9},{9,8},{10,11... | collective-permute-start | bytes 3145736 | tf_op jit(solution)/shard_map/ppermute | solution.py:445
  3.1 10.5 %collective-permute-start.2 = (f32[8,128]{1,0:T(8,128)S(1)}, f32[8,128]{1,0:T(8,128)S(1)}, u32[]{:S(2)}, u32[]{:S(2)}) collective-permute-start(f32[8,128]{1,0:T(8,128)S(1)} %teacher_stats.1.refs_0_), channel_id=1, source_target_pairs={{0,2},{1,3},{2,0},{3,1},{4,6},{5,7},{6,4},{7,5},{8,10},{9,11},{10,... | collective-permute-start | bytes 12296 | tf_op jit(solution)/shard_map/ppermute | solution.py:445
  7.0 2.7 %collective-permute-start = (s32[128]{0:T(128)S(1)}, s32[128]{0:T(128)S(1)}, u32[]{:S(2)}, u32[]{:S(2)}) collective-permute-start(s32[128]{0:T(128)S(1)} %reshape.18.own_ref), channel_id=1, source_target_pairs={{0,1},{1,0},{2,3},{3,2},{4,5},{5,4},{6,7},{7,6},{8,9},{9,8},{10,11... | collective-permute-start | bytes 1544 | tf_op jit(solution)/shard_map/ppermute | solution.py:445
  7.1 6.5 %collective-permute-start.3 = (f32[8,128]{1,0:T(8,128)S(1)}, f32[8,128]{1,0:T(8,128)S(1)}, u32[]{:S(2)}, u32[]{:S(2)}) collective-permute-start(f32[8,128]{1,0:T(8,128)S(1)} %teacher_stats.1.refs_0_), channel_id=1, source_target_pairs={{0,4},{1,5},{2,6},{3,7},{4,0},{5,1},{6,2},{7,3},{8,12},{9,13},{10,... | collective-permute-start | bytes 12296 | tf_op jit(solution)/shard_map/ppermute | solution.py:445
  9.7 5.4 %collective-permute-start.4 = (f32[8,128]{1,0:T(8,128)S(1)}, f32[8,128]{1,0:T(8,128)S(1)}, u32[]{:S(2)}, u32[]{:S(2)}) collective-permute-start(f32[8,128]{1,0:T(8,128)S(1)} %teacher_stats.1.refs_0_), channel_id=1, source_target_pairs={{0,6},{1,7},{2,4},{3,5},{4,2},{5,3},{6,0},{7,1},{8,14},{9,15},{10,... | collective-permute-start | bytes 12296 | tf_op jit(solution)/shard_map/ppermute | solution.py:445
  13.5 1.6 %collective-permute-start.5 = (f32[8,128]{1,0:T(8,128)S(1)}, f32[8,128]{1,0:T(8,128)S(1)}, u32[]{:S(2)}, u32[]{:S(2)}) collective-permute-start(f32[8,128]{1,0:T(8,128)S(1)} %teacher_stats.1.refs_0_), channel_id=1, source_target_pairs={{0,1},{1,0},{2,3},{3,2},{4,5},{5,4},{6,7},{7,6},{8,9},{9,8},{10,11... | collective-permute-start | bytes 12296 | tf_op jit(solution)/shard_map/ppermute | solution.py:445
  13.6 5.2 %collective-permute-start.6 = (f32[8,128]{1,0:T(8,128)S(1)}, f32[8,128]{1,0:T(8,128)S(1)}, u32[]{:S(2)}, u32[]{:S(2)}) collective-permute-start(f32[8,128]{1,0:T(8,128)S(1)} %collective-permute-done.2.refs_1_), channel_id=1, source_target_pairs={{0,1},{1,0},{2,3},{3,2},{4,5},{5,4},{6,7},{7,6},{8,9},{9,8},{10,11... | collective-permute-start | bytes 12296 | tf_op jit(solution)/shard_map/ppermute | solution.py:445
  15.2 3.6 %collective-permute-start.7 = (f32[8,128]{1,0:T(8,128)S(1)}, f32[8,128]{1,0:T(8,128)S(1)}, u32[]{:S(2)}, u32[]{:S(2)}) collective-permute-start(f32[8,128]{1,0:T(8,128)S(1)} %collective-permute-done.3.refs_2_), channel_id=1, source_target_pairs={{0,1},{1,0},{2,3},{3,2},{4,5},{5,4},{6,7},{7,6},{8,9},{9,8},{10,11... | collective-permute-start | bytes 12296 | tf_op jit(solution)/shard_map/ppermute | solution.py:445
  15.2 3.6 %collective-permute-start.8 = (f32[8,128]{1,0:T(8,128)S(1)}, f32[8,128]{1,0:T(8,128)S(1)}, u32[]{:S(2)}, u32[]{:S(2)}) collective-permute-start(f32[8,128]{1,0:T(8,128)S(1)} %collective-permute-done.4.refs_3_), channel_id=1, source_target_pairs={{0,1},{1,0},{2,3},{3,2},{4,5},{5,4},{6,7},{7,6},{8,9},{9,8},{10,11... | collective-permute-start | bytes 12296 | tf_op jit(solution)/shard_map/ppermute | solution.py:445
  28.5 26.1 %collective-permute-start.10 = (bf16[32,128,128]{2,1,0:T(8,128)(2,1)}, bf16[32,128,128]{2,1,0:T(8,128)(2,1)}, u32[]{:S(2)}, u32[]{:S(2)}) collective-permute-start(bf16[32,128,128]{2,1,0:T(8,128)(2,1)} %get-tuple-element.34), channel_id=1, source_target_pairs={{0,2},{1,3},{6,4},{7,5},{8,10},{9,11},{14,12},{15,13},{16,18},{17,... | collective-permute-start | bytes 3145736 | tf_op jit(solution)/shard_map/ppermute | solution.py:471
  31.8 26.7 %collective-permute-start.11 = (bf16[64,4608]{1,0:T(8,128)(2,1)S(1)}, bf16[64,4608]{1,0:T(8,128)(2,1)}, u32[]{:S(2)}, u32[]{:S(2)}) collective-permute-start(bf16[64,4608]{1,0:T(8,128)(2,1)S(1)} %constant_dynamic-slice_fusion), channel_id=1, source_target_pairs={{0,8},{8,0},{16,24},{24,16},{1,9},{9,1},{17,25},{25,17},{2,10},{10... | collective-permute-start | bytes 1769480 | tf_op jit(solution)/shard_map/ppermute | solution.py:445
  33.4 27.4 %collective-permute-start.12 = (bf16[64,4608]{1,0:T(8,128)(2,1)S(1)}, bf16[64,4608]{1,0:T(8,128)(2,1)}, u32[]{:S(2)}, u32[]{:S(2)}) collective-permute-start(bf16[64,4608]{1,0:T(8,128)(2,1)S(1)} %constant_dynamic-slice_fusion), channel_id=1, source_target_pairs={{0,16},{8,24},{16,0},{24,8},{1,17},{9,25},{17,1},{25,9},{2,18},{10... | collective-permute-start | bytes 1769480 | tf_op jit(solution)/shard_map/ppermute | solution.py:445
  35.0 25.9 %collective-permute-start.13 = (bf16[64,4608]{1,0:T(8,128)(2,1)S(1)}, bf16[64,4608]{1,0:T(8,128)(2,1)}, u32[]{:S(2)}, u32[]{:S(2)}) collective-permute-start(bf16[64,4608]{1,0:T(8,128)(2,1)S(1)} %constant_dynamic-slice_fusion), channel_id=1, source_target_pairs={{0,24},{8,16},{16,8},{24,0},{1,25},{9,17},{17,9},{25,1},{2,26},{10... | collective-permute-start | bytes 1769480 | tf_op jit(solution)/shard_map/ppermute | solution.py:445
  45.5 35.5 %collective-permute-start.17 = (bf16[32,128,128]{2,1,0:T(8,128)(2,1)}, bf16[32,128,128]{2,1,0:T(8,128)(2,1)}, u32[]{:S(2)}, u32[]{:S(2)}) collective-permute-start(bf16[32,128,128]{2,1,0:T(8,128)(2,1)} %get-tuple-element.47), channel_id=1, source_target_pairs={{0,2},{1,3},{6,4},{7,5},{8,10},{9,11},{14,12},{15,13},{16,18},{17,... | collective-permute-start | bytes 3145736 | tf_op jit(solution)/shard_map/ppermute | solution.py:471
  57.2 27.5 %collective-permute-start.18 = (bf16[32,128,128]{2,1,0:T(8,128)(2,1)}, bf16[32,128,128]{2,1,0:T(8,128)(2,1)}, u32[]{:S(2)}, u32[]{:S(2)}) collective-permute-start(bf16[32,128,128]{2,1,0:T(8,128)(2,1)} %add_convert_fusion.1), channel_id=1, source_target_pairs={{2,6},{3,7},{4,0},{5,1},{10,14},{11,15},{12,8},{13,9},{18,22},{19,... | collective-permute-start | bytes 3145736 | tf_op jit(solution)/shard_map/ppermute | solution.py:471
  60.9 2.2 %collective-permute-start.14 = (bf16[64,4608]{1,0:T(8,128)(2,1)}, bf16[64,4608]{1,0:T(8,128)(2,1)S(1)}, u32[]{:S(2)}, u32[]{:S(2)}) collective-permute-start(bf16[64,4608]{1,0:T(8,128)(2,1)} %collective-permute-done.11.refs_0_), channel_id=1, source_target_pairs={{0,1},{1,0},{2,3},{3,2},{4,5},{5,4},{6,7},{7,6},{8,9},{9,8},{10,11... | collective-permute-start | bytes 1769480 | tf_op jit(solution)/shard_map/ppermute | solution.py:445
  60.9 3.1 %collective-permute-start.15 = (bf16[64,4608]{1,0:T(8,128)(2,1)}, bf16[64,4608]{1,0:T(8,128)(2,1)S(1)}, u32[]{:S(2)}, u32[]{:S(2)}) collective-permute-start(bf16[64,4608]{1,0:T(8,128)(2,1)} %collective-permute-done.12.refs_1_), channel_id=1, source_target_pairs={{0,1},{1,0},{2,3},{3,2},{4,5},{5,4},{6,7},{7,6},{8,9},{9,8},{10,11... | collective-permute-start | bytes 1769480 | tf_op jit(solution)/shard_map/ppermute | solution.py:445
  61.4 3.4 %collective-permute-start.16 = (bf16[64,4608]{1,0:T(8,128)(2,1)}, bf16[64,4608]{1,0:T(8,128)(2,1)S(1)}, u32[]{:S(2)}, u32[]{:S(2)}) collective-permute-start(bf16[64,4608]{1,0:T(8,128)(2,1)} %collective-permute-done.13.refs_2_), channel_id=1, source_target_pairs={{0,1},{1,0},{2,3},{3,2},{4,5},{5,4},{6,7},{7,6},{8,9},{9,8},{10,11... | collective-permute-start | bytes 1769480 | tf_op jit(solution)/shard_map/ppermute | solution.py:445
  74.9 29.0 %all-to-all-start = ((f32[4,128,1024]{2,1,0:T(8,128)}), f32[4,128,1024]{2,1,0:T(8,128)S(1)}, u32[]{:S(2)}, u32[]{:S(2)}) async-start(f32[4,128,1024]{2,1,0:T(8,128)} %get-tuple-element.46), calls=%async_computation | async-start | bytes 4194304 | tf_op jit(solution)/shard_map/all_to_all | solution.py:467
  78.5 37.1 %collective-permute-start.23 = (bf16[32,128,128]{2,1,0:T(8,128)(2,1)}, bf16[32,128,128]{2,1,0:T(8,128)(2,1)}, u32[]{:S(2)}, u32[]{:S(2)}) collective-permute-start(bf16[32,128,128]{2,1,0:T(8,128)(2,1)} %get-tuple-element.54), channel_id=1, source_target_pairs={{0,2},{1,3},{2,0},{3,1},{4,6},{5,7},{6,4},{7,5},{8,10},{9,11},{10,... | collective-permute-start | bytes 3145736 | tf_op jit(solution)/shard_map/ppermute | solution.py:445
  87.8 27.8 %collective-permute-start.24 = (bf16[32,128,128]{2,1,0:T(8,128)(2,1)}, bf16[32,128,128]{2,1,0:T(8,128)(2,1)}, u32[]{:S(2)}, u32[]{:S(2)}) collective-permute-start(bf16[32,128,128]{2,1,0:T(8,128)(2,1)} %add_convert_fusion), channel_id=1, source_target_pairs={{2,4},{3,5},{4,2},{5,3},{10,12},{11,13},{12,10},{13,11},{18,20},{1... | collective-permute-start | bytes 3145736 | tf_op jit(solution)/shard_map/ppermute | solution.py:471
  105.4 1.2 collective-permute-start.19
  106.6 4.9 %collective-permute-start.20 = (f32[8,128]{1,0:T(8,128)S(1)}, f32[8,128]{1,0:T(8,128)S(1)}, u32[]{:S(2)}, u32[]{:S(2)}) collective-permute-start(f32[8,128]{1,0:T(8,128)S(1)} %merge_stats.1.refs_0_), channel_id=1, source_target_pairs={{0,2},{1,3},{2,0},{3,1},{4,6},{5,7},{6,4},{7,5},{8,10},{9,11},{10,... | collective-permute-start | bytes 12296 | tf_op jit(solution)/shard_map/ppermute | solution.py:445
  109.0 4.5 %collective-permute-start.21 = (f32[8,128]{1,0:T(8,128)S(1)}, f32[8,128]{1,0:T(8,128)S(1)}, u32[]{:S(2)}, u32[]{:S(2)}) collective-permute-start(f32[8,128]{1,0:T(8,128)S(1)} %merge_stats.1.refs_0_), channel_id=1, source_target_pairs={{0,4},{1,5},{2,6},{3,7},{4,0},{5,1},{6,2},{7,3},{8,12},{9,13},{10,... | collective-permute-start | bytes 12296 | tf_op jit(solution)/shard_map/ppermute | solution.py:445
  110.1 5.4 %collective-permute-start.22 = (f32[8,128]{1,0:T(8,128)S(1)}, f32[8,128]{1,0:T(8,128)S(1)}, u32[]{:S(2)}, u32[]{:S(2)}) collective-permute-start(f32[8,128]{1,0:T(8,128)S(1)} %merge_stats.1.refs_0_), channel_id=1, source_target_pairs={{0,6},{1,7},{2,4},{3,5},{4,2},{5,3},{6,0},{7,1},{8,14},{9,15},{10,... | collective-permute-start | bytes 12296 | tf_op jit(solution)/shard_map/ppermute | solution.py:445
  120.3 13.1 %collective-permute-start.28 = (bf16[128,1024]{1,0:T(8,128)(2,1)}, bf16[128,1024]{1,0:T(8,128)(2,1)S(1)}, u32[]{:S(2)}, u32[]{:S(2)}) collective-permute-start(bf16[128,1024]{1,0:T(8,128)(2,1)} %get-tuple-element.58), channel_id=1, source_target_pairs={{0,24},{8,16},{16,8},{24,0},{1,25},{9,17},{17,9},{25,1},{2,26},{10... | collective-permute-start | bytes 786440 | tf_op jit(solution)/shard_map/ppermute | solution.py:445
  121.7 12.0 %collective-permute-start.29 = (bf16[128,1024]{1,0:T(8,128)(2,1)}, bf16[128,1024]{1,0:T(8,128)(2,1)S(1)}, u32[]{:S(2)}, u32[]{:S(2)}) collective-permute-start(bf16[128,1024]{1,0:T(8,128)(2,1)} %get-tuple-element.59), channel_id=1, source_target_pairs={{0,16},{8,24},{16,0},{24,8},{1,17},{9,25},{17,1},{25,9},{2,18},{10... | collective-permute-start | bytes 786440 | tf_op jit(solution)/shard_map/ppermute | solution.py:445
  123.2 10.6 %collective-permute-start.30 = (bf16[128,1024]{1,0:T(8,128)(2,1)}, bf16[128,1024]{1,0:T(8,128)(2,1)S(1)}, u32[]{:S(2)}, u32[]{:S(2)}) collective-permute-start(bf16[128,1024]{1,0:T(8,128)(2,1)} %get-tuple-element.60), channel_id=1, source_target_pairs={{0,8},{8,0},{16,24},{24,16},{1,9},{9,1},{17,25},{25,17},{2,10},{10... | collective-permute-start | bytes 786440 | tf_op jit(solution)/shard_map/ppermute | solution.py:445
  123.8 1.1 collective-permute-start.25
  124.9 3.5 %collective-permute-start.26 = (f32[1,128]{1,0:T(1,128)S(1)}, f32[1,128]{1,0:T(1,128)S(1)}, u32[]{:S(2)}, u32[]{:S(2)}) collective-permute-start(f32[1,128]{1,0:T(1,128)S(1)} %add.78), channel_id=1, source_target_pairs={{0,2},{1,3},{2,0},{3,1},{4,6},{5,7},{6,4},{7,5},{8,10},{9,11},{10,... | collective-permute-start | bytes 1544 | tf_op jit(solution)/shard_map/ppermute | solution.py:445
  128.5 4.4 %collective-permute-start.27 = (f32[1,128]{1,0:T(1,128)S(1)}, f32[1,128]{1,0:T(1,128)S(1)}, u32[]{:S(2)}, u32[]{:S(2)}) collective-permute-start(f32[1,128]{1,0:T(1,128)S(1)} %add.79), channel_id=1, source_target_pairs={{0,4},{1,5},{2,6},{3,7},{4,0},{5,1},{6,2},{7,3},{8,12},{9,13},{10,... | collective-permute-start | bytes 1544 | tf_op jit(solution)/shard_map/ppermute | solution.py:445
  (8 other events, 160.1 us)

commit v2 on v1

--- a/solution.py
+++ b/solution.py
@@ -24,6 +24,10 @@
 
 def in_hbm(x):
     return pltpu.with_memory_space_constraint(x, pltpu.HBM)
+
+
+def in_vmem(x):
+    return pltpu.with_memory_space_constraint(x, pltpu.VMEM)
 
 
 def tree(op, items):
@@ -228,19 +232,19 @@
 
     @pl.when(pl.program_id(0) == 0)
     def _():
-        core, tok = place_ref[0], place_ref[1]
-        everyone[pl.ds(pl.multiple_of(tok * rows, rows), rows), :] = own_ref[...]
+        core = place_ref[0]
+        everyone[0:rows, :] = own_ref[...]
         for r in range(n_other):
-            start = (tok ^ (r + 1)) * rows
+            start = (r + 1) * rows
             everyone[pl.ds(pl.multiple_of(start + core * half, half), half), :] = near[r][...]
             everyone[pl.ds(pl.multiple_of(start + (1 - core) * half, half), half), :] = far[r][...]
 
     result = jnp.dot(everyone[...], head_ref[...], preferred_element_type=F32)
-    for t in range(out_ref.shape[0]):
-        out_ref[t] = result[t * rows : (t + 1) * rows, :]
-    part = turned_ref.shape[0]
+    for r in range(n_other + 1):
+        out_ref[place_ref[1] ^ r] = result[r * rows : (r + 1) * rows, :]
+    part = turned_ref.shape[0] // pl.num_programs(0)
     start = pl.multiple_of(pl.program_id(0) * part, part)
-    turned_ref[...] = everyone[:, pl.ds(start, part)].T
+    turned_ref[pl.ds(start, part), :] = everyone[:, pl.ds(start, part)].T
 
 
 def student_logits(place, after, own, near, far, head):
@@ -258,9 +262,9 @@
         + [pl.BlockSpec((depth, tile), lambda i: (0, i))],
         out_specs=[
             pl.BlockSpec((n_tok, rows, tile), lambda i: (0, 0, i)),
-            pl.BlockSpec((depth * tile // cols, every), lambda i: (i, 0)),
+            VMEM_SPEC,
         ],
-        out_shape=[pltpu.HBM((n_tok, rows, cols), F32), pltpu.HBM((depth, every), BF16)],
+        out_shape=[pltpu.HBM((n_tok, rows, cols), F32), pltpu.VMEM((depth, every), BF16)],
         scratch_shapes=[pltpu.VMEM((every, depth), BF16)],
         compiler_params=params(32),
         cost_estimate=COST,
@@ -382,7 +386,7 @@
 
 
 def token_group(step, tok_ref, n_tok):
-    return tok_ref[0] ^ (n_tok - 1 - step)
+    return tok_ref[0] ^ ((step + 1) % n_tok)
 
 
 def grad_logits(tok, base, label_column, columns, sums, logits):
@@ -408,37 +412,66 @@
     )(tok, base, label_column, columns, *sums, logits)
 
 
-def product_kernel(tok_ref, a_ref, *refs):
-    pieces, o_ref, b_ref = refs[:-2], refs[-2], refs[-1]
+def stack_pieces(pieces, b_ref):
     rows = pieces[0].shape[0]
-    m, n = pl.program_id(0), pl.program_id(1)
-
-    @pl.when((m == 0) & (n == 0))
+
+    @pl.when(pl.program_id(0) == 0)
     def _():
         for r, piece in enumerate(pieces):
-            start = pl.multiple_of(token_group(r, tok_ref, len(pieces)) * rows, rows)
-            for part in range(b_ref.shape[0]):
-                b_ref[part, pl.ds(start, rows), :] = piece[:, part * b_ref.shape[2] : (part + 1) * b_ref.shape[2]]
-
-    o_ref[...] = jnp.dot(a_ref[...], b_ref[n], preferred_element_type=F32).astype(o_ref.dtype)
-
-
-def head_product(tok, a, pieces):
-    m, k = a.shape
+            b_ref[r * rows : (r + 1) * rows, :] = piece[...]
+
+
+def product_part(a_ref, b_ref, first):
+    tile = a_ref.shape[0] // pl.num_programs(0)
+    rows = pl.ds(pl.multiple_of(pl.program_id(0) * tile, tile), tile)
+    return rows, jnp.dot(a_ref[rows, first : first + b_ref.shape[0]], b_ref[...], preferred_element_type=F32)
+
+
+def first_product_kernel(a_ref, *refs):
+    pieces, (acc_ref, b_ref) = refs[:-2], refs[-2:]
+    stack_pieces(pieces, b_ref)
+    rows, part = product_part(a_ref, b_ref, 0)
+    acc_ref[rows, :] = part
+
+
+def last_product_kernel(a_ref, acc_ref, *refs):
+    pieces, (o_ref, end_ref, b_ref) = refs[:-3], refs[-3:]
+    stack_pieces(pieces, b_ref)
+    rows, part = product_part(a_ref, b_ref, a_ref.shape[1] - b_ref.shape[0])
+    o_ref[...] = (acc_ref[rows, :] + part).astype(o_ref.dtype)
+    end_ref[...] = jnp.zeros_like(end_ref)
+
+
+def first_product(a, pieces):
     rows, n = pieces[0].shape
-    steps = 2
-    return pl.pallas_call(
-        product_kernel,
-        grid=(steps, steps),
-        in_specs=[SMEM_SPEC, pl.BlockSpec((m // steps, k), lambda i, j: (i, 0))]
-        + [pl.BlockSpec((rows, n), lambda i, j: (0, 0))] * len(pieces),
-        out_specs=pl.BlockSpec((m // steps, n // steps), lambda i, j: (i, j)),
-        out_shape=jax.ShapeDtypeStruct((m, n), BF16),
-        scratch_shapes=[pltpu.VMEM((steps, k, n // steps), BF16)],
-        compiler_params=params(30),
-        cost_estimate=COST,
-        name="head_product",
-    )(tok, in_hbm(a), *pieces[:-1], in_hbm(pieces[-1]))
+    return pl.pallas_call(
+        first_product_kernel,
+        grid=(4,),
+        in_specs=[VMEM_SPEC] + [pl.BlockSpec((rows, n), lambda i: (0, 0))] * len(pieces),
+        out_specs=VMEM_SPEC,
+        out_shape=pltpu.VMEM((a.shape[0], n), F32),
+        scratch_shapes=[pltpu.VMEM((len(pieces) * rows, n), BF16)],
+        compiler_params=params(16),
+        cost_estimate=COST,
+        name="first_product",
+    )(in_vmem(a), in_hbm(pieces[0]), *pieces[1:])
+
+
+def last_product(a, acc, pieces):
+    m = a.shape[0]
+    rows, n = pieces[0].shape
+    steps = 4
+    return pl.pallas_call(
+        last_product_kernel,
+        grid=(steps,),
+        in_specs=[VMEM_SPEC] * 2 + [pl.BlockSpec((rows, n), lambda i: (0, 0))] * len(pieces),
+        out_specs=[pl.BlockSpec((m // steps, n), lambda i: (i, 0)), pl.BlockSpec((1, rows), lambda i: (0, 0))],
+        out_shape=[jax.ShapeDtypeStruct((m, n), BF16), jax.ShapeDtypeStruct((1, rows), F32)],
+        scratch_shapes=[pltpu.VMEM((len(pieces) * rows, n), BF16)],
+        compiler_params=params(20),
+        cost_estimate=COST,
+        name="last_product",
+    )(in_vmem(a), in_vmem(acc), *pieces)
 
 
 def swap(x, axis, mask):
@@ -555,12 +588,16 @@
     group = tok.astype(jnp.int32).reshape(1)
     columns, base_loss = token_totals(stats)
     *grads, inner = grad_logits(group, base, label_column, columns, sums, scores)
-    grads = [swap(x, "tok", n_tok - 1 - r) for r, x in enumerate(grads[:-1])] + [grads[-1]]
+    grads = [grads[-1]] + [swap(x, "tok", r + 1) for r, x in enumerate(grads[:-1])]
+    split = n_tok // 2
+    acc = first_product(turned, grads[:split])
+    head_grad, end = last_product(turned, acc, grads[split:])
     mask = 1
     while mask < n_vocab:
-        inner = inner + swap(inner, "vocab", mask)
+        other = swap(inner, "vocab", mask)
+        inner = inner + other
         mask *= 2
-    return ((base_loss - inner).reshape(rows), head_product(group, turned, grads))
+    return ((base_loss - inner + end).reshape(rows), head_grad)
 
 
 def solution(mesh):

time: 145 us -> 142 us (0.979)
  waiting for transfers between devices: 46 us -> 41 us
  local copies, waits for them, and re-layouts: 4.83 us -> 7.02 us
    ppermute x27, waiting for transfers between devices: 21.3 us -> 17.2 us  [swap(): lax.ppermute(x, axis, [(i, i ^ mask) for i in range(lax.axis_size(axis))])]
    ppermute x4, waiting for transfers between devices: 10.6 us -> 8.27 us  [send(): lax.ppermute(x, 'vocab', [(2 * a + c, 2 * b + c) for a, b in hops for c i...]
    unnamed x16 -> x22, local copies, waits for them, and re-layouts: 4.41 us -> 6.6 us
    pallas_call x1 -> x2, Pallas kernels: 10.2 us -> 9.44 us  [the longest x1 5.32 us: last_product(): pl.pallas_call(last_product_kernel, grid=(steps,), in_specs=[VMEM_SPEC] *...]
  transfers between devices with their start and end apart: 32 -> 32, of which waited for: 15 -> 15; matrix products, arithmetic and copies ran while one was open for 5% -> 5% of each run, Pallas kernels for 19% -> 26%
where the time goes in v2:
time: 142 us
  Pallas kernels  46.3 us (33%)
  waiting for transfers between devices  41 us (29%)
  starting transfers between devices  39.6 us (28%)
  local copies, waits for them, and re-layouts  7.02 us (5%)
  other arithmetic  7 us (5%)
    ppermute x27, starting transfers between devices, swap(): lax.ppermute(x, axis, [(i, i ^ mask) for i in range(lax.axis_size(axis))])  27.3 us
    ppermute x27, waiting for transfers between devices, swap(): lax.ppermute(x, axis, [(i, i ^ mask) for i in range(lax.axis_size(axis))])  17.2 us
    all_to_all x1, waiting for transfers between devices, exchange_tok(): return lax.all_to_all(x, 'tok', split_axis=0, concat_axis=0, tiled=True)  15.6 us
    pallas_call x2, Pallas kernels, chip_sums(): pl.pallas_call(functools.partial(sums_kernel, first=first, fan=fan, piece...  13.3 us
    pallas_call x1, Pallas kernels, student_logits(): pl.pallas_call(logits_kernel, grid=(cols // tile,), in_specs=[SMEM_SPEC,...  9.55 us
    ppermute x4, starting transfers between devices, send(): lax.ppermute(x, 'vocab', [(2 * a + c, 2 * b + c) for a, b in hops for c i...  8.71 us
    ppermute x4, waiting for transfers between devices, send(): lax.ppermute(x, 'vocab', [(2 * a + c, 2 * b + c) for a, b in hops for c i...  8.27 us
    unnamed x22, local copies, waits for them, and re-layouts  6.6 us
  transfers between devices with their start and end apart: 32, of which 15 were waited for; matrix products, arithmetic and copies ran while one was open for 5% of the time, Pallas kernels for 26%

profile of v2, /device:TPU:0, one launch (start us, length us, event | category | flops | bytes accessed | tf_op | source)
XLA Modules:
  0.0 141.8 jit_solution(14259059138899460617)
XLA Ops:
  3.1 3.0 %collective-permute-start.2 = (f32[8,128]{1,0:T(8,128)S(1)}, f32[8,128]{1,0:T(8,128)S(1)}, u32[]{:S(2)}, u32[]{:S(2)}) collective-permute-start(f32[8,128]{1,0:T(8,128)S(1)} %teacher_stats.1.refs_0_), channel_id=1, source_target_pairs={{0,2},{1,3},{2,0},{3,1},{4,6},{5,7},{6,4},{7,5},{8,10},{9,11},{10,... | collective-permute-start | bytes 12296 | tf_op jit(solution)/shard_map/ppermute | solution.py:478
  7.1 2.7 %collective-permute-start.3 = (f32[8,128]{1,0:T(8,128)S(1)}, f32[8,128]{1,0:T(8,128)S(1)}, u32[]{:S(2)}, u32[]{:S(2)}) collective-permute-start(f32[8,128]{1,0:T(8,128)S(1)} %teacher_stats.1.refs_0_), channel_id=1, source_target_pairs={{0,4},{1,5},{2,6},{3,7},{4,0},{5,1},{6,2},{7,3},{8,12},{9,13},{10,... | collective-permute-start | bytes 12296 | tf_op jit(solution)/shard_map/ppermute | solution.py:478
  9.7 3.8 %collective-permute-start.4 = (f32[8,128]{1,0:T(8,128)S(1)}, f32[8,128]{1,0:T(8,128)S(1)}, u32[]{:S(2)}, u32[]{:S(2)}) collective-permute-start(f32[8,128]{1,0:T(8,128)S(1)} %teacher_stats.1.refs_0_), channel_id=1, source_target_pairs={{0,6},{1,7},{2,4},{3,5},{4,2},{5,3},{6,0},{7,1},{8,14},{9,15},{10,... | collective-permute-start | bytes 12296 | tf_op jit(solution)/shard_map/ppermute | solution.py:478
  15.7 3.0 %entry_lists.1 = (s32[8,264]{1,0:T(8,128)S(1)}, s32[8]{0:T(128)S(1)}) custom-call(s32[128]{0:T(128)S(1)} %reshape.18.own_ref, s32[128]{0:T(128)S(1)} %collective-permute-done.peer_ref), custom_call_target="tpu_custom_call" | custom-call | flops 1024 | bytes 1024 | tf_op jit(solution)/shard_map/entry_lists/pallas_call | solution.py:117
  19.8 3.9 %teacher_probs.1 = bf16[2,32,128,128]{3,2,1,0:T(8,128)(2,1)S(1)} custom-call(bf16[128,4096]{1,0:T(8,128)(2,1)} %x_own.1, bf16[128,4096]{1,0:T(8,128)(2,1)} %copy-done.10, f32[8,128]{1,0:T(8,128)S(1)} %teacher_stats.1.refs_0_, f32[8,128]{1,0:T(8,128)S(1)} %collective-permute-done.2.refs_1_, f32[8,128]{1,0:T(8,128)S(1)} %collective-permute-done.3.refs_2_, ...), custom_call_target="tpu_custom_call" | custom-call | flops 1024 | bytes 1024 | tf_op jit(solution)/shard_map/teacher_probs/pallas_call | solution.py:194
  23.7 4.8 %chip_sums.2 = (bf16[32,128,128]{2,1,0:T(8,128)(2,1)}, f32[8,128]{1,0:T(8,128)S(1)}) custom-call(s32[2]{0:T(128)S(1)} %pad_add_fusion.spot_ref, s32[8,264]{1,0:T(8,128)S(1)} %get-tuple-element.34.list_ref, s32[8]{0:T(128)S(1)} %get-tuple-element.35.count_ref, bf16[64,128,128]{2,1,0:T(8,128)(2,1)S(1)} %bitcast.12, bf16[32,4,128,128]{3,2,1,0:T(8,128)(2,1)S(1)} %copy-done.4, ...), custom_call_target="tpu_custom_call" | custom-call | flops 1024 | bytes 1024 | tf_op jit(solution)/shard_map/chip_sums/pallas_call | solution.py:213
  28.5 3.5 %collective-permute-start.10 = (bf16[32,128,128]{2,1,0:T(8,128)(2,1)}, bf16[32,128,128]{2,1,0:T(8,128)(2,1)}, u32[]{:S(2)}, u32[]{:S(2)}) collective-permute-start(bf16[32,128,128]{2,1,0:T(8,128)(2,1)} %get-tuple-element.36), channel_id=1, source_target_pairs={{0,2},{1,3},{6,4},{7,5},{8,10},{9,11},{14,12},{15,13},{16,18},{17,... | collective-permute-start | bytes 3145736 | tf_op jit(solution)/shard_map/ppermute | solution.py:504
  32.1 1.6 %collective-permute-start.11 = (bf16[64,4608]{1,0:T(8,128)(2,1)S(1)}, bf16[64,4608]{1,0:T(8,128)(2,1)}, u32[]{:S(2)}, u32[]{:S(2)}) collective-permute-start(bf16[64,4608]{1,0:T(8,128)(2,1)S(1)} %constant_dynamic-slice_fusion), channel_id=1, source_target_pairs={{0,8},{8,0},{16,24},{24,16},{1,9},{9,1},{17,25},{25,17},{2,10},{10... | collective-permute-start | bytes 1769480 | tf_op jit(solution)/shard_map/ppermute | solution.py:478
  33.6 1.5 %collective-permute-start.12 = (bf16[64,4608]{1,0:T(8,128)(2,1)S(1)}, bf16[64,4608]{1,0:T(8,128)(2,1)}, u32[]{:S(2)}, u32[]{:S(2)}) collective-permute-start(bf16[64,4608]{1,0:T(8,128)(2,1)S(1)} %constant_dynamic-slice_fusion), channel_id=1, source_target_pairs={{0,16},{8,24},{16,0},{24,8},{1,17},{9,25},{17,1},{25,9},{2,18},{10... | collective-permute-start | bytes 1769480 | tf_op jit(solution)/shard_map/ppermute | solution.py:478
  35.6 2.2 %copy-done.5 = bf16[32,4,128,128]{3,2,1,0:T(8,128)(2,1)S(1)} copy-done((bf16[32,4,128,128]{3,2,1,0:T(8,128)(2,1)S(1)}, bf16[32,4,128,128]{3,2,1,0:T(8,128)(2,1)}, u32[]{:S(2)}) %copy-start.5) | copy-done | bytes 4194328
  37.8 8.5 %chip_sums.3 = (bf16[32,128,128]{2,1,0:T(8,128)(2,1)}, bf16[32,128,128]{2,1,0:T(8,128)(2,1)}, bf16[32,128,128]{2,1,0:T(8,128)(2,1)}, f32[8,128]{1,0:T(8,128)S(1)}) custom-call(s32[2]{0:T(128)S(1)} %pad_add_fusion.spot_ref, s32[8,264]{1,0:T(8,128)S(1)} %get-tuple-element.34.list_ref, s32[8]{0:T(128)S(1)} %get-tuple-element.35.count_ref, ...), custom_call_target="tpu_custom_call" | custom-call | flops 1024 | bytes 1024 | tf_op jit(solution)/shard_map/chip_sums/pallas_call | solution.py:213
  46.3 2.3 %collective-permute-start.17 = (bf16[32,128,128]{2,1,0:T(8,128)(2,1)}, bf16[32,128,128]{2,1,0:T(8,128)(2,1)}, u32[]{:S(2)}, u32[]{:S(2)}) collective-permute-start(bf16[32,128,128]{2,1,0:T(8,128)(2,1)} %get-tuple-element.49), channel_id=1, source_target_pairs={{0,2},{1,3},{6,4},{7,5},{8,10},{9,11},{14,12},{15,13},{16,18},{17,... | collective-permute-start | bytes 3145736 | tf_op jit(solution)/shard_map/ppermute | solution.py:504
  48.6 6.3 %collective-permute-done.10 = bf16[32,128,128]{2,1,0:T(8,128)(2,1)} collective-permute-done((bf16[32,128,128]{2,1,0:T(8,128)(2,1)}, bf16[32,128,128]{2,1,0:T(8,128)(2,1)}, u32[]{:S(2)}, u32[]{:S(2)}) %collective-permute-start.10) | collective-permute-done | bytes 1048608 | tf_op jit(solution)/shard_map/ppermute | solution.py:504
  54.9 2.5 %add_convert_fusion.1 = bf16[32,128,128]{2,1,0:T(8,128)(2,1)} fusion(bf16[32,128,128]{2,1,0:T(8,128)(2,1)} %collective-permute-done.10, bf16[32,128,128]{2,1,0:T(8,128)(2,1)S(1)} %copy-done.9), kind=kLoop, calls=%fused_computation.1 | loop fusion | flops 2097152 | bytes 3145728 | tf_op jit(solution)/shard_map/convert_element_type | solution.py:496
  58.8 1.8 %collective-permute-done.12.refs_1_ = bf16[64,4608]{1,0:T(8,128)(2,1)} collective-permute-done((bf16[64,4608]{1,0:T(8,128)(2,1)S(1)}, bf16[64,4608]{1,0:T(8,128)(2,1)}, u32[]{:S(2)}, u32[]{:S(2)}) %collective-permute-start.12) | collective-permute-done | bytes 589856 | tf_op jit(solution)/shard_map/ppermute | solution.py:478
  61.1 1.6 %collective-permute-done.14.refs_3_ = bf16[64,4608]{1,0:T(8,128)(2,1)S(1)} collective-permute-done((bf16[64,4608]{1,0:T(8,128)(2,1)}, bf16[64,4608]{1,0:T(8,128)(2,1)S(1)}, u32[]{:S(2)}, u32[]{:S(2)}) %collective-permute-start.14) | collective-permute-done | bytes 589856 | tf_op jit(solution)/shard_map/ppermute | solution.py:478
  64.4 9.5 %student_logits.1 = (f32[4,128,1024]{2,1,0:T(8,128)}, bf16[4608,512]{1,0:T(8,128)(2,1)S(1)}) custom-call(s32[2]{0:T(128)S(1)} %pad_add_fusion.1.place_ref, f32[8,128]{1,0:T(8,128)S(1)} %add.78.after_ref.mass_ref, bf16[128,4608]{1,0:T(8,128)(2,1)S(1)} %copy-done.7, bf16[64,4608]{1,0:T(8,128)(2,1)} %collective-permute-done.11.refs_0_, ...), custom_call_target="tpu_custom_call" | custom-call | flops 1024 | bytes 1024 | tf_op jit(solution)/shard_map/student_logits/pallas_call | solution.py:257
  74.0 2.2 %copy-done.2 = bf16[4608,512]{1,0:T(8,128)(2,1)} copy-done((bf16[4608,512]{1,0:T(8,128)(2,1)}, bf16[4608,512]{1,0:T(8,128)(2,1)S(1)}, u32[]{:S(2)}) %copy-start.2) | copy-done | bytes 4718616
  76.2 3.6 %all-to-all-start = ((f32[4,128,1024]{2,1,0:T(8,128)}), f32[4,128,1024]{2,1,0:T(8,128)S(1)}, u32[]{:S(2)}, u32[]{:S(2)}) async-start(f32[4,128,1024]{2,1,0:T(8,128)} %get-tuple-element.48), calls=%async_computation | async-start | bytes 4194304 | tf_op jit(solution)/shard_map/all_to_all | solution.py:500
  79.8 3.0 %collective-permute-start.23 = (bf16[32,128,128]{2,1,0:T(8,128)(2,1)}, bf16[32,128,128]{2,1,0:T(8,128)(2,1)}, u32[]{:S(2)}, u32[]{:S(2)}) collective-permute-start(bf16[32,128,128]{2,1,0:T(8,128)(2,1)} %get-tuple-element.56), channel_id=1, source_target_pairs={{0,2},{1,3},{2,0},{3,1},{4,6},{5,7},{6,4},{7,5},{8,10},{9,11},{10,... | collective-permute-start | bytes 3145736 | tf_op jit(solution)/shard_map/ppermute | solution.py:478
  82.8 1.9 %collective-permute-done.18 = bf16[32,128,128]{2,1,0:T(8,128)(2,1)} collective-permute-done((bf16[32,128,128]{2,1,0:T(8,128)(2,1)}, bf16[32,128,128]{2,1,0:T(8,128)(2,1)}, u32[]{:S(2)}, u32[]{:S(2)}) %collective-permute-start.18) | collective-permute-done | bytes 1048608 | tf_op jit(solution)/shard_map/ppermute | solution.py:504
  84.7 3.1 %add_convert_fusion = bf16[32,128,128]{2,1,0:T(8,128)(2,1)} fusion(bf16[32,128,128]{2,1,0:T(8,128)(2,1)} %collective-permute-done.17, bf16[32,128,128]{2,1,0:T(8,128)(2,1)} %get-tuple-element.49), kind=kLoop, calls=%fused_computation | loop fusion | flops 2097152 | bytes 3145728 | tf_op jit(solution)/shard_map/convert_element_type | solution.py:496
  87.8 1.6 %collective-permute-start.24 = (bf16[32,128,128]{2,1,0:T(8,128)(2,1)}, bf16[32,128,128]{2,1,0:T(8,128)(2,1)}, u32[]{:S(2)}, u32[]{:S(2)}) collective-permute-start(bf16[32,128,128]{2,1,0:T(8,128)(2,1)} %add_convert_fusion), channel_id=1, source_target_pairs={{2,4},{3,5},{4,2},{5,3},{10,12},{11,13},{12,10},{13,11},{18,20},{1... | collective-permute-start | bytes 3145736 | tf_op jit(solution)/shard_map/ppermute | solution.py:504
  89.6 15.6 %all-to-all-done.logits_ref.refs_4_ = f32[4,128,1024]{2,1,0:T(8,128)S(1)} async-done(((f32[4,128,1024]{2,1,0:T(8,128)}), f32[4,128,1024]{2,1,0:T(8,128)S(1)}, u32[]{:S(2)}, u32[]{:S(2)}) %all-to-all-start) | async-done | bytes 2097184 | tf_op jit(solution)/shard_map/all_to_all | solution.py:500
  107.8 3.0 %collective-permute-start.20 = (f32[8,128]{1,0:T(8,128)S(1)}, f32[8,128]{1,0:T(8,128)S(1)}, u32[]{:S(2)}, u32[]{:S(2)}) collective-permute-start(f32[8,128]{1,0:T(8,128)S(1)} %merge_stats.1.refs_0_), channel_id=1, source_target_pairs={{0,2},{1,3},{2,0},{3,1},{4,6},{5,7},{6,4},{7,5},{8,10},{9,11},{10,... | collective-permute-start | bytes 12296 | tf_op jit(solution)/shard_map/ppermute | solution.py:478
  113.3 2.1 %collective-permute-done.21.refs_2_ = f32[8,128]{1,0:T(8,128)S(1)} collective-permute-done((f32[8,128]{1,0:T(8,128)S(1)}, f32[8,128]{1,0:T(8,128)S(1)}, u32[]{:S(2)}, u32[]{:S(2)}) %collective-permute-start.21) | collective-permute-done | bytes 4128 | tf_op jit(solution)/shard_map/ppermute | solution.py:478
  115.3 1.9 %collective-permute-done.22.refs_3_ = f32[8,128]{1,0:T(8,128)S(1)} collective-permute-done((f32[8,128]{1,0:T(8,128)S(1)}, f32[8,128]{1,0:T(8,128)S(1)}, u32[]{:S(2)}, u32[]{:S(2)}) %collective-permute-start.22) | collective-permute-done | bytes 4128 | tf_op jit(solution)/shard_map/ppermute | solution.py:478
  117.4 4.9 %grad_logits.1 = (bf16[128,1024]{1,0:T(8,128)(2,1)}, bf16[128,1024]{1,0:T(8,128)(2,1)}, bf16[128,1024]{1,0:T(8,128)(2,1)}, bf16[128,1024]{1,0:T(8,128)(2,1)}, f32[1,128]{1,0:T(1,128)S(1)}) custom-call(s32[1]{0:T(128)} %bitcast.4.tok_ref, s32[4]{0:T(128)S(1)} %add_multiply_fusion.base_ref, s32[128,1]{1,0:T(8,128)S(1)} %copy.12.labels_ref, ...), custom_call_target="tpu_custom_call" | custom-call | flops 1024 | bytes 1024 | tf_op jit(solution)/shard_map/grad_logits/pallas_call | solution.py:397
  124.3 1.5 %collective-permute-start.30 = (bf16[128,1024]{1,0:T(8,128)(2,1)}, bf16[128,1024]{1,0:T(8,128)(2,1)S(1)}, u32[]{:S(2)}, u32[]{:S(2)}) collective-permute-start(bf16[128,1024]{1,0:T(8,128)(2,1)} %get-tuple-element.63), channel_id=1, source_target_pairs={{0,24},{8,16},{16,8},{24,0},{1,25},{9,17},{17,9},{25,1},{2,26},{10... | collective-permute-start | bytes 786440 | tf_op jit(solution)/shard_map/ppermute | solution.py:478
  127.0 3.5 %collective-permute-done.26 = f32[1,128]{1,0:T(1,128)S(1)} collective-permute-done((f32[1,128]{1,0:T(1,128)S(1)}, f32[1,128]{1,0:T(1,128)S(1)}, u32[]{:S(2)}, u32[]{:S(2)}) %collective-permute-start.26) | collective-permute-done | bytes 544 | tf_op jit(solution)/shard_map/ppermute | solution.py:478
  131.8 4.1 %first_product.1.acc_ref = f32[4608,1024]{1,0:T(8,128)S(1)} custom-call(bf16[4608,512]{1,0:T(8,128)(2,1)S(1)} %copy-done.3, bf16[128,1024]{1,0:T(8,128)(2,1)} %get-tuple-element.60.refs_0_, bf16[128,1024]{1,0:T(8,128)(2,1)S(1)} %collective-permute-done.28.refs_1_), custom_call_target="tpu_custom_call" | custom-call | flops 1024 | bytes 1024 | tf_op jit(solution)/shard_map/first_product/pallas_call | solution.py:447
  136.0 5.3 %last_product.1 = (bf16[4608,1024]{1,0:T(8,128)(2,1)}, f32[1,128]{1,0:T(1,128)S(1)}) custom-call(bf16[4608,512]{1,0:T(8,128)(2,1)S(1)} %copy-done.3, f32[4608,1024]{1,0:T(8,128)S(1)} %first_product.1.acc_ref, bf16[128,1024]{1,0:T(8,128)(2,1)S(1)} %collective-permute-done.29.refs_0_, bf16[128,1024]{1,0:T(8,128)(2,1)S(1)} %collective-permute-done.30.refs_1_), custom_call_target="tpu_custom_call" | custom-call | flops 1024 | bytes 1024 | tf_op jit(solution)/shard_map/last_product/pallas_call | solution.py:464
  (81 shorter events, 21.1 us)
Async XLA Ops:
  0.6 23.0 %collective-permute-start.9 = (bf16[32,4,128,128]{3,2,1,0:T(8,128)(2,1)}, bf16[32,4,128,128]{3,2,1,0:T(8,128)(2,1)}, u32[]{:S(2)}, u32[]{:S(2)}) collective-permute-start(bf16[32,4,128,128]{3,2,1,0:T(8,128)(2,1)} %w_own.3), channel_id=1, source_target_pairs={{0,1},{1,0},{2,3},{3,2},{4,5},{5,4},{6,7},{7,6},{8,9},{9,8},{10,11... | collective-permute-start | bytes 12582920 | tf_op jit(solution)/shard_map/ppermute | solution.py:478
  1.2 17.6 %collective-permute-start.1 = (bf16[128,4096]{1,0:T(8,128)(2,1)}, bf16[128,4096]{1,0:T(8,128)(2,1)S(1)}, u32[]{:S(2)}, u32[]{:S(2)}) collective-permute-start(bf16[128,4096]{1,0:T(8,128)(2,1)} %x_own.1), channel_id=1, source_target_pairs={{0,1},{1,0},{2,3},{3,2},{4,5},{5,4},{6,7},{7,6},{8,9},{9,8},{10,11... | collective-permute-start | bytes 3145736 | tf_op jit(solution)/shard_map/ppermute | solution.py:478
  3.1 10.5 %collective-permute-start.2 = (f32[8,128]{1,0:T(8,128)S(1)}, f32[8,128]{1,0:T(8,128)S(1)}, u32[]{:S(2)}, u32[]{:S(2)}) collective-permute-start(f32[8,128]{1,0:T(8,128)S(1)} %teacher_stats.1.refs_0_), channel_id=1, source_target_pairs={{0,2},{1,3},{2,0},{3,1},{4,6},{5,7},{6,4},{7,5},{8,10},{9,11},{10,... | collective-permute-start | bytes 12296 | tf_op jit(solution)/shard_map/ppermute | solution.py:478
  7.0 2.7 %collective-permute-start = (s32[128]{0:T(128)S(1)}, s32[128]{0:T(128)S(1)}, u32[]{:S(2)}, u32[]{:S(2)}) collective-permute-start(s32[128]{0:T(128)S(1)} %reshape.18.own_ref), channel_id=1, source_target_pairs={{0,1},{1,0},{2,3},{3,2},{4,5},{5,4},{6,7},{7,6},{8,9},{9,8},{10,11... | collective-permute-start | bytes 1544 | tf_op jit(solution)/shard_map/ppermute | solution.py:478
  7.1 6.5 %collective-permute-start.3 = (f32[8,128]{1,0:T(8,128)S(1)}, f32[8,128]{1,0:T(8,128)S(1)}, u32[]{:S(2)}, u32[]{:S(2)}) collective-permute-start(f32[8,128]{1,0:T(8,128)S(1)} %teacher_stats.1.refs_0_), channel_id=1, source_target_pairs={{0,4},{1,5},{2,6},{3,7},{4,0},{5,1},{6,2},{7,3},{8,12},{9,13},{10,... | collective-permute-start | bytes 12296 | tf_op jit(solution)/shard_map/ppermute | solution.py:478
  9.7 5.4 %collective-permute-start.4 = (f32[8,128]{1,0:T(8,128)S(1)}, f32[8,128]{1,0:T(8,128)S(1)}, u32[]{:S(2)}, u32[]{:S(2)}) collective-permute-start(f32[8,128]{1,0:T(8,128)S(1)} %teacher_stats.1.refs_0_), channel_id=1, source_target_pairs={{0,6},{1,7},{2,4},{3,5},{4,2},{5,3},{6,0},{7,1},{8,14},{9,15},{10,... | collective-permute-start | bytes 12296 | tf_op jit(solution)/shard_map/ppermute | solution.py:478
  13.5 1.6 %collective-permute-start.5 = (f32[8,128]{1,0:T(8,128)S(1)}, f32[8,128]{1,0:T(8,128)S(1)}, u32[]{:S(2)}, u32[]{:S(2)}) collective-permute-start(f32[8,128]{1,0:T(8,128)S(1)} %teacher_stats.1.refs_0_), channel_id=1, source_target_pairs={{0,1},{1,0},{2,3},{3,2},{4,5},{5,4},{6,7},{7,6},{8,9},{9,8},{10,11... | collective-permute-start | bytes 12296 | tf_op jit(solution)/shard_map/ppermute | solution.py:478
  13.6 5.2 %collective-permute-start.6 = (f32[8,128]{1,0:T(8,128)S(1)}, f32[8,128]{1,0:T(8,128)S(1)}, u32[]{:S(2)}, u32[]{:S(2)}) collective-permute-start(f32[8,128]{1,0:T(8,128)S(1)} %collective-permute-done.2.refs_1_), channel_id=1, source_target_pairs={{0,1},{1,0},{2,3},{3,2},{4,5},{5,4},{6,7},{7,6},{8,9},{9,8},{10,11... | collective-permute-start | bytes 12296 | tf_op jit(solution)/shard_map/ppermute | solution.py:478
  15.2 3.6 %collective-permute-start.7 = (f32[8,128]{1,0:T(8,128)S(1)}, f32[8,128]{1,0:T(8,128)S(1)}, u32[]{:S(2)}, u32[]{:S(2)}) collective-permute-start(f32[8,128]{1,0:T(8,128)S(1)} %collective-permute-done.3.refs_2_), channel_id=1, source_target_pairs={{0,1},{1,0},{2,3},{3,2},{4,5},{5,4},{6,7},{7,6},{8,9},{9,8},{10,11... | collective-permute-start | bytes 12296 | tf_op jit(solution)/shard_map/ppermute | solution.py:478
  15.2 3.6 %collective-permute-start.8 = (f32[8,128]{1,0:T(8,128)S(1)}, f32[8,128]{1,0:T(8,128)S(1)}, u32[]{:S(2)}, u32[]{:S(2)}) collective-permute-start(f32[8,128]{1,0:T(8,128)S(1)} %collective-permute-done.4.refs_3_), channel_id=1, source_target_pairs={{0,1},{1,0},{2,3},{3,2},{4,5},{5,4},{6,7},{7,6},{8,9},{9,8},{10,11... | collective-permute-start | bytes 12296 | tf_op jit(solution)/shard_map/ppermute | solution.py:478
  28.5 26.4 %collective-permute-start.10 = (bf16[32,128,128]{2,1,0:T(8,128)(2,1)}, bf16[32,128,128]{2,1,0:T(8,128)(2,1)}, u32[]{:S(2)}, u32[]{:S(2)}) collective-permute-start(bf16[32,128,128]{2,1,0:T(8,128)(2,1)} %get-tuple-element.36), channel_id=1, source_target_pairs={{0,2},{1,3},{6,4},{7,5},{8,10},{9,11},{14,12},{15,13},{16,18},{17,... | collective-permute-start | bytes 3145736 | tf_op jit(solution)/shard_map/ppermute | solution.py:504
  32.1 26.7 %collective-permute-start.11 = (bf16[64,4608]{1,0:T(8,128)(2,1)S(1)}, bf16[64,4608]{1,0:T(8,128)(2,1)}, u32[]{:S(2)}, u32[]{:S(2)}) collective-permute-start(bf16[64,4608]{1,0:T(8,128)(2,1)S(1)} %constant_dynamic-slice_fusion), channel_id=1, source_target_pairs={{0,8},{8,0},{16,24},{24,16},{1,9},{9,1},{17,25},{25,17},{2,10},{10... | collective-permute-start | bytes 1769480 | tf_op jit(solution)/shard_map/ppermute | solution.py:478
  33.6 26.9 %collective-permute-start.12 = (bf16[64,4608]{1,0:T(8,128)(2,1)S(1)}, bf16[64,4608]{1,0:T(8,128)(2,1)}, u32[]{:S(2)}, u32[]{:S(2)}) collective-permute-start(bf16[64,4608]{1,0:T(8,128)(2,1)S(1)} %constant_dynamic-slice_fusion), channel_id=1, source_target_pairs={{0,16},{8,24},{16,0},{24,8},{1,17},{9,25},{17,1},{25,9},{2,18},{10... | collective-permute-start | bytes 1769480 | tf_op jit(solution)/shard_map/ppermute | solution.py:478
  35.1 25.4 %collective-permute-start.13 = (bf16[64,4608]{1,0:T(8,128)(2,1)S(1)}, bf16[64,4608]{1,0:T(8,128)(2,1)}, u32[]{:S(2)}, u32[]{:S(2)}) collective-permute-start(bf16[64,4608]{1,0:T(8,128)(2,1)S(1)} %constant_dynamic-slice_fusion), channel_id=1, source_target_pairs={{0,24},{8,16},{16,8},{24,0},{1,25},{9,17},{17,9},{25,1},{2,26},{10... | collective-permute-start | bytes 1769480 | tf_op jit(solution)/shard_map/ppermute | solution.py:478
  46.3 36.5 %collective-permute-start.17 = (bf16[32,128,128]{2,1,0:T(8,128)(2,1)}, bf16[32,128,128]{2,1,0:T(8,128)(2,1)}, u32[]{:S(2)}, u32[]{:S(2)}) collective-permute-start(bf16[32,128,128]{2,1,0:T(8,128)(2,1)} %get-tuple-element.49), channel_id=1, source_target_pairs={{0,2},{1,3},{6,4},{7,5},{8,10},{9,11},{14,12},{15,13},{16,18},{17,... | collective-permute-start | bytes 3145736 | tf_op jit(solution)/shard_map/ppermute | solution.py:504
  57.5 27.3 %collective-permute-start.18 = (bf16[32,128,128]{2,1,0:T(8,128)(2,1)}, bf16[32,128,128]{2,1,0:T(8,128)(2,1)}, u32[]{:S(2)}, u32[]{:S(2)}) collective-permute-start(bf16[32,128,128]{2,1,0:T(8,128)(2,1)} %add_convert_fusion.1), channel_id=1, source_target_pairs={{2,6},{3,7},{4,0},{5,1},{10,14},{11,15},{12,8},{13,9},{18,22},{19,... | collective-permute-start | bytes 3145736 | tf_op jit(solution)/shard_map/ppermute | solution.py:504
  60.5 2.2 %collective-permute-start.14 = (bf16[64,4608]{1,0:T(8,128)(2,1)}, bf16[64,4608]{1,0:T(8,128)(2,1)S(1)}, u32[]{:S(2)}, u32[]{:S(2)}) collective-permute-start(bf16[64,4608]{1,0:T(8,128)(2,1)} %collective-permute-done.11.refs_0_), channel_id=1, source_target_pairs={{0,1},{1,0},{2,3},{3,2},{4,5},{5,4},{6,7},{7,6},{8,9},{9,8},{10,11... | collective-permute-start | bytes 1769480 | tf_op jit(solution)/shard_map/ppermute | solution.py:478
  60.5 3.1 %collective-permute-start.15 = (bf16[64,4608]{1,0:T(8,128)(2,1)}, bf16[64,4608]{1,0:T(8,128)(2,1)S(1)}, u32[]{:S(2)}, u32[]{:S(2)}) collective-permute-start(bf16[64,4608]{1,0:T(8,128)(2,1)} %collective-permute-done.12.refs_1_), channel_id=1, source_target_pairs={{0,1},{1,0},{2,3},{3,2},{4,5},{5,4},{6,7},{7,6},{8,9},{9,8},{10,11... | collective-permute-start | bytes 1769480 | tf_op jit(solution)/shard_map/ppermute | solution.py:478
  61.0 3.4 %collective-permute-start.16 = (bf16[64,4608]{1,0:T(8,128)(2,1)}, bf16[64,4608]{1,0:T(8,128)(2,1)S(1)}, u32[]{:S(2)}, u32[]{:S(2)}) collective-permute-start(bf16[64,4608]{1,0:T(8,128)(2,1)} %collective-permute-done.13.refs_2_), channel_id=1, source_target_pairs={{0,1},{1,0},{2,3},{3,2},{4,5},{5,4},{6,7},{7,6},{8,9},{9,8},{10,11... | collective-permute-start | bytes 1769480 | tf_op jit(solution)/shard_map/ppermute | solution.py:478
  76.2 29.0 %all-to-all-start = ((f32[4,128,1024]{2,1,0:T(8,128)}), f32[4,128,1024]{2,1,0:T(8,128)S(1)}, u32[]{:S(2)}, u32[]{:S(2)}) async-start(f32[4,128,1024]{2,1,0:T(8,128)} %get-tuple-element.48), calls=%async_computation | async-start | bytes 4194304 | tf_op jit(solution)/shard_map/all_to_all | solution.py:500
  79.8 37.6 %collective-permute-start.23 = (bf16[32,128,128]{2,1,0:T(8,128)(2,1)}, bf16[32,128,128]{2,1,0:T(8,128)(2,1)}, u32[]{:S(2)}, u32[]{:S(2)}) collective-permute-start(bf16[32,128,128]{2,1,0:T(8,128)(2,1)} %get-tuple-element.56), channel_id=1, source_target_pairs={{0,2},{1,3},{2,0},{3,1},{4,6},{5,7},{6,4},{7,5},{8,10},{9,11},{10,... | collective-permute-start | bytes 3145736 | tf_op jit(solution)/shard_map/ppermute | solution.py:478
  87.8 29.6 %collective-permute-start.24 = (bf16[32,128,128]{2,1,0:T(8,128)(2,1)}, bf16[32,128,128]{2,1,0:T(8,128)(2,1)}, u32[]{:S(2)}, u32[]{:S(2)}) collective-permute-start(bf16[32,128,128]{2,1,0:T(8,128)(2,1)} %add_convert_fusion), channel_id=1, source_target_pairs={{2,4},{3,5},{4,2},{5,3},{10,12},{11,13},{12,10},{13,11},{18,20},{1... | collective-permute-start | bytes 3145736 | tf_op jit(solution)/shard_map/ppermute | solution.py:504
  106.6 1.2 collective-permute-start.19
  107.8 5.4 %collective-permute-start.20 = (f32[8,128]{1,0:T(8,128)S(1)}, f32[8,128]{1,0:T(8,128)S(1)}, u32[]{:S(2)}, u32[]{:S(2)}) collective-permute-start(f32[8,128]{1,0:T(8,128)S(1)} %merge_stats.1.refs_0_), channel_id=1, source_target_pairs={{0,2},{1,3},{2,0},{3,1},{4,6},{5,7},{6,4},{7,5},{8,10},{9,11},{10,... | collective-permute-start | bytes 12296 | tf_op jit(solution)/shard_map/ppermute | solution.py:478
  110.8 4.5 %collective-permute-start.21 = (f32[8,128]{1,0:T(8,128)S(1)}, f32[8,128]{1,0:T(8,128)S(1)}, u32[]{:S(2)}, u32[]{:S(2)}) collective-permute-start(f32[8,128]{1,0:T(8,128)S(1)} %merge_stats.1.refs_0_), channel_id=1, source_target_pairs={{0,4},{1,5},{2,6},{3,7},{4,0},{5,1},{6,2},{7,3},{8,12},{9,13},{10,... | collective-permute-start | bytes 12296 | tf_op jit(solution)/shard_map/ppermute | solution.py:478
  111.8 5.4 %collective-permute-start.22 = (f32[8,128]{1,0:T(8,128)S(1)}, f32[8,128]{1,0:T(8,128)S(1)}, u32[]{:S(2)}, u32[]{:S(2)}) collective-permute-start(f32[8,128]{1,0:T(8,128)S(1)} %merge_stats.1.refs_0_), channel_id=1, source_target_pairs={{0,6},{1,7},{2,4},{3,5},{4,2},{5,3},{6,0},{7,1},{8,14},{9,15},{10,... | collective-permute-start | bytes 12296 | tf_op jit(solution)/shard_map/ppermute | solution.py:478
  122.3 9.5 %collective-permute-start.28 = (bf16[128,1024]{1,0:T(8,128)(2,1)}, bf16[128,1024]{1,0:T(8,128)(2,1)S(1)}, u32[]{:S(2)}, u32[]{:S(2)}) collective-permute-start(bf16[128,1024]{1,0:T(8,128)(2,1)} %get-tuple-element.61), channel_id=1, source_target_pairs={{0,8},{8,0},{16,24},{24,16},{1,9},{9,1},{17,25},{25,17},{2,10},{10... | collective-permute-start | bytes 786440 | tf_op jit(solution)/shard_map/ppermute | solution.py:478
  123.8 12.2 %collective-permute-start.29 = (bf16[128,1024]{1,0:T(8,128)(2,1)}, bf16[128,1024]{1,0:T(8,128)(2,1)S(1)}, u32[]{:S(2)}, u32[]{:S(2)}) collective-permute-start(bf16[128,1024]{1,0:T(8,128)(2,1)} %get-tuple-element.62), channel_id=1, source_target_pairs={{0,16},{8,24},{16,0},{24,8},{1,17},{9,25},{17,1},{25,9},{2,18},{10... | collective-permute-start | bytes 786440 | tf_op jit(solution)/shard_map/ppermute | solution.py:478
  124.3 11.7 %collective-permute-start.30 = (bf16[128,1024]{1,0:T(8,128)(2,1)}, bf16[128,1024]{1,0:T(8,128)(2,1)S(1)}, u32[]{:S(2)}, u32[]{:S(2)}) collective-permute-start(bf16[128,1024]{1,0:T(8,128)(2,1)} %get-tuple-element.63), channel_id=1, source_target_pairs={{0,24},{8,16},{16,8},{24,0},{1,25},{9,17},{17,9},{25,1},{2,26},{10... | collective-permute-start | bytes 786440 | tf_op jit(solution)/shard_map/ppermute | solution.py:478
  125.8 1.1 collective-permute-start.25
  127.0 3.5 %collective-permute-start.26 = (f32[1,128]{1,0:T(1,128)S(1)}, f32[1,128]{1,0:T(1,128)S(1)}, u32[]{:S(2)}, u32[]{:S(2)}) collective-permute-start(f32[1,128]{1,0:T(1,128)S(1)} %add.81), channel_id=1, source_target_pairs={{0,2},{1,3},{2,0},{3,1},{4,6},{5,7},{6,4},{7,5},{8,10},{9,11},{10,... | collective-permute-start | bytes 1544 | tf_op jit(solution)/shard_map/ppermute | solution.py:478
  130.5 10.8 %collective-permute-start.27 = (f32[1,128]{1,0:T(1,128)S(1)}, f32[1,128]{1,0:T(1,128)S(1)}, u32[]{:S(2)}, u32[]{:S(2)}) collective-permute-start(f32[1,128]{1,0:T(1,128)S(1)} %add.82), channel_id=1, source_target_pairs={{0,4},{1,5},{2,6},{3,7},{4,0},{5,1},{6,2},{7,3},{8,12},{9,13},{10,... | collective-permute-start | bytes 1544 | tf_op jit(solution)/shard_map/ppermute | solution.py:478
  (11 other events, 184.5 us)

commit v3 on v2

--- a/solution.py
+++ b/solution.py
@@ -201,7 +201,7 @@
         compiler_params=params(8),
         cost_estimate=COST,
         name="teacher_probs",
-    )(in_hbm(x_own), in_hbm(x_peer), *stats)
+    )(in_hbm(x_own), x_peer, *stats)
     return probs.reshape(2 * blocks, rows, LANES)
 
 
@@ -242,9 +242,9 @@
     result = jnp.dot(everyone[...], head_ref[...], preferred_element_type=F32)
     for r in range(n_other + 1):
         out_ref[place_ref[1] ^ r] = result[r * rows : (r + 1) * rows, :]
-    part = turned_ref.shape[0] // pl.num_programs(0)
+    part = turned_ref.shape[0]
     start = pl.multiple_of(pl.program_id(0) * part, part)
-    turned_ref[pl.ds(start, part), :] = everyone[:, pl.ds(start, part)].T
+    turned_ref[...] = everyone[:, pl.ds(start, part)].T
 
 
 def student_logits(place, after, own, near, far, head):
@@ -262,9 +262,9 @@
         + [pl.BlockSpec((depth, tile), lambda i: (0, i))],
         out_specs=[
             pl.BlockSpec((n_tok, rows, tile), lambda i: (0, 0, i)),
-            VMEM_SPEC,
+            pl.BlockSpec((depth * tile // cols, every), lambda i: (i, 0)),
         ],
-        out_shape=[pltpu.HBM((n_tok, rows, cols), F32), pltpu.VMEM((depth, every), BF16)],
+        out_shape=[pltpu.HBM((n_tok, rows, cols), F32), pltpu.HBM((depth, every), BF16)],
         scratch_shapes=[pltpu.VMEM((every, depth), BF16)],
         compiler_params=params(32),
         cost_estimate=COST,
@@ -351,7 +351,7 @@
     )(*stats)
 
 
-def grad_kernel(tok_ref, base_ref, labels_ref, columns, *refs, n_sums):
+def grad_kernel(tok_ref, base_ref, labels_ref, columns, *refs, n_sums, groups):
     sums = refs[:n_sums]
     logits_ref, *grads, inner_ref, inner = refs[n_sums:]
     step = pl.program_id(0)
@@ -363,7 +363,7 @@
 
     lane = lax.broadcasted_iota(jnp.int32, (rows, LANES), 1)
     lift, log_total = columns[:, 0:1], columns[:, 1:2]
-    label = labels_ref[...] - base_ref[token_group(step, tok_ref, len(grads))]
+    label = labels_ref[...] - base_ref[token_group(step, tok_ref, groups)]
     for r in range(len(grads)):
 
         @pl.when(step == r)
@@ -385,27 +385,29 @@
         inner_ref[...] = rows_from_columns([jnp.sum(inner[...], axis=1, keepdims=True)])[0:1, :]
 
 
-def token_group(step, tok_ref, n_tok):
-    return tok_ref[0] ^ ((step + 1) % n_tok)
-
-
-def grad_logits(tok, base, label_column, columns, sums, logits):
+def token_group(step, tok_ref, groups):
+    first, last = groups
+    return tok_ref[0] ^ (first + step * (last - first))
+
+
+def grad_logits(tok, base, label_column, columns, sums, logits, groups):
     n_tok, rows, cols = logits.shape
     per = cols // LANES
     whole = lambda shape: pl.BlockSpec(shape, lambda t, tok_ref: (0,) * len(shape))
-    group = lambda t, tok_ref: token_group(t, tok_ref, n_tok)
-    return pl.pallas_call(
-        functools.partial(grad_kernel, n_sums=len(sums)),
+    group = lambda t, tok_ref: token_group(t, tok_ref, groups)
+    n_out = len(groups)
+    return pl.pallas_call(
+        functools.partial(grad_kernel, n_sums=len(sums), groups=groups),
         grid_spec=pltpu.PrefetchScalarGridSpec(
             num_scalar_prefetch=1,
-            grid=(n_tok,),
+            grid=(n_out,),
             in_specs=[SMEM_SPEC, whole(label_column.shape), whole(columns.shape)]
             + [pl.BlockSpec((s.shape[0], per, rows, LANES), lambda t, r: (0, group(t, r), 0, 0)) for s in sums]
             + [pl.BlockSpec((1, rows, cols), lambda t, r: (group(t, r), 0, 0))],
-            out_specs=[whole((rows, cols))] * n_tok + [whole((1, rows))],
+            out_specs=[whole((rows, cols))] * n_out + [whole((1, rows))],
             scratch_shapes=[pltpu.VMEM((rows, LANES), F32)],
         ),
-        out_shape=[pltpu.HBM((rows, cols), BF16)] * n_tok + [jax.ShapeDtypeStruct((1, rows), F32)],
+        out_shape=[pltpu.HBM((rows, cols), BF16)] * n_out + [jax.ShapeDtypeStruct((1, rows), F32)],
         compiler_params=params(14),
         cost_estimate=COST,
         name="grad_logits",
@@ -576,8 +578,8 @@
     label_column = lax.dynamic_slice_in_dim(labels, tok * rows, rows).reshape(rows, 1)
     scores = exchange_tok(scores)
     if in_line:
-        second, arrived, turned = lax.optimization_barrier((second, arrived, turned))
-        merged_inner = plus(far_inner, second)
+        second, turned = lax.optimization_barrier((second, turned))
+        merged_inner, arrived = lax.optimization_barrier((plus(far_inner, second), arrived))
         crossed = send(merged_inner, across)
         scores, merged_inner = lax.optimization_barrier((scores, merged_inner))
         sums = [x[None] for x in (own, third, crossed, arrived)]
@@ -587,11 +589,14 @@
 
     group = tok.astype(jnp.int32).reshape(1)
     columns, base_loss = token_totals(stats)
-    *grads, inner = grad_logits(group, base, label_column, columns, sums, scores)
-    grads = [grads[-1]] + [swap(x, "tok", r + 1) for r, x in enumerate(grads[:-1])]
-    split = n_tok // 2
-    acc = first_product(turned, grads[:split])
-    head_grad, end = last_product(turned, acc, grads[split:])
+    grad_args = (group, base, label_column, columns, sums, scores)
+    beside_x, across_xy, inner = grad_logits(*grad_args, (1, 3))
+    beside_x, across_xy = swap(beside_x, "tok", 1), swap(across_xy, "tok", 3)
+    beside_y, here, inner_b = grad_logits(*grad_args, (2, 0))
+    beside_y = swap(beside_y, "tok", 2)
+    inner = inner + inner_b
+    acc = first_product(turned, [here, beside_x])
+    head_grad, end = last_product(turned, acc, [beside_y, across_xy])
     mask = 1
     while mask < n_vocab:
         other = swap(inner, "vocab", mask)

time: 142 us -> 142 us (level)
  local copies, waits for them, and re-layouts: 7.02 us -> 3.88 us
  waiting for transfers between devices: 41 us -> 42.9 us
    ppermute x4, waiting for transfers between devices: 8.27 us -> 13.7 us  [send(): lax.ppermute(x, 'vocab', [(2 * a + c, 2 * b + c) for a, b in hops for c i...]
    all_to_all x1, waiting for transfers between devices: 15.6 us -> 12.1 us  [exchange_tok(): return lax.all_to_all(x, 'tok', split_axis=0, concat_axis=0, tiled=True)]
    unnamed x22, local copies, waits for them, and re-layouts: 6.6 us -> 3.46 us
    pallas_call x1 -> x2, Pallas kernels: 4.95 us -> 5.84 us  [grad_logits(): pl.pallas_call(functools.partial(grad_kernel, n_sums=len(sums), groups=gr...]
  transfers between devices with their start and end apart: 32 -> 32, of which waited for: 15 -> 14; matrix products, arithmetic and copies ran while one was open for 5% -> 5% of each run, Pallas kernels for 26% -> 28%
where the time goes in v3:
time: 142 us; the launch traced here: 141 us
  Pallas kernels  46.8 us (33%)
  waiting for transfers between devices  42.9 us (30%)
  starting transfers between devices  39.6 us (28%)
  other arithmetic  7.1 us (5%)
  local copies, waits for them, and re-layouts  3.88 us (3%)
    ppermute x27, starting transfers between devices, swap(): lax.ppermute(x, axis, [(i, i ^ mask) for i in range(lax.axis_size(axis))])  26.4 us
    ppermute x27, waiting for transfers between devices, swap(): lax.ppermute(x, axis, [(i, i ^ mask) for i in range(lax.axis_size(axis))])  17.2 us
    ppermute x4, waiting for transfers between devices, send(): lax.ppermute(x, 'vocab', [(2 * a + c, 2 * b + c) for a, b in hops for c i...  13.7 us
    pallas_call x2, Pallas kernels, chip_sums(): pl.pallas_call(functools.partial(sums_kernel, first=first, fan=fan, piece...  12.8 us
    all_to_all x1, waiting for transfers between devices, exchange_tok(): return lax.all_to_all(x, 'tok', split_axis=0, concat_axis=0, tiled=True)  12.1 us
    pallas_call x1, Pallas kernels, student_logits(): pl.pallas_call(logits_kernel, grid=(cols // tile,), in_specs=[SMEM_SPEC,...  10.2 us
    ppermute x4, starting transfers between devices, send(): lax.ppermute(x, 'vocab', [(2 * a + c, 2 * b + c) for a, b in hops for c i...  9.62 us
    pallas_call x2, Pallas kernels, grad_logits(): pl.pallas_call(functools.partial(grad_kernel, n_sums=len(sums), groups=gr...  5.84 us
  transfers between devices with their start and end apart: 32, of which 14 were waited for; matrix products, arithmetic and copies ran while one was open for 5% of the time, Pallas kernels for 28%

profile of v3, /device:TPU:0, one launch (start us, length us, event | category | flops | bytes accessed | tf_op | source)
XLA Modules:
  0.0 141.2 jit_solution(15736811235255577706)
XLA Ops:
  4.6 5.0 %collective-permute-start.4 = (f32[8,128]{1,0:T(8,128)S(1)}, f32[8,128]{1,0:T(8,128)S(1)}, u32[]{:S(2)}, u32[]{:S(2)}) collective-permute-start(f32[8,128]{1,0:T(8,128)S(1)} %teacher_stats.1.refs_0_), channel_id=1, source_target_pairs={{0,6},{1,7},{2,4},{3,5},{4,2},{5,3},{6,0},{7,1},{8,14},{9,15},{10,... | collective-permute-start | bytes 12296 | tf_op jit(solution)/shard_map/ppermute | solution.py:480
  9.6 2.9 %collective-permute-start.3 = (f32[8,128]{1,0:T(8,128)S(1)}, f32[8,128]{1,0:T(8,128)S(1)}, u32[]{:S(2)}, u32[]{:S(2)}) collective-permute-start(f32[8,128]{1,0:T(8,128)S(1)} %teacher_stats.1.refs_0_), channel_id=1, source_target_pairs={{0,4},{1,5},{2,6},{3,7},{4,0},{5,1},{6,2},{7,3},{8,12},{9,13},{10,... | collective-permute-start | bytes 12296 | tf_op jit(solution)/shard_map/ppermute | solution.py:480
  12.6 1.6 %collective-permute-start.2 = (f32[8,128]{1,0:T(8,128)S(1)}, f32[8,128]{1,0:T(8,128)S(1)}, u32[]{:S(2)}, u32[]{:S(2)}) collective-permute-start(f32[8,128]{1,0:T(8,128)S(1)} %teacher_stats.1.refs_0_), channel_id=1, source_target_pairs={{0,2},{1,3},{2,0},{3,1},{4,6},{5,7},{6,4},{7,5},{8,10},{9,11},{10,... | collective-permute-start | bytes 12296 | tf_op jit(solution)/shard_map/ppermute | solution.py:480
  14.7 1.5 %collective-permute-done.2.refs_1_ = f32[8,128]{1,0:T(8,128)S(1)} collective-permute-done((f32[8,128]{1,0:T(8,128)S(1)}, f32[8,128]{1,0:T(8,128)S(1)}, u32[]{:S(2)}, u32[]{:S(2)}) %collective-permute-start.2) | collective-permute-done | bytes 4128 | tf_op jit(solution)/shard_map/ppermute | solution.py:480
  16.2 3.0 %entry_lists.1 = (s32[8,264]{1,0:T(8,128)S(1)}, s32[8]{0:T(128)S(1)}) custom-call(s32[128]{0:T(128)S(1)} %reshape.18.own_ref, s32[128]{0:T(128)S(1)} %collective-permute-done.peer_ref), custom_call_target="tpu_custom_call" | custom-call | flops 1024 | bytes 1024 | tf_op jit(solution)/shard_map/entry_lists/pallas_call | solution.py:117
  19.3 3.3 %teacher_probs.1 = bf16[2,32,128,128]{3,2,1,0:T(8,128)(2,1)S(1)} custom-call(bf16[128,4096]{1,0:T(8,128)(2,1)} %x_own.1, bf16[128,4096]{1,0:T(8,128)(2,1)S(1)} %collective-permute-done.1.x_peer, f32[8,128]{1,0:T(8,128)S(1)} %teacher_stats.1.refs_0_, f32[8,128]{1,0:T(8,128)S(1)} %collective-permute-done.2.refs_1_, ...), custom_call_target="tpu_custom_call" | custom-call | flops 1024 | bytes 1024 | tf_op jit(solution)/shard_map/teacher_probs/pallas_call | solution.py:194
  22.6 4.1 %chip_sums.2 = (bf16[32,128,128]{2,1,0:T(8,128)(2,1)}, f32[8,128]{1,0:T(8,128)S(1)}) custom-call(s32[2]{0:T(128)S(1)} %pad_add_fusion.spot_ref, s32[8,264]{1,0:T(8,128)S(1)} %get-tuple-element.36.list_ref, s32[8]{0:T(128)S(1)} %get-tuple-element.37.count_ref, bf16[64,128,128]{2,1,0:T(8,128)(2,1)S(1)} %bitcast.14, bf16[32,4,128,128]{3,2,1,0:T(8,128)(2,1)S(1)} %copy-done.2, ...), custom_call_target="tpu_custom_call" | custom-call | flops 1024 | bytes 1024 | tf_op jit(solution)/shard_map/chip_sums/pallas_call | solution.py:213
  26.6 4.5 %collective-permute-start.10 = (bf16[32,128,128]{2,1,0:T(8,128)(2,1)}, bf16[32,128,128]{2,1,0:T(8,128)(2,1)}, u32[]{:S(2)}, u32[]{:S(2)}) collective-permute-start(bf16[32,128,128]{2,1,0:T(8,128)(2,1)} %get-tuple-element.38), channel_id=1, source_target_pairs={{0,2},{1,3},{6,4},{7,5},{8,10},{9,11},{14,12},{15,13},{16,18},{17,... | collective-permute-start | bytes 3145736 | tf_op jit(solution)/shard_map/ppermute | solution.py:506
  31.2 2.5 %collective-permute-start.13 = (bf16[64,4608]{1,0:T(8,128)(2,1)S(1)}, bf16[64,4608]{1,0:T(8,128)(2,1)}, u32[]{:S(2)}, u32[]{:S(2)}) collective-permute-start(bf16[64,4608]{1,0:T(8,128)(2,1)S(1)} %constant_dynamic-slice_fusion), channel_id=1, source_target_pairs={{0,24},{8,16},{16,8},{24,0},{1,25},{9,17},{17,9},{25,1},{2,26},{10... | collective-permute-start | bytes 1769480 | tf_op jit(solution)/shard_map/ppermute | solution.py:480
  34.7 2.2 %copy-done.3 = bf16[32,4,128,128]{3,2,1,0:T(8,128)(2,1)S(1)} copy-done((bf16[32,4,128,128]{3,2,1,0:T(8,128)(2,1)S(1)}, bf16[32,4,128,128]{3,2,1,0:T(8,128)(2,1)}, u32[]{:S(2)}) %copy-start.3) | copy-done | bytes 4194328
  36.9 8.8 %chip_sums.3 = (bf16[32,128,128]{2,1,0:T(8,128)(2,1)}, bf16[32,128,128]{2,1,0:T(8,128)(2,1)}, bf16[32,128,128]{2,1,0:T(8,128)(2,1)}, f32[8,128]{1,0:T(8,128)S(1)}) custom-call(s32[2]{0:T(128)S(1)} %pad_add_fusion.spot_ref, s32[8,264]{1,0:T(8,128)S(1)} %get-tuple-element.36.list_ref, s32[8]{0:T(128)S(1)} %get-tuple-element.37.count_ref, ...), custom_call_target="tpu_custom_call" | custom-call | flops 1024 | bytes 1024 | tf_op jit(solution)/shard_map/chip_sums/pallas_call | solution.py:213
  45.7 2.2 %collective-permute-start.17 = (bf16[32,128,128]{2,1,0:T(8,128)(2,1)}, bf16[32,128,128]{2,1,0:T(8,128)(2,1)}, u32[]{:S(2)}, u32[]{:S(2)}) collective-permute-start(bf16[32,128,128]{2,1,0:T(8,128)(2,1)} %get-tuple-element.51), channel_id=1, source_target_pairs={{0,2},{1,3},{6,4},{7,5},{8,10},{9,11},{14,12},{15,13},{16,18},{17,... | collective-permute-start | bytes 3145736 | tf_op jit(solution)/shard_map/ppermute | solution.py:506
  47.9 6.0 %collective-permute-done.10 = bf16[32,128,128]{2,1,0:T(8,128)(2,1)} collective-permute-done((bf16[32,128,128]{2,1,0:T(8,128)(2,1)}, bf16[32,128,128]{2,1,0:T(8,128)(2,1)}, u32[]{:S(2)}, u32[]{:S(2)}) %collective-permute-start.10) | collective-permute-done | bytes 1048608 | tf_op jit(solution)/shard_map/ppermute | solution.py:506
  53.9 2.6 %add_convert_fusion.1 = bf16[32,128,128]{2,1,0:T(8,128)(2,1)} fusion(bf16[32,128,128]{2,1,0:T(8,128)(2,1)} %collective-permute-done.10, bf16[32,128,128]{2,1,0:T(8,128)(2,1)S(1)} %copy-done.7), kind=kLoop, calls=%fused_computation.1 | loop fusion | flops 2097152 | bytes 3145728 | tf_op jit(solution)/shard_map/convert_element_type | solution.py:498
  56.6 4.3 %collective-permute-done.12.refs_1_ = bf16[64,4608]{1,0:T(8,128)(2,1)} collective-permute-done((bf16[64,4608]{1,0:T(8,128)(2,1)S(1)}, bf16[64,4608]{1,0:T(8,128)(2,1)}, u32[]{:S(2)}, u32[]{:S(2)}) %collective-permute-start.12) | collective-permute-done | bytes 589856 | tf_op jit(solution)/shard_map/ppermute | solution.py:480
  64.8 10.2 %student_logits.1 = (f32[4,128,1024]{2,1,0:T(8,128)}, bf16[4608,512]{1,0:T(8,128)(2,1)}) custom-call(s32[2]{0:T(128)S(1)} %pad_add_fusion.1.place_ref, f32[8,128]{1,0:T(8,128)S(1)} %add.81.after_ref.mass_ref, bf16[128,4608]{1,0:T(8,128)(2,1)S(1)} %copy-done.6, bf16[64,4608]{1,0:T(8,128)(2,1)} %collective-permute-done.11.refs_0_, ...), custom_call_target="tpu_custom_call" | custom-call | flops 1024 | bytes 1024 | tf_op jit(solution)/shard_map/student_logits/pallas_call | solution.py:257
  75.1 3.6 %all-to-all-start = ((f32[4,128,1024]{2,1,0:T(8,128)}), f32[4,128,1024]{2,1,0:T(8,128)S(1)}, u32[]{:S(2)}, u32[]{:S(2)}) async-start(f32[4,128,1024]{2,1,0:T(8,128)} %get-tuple-element.50), calls=%async_computation | async-start | bytes 4194304 | tf_op jit(solution)/shard_map/all_to_all | solution.py:502
  79.5 3.1 %add_convert_fusion = bf16[32,128,128]{2,1,0:T(8,128)(2,1)} fusion(bf16[32,128,128]{2,1,0:T(8,128)(2,1)} %collective-permute-done.17, bf16[32,128,128]{2,1,0:T(8,128)(2,1)} %get-tuple-element.51), kind=kLoop, calls=%fused_computation | loop fusion | flops 2097152 | bytes 3145728 | tf_op jit(solution)/shard_map/convert_element_type | solution.py:498
  82.5 7.7 %collective-permute-done.18 = bf16[32,128,128]{2,1,0:T(8,128)(2,1)} collective-permute-done((bf16[32,128,128]{2,1,0:T(8,128)(2,1)}, bf16[32,128,128]{2,1,0:T(8,128)(2,1)}, u32[]{:S(2)}, u32[]{:S(2)}) %collective-permute-start.18) | collective-permute-done | bytes 1048608 | tf_op jit(solution)/shard_map/ppermute | solution.py:506
  90.2 1.6 %collective-permute-start.24 = (bf16[32,128,128]{2,1,0:T(8,128)(2,1)}, bf16[32,128,128]{2,1,0:T(8,128)(2,1)}, u32[]{:S(2)}, u32[]{:S(2)}) collective-permute-start(bf16[32,128,128]{2,1,0:T(8,128)(2,1)} %add_convert_fusion), channel_id=1, source_target_pairs={{2,4},{3,5},{4,2},{5,3},{10,12},{11,13},{12,10},{13,11},{18,20},{1... | collective-permute-start | bytes 3145736 | tf_op jit(solution)/shard_map/ppermute | solution.py:506
  92.1 12.1 %all-to-all-done.logits_ref.refs_4_ = f32[4,128,1024]{2,1,0:T(8,128)S(1)} async-done(((f32[4,128,1024]{2,1,0:T(8,128)}), f32[4,128,1024]{2,1,0:T(8,128)S(1)}, u32[]{:S(2)}, u32[]{:S(2)}) %all-to-all-start) | async-done | bytes 2097184 | tf_op jit(solution)/shard_map/all_to_all | solution.py:502
  104.1 1.4 %student_stats.1.refs_0_ = f32[8,128]{1,0:T(8,128)S(1)} custom-call(s32[4]{0:T(128)S(1)} %add_multiply_fusion.base_ref, s32[128,1]{1,0:T(8,128)S(1)} %copy.13.labels_ref, f32[8,128]{1,0:T(8,128)S(1)} %add.81.after_ref.mass_ref, f32[4,128,1024]{2,1,0:T(8,128)S(1)} %all-to-all-done.logits_ref.refs_4_), custom_call_target="tpu_custom_call" | custom-call | flops 1024 | bytes 1024 | tf_op jit(solution)/shard_map/student_stats/pallas_call | solution.py:298
  107.4 2.2 %collective-permute-start.21 = (f32[8,128]{1,0:T(8,128)S(1)}, f32[8,128]{1,0:T(8,128)S(1)}, u32[]{:S(2)}, u32[]{:S(2)}) collective-permute-start(f32[8,128]{1,0:T(8,128)S(1)} %merge_stats.1.refs_0_), channel_id=1, source_target_pairs={{0,4},{1,5},{2,6},{3,7},{4,0},{5,1},{6,2},{7,3},{8,12},{9,13},{10,... | collective-permute-start | bytes 12296 | tf_op jit(solution)/shard_map/ppermute | solution.py:480
  109.5 1.7 %collective-permute-start.20 = (f32[8,128]{1,0:T(8,128)S(1)}, f32[8,128]{1,0:T(8,128)S(1)}, u32[]{:S(2)}, u32[]{:S(2)}) collective-permute-start(f32[8,128]{1,0:T(8,128)S(1)} %merge_stats.1.refs_0_), channel_id=1, source_target_pairs={{0,2},{1,3},{2,0},{3,1},{4,6},{5,7},{6,4},{7,5},{8,10},{9,11},{10,... | collective-permute-start | bytes 12296 | tf_op jit(solution)/shard_map/ppermute | solution.py:480
  112.3 2.9 %collective-permute-done.21.refs_2_ = f32[8,128]{1,0:T(8,128)S(1)} collective-permute-done((f32[8,128]{1,0:T(8,128)S(1)}, f32[8,128]{1,0:T(8,128)S(1)}, u32[]{:S(2)}, u32[]{:S(2)}) %collective-permute-start.21) | collective-permute-done | bytes 4128 | tf_op jit(solution)/shard_map/ppermute | solution.py:480
  115.4 3.0 %grad_logits.2 = (bf16[128,1024]{1,0:T(8,128)(2,1)}, bf16[128,1024]{1,0:T(8,128)(2,1)}, f32[1,128]{1,0:T(1,128)S(1)}) custom-call(s32[1]{0:T(128)} %bitcast.4.tok_ref, s32[4]{0:T(128)S(1)} %add_multiply_fusion.base_ref, s32[128,1]{1,0:T(8,128)S(1)} %copy.13.labels_ref, f32[128,128]{1,0:T(8,128)S(1)} %get-tuple-element.57.columns, ...), custom_call_target="tpu_custom_call" | custom-call | flops 1024 | bytes 1024 | tf_op jit(solution)/shard_map/grad_logits/pallas_call | solution.py:399
  118.4 1.5 %collective-permute-start.28 = (bf16[128,1024]{1,0:T(8,128)(2,1)}, bf16[128,1024]{1,0:T(8,128)(2,1)S(1)}, u32[]{:S(2)}, u32[]{:S(2)}) collective-permute-start(bf16[128,1024]{1,0:T(8,128)(2,1)} %get-tuple-element.65), channel_id=1, source_target_pairs={{0,8},{8,0},{16,24},{24,16},{1,9},{9,1},{17,25},{25,17},{2,10},{10... | collective-permute-start | bytes 786440 | tf_op jit(solution)/shard_map/ppermute | solution.py:480
  119.9 2.8 %grad_logits.3 = (bf16[128,1024]{1,0:T(8,128)(2,1)}, bf16[128,1024]{1,0:T(8,128)(2,1)}, f32[1,128]{1,0:T(1,128)S(1)}) custom-call(s32[1]{0:T(128)} %bitcast.4.tok_ref, s32[4]{0:T(128)S(1)} %add_multiply_fusion.base_ref, s32[128,1]{1,0:T(8,128)S(1)} %copy.13.labels_ref, f32[128,128]{1,0:T(8,128)S(1)} %get-tuple-element.57.columns, ...), custom_call_target="tpu_custom_call" | custom-call | flops 1024 | bytes 1024 | tf_op jit(solution)/shard_map/grad_logits/pallas_call | solution.py:399
  126.4 3.0 %collective-permute-done.26 = f32[1,128]{1,0:T(1,128)S(1)} collective-permute-done((f32[1,128]{1,0:T(1,128)S(1)}, f32[1,128]{1,0:T(1,128)S(1)}, u32[]{:S(2)}, u32[]{:S(2)}) %collective-permute-start.26) | collective-permute-done | bytes 544 | tf_op jit(solution)/shard_map/ppermute | solution.py:480
  129.4 1.8 %collective-permute-start.27 = (f32[1,128]{1,0:T(1,128)S(1)}, f32[1,128]{1,0:T(1,128)S(1)}, u32[]{:S(2)}, u32[]{:S(2)}) collective-permute-start(f32[1,128]{1,0:T(1,128)S(1)} %add.86), channel_id=1, source_target_pairs={{0,4},{1,5},{2,6},{3,7},{4,0},{5,1},{6,2},{7,3},{8,12},{9,13},{10,... | collective-permute-start | bytes 1544 | tf_op jit(solution)/shard_map/ppermute | solution.py:480
  131.2 4.1 %first_product.1.acc_ref = f32[4608,1024]{1,0:T(8,128)S(1)} custom-call(bf16[4608,512]{1,0:T(8,128)(2,1)S(1)} %bitcast.13, bf16[128,1024]{1,0:T(8,128)(2,1)} %get-tuple-element.64.refs_0_, bf16[128,1024]{1,0:T(8,128)(2,1)S(1)} %collective-permute-done.28.refs_1_), custom_call_target="tpu_custom_call" | custom-call | flops 1024 | bytes 1024 | tf_op jit(solution)/shard_map/first_product/pallas_call | solution.py:449
  135.3 5.3 %last_product.1 = (bf16[4608,1024]{1,0:T(8,128)(2,1)}, f32[1,128]{1,0:T(1,128)S(1)}) custom-call(bf16[4608,512]{1,0:T(8,128)(2,1)S(1)} %bitcast.13, f32[4608,1024]{1,0:T(8,128)S(1)} %first_product.1.acc_ref, bf16[128,1024]{1,0:T(8,128)(2,1)S(1)} %collective-permute-done.29.refs_0_, bf16[128,1024]{1,0:T(8,128)(2,1)S(1)} %collective-permute-done.30.refs_1_), custom_call_target="tpu_custom_call" | custom-call | flops 1024 | bytes 1024 | tf_op jit(solution)/shard_map/last_product/pallas_call | solution.py:466
  (84 shorter events, 17.9 us)
Async XLA Ops:
  0.6 21.9 %collective-permute-start.9 = (bf16[32,4,128,128]{3,2,1,0:T(8,128)(2,1)}, bf16[32,4,128,128]{3,2,1,0:T(8,128)(2,1)}, u32[]{:S(2)}, u32[]{:S(2)}) collective-permute-start(bf16[32,4,128,128]{3,2,1,0:T(8,128)(2,1)} %w_own.3), channel_id=1, source_target_pairs={{0,1},{1,0},{2,3},{3,2},{4,5},{5,4},{6,7},{7,6},{8,9},{9,8},{10,11... | collective-permute-start | bytes 12582920 | tf_op jit(solution)/shard_map/ppermute | solution.py:480
  1.2 18.1 %collective-permute-start.1 = (bf16[128,4096]{1,0:T(8,128)(2,1)}, bf16[128,4096]{1,0:T(8,128)(2,1)S(1)}, u32[]{:S(2)}, u32[]{:S(2)}) collective-permute-start(bf16[128,4096]{1,0:T(8,128)(2,1)} %x_own.1), channel_id=1, source_target_pairs={{0,1},{1,0},{2,3},{3,2},{4,5},{5,4},{6,7},{7,6},{8,9},{9,8},{10,11... | collective-permute-start | bytes 3145736 | tf_op jit(solution)/shard_map/ppermute | solution.py:480
  3.1 9.5 %collective-permute-start.5 = (f32[8,128]{1,0:T(8,128)S(1)}, f32[8,128]{1,0:T(8,128)S(1)}, u32[]{:S(2)}, u32[]{:S(2)}) collective-permute-start(f32[8,128]{1,0:T(8,128)S(1)} %teacher_stats.1.refs_0_), channel_id=1, source_target_pairs={{0,1},{1,0},{2,3},{3,2},{4,5},{5,4},{6,7},{7,6},{8,9},{9,8},{10,11... | collective-permute-start | bytes 12296 | tf_op jit(solution)/shard_map/ppermute | solution.py:480
  4.4 5.2 %collective-permute-start = (s32[128]{0:T(128)S(1)}, s32[128]{0:T(128)S(1)}, u32[]{:S(2)}, u32[]{:S(2)}) collective-permute-start(s32[128]{0:T(128)S(1)} %reshape.18.own_ref), channel_id=1, source_target_pairs={{0,1},{1,0},{2,3},{3,2},{4,5},{5,4},{6,7},{7,6},{8,9},{9,8},{10,11... | collective-permute-start | bytes 1544 | tf_op jit(solution)/shard_map/ppermute | solution.py:480
  4.6 9.6 %collective-permute-start.4 = (f32[8,128]{1,0:T(8,128)S(1)}, f32[8,128]{1,0:T(8,128)S(1)}, u32[]{:S(2)}, u32[]{:S(2)}) collective-permute-start(f32[8,128]{1,0:T(8,128)S(1)} %teacher_stats.1.refs_0_), channel_id=1, source_target_pairs={{0,6},{1,7},{2,4},{3,5},{4,2},{5,3},{6,0},{7,1},{8,14},{9,15},{10,... | collective-permute-start | bytes 12296 | tf_op jit(solution)/shard_map/ppermute | solution.py:480
  9.6 4.5 %collective-permute-start.3 = (f32[8,128]{1,0:T(8,128)S(1)}, f32[8,128]{1,0:T(8,128)S(1)}, u32[]{:S(2)}, u32[]{:S(2)}) collective-permute-start(f32[8,128]{1,0:T(8,128)S(1)} %teacher_stats.1.refs_0_), channel_id=1, source_target_pairs={{0,4},{1,5},{2,6},{3,7},{4,0},{5,1},{6,2},{7,3},{8,12},{9,13},{10,... | collective-permute-start | bytes 12296 | tf_op jit(solution)/shard_map/ppermute | solution.py:480
  12.6 3.6 %collective-permute-start.2 = (f32[8,128]{1,0:T(8,128)S(1)}, f32[8,128]{1,0:T(8,128)S(1)}, u32[]{:S(2)}, u32[]{:S(2)}) collective-permute-start(f32[8,128]{1,0:T(8,128)S(1)} %teacher_stats.1.refs_0_), channel_id=1, source_target_pairs={{0,2},{1,3},{2,0},{3,1},{4,6},{5,7},{6,4},{7,5},{8,10},{9,11},{10,... | collective-permute-start | bytes 12296 | tf_op jit(solution)/shard_map/ppermute | solution.py:480
  14.1 5.1 %collective-permute-start.8 = (f32[8,128]{1,0:T(8,128)S(1)}, f32[8,128]{1,0:T(8,128)S(1)}, u32[]{:S(2)}, u32[]{:S(2)}) collective-permute-start(f32[8,128]{1,0:T(8,128)S(1)} %collective-permute-done.4.refs_3_), channel_id=1, source_target_pairs={{0,1},{1,0},{2,3},{3,2},{4,5},{5,4},{6,7},{7,6},{8,9},{9,8},{10,11... | collective-permute-start | bytes 12296 | tf_op jit(solution)/shard_map/ppermute | solution.py:480
  14.1 5.1 %collective-permute-start.7 = (f32[8,128]{1,0:T(8,128)S(1)}, f32[8,128]{1,0:T(8,128)S(1)}, u32[]{:S(2)}, u32[]{:S(2)}) collective-permute-start(f32[8,128]{1,0:T(8,128)S(1)} %collective-permute-done.3.refs_2_), channel_id=1, source_target_pairs={{0,1},{1,0},{2,3},{3,2},{4,5},{5,4},{6,7},{7,6},{8,9},{9,8},{10,11... | collective-permute-start | bytes 12296 | tf_op jit(solution)/shard_map/ppermute | solution.py:480
  16.2 3.1 %collective-permute-start.6 = (f32[8,128]{1,0:T(8,128)S(1)}, f32[8,128]{1,0:T(8,128)S(1)}, u32[]{:S(2)}, u32[]{:S(2)}) collective-permute-start(f32[8,128]{1,0:T(8,128)S(1)} %collective-permute-done.2.refs_1_), channel_id=1, source_target_pairs={{0,1},{1,0},{2,3},{3,2},{4,5},{5,4},{6,7},{7,6},{8,9},{9,8},{10,11... | collective-permute-start | bytes 12296 | tf_op jit(solution)/shard_map/ppermute | solution.py:480
  26.6 27.3 %collective-permute-start.10 = (bf16[32,128,128]{2,1,0:T(8,128)(2,1)}, bf16[32,128,128]{2,1,0:T(8,128)(2,1)}, u32[]{:S(2)}, u32[]{:S(2)}) collective-permute-start(bf16[32,128,128]{2,1,0:T(8,128)(2,1)} %get-tuple-element.38), channel_id=1, source_target_pairs={{0,2},{1,3},{6,4},{7,5},{8,10},{9,11},{14,12},{15,13},{16,18},{17,... | collective-permute-start | bytes 3145736 | tf_op jit(solution)/shard_map/ppermute | solution.py:506
  31.2 25.4 %collective-permute-start.13 = (bf16[64,4608]{1,0:T(8,128)(2,1)S(1)}, bf16[64,4608]{1,0:T(8,128)(2,1)}, u32[]{:S(2)}, u32[]{:S(2)}) collective-permute-start(bf16[64,4608]{1,0:T(8,128)(2,1)S(1)} %constant_dynamic-slice_fusion), channel_id=1, source_target_pairs={{0,24},{8,16},{16,8},{24,0},{1,25},{9,17},{17,9},{25,1},{2,26},{10... | collective-permute-start | bytes 1769480 | tf_op jit(solution)/shard_map/ppermute | solution.py:480
  33.7 27.2 %collective-permute-start.12 = (bf16[64,4608]{1,0:T(8,128)(2,1)S(1)}, bf16[64,4608]{1,0:T(8,128)(2,1)}, u32[]{:S(2)}, u32[]{:S(2)}) collective-permute-start(bf16[64,4608]{1,0:T(8,128)(2,1)S(1)} %constant_dynamic-slice_fusion), channel_id=1, source_target_pairs={{0,16},{8,24},{16,0},{24,8},{1,17},{9,25},{17,1},{25,9},{2,18},{10... | collective-permute-start | bytes 1769480 | tf_op jit(solution)/shard_map/ppermute | solution.py:480
  34.2 26.8 %collective-permute-start.11 = (bf16[64,4608]{1,0:T(8,128)(2,1)S(1)}, bf16[64,4608]{1,0:T(8,128)(2,1)}, u32[]{:S(2)}, u32[]{:S(2)}) collective-permute-start(bf16[64,4608]{1,0:T(8,128)(2,1)S(1)} %constant_dynamic-slice_fusion), channel_id=1, source_target_pairs={{0,8},{8,0},{16,24},{24,16},{1,9},{9,1},{17,25},{25,17},{2,10},{10... | collective-permute-start | bytes 1769480 | tf_op jit(solution)/shard_map/ppermute | solution.py:480
  45.7 33.8 %collective-permute-start.17 = (bf16[32,128,128]{2,1,0:T(8,128)(2,1)}, bf16[32,128,128]{2,1,0:T(8,128)(2,1)}, u32[]{:S(2)}, u32[]{:S(2)}) collective-permute-start(bf16[32,128,128]{2,1,0:T(8,128)(2,1)} %get-tuple-element.51), channel_id=1, source_target_pairs={{0,2},{1,3},{6,4},{7,5},{8,10},{9,11},{14,12},{15,13},{16,18},{17,... | collective-permute-start | bytes 3145736 | tf_op jit(solution)/shard_map/ppermute | solution.py:506
  60.9 2.2 %collective-permute-start.14 = (bf16[64,4608]{1,0:T(8,128)(2,1)}, bf16[64,4608]{1,0:T(8,128)(2,1)S(1)}, u32[]{:S(2)}, u32[]{:S(2)}) collective-permute-start(bf16[64,4608]{1,0:T(8,128)(2,1)} %collective-permute-done.11.refs_0_), channel_id=1, source_target_pairs={{0,1},{1,0},{2,3},{3,2},{4,5},{5,4},{6,7},{7,6},{8,9},{9,8},{10,11... | collective-permute-start | bytes 1769480 | tf_op jit(solution)/shard_map/ppermute | solution.py:480
  60.9 3.1 %collective-permute-start.15 = (bf16[64,4608]{1,0:T(8,128)(2,1)}, bf16[64,4608]{1,0:T(8,128)(2,1)S(1)}, u32[]{:S(2)}, u32[]{:S(2)}) collective-permute-start(bf16[64,4608]{1,0:T(8,128)(2,1)} %collective-permute-done.12.refs_1_), channel_id=1, source_target_pairs={{0,1},{1,0},{2,3},{3,2},{4,5},{5,4},{6,7},{7,6},{8,9},{9,8},{10,11... | collective-permute-start | bytes 1769480 | tf_op jit(solution)/shard_map/ppermute | solution.py:480
  61.4 3.4 %collective-permute-start.16 = (bf16[64,4608]{1,0:T(8,128)(2,1)}, bf16[64,4608]{1,0:T(8,128)(2,1)S(1)}, u32[]{:S(2)}, u32[]{:S(2)}) collective-permute-start(bf16[64,4608]{1,0:T(8,128)(2,1)} %collective-permute-done.13.refs_2_), channel_id=1, source_target_pairs={{0,1},{1,0},{2,3},{3,2},{4,5},{5,4},{6,7},{7,6},{8,9},{9,8},{10,11... | collective-permute-start | bytes 1769480 | tf_op jit(solution)/shard_map/ppermute | solution.py:480
  61.4 28.8 %collective-permute-start.18 = (bf16[32,128,128]{2,1,0:T(8,128)(2,1)}, bf16[32,128,128]{2,1,0:T(8,128)(2,1)}, u32[]{:S(2)}, u32[]{:S(2)}) collective-permute-start(bf16[32,128,128]{2,1,0:T(8,128)(2,1)} %add_convert_fusion.1), channel_id=1, source_target_pairs={{2,6},{3,7},{4,0},{5,1},{10,14},{11,15},{12,8},{13,9},{18,22},{19,... | collective-permute-start | bytes 3145736 | tf_op jit(solution)/shard_map/ppermute | solution.py:506
  75.1 29.0 %all-to-all-start = ((f32[4,128,1024]{2,1,0:T(8,128)}), f32[4,128,1024]{2,1,0:T(8,128)S(1)}, u32[]{:S(2)}, u32[]{:S(2)}) async-start(f32[4,128,1024]{2,1,0:T(8,128)} %get-tuple-element.50), calls=%async_computation | async-start | bytes 4194304 | tf_op jit(solution)/shard_map/all_to_all | solution.py:502
  78.7 36.6 %collective-permute-start.23 = (bf16[32,128,128]{2,1,0:T(8,128)(2,1)}, bf16[32,128,128]{2,1,0:T(8,128)(2,1)}, u32[]{:S(2)}, u32[]{:S(2)}) collective-permute-start(bf16[32,128,128]{2,1,0:T(8,128)(2,1)} %get-tuple-element.59), channel_id=1, source_target_pairs={{0,2},{1,3},{2,0},{3,1},{4,6},{5,7},{6,4},{7,5},{8,10},{9,11},{10,... | collective-permute-start | bytes 3145736 | tf_op jit(solution)/shard_map/ppermute | solution.py:480
  90.2 25.1 %collective-permute-start.24 = (bf16[32,128,128]{2,1,0:T(8,128)(2,1)}, bf16[32,128,128]{2,1,0:T(8,128)(2,1)}, u32[]{:S(2)}, u32[]{:S(2)}) collective-permute-start(bf16[32,128,128]{2,1,0:T(8,128)(2,1)} %add_convert_fusion), channel_id=1, source_target_pairs={{2,4},{3,5},{4,2},{5,3},{10,12},{11,13},{12,10},{13,11},{18,20},{1... | collective-permute-start | bytes 3145736 | tf_op jit(solution)/shard_map/ppermute | solution.py:506
  105.6 1.2 collective-permute-start.19
  106.8 5.6 %collective-permute-start.22 = (f32[8,128]{1,0:T(8,128)S(1)}, f32[8,128]{1,0:T(8,128)S(1)}, u32[]{:S(2)}, u32[]{:S(2)}) collective-permute-start(f32[8,128]{1,0:T(8,128)S(1)} %merge_stats.1.refs_0_), channel_id=1, source_target_pairs={{0,6},{1,7},{2,4},{3,5},{4,2},{5,3},{6,0},{7,1},{8,14},{9,15},{10,... | collective-permute-start | bytes 12296 | tf_op jit(solution)/shard_map/ppermute | solution.py:480
  107.4 7.8 %collective-permute-start.21 = (f32[8,128]{1,0:T(8,128)S(1)}, f32[8,128]{1,0:T(8,128)S(1)}, u32[]{:S(2)}, u32[]{:S(2)}) collective-permute-start(f32[8,128]{1,0:T(8,128)S(1)} %merge_stats.1.refs_0_), channel_id=1, source_target_pairs={{0,4},{1,5},{2,6},{3,7},{4,0},{5,1},{6,2},{7,3},{8,12},{9,13},{10,... | collective-permute-start | bytes 12296 | tf_op jit(solution)/shard_map/ppermute | solution.py:480
  109.5 5.7 %collective-permute-start.20 = (f32[8,128]{1,0:T(8,128)S(1)}, f32[8,128]{1,0:T(8,128)S(1)}, u32[]{:S(2)}, u32[]{:S(2)}) collective-permute-start(f32[8,128]{1,0:T(8,128)S(1)} %merge_stats.1.refs_0_), channel_id=1, source_target_pairs={{0,2},{1,3},{2,0},{3,1},{4,6},{5,7},{6,4},{7,5},{8,10},{9,11},{10,... | collective-permute-start | bytes 12296 | tf_op jit(solution)/shard_map/ppermute | solution.py:480
  118.4 12.8 %collective-permute-start.28 = (bf16[128,1024]{1,0:T(8,128)(2,1)}, bf16[128,1024]{1,0:T(8,128)(2,1)S(1)}, u32[]{:S(2)}, u32[]{:S(2)}) collective-permute-start(bf16[128,1024]{1,0:T(8,128)(2,1)} %get-tuple-element.65), channel_id=1, source_target_pairs={{0,8},{8,0},{16,24},{24,16},{1,9},{9,1},{17,25},{25,17},{2,10},{10... | collective-permute-start | bytes 786440 | tf_op jit(solution)/shard_map/ppermute | solution.py:480
  122.7 12.6 %collective-permute-start.29 = (bf16[128,1024]{1,0:T(8,128)(2,1)}, bf16[128,1024]{1,0:T(8,128)(2,1)S(1)}, u32[]{:S(2)}, u32[]{:S(2)}) collective-permute-start(bf16[128,1024]{1,0:T(8,128)(2,1)} %get-tuple-element.66), channel_id=1, source_target_pairs={{0,16},{8,24},{16,0},{24,8},{1,17},{9,25},{17,1},{25,9},{2,18},{10... | collective-permute-start | bytes 786440 | tf_op jit(solution)/shard_map/ppermute | solution.py:480
  123.4 11.9 %collective-permute-start.30 = (bf16[128,1024]{1,0:T(8,128)(2,1)S(1)}, bf16[128,1024]{1,0:T(8,128)(2,1)S(1)}, u32[]{:S(2)}, u32[]{:S(2)}) collective-permute-start(bf16[128,1024]{1,0:T(8,128)(2,1)S(1)} %copy-done.8), channel_id=1, source_target_pairs={{0,24},{8,16},{16,8},{24,0},{1,25},{9,17},{17,9},{25,1},{2,26},{10... | collective-permute-start | bytes 786440 | tf_op jit(solution)/shard_map/ppermute | solution.py:480
  124.7 1.1 collective-permute-start.25
  125.8 3.5 %collective-permute-start.26 = (f32[1,128]{1,0:T(1,128)S(1)}, f32[1,128]{1,0:T(1,128)S(1)}, u32[]{:S(2)}, u32[]{:S(2)}) collective-permute-start(f32[1,128]{1,0:T(1,128)S(1)} %add.85), channel_id=1, source_target_pairs={{0,2},{1,3},{2,0},{3,1},{4,6},{5,7},{6,4},{7,5},{8,10},{9,11},{10,... | collective-permute-start | bytes 1544 | tf_op jit(solution)/shard_map/ppermute | solution.py:480
  129.4 11.3 %collective-permute-start.27 = (f32[1,128]{1,0:T(1,128)S(1)}, f32[1,128]{1,0:T(1,128)S(1)}, u32[]{:S(2)}, u32[]{:S(2)}) collective-permute-start(f32[1,128]{1,0:T(1,128)S(1)} %add.86), channel_id=1, source_target_pairs={{0,4},{1,5},{2,6},{3,7},{4,0},{5,1},{6,2},{7,3},{8,12},{9,13},{10,... | collective-permute-start | bytes 1544 | tf_op jit(solution)/shard_map/ppermute | solution.py:480
  (11 other events, 207.8 us)

commit v4 on v3

--- a/solution.py
+++ b/solution.py
@@ -269,7 +269,7 @@
         compiler_params=params(32),
         cost_estimate=COST,
         name="student_logits",
-    )(place, after, own, *near, *far, in_hbm(head))
+    )(place, after, own, *near, *far, head)
 
 
 def student_kernel(base_ref, labels_ref, mass_ref, logits_ref, stat_ref):
@@ -578,8 +578,8 @@
     label_column = lax.dynamic_slice_in_dim(labels, tok * rows, rows).reshape(rows, 1)
     scores = exchange_tok(scores)
     if in_line:
-        second, turned = lax.optimization_barrier((second, turned))
-        merged_inner, arrived = lax.optimization_barrier((plus(far_inner, second), arrived))
+        second, arrived, turned = lax.optimization_barrier((second, arrived, turned))
+        merged_inner = plus(far_inner, second)
         crossed = send(merged_inner, across)
         scores, merged_inner = lax.optimization_barrier((scores, merged_inner))
         sums = [x[None] for x in (own, third, crossed, arrived)]

time: 142 us -> 143 us (level)
  local copies, waits for them, and re-layouts: 3.88 us -> 8.62 us
  waiting for transfers between devices: 42.9 us -> 39.4 us
    ppermute x4, waiting for transfers between devices: 13.7 us -> 8.66 us  [send(): lax.ppermute(x, 'vocab', [(2 * a + c, 2 * b + c) for a, b in hops for c i...]
    unnamed x22 -> x30, local copies, waits for them, and re-layouts: 3.46 us -> 8.2 us
    all_to_all x1, waiting for transfers between devices: 12.1 us -> 16.8 us  [exchange_tok(): return lax.all_to_all(x, 'tok', split_axis=0, concat_axis=0, tiled=True)]
    ppermute x27, waiting for transfers between devices: 17.2 us -> 13.9 us  [swap(): lax.ppermute(x, axis, [(i, i ^ mask) for i in range(lax.axis_size(axis))])]
  transfers between devices with their start and end apart: 32 -> 32, of which waited for: 14 -> 15; matrix products, arithmetic and copies ran while one was open for 5% -> 5% of each run, Pallas kernels for 28% -> 27%
where the time goes in v4:
time: 143 us; the launch traced here: 142 us
  Pallas kernels  46.5 us (33%)
  starting transfers between devices  39.8 us (28%)
  waiting for transfers between devices  39.4 us (28%)
  local copies, waits for them, and re-layouts  8.62 us (6%)
  other arithmetic  7.1 us (5%)
    ppermute x27, starting transfers between devices, swap(): lax.ppermute(x, axis, [(i, i ^ mask) for i in range(lax.axis_size(axis))])  26.9 us
    all_to_all x1, waiting for transfers between devices, exchange_tok(): return lax.all_to_all(x, 'tok', split_axis=0, concat_axis=0, tiled=True)  16.8 us
    ppermute x27, waiting for transfers between devices, swap(): lax.ppermute(x, axis, [(i, i ^ mask) for i in range(lax.axis_size(axis))])  13.9 us
    pallas_call x2, Pallas kernels, chip_sums(): pl.pallas_call(functools.partial(sums_kernel, first=first, fan=fan, piece...  13 us
    pallas_call x1, Pallas kernels, student_logits(): pl.pallas_call(logits_kernel, grid=(cols // tile,), in_specs=[SMEM_SPEC,...  9.89 us
    ppermute x4, starting transfers between devices, send(): lax.ppermute(x, 'vocab', [(2 * a + c, 2 * b + c) for a, b in hops for c i...  9.24 us
    ppermute x4, waiting for transfers between devices, send(): lax.ppermute(x, 'vocab', [(2 * a + c, 2 * b + c) for a, b in hops for c i...  8.66 us
    unnamed x30, local copies, waits for them, and re-layouts  8.2 us
  transfers between devices with their start and end apart: 32, of which 15 were waited for; matrix products, arithmetic and copies ran while one was open for 5% of the time, Pallas kernels for 27%

profile of v4, /device:TPU:0, one launch (start us, length us, event | category | flops | bytes accessed | tf_op | source)
XLA Modules:
  0.0 142.2 jit_solution(7066413623720186846)
XLA Ops:
  4.6 5.0 %collective-permute-start.4 = (f32[8,128]{1,0:T(8,128)S(1)}, f32[8,128]{1,0:T(8,128)S(1)}, u32[]{:S(2)}, u32[]{:S(2)}) collective-permute-start(f32[8,128]{1,0:T(8,128)S(1)} %teacher_stats.1.refs_0_), channel_id=1, source_target_pairs={{0,6},{1,7},{2,4},{3,5},{4,2},{5,3},{6,0},{7,1},{8,14},{9,15},{10,... | collective-permute-start | bytes 12296 | tf_op jit(solution)/shard_map/ppermute | solution.py:480
  9.6 2.9 %collective-permute-start.3 = (f32[8,128]{1,0:T(8,128)S(1)}, f32[8,128]{1,0:T(8,128)S(1)}, u32[]{:S(2)}, u32[]{:S(2)}) collective-permute-start(f32[8,128]{1,0:T(8,128)S(1)} %teacher_stats.1.refs_0_), channel_id=1, source_target_pairs={{0,4},{1,5},{2,6},{3,7},{4,0},{5,1},{6,2},{7,3},{8,12},{9,13},{10,... | collective-permute-start | bytes 12296 | tf_op jit(solution)/shard_map/ppermute | solution.py:480
  12.6 1.6 %collective-permute-start.2 = (f32[8,128]{1,0:T(8,128)S(1)}, f32[8,128]{1,0:T(8,128)S(1)}, u32[]{:S(2)}, u32[]{:S(2)}) collective-permute-start(f32[8,128]{1,0:T(8,128)S(1)} %teacher_stats.1.refs_0_), channel_id=1, source_target_pairs={{0,2},{1,3},{2,0},{3,1},{4,6},{5,7},{6,4},{7,5},{8,10},{9,11},{10,... | collective-permute-start | bytes 12296 | tf_op jit(solution)/shard_map/ppermute | solution.py:480
  14.7 1.5 %collective-permute-done.2.refs_1_ = f32[8,128]{1,0:T(8,128)S(1)} collective-permute-done((f32[8,128]{1,0:T(8,128)S(1)}, f32[8,128]{1,0:T(8,128)S(1)}, u32[]{:S(2)}, u32[]{:S(2)}) %collective-permute-start.2) | collective-permute-done | bytes 4128 | tf_op jit(solution)/shard_map/ppermute | solution.py:480
  16.2 3.0 %entry_lists.1 = (s32[8,264]{1,0:T(8,128)S(1)}, s32[8]{0:T(128)S(1)}) custom-call(s32[128]{0:T(128)S(1)} %reshape.18.own_ref, s32[128]{0:T(128)S(1)} %collective-permute-done.peer_ref), custom_call_target="tpu_custom_call" | custom-call | flops 1024 | bytes 1024 | tf_op jit(solution)/shard_map/entry_lists/pallas_call | solution.py:117
  19.3 3.3 %teacher_probs.1 = bf16[2,32,128,128]{3,2,1,0:T(8,128)(2,1)S(1)} custom-call(bf16[128,4096]{1,0:T(8,128)(2,1)} %x_own.1, bf16[128,4096]{1,0:T(8,128)(2,1)S(1)} %collective-permute-done.1.x_peer, f32[8,128]{1,0:T(8,128)S(1)} %teacher_stats.1.refs_0_, f32[8,128]{1,0:T(8,128)S(1)} %collective-permute-done.2.refs_1_, ...), custom_call_target="tpu_custom_call" | custom-call | flops 1024 | bytes 1024 | tf_op jit(solution)/shard_map/teacher_probs/pallas_call | solution.py:194
  22.6 4.6 %chip_sums.2 = (bf16[32,128,128]{2,1,0:T(8,128)(2,1)}, f32[8,128]{1,0:T(8,128)S(1)}) custom-call(s32[2]{0:T(128)S(1)} %pad_add_fusion.spot_ref, s32[8,264]{1,0:T(8,128)S(1)} %get-tuple-element.35.list_ref, s32[8]{0:T(128)S(1)} %get-tuple-element.36.count_ref, bf16[64,128,128]{2,1,0:T(8,128)(2,1)S(1)} %bitcast.14, bf16[32,4,128,128]{3,2,1,0:T(8,128)(2,1)S(1)} %copy-done.2, ...), custom_call_target="tpu_custom_call" | custom-call | flops 1024 | bytes 1024 | tf_op jit(solution)/shard_map/chip_sums/pallas_call | solution.py:213
  27.2 3.9 %collective-permute-start.10 = (bf16[32,128,128]{2,1,0:T(8,128)(2,1)}, bf16[32,128,128]{2,1,0:T(8,128)(2,1)}, u32[]{:S(2)}, u32[]{:S(2)}) collective-permute-start(bf16[32,128,128]{2,1,0:T(8,128)(2,1)} %get-tuple-element.37), channel_id=1, source_target_pairs={{0,2},{1,3},{6,4},{7,5},{8,10},{9,11},{14,12},{15,13},{16,18},{17,... | collective-permute-start | bytes 3145736 | tf_op jit(solution)/shard_map/ppermute | solution.py:506
  31.1 2.5 %collective-permute-start.13 = (bf16[64,4608]{1,0:T(8,128)(2,1)S(1)}, bf16[64,4608]{1,0:T(8,128)(2,1)}, u32[]{:S(2)}, u32[]{:S(2)}) collective-permute-start(bf16[64,4608]{1,0:T(8,128)(2,1)S(1)} %constant_dynamic-slice_fusion), channel_id=1, source_target_pairs={{0,24},{8,16},{16,8},{24,0},{1,25},{9,17},{17,9},{25,1},{2,26},{10... | collective-permute-start | bytes 1769480 | tf_op jit(solution)/shard_map/ppermute | solution.py:480
  34.7 2.2 %copy-done.3 = bf16[32,4,128,128]{3,2,1,0:T(8,128)(2,1)S(1)} copy-done((bf16[32,4,128,128]{3,2,1,0:T(8,128)(2,1)S(1)}, bf16[32,4,128,128]{3,2,1,0:T(8,128)(2,1)}, u32[]{:S(2)}) %copy-start.3) | copy-done | bytes 4194328
  36.9 8.4 %chip_sums.3 = (bf16[32,128,128]{2,1,0:T(8,128)(2,1)}, bf16[32,128,128]{2,1,0:T(8,128)(2,1)}, bf16[32,128,128]{2,1,0:T(8,128)(2,1)}, f32[8,128]{1,0:T(8,128)S(1)}) custom-call(s32[2]{0:T(128)S(1)} %pad_add_fusion.spot_ref, s32[8,264]{1,0:T(8,128)S(1)} %get-tuple-element.35.list_ref, s32[8]{0:T(128)S(1)} %get-tuple-element.36.count_ref, ...), custom_call_target="tpu_custom_call" | custom-call | flops 1024 | bytes 1024 | tf_op jit(solution)/shard_map/chip_sums/pallas_call | solution.py:213
  45.3 2.4 %collective-permute-start.17 = (bf16[32,128,128]{2,1,0:T(8,128)(2,1)}, bf16[32,128,128]{2,1,0:T(8,128)(2,1)}, u32[]{:S(2)}, u32[]{:S(2)}) collective-permute-start(bf16[32,128,128]{2,1,0:T(8,128)(2,1)} %get-tuple-element.50), channel_id=1, source_target_pairs={{0,2},{1,3},{6,4},{7,5},{8,10},{9,11},{14,12},{15,13},{16,18},{17,... | collective-permute-start | bytes 3145736 | tf_op jit(solution)/shard_map/ppermute | solution.py:506
  47.7 6.2 %collective-permute-done.10 = bf16[32,128,128]{2,1,0:T(8,128)(2,1)} collective-permute-done((bf16[32,128,128]{2,1,0:T(8,128)(2,1)}, bf16[32,128,128]{2,1,0:T(8,128)(2,1)}, u32[]{:S(2)}, u32[]{:S(2)}) %collective-permute-start.10) | collective-permute-done | bytes 1048608 | tf_op jit(solution)/shard_map/ppermute | solution.py:506
  53.9 2.6 %add_convert_fusion.1 = bf16[32,128,128]{2,1,0:T(8,128)(2,1)} fusion(bf16[32,128,128]{2,1,0:T(8,128)(2,1)} %collective-permute-done.10, bf16[32,128,128]{2,1,0:T(8,128)(2,1)S(1)} %copy-done.11), kind=kLoop, calls=%fused_computation.1 | loop fusion | flops 2097152 | bytes 3145728 | tf_op jit(solution)/shard_map/convert_element_type | solution.py:498
  57.9 3.0 %collective-permute-done.12.refs_1_ = bf16[64,4608]{1,0:T(8,128)(2,1)} collective-permute-done((bf16[64,4608]{1,0:T(8,128)(2,1)S(1)}, bf16[64,4608]{1,0:T(8,128)(2,1)}, u32[]{:S(2)}, u32[]{:S(2)}) %collective-permute-start.12) | collective-permute-done | bytes 589856 | tf_op jit(solution)/shard_map/ppermute | solution.py:480
  61.5 2.4 %collective-permute-done.14.refs_3_ = bf16[64,4608]{1,0:T(8,128)(2,1)S(1)} collective-permute-done((bf16[64,4608]{1,0:T(8,128)(2,1)}, bf16[64,4608]{1,0:T(8,128)(2,1)S(1)}, u32[]{:S(2)}, u32[]{:S(2)}) %collective-permute-start.14) | collective-permute-done | bytes 589856 | tf_op jit(solution)/shard_map/ppermute | solution.py:480
  65.0 3.7 %copy-done.4 = bf16[4608,1024]{1,0:T(8,128)(2,1)S(1)} copy-done((bf16[4608,1024]{1,0:T(8,128)(2,1)S(1)}, bf16[4608,1024]{1,0:T(8,128)(2,1)}, u32[]{:S(2)}) %copy-start.4) | copy-done | bytes 9437208
  68.7 9.9 %student_logits.1 = (f32[4,128,1024]{2,1,0:T(8,128)}, bf16[4608,512]{1,0:T(8,128)(2,1)}) custom-call(s32[2]{0:T(128)S(1)} %pad_add_fusion.1.place_ref, f32[8,128]{1,0:T(8,128)S(1)} %add.81.after_ref.mass_ref, bf16[128,4608]{1,0:T(8,128)(2,1)S(1)} %copy-done.10, bf16[64,4608]{1,0:T(8,128)(2,1)} %collective-permute-done.11.refs_0_, ...), custom_call_target="tpu_custom_call" | custom-call | flops 1024 | bytes 1024 | tf_op jit(solution)/shard_map/student_logits/pallas_call | solution.py:257
  78.6 3.6 %all-to-all-start = ((f32[4,128,1024]{2,1,0:T(8,128)}), f32[4,128,1024]{2,1,0:T(8,128)S(1)}, u32[]{:S(2)}, u32[]{:S(2)}) async-start(f32[4,128,1024]{2,1,0:T(8,128)} %get-tuple-element.49), calls=%async_computation | async-start | bytes 4194304 | tf_op jit(solution)/shard_map/all_to_all | solution.py:502
  82.4 2.5 %collective-permute-done.18 = bf16[32,128,128]{2,1,0:T(8,128)(2,1)S(1)} collective-permute-done((bf16[32,128,128]{2,1,0:T(8,128)(2,1)}, bf16[32,128,128]{2,1,0:T(8,128)(2,1)S(1)}, u32[]{:S(2)}, u32[]{:S(2)}) %collective-permute-start.18) | collective-permute-done | bytes 1048608 | tf_op jit(solution)/shard_map/ppermute | solution.py:506
  85.9 3.0 %add_convert_fusion = bf16[32,128,128]{2,1,0:T(8,128)(2,1)} fusion(bf16[32,128,128]{2,1,0:T(8,128)(2,1)} %collective-permute-done.17, bf16[32,128,128]{2,1,0:T(8,128)(2,1)} %get-tuple-element.50), kind=kLoop, calls=%fused_computation | loop fusion | flops 2097152 | bytes 3145728 | tf_op jit(solution)/shard_map/convert_element_type | solution.py:498
  89.0 1.6 %collective-permute-start.24 = (bf16[32,128,128]{2,1,0:T(8,128)(2,1)}, bf16[32,128,128]{2,1,0:T(8,128)(2,1)}, u32[]{:S(2)}, u32[]{:S(2)}) collective-permute-start(bf16[32,128,128]{2,1,0:T(8,128)(2,1)} %add_convert_fusion), channel_id=1, source_target_pairs={{2,4},{3,5},{4,2},{5,3},{10,12},{11,13},{12,10},{13,11},{18,20},{1... | collective-permute-start | bytes 3145736 | tf_op jit(solution)/shard_map/ppermute | solution.py:506
  90.8 16.8 %all-to-all-done.logits_ref.refs_4_ = f32[4,128,1024]{2,1,0:T(8,128)S(1)} async-done(((f32[4,128,1024]{2,1,0:T(8,128)}), f32[4,128,1024]{2,1,0:T(8,128)S(1)}, u32[]{:S(2)}, u32[]{:S(2)}) %all-to-all-start) | async-done | bytes 2097184 | tf_op jit(solution)/shard_map/all_to_all | solution.py:502
  107.6 1.4 %student_stats.1.refs_0_ = f32[8,128]{1,0:T(8,128)S(1)} custom-call(s32[4]{0:T(128)S(1)} %add_multiply_fusion.base_ref, s32[128,1]{1,0:T(8,128)S(1)} %copy.13.labels_ref, f32[8,128]{1,0:T(8,128)S(1)} %add.81.after_ref.mass_ref, f32[4,128,1024]{2,1,0:T(8,128)S(1)} %all-to-all-done.logits_ref.refs_4_), custom_call_target="tpu_custom_call" | custom-call | flops 1024 | bytes 1024 | tf_op jit(solution)/shard_map/student_stats/pallas_call | solution.py:298
  111.9 2.8 %collective-permute-start.20 = (f32[8,128]{1,0:T(8,128)S(1)}, f32[8,128]{1,0:T(8,128)S(1)}, u32[]{:S(2)}, u32[]{:S(2)}) collective-permute-start(f32[8,128]{1,0:T(8,128)S(1)} %merge_stats.1.refs_0_), channel_id=1, source_target_pairs={{0,2},{1,3},{2,0},{3,1},{4,6},{5,7},{6,4},{7,5},{8,10},{9,11},{10,... | collective-permute-start | bytes 12296 | tf_op jit(solution)/shard_map/ppermute | solution.py:480
  116.5 2.9 %grad_logits.2 = (bf16[128,1024]{1,0:T(8,128)(2,1)}, bf16[128,1024]{1,0:T(8,128)(2,1)}, f32[1,128]{1,0:T(1,128)S(1)}) custom-call(s32[1]{0:T(128)} %bitcast.4.tok_ref, s32[4]{0:T(128)S(1)} %add_multiply_fusion.base_ref, s32[128,1]{1,0:T(8,128)S(1)} %copy.13.labels_ref, f32[128,128]{1,0:T(8,128)S(1)} %get-tuple-element.55.columns, ...), custom_call_target="tpu_custom_call" | custom-call | flops 1024 | bytes 1024 | tf_op jit(solution)/shard_map/grad_logits/pallas_call | solution.py:399
  120.8 2.8 %grad_logits.3 = (bf16[128,1024]{1,0:T(8,128)(2,1)}, bf16[128,1024]{1,0:T(8,128)(2,1)}, f32[1,128]{1,0:T(1,128)S(1)}) custom-call(s32[1]{0:T(128)} %bitcast.4.tok_ref, s32[4]{0:T(128)S(1)} %add_multiply_fusion.base_ref, s32[128,1]{1,0:T(8,128)S(1)} %copy.13.labels_ref, f32[128,128]{1,0:T(8,128)S(1)} %get-tuple-element.55.columns, ...), custom_call_target="tpu_custom_call" | custom-call | flops 1024 | bytes 1024 | tf_op jit(solution)/shard_map/grad_logits/pallas_call | solution.py:399
  124.2 1.5 %collective-permute-start.30 = (bf16[128,1024]{1,0:T(8,128)(2,1)S(1)}, bf16[128,1024]{1,0:T(8,128)(2,1)S(1)}, u32[]{:S(2)}, u32[]{:S(2)}) collective-permute-start(bf16[128,1024]{1,0:T(8,128)(2,1)S(1)} %copy-done.12), channel_id=1, source_target_pairs={{0,24},{8,16},{16,8},{24,0},{1,25},{9,17},{17,9},{25,1},{2,26},{10... | collective-permute-start | bytes 786440 | tf_op jit(solution)/shard_map/ppermute | solution.py:480
  126.8 2.0 %collective-permute-start.26 = (f32[1,128]{1,0:T(1,128)S(1)}, f32[1,128]{1,0:T(1,128)S(1)}, u32[]{:S(2)}, u32[]{:S(2)}) collective-permute-start(f32[1,128]{1,0:T(1,128)S(1)} %add.85), channel_id=1, source_target_pairs={{0,2},{1,3},{2,0},{3,1},{4,6},{5,7},{6,4},{7,5},{8,10},{9,11},{10,... | collective-permute-start | bytes 1544 | tf_op jit(solution)/shard_map/ppermute | solution.py:480
  128.8 1.5 %collective-permute-done.26 = f32[1,128]{1,0:T(1,128)S(1)} collective-permute-done((f32[1,128]{1,0:T(1,128)S(1)}, f32[1,128]{1,0:T(1,128)S(1)}, u32[]{:S(2)}, u32[]{:S(2)}) %collective-permute-start.26) | collective-permute-done | bytes 544 | tf_op jit(solution)/shard_map/ppermute | solution.py:480
  131.7 4.2 %first_product.1.acc_ref = f32[4608,1024]{1,0:T(8,128)S(1)} custom-call(bf16[4608,512]{1,0:T(8,128)(2,1)S(1)} %bitcast.13, bf16[128,1024]{1,0:T(8,128)(2,1)} %get-tuple-element.62.refs_0_, bf16[128,1024]{1,0:T(8,128)(2,1)S(1)} %collective-permute-done.28.refs_1_), custom_call_target="tpu_custom_call" | custom-call | flops 1024 | bytes 1024 | tf_op jit(solution)/shard_map/first_product/pallas_call | solution.py:449
  136.4 5.3 %last_product.1 = (bf16[4608,1024]{1,0:T(8,128)(2,1)}, f32[1,128]{1,0:T(1,128)S(1)}) custom-call(bf16[4608,512]{1,0:T(8,128)(2,1)S(1)} %bitcast.13, f32[4608,1024]{1,0:T(8,128)S(1)} %first_product.1.acc_ref, bf16[128,1024]{1,0:T(8,128)(2,1)S(1)} %collective-permute-done.29.refs_0_, bf16[128,1024]{1,0:T(8,128)(2,1)S(1)} %collective-permute-done.30.refs_1_), custom_call_target="tpu_custom_call" | custom-call | flops 1024 | bytes 1024 | tf_op jit(solution)/shard_map/last_product/pallas_call | solution.py:466
  (92 shorter events, 20.3 us)
Async XLA Ops:
  0.6 21.9 %collective-permute-start.9 = (bf16[32,4,128,128]{3,2,1,0:T(8,128)(2,1)}, bf16[32,4,128,128]{3,2,1,0:T(8,128)(2,1)}, u32[]{:S(2)}, u32[]{:S(2)}) collective-permute-start(bf16[32,4,128,128]{3,2,1,0:T(8,128)(2,1)} %w_own.3), channel_id=1, source_target_pairs={{0,1},{1,0},{2,3},{3,2},{4,5},{5,4},{6,7},{7,6},{8,9},{9,8},{10,11... | collective-permute-start | bytes 12582920 | tf_op jit(solution)/shard_map/ppermute | solution.py:480
  1.2 18.1 %collective-permute-start.1 = (bf16[128,4096]{1,0:T(8,128)(2,1)}, bf16[128,4096]{1,0:T(8,128)(2,1)S(1)}, u32[]{:S(2)}, u32[]{:S(2)}) collective-permute-start(bf16[128,4096]{1,0:T(8,128)(2,1)} %x_own.1), channel_id=1, source_target_pairs={{0,1},{1,0},{2,3},{3,2},{4,5},{5,4},{6,7},{7,6},{8,9},{9,8},{10,11... | collective-permute-start | bytes 3145736 | tf_op jit(solution)/shard_map/ppermute | solution.py:480
  3.1 9.5 %collective-permute-start.5 = (f32[8,128]{1,0:T(8,128)S(1)}, f32[8,128]{1,0:T(8,128)S(1)}, u32[]{:S(2)}, u32[]{:S(2)}) collective-permute-start(f32[8,128]{1,0:T(8,128)S(1)} %teacher_stats.1.refs_0_), channel_id=1, source_target_pairs={{0,1},{1,0},{2,3},{3,2},{4,5},{5,4},{6,7},{7,6},{8,9},{9,8},{10,11... | collective-permute-start | bytes 12296 | tf_op jit(solution)/shard_map/ppermute | solution.py:480
  4.4 5.2 %collective-permute-start = (s32[128]{0:T(128)S(1)}, s32[128]{0:T(128)S(1)}, u32[]{:S(2)}, u32[]{:S(2)}) collective-permute-start(s32[128]{0:T(128)S(1)} %reshape.18.own_ref), channel_id=1, source_target_pairs={{0,1},{1,0},{2,3},{3,2},{4,5},{5,4},{6,7},{7,6},{8,9},{9,8},{10,11... | collective-permute-start | bytes 1544 | tf_op jit(solution)/shard_map/ppermute | solution.py:480
  4.6 9.6 %collective-permute-start.4 = (f32[8,128]{1,0:T(8,128)S(1)}, f32[8,128]{1,0:T(8,128)S(1)}, u32[]{:S(2)}, u32[]{:S(2)}) collective-permute-start(f32[8,128]{1,0:T(8,128)S(1)} %teacher_stats.1.refs_0_), channel_id=1, source_target_pairs={{0,6},{1,7},{2,4},{3,5},{4,2},{5,3},{6,0},{7,1},{8,14},{9,15},{10,... | collective-permute-start | bytes 12296 | tf_op jit(solution)/shard_map/ppermute | solution.py:480
  9.6 4.5 %collective-permute-start.3 = (f32[8,128]{1,0:T(8,128)S(1)}, f32[8,128]{1,0:T(8,128)S(1)}, u32[]{:S(2)}, u32[]{:S(2)}) collective-permute-start(f32[8,128]{1,0:T(8,128)S(1)} %teacher_stats.1.refs_0_), channel_id=1, source_target_pairs={{0,4},{1,5},{2,6},{3,7},{4,0},{5,1},{6,2},{7,3},{8,12},{9,13},{10,... | collective-permute-start | bytes 12296 | tf_op jit(solution)/shard_map/ppermute | solution.py:480
  12.6 3.6 %collective-permute-start.2 = (f32[8,128]{1,0:T(8,128)S(1)}, f32[8,128]{1,0:T(8,128)S(1)}, u32[]{:S(2)}, u32[]{:S(2)}) collective-permute-start(f32[8,128]{1,0:T(8,128)S(1)} %teacher_stats.1.refs_0_), channel_id=1, source_target_pairs={{0,2},{1,3},{2,0},{3,1},{4,6},{5,7},{6,4},{7,5},{8,10},{9,11},{10,... | collective-permute-start | bytes 12296 | tf_op jit(solution)/shard_map/ppermute | solution.py:480
  14.1 5.1 %collective-permute-start.8 = (f32[8,128]{1,0:T(8,128)S(1)}, f32[8,128]{1,0:T(8,128)S(1)}, u32[]{:S(2)}, u32[]{:S(2)}) collective-permute-start(f32[8,128]{1,0:T(8,128)S(1)} %collective-permute-done.4.refs_3_), channel_id=1, source_target_pairs={{0,1},{1,0},{2,3},{3,2},{4,5},{5,4},{6,7},{7,6},{8,9},{9,8},{10,11... | collective-permute-start | bytes 12296 | tf_op jit(solution)/shard_map/ppermute | solution.py:480
  14.1 5.1 %collective-permute-start.7 = (f32[8,128]{1,0:T(8,128)S(1)}, f32[8,128]{1,0:T(8,128)S(1)}, u32[]{:S(2)}, u32[]{:S(2)}) collective-permute-start(f32[8,128]{1,0:T(8,128)S(1)} %collective-permute-done.3.refs_2_), channel_id=1, source_target_pairs={{0,1},{1,0},{2,3},{3,2},{4,5},{5,4},{6,7},{7,6},{8,9},{9,8},{10,11... | collective-permute-start | bytes 12296 | tf_op jit(solution)/shard_map/ppermute | solution.py:480
  16.2 3.1 %collective-permute-start.6 = (f32[8,128]{1,0:T(8,128)S(1)}, f32[8,128]{1,0:T(8,128)S(1)}, u32[]{:S(2)}, u32[]{:S(2)}) collective-permute-start(f32[8,128]{1,0:T(8,128)S(1)} %collective-permute-done.2.refs_1_), channel_id=1, source_target_pairs={{0,1},{1,0},{2,3},{3,2},{4,5},{5,4},{6,7},{7,6},{8,9},{9,8},{10,11... | collective-permute-start | bytes 12296 | tf_op jit(solution)/shard_map/ppermute | solution.py:480
  27.2 26.7 %collective-permute-start.10 = (bf16[32,128,128]{2,1,0:T(8,128)(2,1)}, bf16[32,128,128]{2,1,0:T(8,128)(2,1)}, u32[]{:S(2)}, u32[]{:S(2)}) collective-permute-start(bf16[32,128,128]{2,1,0:T(8,128)(2,1)} %get-tuple-element.37), channel_id=1, source_target_pairs={{0,2},{1,3},{6,4},{7,5},{8,10},{9,11},{14,12},{15,13},{16,18},{17,... | collective-permute-start | bytes 3145736 | tf_op jit(solution)/shard_map/ppermute | solution.py:506
  31.1 26.7 %collective-permute-start.13 = (bf16[64,4608]{1,0:T(8,128)(2,1)S(1)}, bf16[64,4608]{1,0:T(8,128)(2,1)}, u32[]{:S(2)}, u32[]{:S(2)}) collective-permute-start(bf16[64,4608]{1,0:T(8,128)(2,1)S(1)} %constant_dynamic-slice_fusion), channel_id=1, source_target_pairs={{0,24},{8,16},{16,8},{24,0},{1,25},{9,17},{17,9},{25,1},{2,26},{10... | collective-permute-start | bytes 1769480 | tf_op jit(solution)/shard_map/ppermute | solution.py:480
  33.7 27.2 %collective-permute-start.12 = (bf16[64,4608]{1,0:T(8,128)(2,1)S(1)}, bf16[64,4608]{1,0:T(8,128)(2,1)}, u32[]{:S(2)}, u32[]{:S(2)}) collective-permute-start(bf16[64,4608]{1,0:T(8,128)(2,1)S(1)} %constant_dynamic-slice_fusion), channel_id=1, source_target_pairs={{0,16},{8,24},{16,0},{24,8},{1,17},{9,25},{17,1},{25,9},{2,18},{10... | collective-permute-start | bytes 1769480 | tf_op jit(solution)/shard_map/ppermute | solution.py:480
  34.2 26.8 %collective-permute-start.11 = (bf16[64,4608]{1,0:T(8,128)(2,1)S(1)}, bf16[64,4608]{1,0:T(8,128)(2,1)}, u32[]{:S(2)}, u32[]{:S(2)}) collective-permute-start(bf16[64,4608]{1,0:T(8,128)(2,1)S(1)} %constant_dynamic-slice_fusion), channel_id=1, source_target_pairs={{0,8},{8,0},{16,24},{24,16},{1,9},{9,1},{17,25},{25,17},{2,10},{10... | collective-permute-start | bytes 1769480 | tf_op jit(solution)/shard_map/ppermute | solution.py:480
  45.3 37.1 %collective-permute-start.17 = (bf16[32,128,128]{2,1,0:T(8,128)(2,1)}, bf16[32,128,128]{2,1,0:T(8,128)(2,1)}, u32[]{:S(2)}, u32[]{:S(2)}) collective-permute-start(bf16[32,128,128]{2,1,0:T(8,128)(2,1)} %get-tuple-element.50), channel_id=1, source_target_pairs={{0,2},{1,3},{6,4},{7,5},{8,10},{9,11},{14,12},{15,13},{16,18},{17,... | collective-permute-start | bytes 3145736 | tf_op jit(solution)/shard_map/ppermute | solution.py:506
  56.6 28.3 %collective-permute-start.18 = (bf16[32,128,128]{2,1,0:T(8,128)(2,1)}, bf16[32,128,128]{2,1,0:T(8,128)(2,1)S(1)}, u32[]{:S(2)}, u32[]{:S(2)}) collective-permute-start(bf16[32,128,128]{2,1,0:T(8,128)(2,1)} %add_convert_fusion.1), channel_id=1, source_target_pairs={{2,6},{3,7},{4,0},{5,1},{10,14},{11,15},{12,8},{13,9},{18,22},{19,... | collective-permute-start | bytes 3145736 | tf_op jit(solution)/shard_map/ppermute | solution.py:506
  60.9 3.0 %collective-permute-start.14 = (bf16[64,4608]{1,0:T(8,128)(2,1)}, bf16[64,4608]{1,0:T(8,128)(2,1)S(1)}, u32[]{:S(2)}, u32[]{:S(2)}) collective-permute-start(bf16[64,4608]{1,0:T(8,128)(2,1)} %collective-permute-done.11.refs_0_), channel_id=1, source_target_pairs={{0,1},{1,0},{2,3},{3,2},{4,5},{5,4},{6,7},{7,6},{8,9},{9,8},{10,11... | collective-permute-start | bytes 1769480 | tf_op jit(solution)/shard_map/ppermute | solution.py:480
  60.9 3.2 %collective-permute-start.15 = (bf16[64,4608]{1,0:T(8,128)(2,1)}, bf16[64,4608]{1,0:T(8,128)(2,1)}, u32[]{:S(2)}, u32[]{:S(2)}) collective-permute-start(bf16[64,4608]{1,0:T(8,128)(2,1)} %collective-permute-done.12.refs_1_), channel_id=1, source_target_pairs={{0,1},{1,0},{2,3},{3,2},{4,5},{5,4},{6,7},{7,6},{8,9},{9,8},{10,11... | collective-permute-start | bytes 1769480 | tf_op jit(solution)/shard_map/ppermute | solution.py:480
  61.5 3.5 %collective-permute-start.16 = (bf16[64,4608]{1,0:T(8,128)(2,1)}, bf16[64,4608]{1,0:T(8,128)(2,1)}, u32[]{:S(2)}, u32[]{:S(2)}) collective-permute-start(bf16[64,4608]{1,0:T(8,128)(2,1)} %collective-permute-done.13.refs_2_), channel_id=1, source_target_pairs={{0,1},{1,0},{2,3},{3,2},{4,5},{5,4},{6,7},{7,6},{8,9},{9,8},{10,11... | collective-permute-start | bytes 1769480 | tf_op jit(solution)/shard_map/ppermute | solution.py:480
  78.6 29.0 %all-to-all-start = ((f32[4,128,1024]{2,1,0:T(8,128)}), f32[4,128,1024]{2,1,0:T(8,128)S(1)}, u32[]{:S(2)}, u32[]{:S(2)}) async-start(f32[4,128,1024]{2,1,0:T(8,128)} %get-tuple-element.49), calls=%async_computation | async-start | bytes 4194304 | tf_op jit(solution)/shard_map/all_to_all | solution.py:502
  82.2 34.2 %collective-permute-start.23 = (bf16[32,128,128]{2,1,0:T(8,128)(2,1)}, bf16[32,128,128]{2,1,0:T(8,128)(2,1)}, u32[]{:S(2)}, u32[]{:S(2)}) collective-permute-start(bf16[32,128,128]{2,1,0:T(8,128)(2,1)} %get-tuple-element.57), channel_id=1, source_target_pairs={{0,2},{1,3},{2,0},{3,1},{4,6},{5,7},{6,4},{7,5},{8,10},{9,11},{10,... | collective-permute-start | bytes 3145736 | tf_op jit(solution)/shard_map/ppermute | solution.py:480
  89.0 27.4 %collective-permute-start.24 = (bf16[32,128,128]{2,1,0:T(8,128)(2,1)}, bf16[32,128,128]{2,1,0:T(8,128)(2,1)}, u32[]{:S(2)}, u32[]{:S(2)}) collective-permute-start(bf16[32,128,128]{2,1,0:T(8,128)(2,1)} %add_convert_fusion), channel_id=1, source_target_pairs={{2,4},{3,5},{4,2},{5,3},{10,12},{11,13},{12,10},{13,11},{18,20},{1... | collective-permute-start | bytes 3145736 | tf_op jit(solution)/shard_map/ppermute | solution.py:506
  109.0 1.2 collective-permute-start.19
  110.2 5.5 %collective-permute-start.22 = (f32[8,128]{1,0:T(8,128)S(1)}, f32[8,128]{1,0:T(8,128)S(1)}, u32[]{:S(2)}, u32[]{:S(2)}) collective-permute-start(f32[8,128]{1,0:T(8,128)S(1)} %merge_stats.1.refs_0_), channel_id=1, source_target_pairs={{0,6},{1,7},{2,4},{3,5},{4,2},{5,3},{6,0},{7,1},{8,14},{9,15},{10,... | collective-permute-start | bytes 12296 | tf_op jit(solution)/shard_map/ppermute | solution.py:480
  111.1 4.7 %collective-permute-start.21 = (f32[8,128]{1,0:T(8,128)S(1)}, f32[8,128]{1,0:T(8,128)S(1)}, u32[]{:S(2)}, u32[]{:S(2)}) collective-permute-start(f32[8,128]{1,0:T(8,128)S(1)} %merge_stats.1.refs_0_), channel_id=1, source_target_pairs={{0,4},{1,5},{2,6},{3,7},{4,0},{5,1},{6,2},{7,3},{8,12},{9,13},{10,... | collective-permute-start | bytes 12296 | tf_op jit(solution)/shard_map/ppermute | solution.py:480
  111.9 4.4 %collective-permute-start.20 = (f32[8,128]{1,0:T(8,128)S(1)}, f32[8,128]{1,0:T(8,128)S(1)}, u32[]{:S(2)}, u32[]{:S(2)}) collective-permute-start(f32[8,128]{1,0:T(8,128)S(1)} %merge_stats.1.refs_0_), channel_id=1, source_target_pairs={{0,2},{1,3},{2,0},{3,1},{4,6},{5,7},{6,4},{7,5},{8,10},{9,11},{10,... | collective-permute-start | bytes 12296 | tf_op jit(solution)/shard_map/ppermute | solution.py:480
  119.4 12.3 %collective-permute-start.28 = (bf16[128,1024]{1,0:T(8,128)(2,1)}, bf16[128,1024]{1,0:T(8,128)(2,1)S(1)}, u32[]{:S(2)}, u32[]{:S(2)}) collective-permute-start(bf16[128,1024]{1,0:T(8,128)(2,1)} %get-tuple-element.63), channel_id=1, source_target_pairs={{0,8},{8,0},{16,24},{24,16},{1,9},{9,1},{17,25},{25,17},{2,10},{10... | collective-permute-start | bytes 786440 | tf_op jit(solution)/shard_map/ppermute | solution.py:480
  123.6 12.8 %collective-permute-start.29 = (bf16[128,1024]{1,0:T(8,128)(2,1)}, bf16[128,1024]{1,0:T(8,128)(2,1)S(1)}, u32[]{:S(2)}, u32[]{:S(2)}) collective-permute-start(bf16[128,1024]{1,0:T(8,128)(2,1)} %get-tuple-element.64), channel_id=1, source_target_pairs={{0,16},{8,24},{16,0},{24,8},{1,17},{9,25},{17,1},{25,9},{2,18},{10... | collective-permute-start | bytes 786440 | tf_op jit(solution)/shard_map/ppermute | solution.py:480
  124.2 12.2 %collective-permute-start.30 = (bf16[128,1024]{1,0:T(8,128)(2,1)S(1)}, bf16[128,1024]{1,0:T(8,128)(2,1)S(1)}, u32[]{:S(2)}, u32[]{:S(2)}) collective-permute-start(bf16[128,1024]{1,0:T(8,128)(2,1)S(1)} %copy-done.12), channel_id=1, source_target_pairs={{0,24},{8,16},{16,8},{24,0},{1,25},{9,17},{17,9},{25,1},{2,26},{10... | collective-permute-start | bytes 786440 | tf_op jit(solution)/shard_map/ppermute | solution.py:480
  125.7 1.1 collective-permute-start.25
  126.8 3.5 %collective-permute-start.26 = (f32[1,128]{1,0:T(1,128)S(1)}, f32[1,128]{1,0:T(1,128)S(1)}, u32[]{:S(2)}, u32[]{:S(2)}) collective-permute-start(f32[1,128]{1,0:T(1,128)S(1)} %add.85), channel_id=1, source_target_pairs={{0,2},{1,3},{2,0},{3,1},{4,6},{5,7},{6,4},{7,5},{8,10},{9,11},{10,... | collective-permute-start | bytes 1544 | tf_op jit(solution)/shard_map/ppermute | solution.py:480
  130.3 11.4 %collective-permute-start.27 = (f32[1,128]{1,0:T(1,128)S(1)}, f32[1,128]{1,0:T(1,128)S(1)}, u32[]{:S(2)}, u32[]{:S(2)}) collective-permute-start(f32[1,128]{1,0:T(1,128)S(1)} %add.86), channel_id=1, source_target_pairs={{0,4},{1,5},{2,6},{3,7},{4,0},{5,1},{6,2},{7,3},{8,12},{9,13},{10,... | collective-permute-start | bytes 1544 | tf_op jit(solution)/shard_map/ppermute | solution.py:480
  (15 other events, 233.1 us)

commit v5 on v4

--- a/solution.py
+++ b/solution.py
@@ -71,7 +71,7 @@
     total = jnp.zeros((rows, LANES), F32)
     for place in places:
         total = total + jnp.exp(read(place) - top)
-    stat_ref[...] = rows_from_columns([top, jnp.sum(total, axis=1, keepdims=True)])
+    stat_ref[...] = rows_from_columns([jnp.zeros_like(top), top, jnp.sum(total, axis=1, keepdims=True)])
 
 
 def teacher_stats(x):
@@ -130,7 +130,7 @@
 
     @pl.when(pl.program_id(0) == 0)
     def _():
-        top, total = total_at(split_rows(stats), 0, 1)
+        top, total = total_at(split_rows(stats), 1, 2)
         columns[...] = columns_from_rows([top, 1.0 / total])
 
     top, scale = columns[:, 0:1], columns[:, 1:2]
@@ -223,28 +223,55 @@
     )(spot, lists, counts, probs, w_own, w_peer)
 
 
-def logits_kernel(place_ref, after_ref, own_ref, *refs):
-    n_other = (len(refs) - 4) // 2
-    near, far, (head_ref, out_ref, turned_ref, everyone) = refs[:n_other], refs[n_other : 2 * n_other], refs[-4:]
+def stack_rows(place_ref, own_ref, near, far, everyone):
     rows = own_ref.shape[0]
     half = rows // 2
+    core = place_ref[0]
+    everyone[0:rows, :] = own_ref[...]
+    for r in range(len(near)):
+        start = (r + 1) * rows
+        everyone[pl.ds(pl.multiple_of(start + core * half, half), half), :] = near[r][...]
+        everyone[pl.ds(pl.multiple_of(start + (1 - core) * half, half), half), :] = far[r][...]
+
+
+def logits_kernel(place_ref, after_ref, own_ref, *refs):
+    n_other = (len(refs) - 3) // 2
+    near, far, (head_ref, out_ref, everyone) = refs[:n_other], refs[n_other : 2 * n_other], refs[-3:]
+    rows = own_ref.shape[0]
     del after_ref
 
     @pl.when(pl.program_id(0) == 0)
     def _():
-        core = place_ref[0]
-        everyone[0:rows, :] = own_ref[...]
-        for r in range(n_other):
-            start = (r + 1) * rows
-            everyone[pl.ds(pl.multiple_of(start + core * half, half), half), :] = near[r][...]
-            everyone[pl.ds(pl.multiple_of(start + (1 - core) * half, half), half), :] = far[r][...]
+        stack_rows(place_ref, own_ref, near, far, everyone)
 
     result = jnp.dot(everyone[...], head_ref[...], preferred_element_type=F32)
     for r in range(n_other + 1):
         out_ref[place_ref[1] ^ r] = result[r * rows : (r + 1) * rows, :]
-    part = turned_ref.shape[0]
-    start = pl.multiple_of(pl.program_id(0) * part, part)
-    turned_ref[...] = everyone[:, pl.ds(start, part)].T
+
+
+def turn_kernel(place_ref, own_ref, *refs):
+    n_other = (len(refs) - 2) // 2
+    near, far, (turned_ref, everyone) = refs[:n_other], refs[n_other : 2 * n_other], refs[-2:]
+    stack_rows(place_ref, own_ref, near, far, everyone)
+    turned_ref[...] = everyone[...].T
+
+
+def turned_rows(place, own, near, far):
+    rows, depth = own.shape
+    every = (len(near) + 1) * rows
+    steps = 4
+    part = depth // steps
+    return pl.pallas_call(
+        turn_kernel,
+        grid=(steps,),
+        in_specs=[SMEM_SPEC] + [pl.BlockSpec((x.shape[0], part), lambda i: (0, i)) for x in (own, *near, *far)],
+        out_specs=pl.BlockSpec((part, every), lambda i: (i, 0)),
+        out_shape=pltpu.HBM((depth, every), BF16),
+        scratch_shapes=[pltpu.VMEM((every, part), BF16)],
+        compiler_params=params(12),
+        cost_estimate=COST,
+        name="turned_rows",
+    )(place, own, *near, *far)
 
 
 def student_logits(place, after, own, near, far, head):
@@ -260,16 +287,13 @@
         in_specs=[SMEM_SPEC, pl.BlockSpec(memory_space=pl.ANY), whole(own.shape)]
         + [whole(x.shape) for x in near + far]
         + [pl.BlockSpec((depth, tile), lambda i: (0, i))],
-        out_specs=[
-            pl.BlockSpec((n_tok, rows, tile), lambda i: (0, 0, i)),
-            pl.BlockSpec((depth * tile // cols, every), lambda i: (i, 0)),
-        ],
-        out_shape=[pltpu.HBM((n_tok, rows, cols), F32), pltpu.HBM((depth, every), BF16)],
+        out_specs=pl.BlockSpec((n_tok, rows, tile), lambda i: (0, 0, i)),
+        out_shape=pltpu.HBM((n_tok, rows, cols), F32),
         scratch_shapes=[pltpu.VMEM((every, depth), BF16)],
         compiler_params=params(32),
         cost_estimate=COST,
         name="student_logits",
-    )(place, after, own, *near, *far, head)
+    )(place, after, own, *near, *far, in_hbm(head))
 
 
 def student_kernel(base_ref, labels_ref, mass_ref, logits_ref, stat_ref):
@@ -489,9 +513,17 @@
     return [x] + [swap(x, "vocab", r) for r in range(2, n, 2)]
 
 
-def gather_cores(x):
-    chips = gather_chips(x)
-    return chips + [swap(chip, "vocab", 1) for chip in chips]
+def butterfly(tile):
+    tiles, mask = [tile], 1
+    while mask < lax.axis_size("vocab"):
+        tile = merge_stats(tiles) if len(tiles) > 1 else tile
+        tiles = [tile, swap(tile, "vocab", mask)]
+        mask *= 2
+    return tiles
+
+
+def exchange_tok(x):
+    return lax.all_to_all(x, "tok", split_axis=0, concat_axis=0, tiled=True)
 
 
 def plus(a, b):
@@ -536,8 +568,7 @@
     peer_logits = swap(teacher_logits, "vocab", 1)
     peer_code = swap(code, "vocab", 1)
     peer_weight = swap(map_weight, "vocab", 1)
-    teacher = teacher_stats(teacher_logits)
-    totals = gather_cores(teacher)
+    totals = butterfly(teacher_stats(teacher_logits))
     lists, counts = plan(code, peer_code, 2 * n_z)
     probs = teacher_probs(teacher_logits, peer_logits, totals)
 
@@ -573,16 +604,20 @@
 
     far = [swap(x, "vocab", 1) for x in near]
     where = jnp.stack([vocab % 2, tok]).astype(jnp.int32)
-    scores, turned = student_logits(where, mass, hidden, near, far, new_head)
+    logits = student_logits(where, mass, hidden, near, far, new_head)
     base = (jnp.arange(n_tok, dtype=jnp.int32) * n_vocab + vocab) * new_cols
     label_column = lax.dynamic_slice_in_dim(labels, tok * rows, rows).reshape(rows, 1)
-    scores = exchange_tok(scores)
+    scores = exchange_tok(logits)
     if in_line:
-        second, arrived, turned = lax.optimization_barrier((second, arrived, turned))
+        second, arrived, logits = lax.optimization_barrier((second, arrived, logits))
         merged_inner = plus(far_inner, second)
         crossed = send(merged_inner, across)
-        scores, merged_inner = lax.optimization_barrier((scores, merged_inner))
+        where, merged_inner = lax.optimization_barrier((where, merged_inner))
+        turned = turned_rows(where, hidden, near, far)
+        scores, merged_inner, turned = lax.optimization_barrier((scores, merged_inner, turned))
         sums = [x[None] for x in (own, third, crossed, arrived)]
+    else:
+        turned = turned_rows(where, hidden, near, far)
     student = student_stats(base, label_column, mass, scores)
     student = merge_stats([student, swap(student, "vocab", 1)])
     stats = gather_chips(student)

time: 143 us -> 139 us (0.972)
  Pallas kernels: 46.5 us -> 51.3 us
  starting transfers between devices: 39.8 us -> 35.9 us
  waiting for transfers between devices: 39.4 us -> 36 us
  local copies, waits for them, and re-layouts: 8.62 us -> 7.08 us
    all_to_all x1, waiting for transfers between devices: 16.8 us -> 7 us  [exchange_tok(): return lax.all_to_all(x, 'tok', split_axis=0, concat_axis=0, tiled=True)]
    ppermute x27 -> x23, waiting for transfers between devices: 13.9 us -> 19.7 us  [swap(): lax.ppermute(x, axis, [(i, i ^ mask) for i in range(lax.axis_size(axis))])]
    pallas_call x0 -> x1, Pallas kernels: none -> 5.13 us  [turned_rows(): pl.pallas_call(turn_kernel, grid=(steps,), in_specs=[SMEM_SPEC] + [pl.Blo...]
    ppermute x27 -> x23, starting transfers between devices: 26.9 us -> 22.9 us  [swap(): lax.ppermute(x, axis, [(i, i ^ mask) for i in range(lax.axis_size(axis))])]
    unnamed x30 -> x34, local copies, waits for them, and re-layouts: 8.2 us -> 6.66 us
  transfers between devices with their start and end apart: 32 -> 28, of which waited for: 15 -> 17; matrix products, arithmetic and copies ran while one was open for 5% -> 5% of each run, Pallas kernels for 27% -> 32%
where the time goes in v5:
time: 139 us; the launch traced here: 138 us
  Pallas kernels  51.3 us (37%)
  waiting for transfers between devices  36 us (26%)
  starting transfers between devices  35.9 us (26%)
  other arithmetic  7.09 us (5%)
  local copies, waits for them, and re-layouts  7.08 us (5%)
    ppermute x23, starting transfers between devices, swap(): lax.ppermute(x, axis, [(i, i ^ mask) for i in range(lax.axis_size(axis))])  22.9 us
    ppermute x23, waiting for transfers between devices, swap(): lax.ppermute(x, axis, [(i, i ^ mask) for i in range(lax.axis_size(axis))])  19.7 us
    pallas_call x2, Pallas kernels, chip_sums(): pl.pallas_call(functools.partial(sums_kernel, first=first, fan=fan, piece...  12.7 us
    pallas_call x1, Pallas kernels, student_logits(): pl.pallas_call(logits_kernel, grid=(cols // tile,), in_specs=[SMEM_SPEC,...  9.7 us
    ppermute x4, starting transfers between devices, send(): lax.ppermute(x, 'vocab', [(2 * a + c, 2 * b + c) for a, b in hops for c i...  9.42 us
    ppermute x4, waiting for transfers between devices, send(): lax.ppermute(x, 'vocab', [(2 * a + c, 2 * b + c) for a, b in hops for c i...  9.24 us
    all_to_all x1, waiting for transfers between devices, exchange_tok(): return lax.all_to_all(x, 'tok', split_axis=0, concat_axis=0, tiled=True)  7 us
    unnamed x34, local copies, waits for them, and re-layouts  6.66 us
  transfers between devices with their start and end apart: 28, of which 17 were waited for; matrix products, arithmetic and copies ran while one was open for 5% of the time, Pallas kernels for 32%

profile of v5, /device:TPU:0, one launch (start us, length us, event | category | flops | bytes accessed | tf_op | source)
XLA Modules:
  0.0 138.3 jit_solution(16256997485272959224)
XLA Ops:
  3.5 5.8 %collective-permute-done.2.refs_1_ = f32[8,128]{1,0:T(8,128)S(1)} collective-permute-done((f32[8,128]{1,0:T(8,128)S(1)}, f32[8,128]{1,0:T(8,128)S(1)}, u32[]{:S(2)}, u32[]{:S(2)}) %collective-permute-start.2) | collective-permute-done | bytes 4128 | tf_op jit(solution)/shard_map/ppermute | solution.py:504
  9.4 2.3 %collective-permute-start.3 = (f32[8,128]{1,0:T(8,128)S(1)}, f32[8,128]{1,0:T(8,128)S(1)}, u32[]{:S(2)}, u32[]{:S(2)}) collective-permute-start(f32[8,128]{1,0:T(8,128)S(1)} %merge_stats.3.refs_0_), channel_id=1, source_target_pairs={{0,2},{1,3},{2,0},{3,1},{4,6},{5,7},{6,4},{7,5},{8,10},{9,11},{10,... | collective-permute-start | bytes 12296 | tf_op jit(solution)/shard_map/ppermute | solution.py:504
  13.2 3.1 %collective-permute-start.4 = (f32[8,128]{1,0:T(8,128)S(1)}, f32[8,128]{1,0:T(8,128)S(1)}, u32[]{:S(2)}, u32[]{:S(2)}) collective-permute-start(f32[8,128]{1,0:T(8,128)S(1)} %merge_stats.4.refs_0_), channel_id=1, source_target_pairs={{0,4},{1,5},{2,6},{3,7},{4,0},{5,1},{6,2},{7,3},{8,12},{9,13},{10,... | collective-permute-start | bytes 12296 | tf_op jit(solution)/shard_map/ppermute | solution.py:504
  16.4 3.0 %entry_lists.1 = (s32[8,264]{1,0:T(8,128)S(1)}, s32[8]{0:T(128)S(1)}) custom-call(s32[128]{0:T(128)S(1)} %reshape.18.own_ref, s32[128]{0:T(128)S(1)} %collective-permute-done.peer_ref), custom_call_target="tpu_custom_call" | custom-call | flops 1024 | bytes 1024 | tf_op jit(solution)/shard_map/entry_lists/pallas_call | solution.py:117
  19.4 3.2 %teacher_probs.1 = bf16[2,32,128,128]{3,2,1,0:T(8,128)(2,1)S(1)} custom-call(bf16[128,4096]{1,0:T(8,128)(2,1)} %x_own.1, bf16[128,4096]{1,0:T(8,128)(2,1)S(1)} %collective-permute-done.1.x_peer, f32[8,128]{1,0:T(8,128)S(1)} %merge_stats.4.refs_0_, f32[8,128]{1,0:T(8,128)S(1)} %collective-permute-done.4.refs_1_), custom_call_target="tpu_custom_call" | custom-call | flops 1024 | bytes 1024 | tf_op jit(solution)/shard_map/teacher_probs/pallas_call | solution.py:194
  22.7 4.6 %chip_sums.2 = (bf16[32,128,128]{2,1,0:T(8,128)(2,1)}, f32[8,128]{1,0:T(8,128)S(1)}) custom-call(s32[2]{0:T(128)S(1)} %pad_add_fusion.spot_ref, s32[8,264]{1,0:T(8,128)S(1)} %get-tuple-element.34.list_ref, s32[8]{0:T(128)S(1)} %get-tuple-element.35.count_ref, bf16[64,128,128]{2,1,0:T(8,128)(2,1)S(1)} %bitcast.14, bf16[32,4,128,128]{3,2,1,0:T(8,128)(2,1)S(1)} %copy-done.2, ...), custom_call_target="tpu_custom_call" | custom-call | flops 1024 | bytes 1024 | tf_op jit(solution)/shard_map/chip_sums/pallas_call | solution.py:213
  27.3 4.3 %collective-permute-start.6 = (bf16[32,128,128]{2,1,0:T(8,128)(2,1)}, bf16[32,128,128]{2,1,0:T(8,128)(2,1)}, u32[]{:S(2)}, u32[]{:S(2)}) collective-permute-start(bf16[32,128,128]{2,1,0:T(8,128)(2,1)} %get-tuple-element.36), channel_id=1, source_target_pairs={{0,2},{1,3},{6,4},{7,5},{8,10},{9,11},{14,12},{15,13},{16,18},{17,... | collective-permute-start | bytes 3145736 | tf_op jit(solution)/shard_map/ppermute | solution.py:538
  31.6 2.5 %collective-permute-start.9 = (bf16[64,4608]{1,0:T(8,128)(2,1)S(1)}, bf16[64,4608]{1,0:T(8,128)(2,1)}, u32[]{:S(2)}, u32[]{:S(2)}) collective-permute-start(bf16[64,4608]{1,0:T(8,128)(2,1)S(1)} %constant_dynamic-slice_fusion), channel_id=1, source_target_pairs={{0,24},{8,16},{16,8},{24,0},{1,25},{9,17},{17,9},{25,1},{2,26},{10... | collective-permute-start | bytes 1769480 | tf_op jit(solution)/shard_map/ppermute | solution.py:504
  35.1 2.2 %copy-done.3 = bf16[32,4,128,128]{3,2,1,0:T(8,128)(2,1)S(1)} copy-done((bf16[32,4,128,128]{3,2,1,0:T(8,128)(2,1)S(1)}, bf16[32,4,128,128]{3,2,1,0:T(8,128)(2,1)}, u32[]{:S(2)}) %copy-start.3) | copy-done | bytes 4194328
  37.3 8.1 %chip_sums.3 = (bf16[32,128,128]{2,1,0:T(8,128)(2,1)}, bf16[32,128,128]{2,1,0:T(8,128)(2,1)}, bf16[32,128,128]{2,1,0:T(8,128)(2,1)}, f32[8,128]{1,0:T(8,128)S(1)}) custom-call(s32[2]{0:T(128)S(1)} %pad_add_fusion.spot_ref, s32[8,264]{1,0:T(8,128)S(1)} %get-tuple-element.34.list_ref, s32[8]{0:T(128)S(1)} %get-tuple-element.35.count_ref, ...), custom_call_target="tpu_custom_call" | custom-call | flops 1024 | bytes 1024 | tf_op jit(solution)/shard_map/chip_sums/pallas_call | solution.py:213
  45.5 2.2 %collective-permute-start.13 = (bf16[32,128,128]{2,1,0:T(8,128)(2,1)}, bf16[32,128,128]{2,1,0:T(8,128)(2,1)}, u32[]{:S(2)}, u32[]{:S(2)}) collective-permute-start(bf16[32,128,128]{2,1,0:T(8,128)(2,1)} %get-tuple-element.48), channel_id=1, source_target_pairs={{0,2},{1,3},{6,4},{7,5},{8,10},{9,11},{14,12},{15,13},{16,18},{17,... | collective-permute-start | bytes 3145736 | tf_op jit(solution)/shard_map/ppermute | solution.py:538
  47.7 6.7 %collective-permute-done.6 = bf16[32,128,128]{2,1,0:T(8,128)(2,1)} collective-permute-done((bf16[32,128,128]{2,1,0:T(8,128)(2,1)}, bf16[32,128,128]{2,1,0:T(8,128)(2,1)}, u32[]{:S(2)}, u32[]{:S(2)}) %collective-permute-start.6) | collective-permute-done | bytes 1048608 | tf_op jit(solution)/shard_map/ppermute | solution.py:538
  54.4 2.6 %add_convert_fusion.1 = bf16[32,128,128]{2,1,0:T(8,128)(2,1)} fusion(bf16[32,128,128]{2,1,0:T(8,128)(2,1)} %collective-permute-done.6, bf16[32,128,128]{2,1,0:T(8,128)(2,1)S(1)} %copy-done.13), kind=kLoop, calls=%fused_computation.1 | loop fusion | flops 2097152 | bytes 3145728 | tf_op jit(solution)/shard_map/convert_element_type | solution.py:530
  60.4 1.6 %collective-permute-done.10.refs_3_ = bf16[64,4608]{1,0:T(8,128)(2,1)S(1)} collective-permute-done((bf16[64,4608]{1,0:T(8,128)(2,1)}, bf16[64,4608]{1,0:T(8,128)(2,1)S(1)}, u32[]{:S(2)}, u32[]{:S(2)}) %collective-permute-start.10) | collective-permute-done | bytes 589856 | tf_op jit(solution)/shard_map/ppermute | solution.py:504
  63.7 9.7 %student_logits.1 = f32[4,128,1024]{2,1,0:T(8,128)} custom-call(s32[2]{0:T(128)S(1)} %pad_add_fusion.1.place_ref, f32[8,128]{1,0:T(8,128)S(1)} %add.81.after_ref.mass_ref, bf16[128,4608]{1,0:T(8,128)(2,1)S(1)} %copy-done.4, bf16[64,4608]{1,0:T(8,128)(2,1)} %collective-permute-done.7.refs_0_, bf16[64,4608]{1,0:T(8,128)(2,1)} %collective-permute-done.8.refs_1_, ...), custom_call_target="tpu_custom_call" | custom-call | flops 1024 | bytes 1024 | tf_op jit(solution)/shard_map/student_logits/pallas_call | solution.py:284
  73.4 3.6 %all-to-all-start = ((f32[4,128,1024]{2,1,0:T(8,128)}), f32[4,128,1024]{2,1,0:T(8,128)S(1)}, u32[]{:S(2)}, u32[]{:S(2)}) async-start(f32[4,128,1024]{2,1,0:T(8,128)} %student_logits.1), calls=%async_computation | async-start | bytes 4194304 | tf_op jit(solution)/shard_map/all_to_all | solution.py:534
  77.0 2.7 %collective-permute-start.19 = (bf16[32,128,128]{2,1,0:T(8,128)(2,1)}, bf16[32,128,128]{2,1,0:T(8,128)(2,1)}, u32[]{:S(2)}, u32[]{:S(2)}) collective-permute-start(bf16[32,128,128]{2,1,0:T(8,128)(2,1)} %get-tuple-element.55), channel_id=1, source_target_pairs={{0,2},{1,3},{2,0},{3,1},{4,6},{5,7},{6,4},{7,5},{8,10},{9,11},{10,... | collective-permute-start | bytes 3145736 | tf_op jit(solution)/shard_map/ppermute | solution.py:504
  79.7 2.5 %collective-permute-done.14 = bf16[32,128,128]{2,1,0:T(8,128)(2,1)} collective-permute-done((bf16[32,128,128]{2,1,0:T(8,128)(2,1)}, bf16[32,128,128]{2,1,0:T(8,128)(2,1)}, u32[]{:S(2)}, u32[]{:S(2)}) %collective-permute-start.14) | collective-permute-done | bytes 1048608 | tf_op jit(solution)/shard_map/ppermute | solution.py:538
  82.2 3.0 %add_convert_fusion = bf16[32,128,128]{2,1,0:T(8,128)(2,1)} fusion(bf16[32,128,128]{2,1,0:T(8,128)(2,1)} %collective-permute-done.13, bf16[32,128,128]{2,1,0:T(8,128)(2,1)} %get-tuple-element.48), kind=kLoop, calls=%fused_computation | loop fusion | flops 2097152 | bytes 3145728 | tf_op jit(solution)/shard_map/convert_element_type | solution.py:530
  85.3 1.6 %collective-permute-start.20 = (bf16[32,128,128]{2,1,0:T(8,128)(2,1)}, bf16[32,128,128]{2,1,0:T(8,128)(2,1)}, u32[]{:S(2)}, u32[]{:S(2)}) collective-permute-start(bf16[32,128,128]{2,1,0:T(8,128)(2,1)} %add_convert_fusion), channel_id=1, source_target_pairs={{2,4},{3,5},{4,2},{5,3},{10,12},{11,13},{12,10},{13,11},{18,20},{1... | collective-permute-start | bytes 3145736 | tf_op jit(solution)/shard_map/ppermute | solution.py:538
  90.3 5.1 %turned_rows.1.a_ref = bf16[4608,512]{1,0:T(8,128)(2,1)} custom-call(s32[2]{0:T(128)S(1)} %pad_add_fusion.1.place_ref, bf16[128,4608]{1,0:T(8,128)(2,1)S(1)} %copy-done.4, bf16[64,4608]{1,0:T(8,128)(2,1)} %collective-permute-done.7.refs_0_, bf16[64,4608]{1,0:T(8,128)(2,1)} %collective-permute-done.8.refs_1_, ...), custom_call_target="tpu_custom_call" | custom-call | flops 1024 | bytes 1024 | tf_op jit(solution)/shard_map/turned_rows/pallas_call | solution.py:264
  95.4 7.0 %all-to-all-done.logits_ref.refs_4_ = f32[4,128,1024]{2,1,0:T(8,128)S(1)} async-done(((f32[4,128,1024]{2,1,0:T(8,128)}), f32[4,128,1024]{2,1,0:T(8,128)S(1)}, u32[]{:S(2)}, u32[]{:S(2)}) %all-to-all-start) | async-done | bytes 2097184 | tf_op jit(solution)/shard_map/all_to_all | solution.py:534
  102.5 1.5 %student_stats.1.refs_0_ = f32[8,128]{1,0:T(8,128)S(1)} custom-call(s32[4]{0:T(128)S(1)} %add_multiply_fusion.base_ref, s32[128,1]{1,0:T(8,128)S(1)} %copy.13.labels_ref, f32[8,128]{1,0:T(8,128)S(1)} %add.81.after_ref.mass_ref, f32[4,128,1024]{2,1,0:T(8,128)S(1)} %all-to-all-done.logits_ref.refs_4_), custom_call_target="tpu_custom_call" | custom-call | flops 1024 | bytes 1024 | tf_op jit(solution)/shard_map/student_stats/pallas_call | solution.py:322
  105.8 3.3 %collective-permute-start.17 = (f32[8,128]{1,0:T(8,128)S(1)}, f32[8,128]{1,0:T(8,128)S(1)}, u32[]{:S(2)}, u32[]{:S(2)}) collective-permute-start(f32[8,128]{1,0:T(8,128)S(1)} %merge_stats.5.refs_0_), channel_id=1, source_target_pairs={{0,4},{1,5},{2,6},{3,7},{4,0},{5,1},{6,2},{7,3},{8,12},{9,13},{10,... | collective-permute-start | bytes 12296 | tf_op jit(solution)/shard_map/ppermute | solution.py:504
  110.7 2.0 %collective-permute-done.16.refs_1_ = f32[8,128]{1,0:T(8,128)S(1)} collective-permute-done((f32[8,128]{1,0:T(8,128)S(1)}, f32[8,128]{1,0:T(8,128)S(1)}, u32[]{:S(2)}, u32[]{:S(2)}) %collective-permute-start.16) | collective-permute-done | bytes 4128 | tf_op jit(solution)/shard_map/ppermute | solution.py:504
  112.9 3.0 %grad_logits.2 = (bf16[128,1024]{1,0:T(8,128)(2,1)}, bf16[128,1024]{1,0:T(8,128)(2,1)}, f32[1,128]{1,0:T(1,128)S(1)}) custom-call(s32[1]{0:T(128)} %bitcast.4.tok_ref, s32[4]{0:T(128)S(1)} %add_multiply_fusion.base_ref, s32[128,1]{1,0:T(8,128)S(1)} %copy.13.labels_ref, f32[128,128]{1,0:T(8,128)S(1)} %get-tuple-element.53.columns, ...), custom_call_target="tpu_custom_call" | custom-call | flops 1024 | bytes 1024 | tf_op jit(solution)/shard_map/grad_logits/pallas_call | solution.py:423
  115.9 1.4 %collective-permute-start.24 = (bf16[128,1024]{1,0:T(8,128)(2,1)}, bf16[128,1024]{1,0:T(8,128)(2,1)S(1)}, u32[]{:S(2)}, u32[]{:S(2)}) collective-permute-start(bf16[128,1024]{1,0:T(8,128)(2,1)} %get-tuple-element.61), channel_id=1, source_target_pairs={{0,8},{8,0},{16,24},{24,16},{1,9},{9,1},{17,25},{25,17},{2,10},{10... | collective-permute-start | bytes 786440 | tf_op jit(solution)/shard_map/ppermute | solution.py:504
  117.3 2.9 %grad_logits.3 = (bf16[128,1024]{1,0:T(8,128)(2,1)}, bf16[128,1024]{1,0:T(8,128)(2,1)}, f32[1,128]{1,0:T(1,128)S(1)}) custom-call(s32[1]{0:T(128)} %bitcast.4.tok_ref, s32[4]{0:T(128)S(1)} %add_multiply_fusion.base_ref, s32[128,1]{1,0:T(8,128)S(1)} %copy.13.labels_ref, f32[128,128]{1,0:T(8,128)S(1)} %get-tuple-element.53.columns, ...), custom_call_target="tpu_custom_call" | custom-call | flops 1024 | bytes 1024 | tf_op jit(solution)/shard_map/grad_logits/pallas_call | solution.py:423
  120.8 1.5 %collective-permute-start.26 = (bf16[128,1024]{1,0:T(8,128)(2,1)S(1)}, bf16[128,1024]{1,0:T(8,128)(2,1)S(1)}, u32[]{:S(2)}, u32[]{:S(2)}) collective-permute-start(bf16[128,1024]{1,0:T(8,128)(2,1)S(1)} %copy-done.14), channel_id=1, source_target_pairs={{0,24},{8,16},{16,8},{24,0},{1,25},{9,17},{17,9},{25,1},{2,26},{10... | collective-permute-start | bytes 786440 | tf_op jit(solution)/shard_map/ppermute | solution.py:504
  124.1 2.8 %collective-permute-done.22 = f32[1,128]{1,0:T(1,128)S(1)} collective-permute-done((f32[1,128]{1,0:T(1,128)S(1)}, f32[1,128]{1,0:T(1,128)S(1)}, u32[]{:S(2)}, u32[]{:S(2)}) %collective-permute-start.22) | collective-permute-done | bytes 544 | tf_op jit(solution)/shard_map/ppermute | solution.py:504
  127.9 4.1 %first_product.1.acc_ref = f32[4608,1024]{1,0:T(8,128)S(1)} custom-call(bf16[4608,512]{1,0:T(8,128)(2,1)S(1)} %bitcast.13, bf16[128,1024]{1,0:T(8,128)(2,1)} %get-tuple-element.60.refs_0_, bf16[128,1024]{1,0:T(8,128)(2,1)S(1)} %collective-permute-done.24.refs_1_), custom_call_target="tpu_custom_call" | custom-call | flops 1024 | bytes 1024 | tf_op jit(solution)/shard_map/first_product/pallas_call | solution.py:473
  132.4 5.3 %last_product.1 = (bf16[4608,1024]{1,0:T(8,128)(2,1)}, f32[1,128]{1,0:T(1,128)S(1)}) custom-call(bf16[4608,512]{1,0:T(8,128)(2,1)S(1)} %bitcast.13, f32[4608,1024]{1,0:T(8,128)S(1)} %first_product.1.acc_ref, bf16[128,1024]{1,0:T(8,128)(2,1)S(1)} %collective-permute-done.25.refs_0_, bf16[128,1024]{1,0:T(8,128)(2,1)S(1)} %collective-permute-done.26.refs_1_), custom_call_target="tpu_custom_call" | custom-call | flops 1024 | bytes 1024 | tf_op jit(solution)/shard_map/last_product/pallas_call | solution.py:490
  (91 shorter events, 21.9 us)
Async XLA Ops:
  0.6 86.3 %copy-start = (s32[512]{0:T(512)S(1)}, s32[512]{0:T(512)}, u32[]{:S(2)}) copy-start(s32[512]{0:T(512)} %param.9) | copy-start | bytes 6148
  0.6 22.0 %collective-permute-start.5 = (bf16[32,4,128,128]{3,2,1,0:T(8,128)(2,1)}, bf16[32,4,128,128]{3,2,1,0:T(8,128)(2,1)}, u32[]{:S(2)}, u32[]{:S(2)}) collective-permute-start(bf16[32,4,128,128]{3,2,1,0:T(8,128)(2,1)} %w_own.3), channel_id=1, source_target_pairs={{0,1},{1,0},{2,3},{3,2},{4,5},{5,4},{6,7},{7,6},{8,9},{9,8},{10,11... | collective-permute-start | bytes 12582920 | tf_op jit(solution)/shard_map/ppermute | solution.py:504
  1.2 18.3 %collective-permute-start.1 = (bf16[128,4096]{1,0:T(8,128)(2,1)}, bf16[128,4096]{1,0:T(8,128)(2,1)S(1)}, u32[]{:S(2)}, u32[]{:S(2)}) collective-permute-start(bf16[128,4096]{1,0:T(8,128)(2,1)} %x_own.1), channel_id=1, source_target_pairs={{0,1},{1,0},{2,3},{3,2},{4,5},{5,4},{6,7},{7,6},{8,9},{9,8},{10,11... | collective-permute-start | bytes 3145736 | tf_op jit(solution)/shard_map/ppermute | solution.py:504
  3.1 6.3 %collective-permute-start.2 = (f32[8,128]{1,0:T(8,128)S(1)}, f32[8,128]{1,0:T(8,128)S(1)}, u32[]{:S(2)}, u32[]{:S(2)}) collective-permute-start(f32[8,128]{1,0:T(8,128)S(1)} %teacher_stats.1.refs_0_), channel_id=1, source_target_pairs={{0,1},{1,0},{2,3},{3,2},{4,5},{5,4},{6,7},{7,6},{8,9},{9,8},{10,11... | collective-permute-start | bytes 12296 | tf_op jit(solution)/shard_map/ppermute | solution.py:504
  9.4 3.8 %collective-permute-start.3 = (f32[8,128]{1,0:T(8,128)S(1)}, f32[8,128]{1,0:T(8,128)S(1)}, u32[]{:S(2)}, u32[]{:S(2)}) collective-permute-start(f32[8,128]{1,0:T(8,128)S(1)} %merge_stats.3.refs_0_), channel_id=1, source_target_pairs={{0,2},{1,3},{2,0},{3,1},{4,6},{5,7},{6,4},{7,5},{8,10},{9,11},{10,... | collective-permute-start | bytes 12296 | tf_op jit(solution)/shard_map/ppermute | solution.py:504
  12.5 3.9 %collective-permute-start = (s32[128]{0:T(128)S(1)}, s32[128]{0:T(128)S(1)}, u32[]{:S(2)}, u32[]{:S(2)}) collective-permute-start(s32[128]{0:T(128)S(1)} %reshape.18.own_ref), channel_id=1, source_target_pairs={{0,1},{1,0},{2,3},{3,2},{4,5},{5,4},{6,7},{7,6},{8,9},{9,8},{10,11... | collective-permute-start | bytes 1544 | tf_op jit(solution)/shard_map/ppermute | solution.py:504
  13.2 6.2 %collective-permute-start.4 = (f32[8,128]{1,0:T(8,128)S(1)}, f32[8,128]{1,0:T(8,128)S(1)}, u32[]{:S(2)}, u32[]{:S(2)}) collective-permute-start(f32[8,128]{1,0:T(8,128)S(1)} %merge_stats.4.refs_0_), channel_id=1, source_target_pairs={{0,4},{1,5},{2,6},{3,7},{4,0},{5,1},{6,2},{7,3},{8,12},{9,13},{10,... | collective-permute-start | bytes 12296 | tf_op jit(solution)/shard_map/ppermute | solution.py:504
  27.3 27.1 %collective-permute-start.6 = (bf16[32,128,128]{2,1,0:T(8,128)(2,1)}, bf16[32,128,128]{2,1,0:T(8,128)(2,1)}, u32[]{:S(2)}, u32[]{:S(2)}) collective-permute-start(bf16[32,128,128]{2,1,0:T(8,128)(2,1)} %get-tuple-element.36), channel_id=1, source_target_pairs={{0,2},{1,3},{6,4},{7,5},{8,10},{9,11},{14,12},{15,13},{16,18},{17,... | collective-permute-start | bytes 3145736 | tf_op jit(solution)/shard_map/ppermute | solution.py:538
  31.5 22.9 %copy-start.13 = (bf16[32,128,128]{2,1,0:T(8,128)(2,1)S(1)}, bf16[32,128,128]{2,1,0:T(8,128)(2,1)}, u32[]{:S(2)}) copy-start(bf16[32,128,128]{2,1,0:T(8,128)(2,1)} %get-tuple-element.36) | copy-start | bytes 3145732
  31.6 26.8 %collective-permute-start.9 = (bf16[64,4608]{1,0:T(8,128)(2,1)S(1)}, bf16[64,4608]{1,0:T(8,128)(2,1)}, u32[]{:S(2)}, u32[]{:S(2)}) collective-permute-start(bf16[64,4608]{1,0:T(8,128)(2,1)S(1)} %constant_dynamic-slice_fusion), channel_id=1, source_target_pairs={{0,24},{8,16},{16,8},{24,0},{1,25},{9,17},{17,9},{25,1},{2,26},{10... | collective-permute-start | bytes 1769480 | tf_op jit(solution)/shard_map/ppermute | solution.py:504
  34.1 25.6 %collective-permute-start.8 = (bf16[64,4608]{1,0:T(8,128)(2,1)S(1)}, bf16[64,4608]{1,0:T(8,128)(2,1)}, u32[]{:S(2)}, u32[]{:S(2)}) collective-permute-start(bf16[64,4608]{1,0:T(8,128)(2,1)S(1)} %constant_dynamic-slice_fusion), channel_id=1, source_target_pairs={{0,16},{8,24},{16,0},{24,8},{1,17},{9,25},{17,1},{25,9},{2,18},{10... | collective-permute-start | bytes 1769480 | tf_op jit(solution)/shard_map/ppermute | solution.py:504
  34.6 25.2 %collective-permute-start.7 = (bf16[64,4608]{1,0:T(8,128)(2,1)S(1)}, bf16[64,4608]{1,0:T(8,128)(2,1)}, u32[]{:S(2)}, u32[]{:S(2)}) collective-permute-start(bf16[64,4608]{1,0:T(8,128)(2,1)S(1)} %constant_dynamic-slice_fusion), channel_id=1, source_target_pairs={{0,8},{8,0},{16,24},{24,16},{1,9},{9,1},{17,25},{25,17},{2,10},{10... | collective-permute-start | bytes 1769480 | tf_op jit(solution)/shard_map/ppermute | solution.py:504
  45.5 34.2 %collective-permute-start.13 = (bf16[32,128,128]{2,1,0:T(8,128)(2,1)}, bf16[32,128,128]{2,1,0:T(8,128)(2,1)}, u32[]{:S(2)}, u32[]{:S(2)}) collective-permute-start(bf16[32,128,128]{2,1,0:T(8,128)(2,1)} %get-tuple-element.48), channel_id=1, source_target_pairs={{0,2},{1,3},{6,4},{7,5},{8,10},{9,11},{14,12},{15,13},{16,18},{17,... | collective-permute-start | bytes 3145736 | tf_op jit(solution)/shard_map/ppermute | solution.py:538
  57.1 25.2 %collective-permute-start.14 = (bf16[32,128,128]{2,1,0:T(8,128)(2,1)}, bf16[32,128,128]{2,1,0:T(8,128)(2,1)}, u32[]{:S(2)}, u32[]{:S(2)}) collective-permute-start(bf16[32,128,128]{2,1,0:T(8,128)(2,1)} %add_convert_fusion.1), channel_id=1, source_target_pairs={{2,6},{3,7},{4,0},{5,1},{10,14},{11,15},{12,8},{13,9},{18,22},{19,... | collective-permute-start | bytes 3145736 | tf_op jit(solution)/shard_map/ppermute | solution.py:538
  59.8 2.2 %collective-permute-start.10 = (bf16[64,4608]{1,0:T(8,128)(2,1)}, bf16[64,4608]{1,0:T(8,128)(2,1)S(1)}, u32[]{:S(2)}, u32[]{:S(2)}) collective-permute-start(bf16[64,4608]{1,0:T(8,128)(2,1)} %collective-permute-done.7.refs_0_), channel_id=1, source_target_pairs={{0,1},{1,0},{2,3},{3,2},{4,5},{5,4},{6,7},{7,6},{8,9},{9,8},{10,11... | collective-permute-start | bytes 1769480 | tf_op jit(solution)/shard_map/ppermute | solution.py:504
  59.8 3.1 %collective-permute-start.11 = (bf16[64,4608]{1,0:T(8,128)(2,1)}, bf16[64,4608]{1,0:T(8,128)(2,1)S(1)}, u32[]{:S(2)}, u32[]{:S(2)}) collective-permute-start(bf16[64,4608]{1,0:T(8,128)(2,1)} %collective-permute-done.8.refs_1_), channel_id=1, source_target_pairs={{0,1},{1,0},{2,3},{3,2},{4,5},{5,4},{6,7},{7,6},{8,9},{9,8},{10,11... | collective-permute-start | bytes 1769480 | tf_op jit(solution)/shard_map/ppermute | solution.py:504
  60.3 3.4 %collective-permute-start.12 = (bf16[64,4608]{1,0:T(8,128)(2,1)}, bf16[64,4608]{1,0:T(8,128)(2,1)S(1)}, u32[]{:S(2)}, u32[]{:S(2)}) collective-permute-start(bf16[64,4608]{1,0:T(8,128)(2,1)} %collective-permute-done.9.refs_2_), channel_id=1, source_target_pairs={{0,1},{1,0},{2,3},{3,2},{4,5},{5,4},{6,7},{7,6},{8,9},{9,8},{10,11... | collective-permute-start | bytes 1769480 | tf_op jit(solution)/shard_map/ppermute | solution.py:504
  73.4 29.0 %all-to-all-start = ((f32[4,128,1024]{2,1,0:T(8,128)}), f32[4,128,1024]{2,1,0:T(8,128)S(1)}, u32[]{:S(2)}, u32[]{:S(2)}) async-start(f32[4,128,1024]{2,1,0:T(8,128)} %student_logits.1), calls=%async_computation | async-start | bytes 4194304 | tf_op jit(solution)/shard_map/all_to_all | solution.py:534
  77.0 35.8 %collective-permute-start.19 = (bf16[32,128,128]{2,1,0:T(8,128)(2,1)}, bf16[32,128,128]{2,1,0:T(8,128)(2,1)}, u32[]{:S(2)}, u32[]{:S(2)}) collective-permute-start(bf16[32,128,128]{2,1,0:T(8,128)(2,1)} %get-tuple-element.55), channel_id=1, source_target_pairs={{0,2},{1,3},{2,0},{3,1},{4,6},{5,7},{6,4},{7,5},{8,10},{9,11},{10,... | collective-permute-start | bytes 3145736 | tf_op jit(solution)/shard_map/ppermute | solution.py:504
  85.3 27.5 %collective-permute-start.20 = (bf16[32,128,128]{2,1,0:T(8,128)(2,1)}, bf16[32,128,128]{2,1,0:T(8,128)(2,1)}, u32[]{:S(2)}, u32[]{:S(2)}) collective-permute-start(bf16[32,128,128]{2,1,0:T(8,128)(2,1)} %add_convert_fusion), channel_id=1, source_target_pairs={{2,4},{3,5},{4,2},{5,3},{10,12},{11,13},{12,10},{13,11},{18,20},{1... | collective-permute-start | bytes 3145736 | tf_op jit(solution)/shard_map/ppermute | solution.py:538
  95.4 17.4 %copy-start.6 = (bf16[32,128,128]{2,1,0:T(8,128)(2,1)S(1)}, bf16[32,128,128]{2,1,0:T(8,128)(2,1)}, u32[]{:S(2)}) copy-start(bf16[32,128,128]{2,1,0:T(8,128)(2,1)} %get-tuple-element.54) | copy-start | bytes 3145732
  103.9 1.2 collective-permute-start.15
  105.1 5.5 %collective-permute-start.18 = (f32[8,128]{1,0:T(8,128)S(1)}, f32[8,128]{1,0:T(8,128)S(1)}, u32[]{:S(2)}, u32[]{:S(2)}) collective-permute-start(f32[8,128]{1,0:T(8,128)S(1)} %merge_stats.5.refs_0_), channel_id=1, source_target_pairs={{0,6},{1,7},{2,4},{3,5},{4,2},{5,3},{6,0},{7,1},{8,14},{9,15},{10,... | collective-permute-start | bytes 12296 | tf_op jit(solution)/shard_map/ppermute | solution.py:504
  105.8 5.0 %collective-permute-start.17 = (f32[8,128]{1,0:T(8,128)S(1)}, f32[8,128]{1,0:T(8,128)S(1)}, u32[]{:S(2)}, u32[]{:S(2)}) collective-permute-start(f32[8,128]{1,0:T(8,128)S(1)} %merge_stats.5.refs_0_), channel_id=1, source_target_pairs={{0,4},{1,5},{2,6},{3,7},{4,0},{5,1},{6,2},{7,3},{8,12},{9,13},{10,... | collective-permute-start | bytes 12296 | tf_op jit(solution)/shard_map/ppermute | solution.py:504
  109.1 3.6 %collective-permute-start.16 = (f32[8,128]{1,0:T(8,128)S(1)}, f32[8,128]{1,0:T(8,128)S(1)}, u32[]{:S(2)}, u32[]{:S(2)}) collective-permute-start(f32[8,128]{1,0:T(8,128)S(1)} %merge_stats.5.refs_0_), channel_id=1, source_target_pairs={{0,2},{1,3},{2,0},{3,1},{4,6},{5,7},{6,4},{7,5},{8,10},{9,11},{10,... | collective-permute-start | bytes 12296 | tf_op jit(solution)/shard_map/ppermute | solution.py:504
  112.7 15.2 %slice-start = ((s8[4718592]{0:T(1024)(128)(4,1)}), s8[4194304]{0:T(1024)(128)(4,1)S(1)}, s32[]{:S(2)}) async-start(s8[4718592]{0:T(1024)(128)(4,1)} %bitcast.12), calls=%async_computation.1 | async-start | bytes 8388608
  115.9 11.9 %collective-permute-start.24 = (bf16[128,1024]{1,0:T(8,128)(2,1)}, bf16[128,1024]{1,0:T(8,128)(2,1)S(1)}, u32[]{:S(2)}, u32[]{:S(2)}) collective-permute-start(bf16[128,1024]{1,0:T(8,128)(2,1)} %get-tuple-element.61), channel_id=1, source_target_pairs={{0,8},{8,0},{16,24},{24,16},{1,9},{9,1},{17,25},{25,17},{2,10},{10... | collective-permute-start | bytes 786440 | tf_op jit(solution)/shard_map/ppermute | solution.py:504
  120.2 12.2 %collective-permute-start.25 = (bf16[128,1024]{1,0:T(8,128)(2,1)}, bf16[128,1024]{1,0:T(8,128)(2,1)S(1)}, u32[]{:S(2)}, u32[]{:S(2)}) collective-permute-start(bf16[128,1024]{1,0:T(8,128)(2,1)} %get-tuple-element.62), channel_id=1, source_target_pairs={{0,16},{8,24},{16,0},{24,8},{1,17},{9,25},{17,1},{25,9},{2,18},{10... | collective-permute-start | bytes 786440 | tf_op jit(solution)/shard_map/ppermute | solution.py:504
  120.8 11.7 %collective-permute-start.26 = (bf16[128,1024]{1,0:T(8,128)(2,1)S(1)}, bf16[128,1024]{1,0:T(8,128)(2,1)S(1)}, u32[]{:S(2)}, u32[]{:S(2)}) collective-permute-start(bf16[128,1024]{1,0:T(8,128)(2,1)S(1)} %copy-done.14), channel_id=1, source_target_pairs={{0,24},{8,16},{16,8},{24,0},{1,25},{9,17},{17,9},{25,1},{2,26},{10... | collective-permute-start | bytes 786440 | tf_op jit(solution)/shard_map/ppermute | solution.py:504
  122.3 1.1 collective-permute-start.21
  123.4 3.5 %collective-permute-start.22 = (f32[1,128]{1,0:T(1,128)S(1)}, f32[1,128]{1,0:T(1,128)S(1)}, u32[]{:S(2)}, u32[]{:S(2)}) collective-permute-start(f32[1,128]{1,0:T(1,128)S(1)} %add.85), channel_id=1, source_target_pairs={{0,2},{1,3},{2,0},{3,1},{4,6},{5,7},{6,4},{7,5},{8,10},{9,11},{10,... | collective-permute-start | bytes 1544 | tf_op jit(solution)/shard_map/ppermute | solution.py:504
  126.9 10.8 %collective-permute-start.23 = (f32[1,128]{1,0:T(1,128)S(1)}, f32[1,128]{1,0:T(1,128)S(1)}, u32[]{:S(2)}, u32[]{:S(2)}) collective-permute-start(f32[1,128]{1,0:T(1,128)S(1)} %add.86), channel_id=1, source_target_pairs={{0,4},{1,5},{2,6},{3,7},{4,0},{5,1},{6,2},{7,3},{8,12},{9,13},{10,... | collective-permute-start | bytes 1544 | tf_op jit(solution)/shard_map/ppermute | solution.py:504
  (13 other events, 76.1 us)

commit v6 on v5

--- a/solution.py
+++ b/solution.py
@@ -410,8 +410,10 @@
 
 
 def token_group(step, tok_ref, groups):
-    first, last = groups
-    return tok_ref[0] ^ (first + step * (last - first))
+    r = groups[0]
+    for i in range(1, len(groups)):
+        r = jnp.where(step == i, groups[i], r)
+    return tok_ref[0] ^ r
 
 
 def grad_logits(tok, base, label_column, columns, sums, logits, groups):
@@ -454,10 +456,11 @@
 
 
 def first_product_kernel(a_ref, *refs):
-    pieces, (acc_ref, b_ref) = refs[:-2], refs[-2:]
+    pieces, (acc_ref, end_ref, b_ref) = refs[:-3], refs[-3:]
     stack_pieces(pieces, b_ref)
     rows, part = product_part(a_ref, b_ref, 0)
     acc_ref[rows, :] = part
+    end_ref[...] = jnp.zeros_like(end_ref)
 
 
 def last_product_kernel(a_ref, acc_ref, *refs):
@@ -474,8 +477,8 @@
         first_product_kernel,
         grid=(4,),
         in_specs=[VMEM_SPEC] + [pl.BlockSpec((rows, n), lambda i: (0, 0))] * len(pieces),
-        out_specs=VMEM_SPEC,
-        out_shape=pltpu.VMEM((a.shape[0], n), F32),
+        out_specs=[VMEM_SPEC, pl.BlockSpec((1, rows), lambda i: (0, 0))],
+        out_shape=[pltpu.VMEM((a.shape[0], n), F32), jax.ShapeDtypeStruct((1, rows), F32)],
         scratch_shapes=[pltpu.VMEM((len(pieces) * rows, n), BF16)],
         compiler_params=params(16),
         cost_estimate=COST,
@@ -514,11 +517,11 @@
 
 
 def butterfly(tile):
-    tiles, mask = [tile], 1
-    while mask < lax.axis_size("vocab"):
+    n = lax.axis_size("vocab")
+    tiles, masks = [tile], [1 << k for k in range(1, n.bit_length() - 1)] + [1]
+    for mask in masks:
         tile = merge_stats(tiles) if len(tiles) > 1 else tile
         tiles = [tile, swap(tile, "vocab", mask)]
-        mask *= 2
     return tiles
 
 
@@ -613,11 +616,11 @@
         merged_inner = plus(far_inner, second)
         crossed = send(merged_inner, across)
         where, merged_inner = lax.optimization_barrier((where, merged_inner))
-        turned = turned_rows(where, hidden, near, far)
+        turned = turned_rows(where, hidden, near[-1:] + near[:-1], far[-1:] + far[:-1])
         scores, merged_inner, turned = lax.optimization_barrier((scores, merged_inner, turned))
         sums = [x[None] for x in (own, third, crossed, arrived)]
     else:
-        turned = turned_rows(where, hidden, near, far)
+        turned = turned_rows(where, hidden, near[-1:] + near[:-1], far[-1:] + far[:-1])
     student = student_stats(base, label_column, mass, scores)
     student = merge_stats([student, swap(student, "vocab", 1)])
     stats = gather_chips(student)
@@ -625,17 +628,18 @@
     group = tok.astype(jnp.int32).reshape(1)
     columns, base_loss = token_totals(stats)
     grad_args = (group, base, label_column, columns, sums, scores)
-    beside_x, across_xy, inner = grad_logits(*grad_args, (1, 3))
-    beside_x, across_xy = swap(beside_x, "tok", 1), swap(across_xy, "tok", 3)
-    beside_y, here, inner_b = grad_logits(*grad_args, (2, 0))
-    beside_y = swap(beside_y, "tok", 2)
+    far_group, inner = grad_logits(*grad_args, (3,))
+    far_group = swap(far_group, "tok", 3)
+    beside_x, beside_y, here, inner_b = grad_logits(*grad_args, (1, 2, 0))
+    beside_x, beside_y = swap(beside_x, "tok", 1), swap(beside_y, "tok", 2)
     inner = inner + inner_b
-    acc = first_product(turned, [here, beside_x])
-    head_grad, end = last_product(turned, acc, [beside_y, across_xy])
+    acc, middle = first_product(turned, [here, far_group])
+    head_grad, end = last_product(turned, acc, [beside_x, beside_y])
     mask = 1
     while mask < n_vocab:
-        other = swap(inner, "vocab", mask)
-        inner = inner + other
+        inner = inner + swap(inner, "vocab", mask)
+        if mask == 2:
+            inner = inner + middle
         mask *= 2
     return ((base_loss - inner + end).reshape(rows), head_grad)
 

time: 139 us -> 135 us (0.971)
  waiting for transfers between devices: 36 us -> 31.2 us
    ppermute x23, waiting for transfers between devices: 19.7 us -> 14 us  [swap(): lax.ppermute(x, axis, [(i, i ^ mask) for i in range(lax.axis_size(axis))])]
    ppermute x4, waiting for transfers between devices: 9.24 us -> 12.3 us  [send(): lax.ppermute(x, 'vocab', [(2 * a + c, 2 * b + c) for a, b in hops for c i...]
    all_to_all x1, waiting for transfers between devices: 7 us -> 4.89 us  [exchange_tok(): return lax.all_to_all(x, 'tok', split_axis=0, concat_axis=0, tiled=True)]
    unnamed x34 -> x32, local copies, waits for them, and re-layouts: 6.66 us -> 6.65 us
  transfers between devices with their start and end apart: 28 -> 28, of which waited for: 17 -> 15; matrix products, arithmetic and copies ran while one was open for 5% -> 5% of each run, Pallas kernels for 32% -> 33%
where the time goes in v6:
time: 135 us; the launch traced here: 134 us
  Pallas kernels  51.7 us (38%)
  starting transfers between devices  36.5 us (27%)
  waiting for transfers between devices  31.2 us (23%)
  other arithmetic  7.1 us (5%)
  local copies, waits for them, and re-layouts  7.07 us (5%)
    ppermute x23, starting transfers between devices, swap(): lax.ppermute(x, axis, [(i, i ^ mask) for i in range(lax.axis_size(axis))])  23.7 us
    ppermute x23, waiting for transfers between devices, swap(): lax.ppermute(x, axis, [(i, i ^ mask) for i in range(lax.axis_size(axis))])  14 us
    pallas_call x2, Pallas kernels, chip_sums(): pl.pallas_call(functools.partial(sums_kernel, first=first, fan=fan, piece...  12.4 us
    ppermute x4, waiting for transfers between devices, send(): lax.ppermute(x, 'vocab', [(2 * a + c, 2 * b + c) for a, b in hops for c i...  12.3 us
    pallas_call x1, Pallas kernels, student_logits(): pl.pallas_call(logits_kernel, grid=(cols // tile,), in_specs=[SMEM_SPEC,...  9.7 us
    ppermute x4, starting transfers between devices, send(): lax.ppermute(x, 'vocab', [(2 * a + c, 2 * b + c) for a, b in hops for c i...  9.16 us
    unnamed x32, local copies, waits for them, and re-layouts  6.65 us
    pallas_call x2, Pallas kernels, grad_logits(): pl.pallas_call(functools.partial(grad_kernel, n_sums=len(sums), groups=gr...  6.49 us
  transfers between devices with their start and end apart: 28, of which 15 were waited for; matrix products, arithmetic and copies ran while one was open for 5% of the time, Pallas kernels for 33%

profile of v6, /device:TPU:0, one launch (start us, length us, event | category | flops | bytes accessed | tf_op | source)
XLA Modules:
  0.0 134.4 jit_solution(16276255854462793624)
XLA Ops:
  3.1 3.0 %collective-permute-start.2 = (f32[8,128]{1,0:T(8,128)S(1)}, f32[8,128]{1,0:T(8,128)S(1)}, u32[]{:S(2)}, u32[]{:S(2)}) collective-permute-start(f32[8,128]{1,0:T(8,128)S(1)} %teacher_stats.1.refs_0_), channel_id=1, source_target_pairs={{0,2},{1,3},{2,0},{3,1},{4,6},{5,7},{6,4},{7,5},{8,10},{9,11},{10,... | collective-permute-start | bytes 12296 | tf_op jit(solution)/shard_map/ppermute | solution.py:507
  6.1 1.6 %collective-permute-done.2.refs_1_ = f32[8,128]{1,0:T(8,128)S(1)} collective-permute-done((f32[8,128]{1,0:T(8,128)S(1)}, f32[8,128]{1,0:T(8,128)S(1)}, u32[]{:S(2)}, u32[]{:S(2)}) %collective-permute-start.2) | collective-permute-done | bytes 4128 | tf_op jit(solution)/shard_map/ppermute | solution.py:507
  7.7 3.1 %collective-permute-start.3 = (f32[8,128]{1,0:T(8,128)S(1)}, f32[8,128]{1,0:T(8,128)S(1)}, u32[]{:S(2)}, u32[]{:S(2)}) collective-permute-start(f32[8,128]{1,0:T(8,128)S(1)} %merge_stats.3.refs_0_), channel_id=1, source_target_pairs={{0,4},{1,5},{2,6},{3,7},{4,0},{5,1},{6,2},{7,3},{8,12},{9,13},{10,... | collective-permute-start | bytes 12296 | tf_op jit(solution)/shard_map/ppermute | solution.py:507
  12.9 3.0 %entry_lists.1 = (s32[8,264]{1,0:T(8,128)S(1)}, s32[8]{0:T(128)S(1)}) custom-call(s32[128]{0:T(128)S(1)} %reshape.18.own_ref, s32[128]{0:T(128)S(1)} %collective-permute-done.peer_ref), custom_call_target="tpu_custom_call" | custom-call | flops 1024 | bytes 1024 | tf_op jit(solution)/shard_map/entry_lists/pallas_call | solution.py:117
  15.9 3.2 %teacher_probs.1 = bf16[2,32,128,128]{3,2,1,0:T(8,128)(2,1)S(1)} custom-call(bf16[128,4096]{1,0:T(8,128)(2,1)} %x_own.1, bf16[128,4096]{1,0:T(8,128)(2,1)S(1)} %collective-permute-done.1.x_peer, f32[8,128]{1,0:T(8,128)S(1)} %merge_stats.4.refs_0_, f32[8,128]{1,0:T(8,128)S(1)} %collective-permute-done.4.refs_1_), custom_call_target="tpu_custom_call" | custom-call | flops 1024 | bytes 1024 | tf_op jit(solution)/shard_map/teacher_probs/pallas_call | solution.py:194
  19.2 5.1 %chip_sums.2 = (bf16[32,128,128]{2,1,0:T(8,128)(2,1)}, f32[8,128]{1,0:T(8,128)S(1)}) custom-call(s32[2]{0:T(128)S(1)} %pad_add_fusion.spot_ref, s32[8,264]{1,0:T(8,128)S(1)} %get-tuple-element.36.list_ref, s32[8]{0:T(128)S(1)} %get-tuple-element.37.count_ref, bf16[64,128,128]{2,1,0:T(8,128)(2,1)S(1)} %bitcast.14, bf16[32,4,128,128]{3,2,1,0:T(8,128)(2,1)S(1)} %copy-done.2, ...), custom_call_target="tpu_custom_call" | custom-call | flops 1024 | bytes 1024 | tf_op jit(solution)/shard_map/chip_sums/pallas_call | solution.py:213
  24.3 4.0 %collective-permute-start.6 = (bf16[32,128,128]{2,1,0:T(8,128)(2,1)}, bf16[32,128,128]{2,1,0:T(8,128)(2,1)}, u32[]{:S(2)}, u32[]{:S(2)}) collective-permute-start(bf16[32,128,128]{2,1,0:T(8,128)(2,1)} %get-tuple-element.38), channel_id=1, source_target_pairs={{0,2},{1,3},{6,4},{7,5},{8,10},{9,11},{14,12},{15,13},{16,18},{17,... | collective-permute-start | bytes 3145736 | tf_op jit(solution)/shard_map/ppermute | solution.py:541
  28.3 2.5 %collective-permute-start.9 = (bf16[64,4608]{1,0:T(8,128)(2,1)S(1)}, bf16[64,4608]{1,0:T(8,128)(2,1)}, u32[]{:S(2)}, u32[]{:S(2)}) collective-permute-start(bf16[64,4608]{1,0:T(8,128)(2,1)S(1)} %constant_dynamic-slice_fusion), channel_id=1, source_target_pairs={{0,24},{8,16},{16,8},{24,0},{1,25},{9,17},{17,9},{25,1},{2,26},{10... | collective-permute-start | bytes 1769480 | tf_op jit(solution)/shard_map/ppermute | solution.py:507
  31.9 2.2 %copy-done.3 = bf16[32,4,128,128]{3,2,1,0:T(8,128)(2,1)S(1)} copy-done((bf16[32,4,128,128]{3,2,1,0:T(8,128)(2,1)S(1)}, bf16[32,4,128,128]{3,2,1,0:T(8,128)(2,1)}, u32[]{:S(2)}) %copy-start.3) | copy-done | bytes 4194328
  34.1 7.4 %chip_sums.3 = (bf16[32,128,128]{2,1,0:T(8,128)(2,1)}, bf16[32,128,128]{2,1,0:T(8,128)(2,1)}, bf16[32,128,128]{2,1,0:T(8,128)(2,1)}, f32[8,128]{1,0:T(8,128)S(1)}) custom-call(s32[2]{0:T(128)S(1)} %pad_add_fusion.spot_ref, s32[8,264]{1,0:T(8,128)S(1)} %get-tuple-element.36.list_ref, s32[8]{0:T(128)S(1)} %get-tuple-element.37.count_ref, ...), custom_call_target="tpu_custom_call" | custom-call | flops 1024 | bytes 1024 | tf_op jit(solution)/shard_map/chip_sums/pallas_call | solution.py:213
  41.4 2.2 %collective-permute-start.13 = (bf16[32,128,128]{2,1,0:T(8,128)(2,1)}, bf16[32,128,128]{2,1,0:T(8,128)(2,1)}, u32[]{:S(2)}, u32[]{:S(2)}) collective-permute-start(bf16[32,128,128]{2,1,0:T(8,128)(2,1)} %get-tuple-element.50), channel_id=1, source_target_pairs={{0,2},{1,3},{6,4},{7,5},{8,10},{9,11},{14,12},{15,13},{16,18},{17,... | collective-permute-start | bytes 3145736 | tf_op jit(solution)/shard_map/ppermute | solution.py:541
  43.7 7.4 %collective-permute-done.6 = bf16[32,128,128]{2,1,0:T(8,128)(2,1)} collective-permute-done((bf16[32,128,128]{2,1,0:T(8,128)(2,1)}, bf16[32,128,128]{2,1,0:T(8,128)(2,1)}, u32[]{:S(2)}, u32[]{:S(2)}) %collective-permute-start.6) | collective-permute-done | bytes 1048608 | tf_op jit(solution)/shard_map/ppermute | solution.py:541
  51.1 2.6 %add_convert_fusion.1 = bf16[32,128,128]{2,1,0:T(8,128)(2,1)} fusion(bf16[32,128,128]{2,1,0:T(8,128)(2,1)} %collective-permute-done.6, bf16[32,128,128]{2,1,0:T(8,128)(2,1)S(1)} %copy-done.13), kind=kLoop, calls=%fused_computation.1 | loop fusion | flops 2097152 | bytes 3145728 | tf_op jit(solution)/shard_map/convert_element_type | solution.py:533
  55.0 2.7 %collective-permute-done.8.refs_1_.refs_2_ = bf16[64,4608]{1,0:T(8,128)(2,1)} collective-permute-done((bf16[64,4608]{1,0:T(8,128)(2,1)S(1)}, bf16[64,4608]{1,0:T(8,128)(2,1)}, u32[]{:S(2)}, u32[]{:S(2)}) %collective-permute-start.8) | collective-permute-done | bytes 589856 | tf_op jit(solution)/shard_map/ppermute | solution.py:507
  58.4 1.6 %collective-permute-done.10.refs_3_.refs_4_ = bf16[64,4608]{1,0:T(8,128)(2,1)S(1)} collective-permute-done((bf16[64,4608]{1,0:T(8,128)(2,1)}, bf16[64,4608]{1,0:T(8,128)(2,1)S(1)}, u32[]{:S(2)}, u32[]{:S(2)}) %collective-permute-start.10) | collective-permute-done | bytes 589856 | tf_op jit(solution)/shard_map/ppermute | solution.py:507
  61.8 9.7 %student_logits.1 = f32[4,128,1024]{2,1,0:T(8,128)} custom-call(s32[2]{0:T(128)S(1)} %pad_add_fusion.1.place_ref, f32[8,128]{1,0:T(8,128)S(1)} %add.84.after_ref.mass_ref, bf16[128,4608]{1,0:T(8,128)(2,1)S(1)} %copy-done.4, bf16[64,4608]{1,0:T(8,128)(2,1)} %collective-permute-done.7.refs_0_.refs_1_, bf16[64,4608]{1,0:T(8,128)(2,1)} %collective-permute-done.8.refs_1_.refs_2_, ...), custom_call_target="tpu_custom_call" | custom-call | flops 1024 | bytes 1024 | tf_op jit(solution)/shard_map/student_logits/pallas_call | solution.py:284
  71.5 3.6 %all-to-all-start = ((f32[4,128,1024]{2,1,0:T(8,128)}), f32[4,128,1024]{2,1,0:T(8,128)S(1)}, u32[]{:S(2)}, u32[]{:S(2)}) async-start(f32[4,128,1024]{2,1,0:T(8,128)} %student_logits.1), calls=%async_computation | async-start | bytes 4194304 | tf_op jit(solution)/shard_map/all_to_all | solution.py:537
  75.1 2.5 %collective-permute-start.19 = (bf16[32,128,128]{2,1,0:T(8,128)(2,1)}, bf16[32,128,128]{2,1,0:T(8,128)(2,1)}, u32[]{:S(2)}, u32[]{:S(2)}) collective-permute-start(bf16[32,128,128]{2,1,0:T(8,128)(2,1)} %get-tuple-element.57), channel_id=1, source_target_pairs={{0,2},{1,3},{2,0},{3,1},{4,6},{5,7},{6,4},{7,5},{8,10},{9,11},{10,... | collective-permute-start | bytes 3145736 | tf_op jit(solution)/shard_map/ppermute | solution.py:507
  77.6 4.8 %collective-permute-done.14 = bf16[32,128,128]{2,1,0:T(8,128)(2,1)} collective-permute-done((bf16[32,128,128]{2,1,0:T(8,128)(2,1)}, bf16[32,128,128]{2,1,0:T(8,128)(2,1)}, u32[]{:S(2)}, u32[]{:S(2)}) %collective-permute-start.14) | collective-permute-done | bytes 1048608 | tf_op jit(solution)/shard_map/ppermute | solution.py:541
  82.4 3.0 %add_convert_fusion = bf16[32,128,128]{2,1,0:T(8,128)(2,1)} fusion(bf16[32,128,128]{2,1,0:T(8,128)(2,1)} %collective-permute-done.13, bf16[32,128,128]{2,1,0:T(8,128)(2,1)} %get-tuple-element.50), kind=kLoop, calls=%fused_computation | loop fusion | flops 2097152 | bytes 3145728 | tf_op jit(solution)/shard_map/convert_element_type | solution.py:533
  85.5 1.6 %collective-permute-start.20 = (bf16[32,128,128]{2,1,0:T(8,128)(2,1)}, bf16[32,128,128]{2,1,0:T(8,128)(2,1)}, u32[]{:S(2)}, u32[]{:S(2)}) collective-permute-start(bf16[32,128,128]{2,1,0:T(8,128)(2,1)} %add_convert_fusion), channel_id=1, source_target_pairs={{2,4},{3,5},{4,2},{5,3},{10,12},{11,13},{12,10},{13,11},{18,20},{1... | collective-permute-start | bytes 3145736 | tf_op jit(solution)/shard_map/ppermute | solution.py:541
  90.5 5.1 %turned_rows.1.a_ref = bf16[4608,512]{1,0:T(8,128)(2,1)} custom-call(s32[2]{0:T(128)S(1)} %pad_add_fusion.1.place_ref, bf16[128,4608]{1,0:T(8,128)(2,1)S(1)} %copy-done.4, bf16[64,4608]{1,0:T(8,128)(2,1)} %collective-permute-done.9.refs_2_.refs_0_, bf16[64,4608]{1,0:T(8,128)(2,1)} %collective-permute-done.7.refs_0_.refs_1_, ...), custom_call_target="tpu_custom_call" | custom-call | flops 1024 | bytes 1024 | tf_op jit(solution)/shard_map/turned_rows/pallas_call | solution.py:264
  95.6 4.9 %all-to-all-done.logits_ref.refs_4_ = f32[4,128,1024]{2,1,0:T(8,128)S(1)} async-done(((f32[4,128,1024]{2,1,0:T(8,128)}), f32[4,128,1024]{2,1,0:T(8,128)S(1)}, u32[]{:S(2)}, u32[]{:S(2)}) %all-to-all-start) | async-done | bytes 2097184 | tf_op jit(solution)/shard_map/all_to_all | solution.py:537
  100.5 1.5 %student_stats.1.refs_0_ = f32[8,128]{1,0:T(8,128)S(1)} custom-call(s32[4]{0:T(128)S(1)} %add_multiply_fusion.base_ref, s32[128,1]{1,0:T(8,128)S(1)} %copy.13.labels_ref, f32[8,128]{1,0:T(8,128)S(1)} %add.84.after_ref.mass_ref, f32[4,128,1024]{2,1,0:T(8,128)S(1)} %all-to-all-done.logits_ref.refs_4_), custom_call_target="tpu_custom_call" | custom-call | flops 1024 | bytes 1024 | tf_op jit(solution)/shard_map/student_stats/pallas_call | solution.py:322
  103.2 3.1 %collective-permute-start.18 = (f32[8,128]{1,0:T(8,128)S(1)}, f32[8,128]{1,0:T(8,128)S(1)}, u32[]{:S(2)}, u32[]{:S(2)}) collective-permute-start(f32[8,128]{1,0:T(8,128)S(1)} %merge_stats.5.refs_0_), channel_id=1, source_target_pairs={{0,6},{1,7},{2,4},{3,5},{4,2},{5,3},{6,0},{7,1},{8,14},{9,15},{10,... | collective-permute-start | bytes 12296 | tf_op jit(solution)/shard_map/ppermute | solution.py:507
  108.8 2.0 %collective-permute-done.17.refs_2_ = f32[8,128]{1,0:T(8,128)S(1)} collective-permute-done((f32[8,128]{1,0:T(8,128)S(1)}, f32[8,128]{1,0:T(8,128)S(1)}, u32[]{:S(2)}, u32[]{:S(2)}) %collective-permute-start.17) | collective-permute-done | bytes 4128 | tf_op jit(solution)/shard_map/ppermute | solution.py:507
  110.9 2.4 %grad_logits.2 = (bf16[128,1024]{1,0:T(8,128)(2,1)}, f32[1,128]{1,0:T(1,128)S(1)}) custom-call(s32[1]{0:T(128)} %bitcast.4.tok_ref, s32[4]{0:T(128)S(1)} %add_multiply_fusion.base_ref, s32[128,1]{1,0:T(8,128)S(1)} %copy.13.labels_ref, f32[128,128]{1,0:T(8,128)S(1)} %get-tuple-element.55.columns, bf16[1,32,128,128]{3,2,1,0:T(8,128)(2,1)S(1)} %bitcast.16, ...), custom_call_target="tpu_custom_call" | custom-call | flops 1024 | bytes 1024 | tf_op jit(solution)/shard_map/grad_logits/pallas_call | solution.py:425
  113.4 2.3 %collective-permute-start.23 = (bf16[128,1024]{1,0:T(8,128)(2,1)}, bf16[128,1024]{1,0:T(8,128)(2,1)S(1)}, u32[]{:S(2)}, u32[]{:S(2)}) collective-permute-start(bf16[128,1024]{1,0:T(8,128)(2,1)} %get-tuple-element.63), channel_id=1, source_target_pairs={{0,24},{8,16},{16,8},{24,0},{1,25},{9,17},{17,9},{25,1},{2,26},{10... | collective-permute-start | bytes 786440 | tf_op jit(solution)/shard_map/ppermute | solution.py:507
  115.6 4.1 %grad_logits.3 = (bf16[128,1024]{1,0:T(8,128)(2,1)}, bf16[128,1024]{1,0:T(8,128)(2,1)}, bf16[128,1024]{1,0:T(8,128)(2,1)}, f32[1,128]{1,0:T(1,128)S(1)}) custom-call(s32[1]{0:T(128)} %bitcast.4.tok_ref, s32[4]{0:T(128)S(1)} %add_multiply_fusion.base_ref, s32[128,1]{1,0:T(8,128)S(1)} %copy.13.labels_ref, f32[128,128]{1,0:T(8,128)S(1)} %get-tuple-element.55.columns, ...), custom_call_target="tpu_custom_call" | custom-call | flops 1024 | bytes 1024 | tf_op jit(solution)/shard_map/grad_logits/pallas_call | solution.py:425
  122.5 4.1 %first_product.1 = (f32[4608,1024]{1,0:T(8,128)S(1)}, f32[1,128]{1,0:T(1,128)S(1)}) custom-call(bf16[4608,512]{1,0:T(8,128)(2,1)S(1)} %bitcast.13, bf16[128,1024]{1,0:T(8,128)(2,1)} %get-tuple-element.62.refs_0_, bf16[128,1024]{1,0:T(8,128)(2,1)S(1)} %collective-permute-done.23.refs_1_), custom_call_target="tpu_custom_call" | custom-call | flops 1024 | bytes 1024 | tf_op jit(solution)/shard_map/first_product/pallas_call | solution.py:476
  126.7 1.8 %collective-permute-start.24 = (f32[1,128]{1,0:T(1,128)S(1)}, f32[1,128]{1,0:T(1,128)S(1)}, u32[]{:S(2)}, u32[]{:S(2)}) collective-permute-start(f32[1,128]{1,0:T(1,128)S(1)} %add_add_fusion), channel_id=1, source_target_pairs={{0,4},{1,5},{2,6},{3,7},{4,0},{5,1},{6,2},{7,3},{8,12},{9,13},{10,... | collective-permute-start | bytes 1544 | tf_op jit(solution)/shard_map/ppermute | solution.py:507
  128.5 5.3 %last_product.1 = (bf16[4608,1024]{1,0:T(8,128)(2,1)}, f32[1,128]{1,0:T(1,128)S(1)}) custom-call(bf16[4608,512]{1,0:T(8,128)(2,1)S(1)} %bitcast.13, f32[4608,1024]{1,0:T(8,128)S(1)} %get-tuple-element.65.acc_ref, bf16[128,1024]{1,0:T(8,128)(2,1)S(1)} %collective-permute-done.25.refs_0_, bf16[128,1024]{1,0:T(8,128)(2,1)S(1)} %collective-permute-done.26.refs_1_), custom_call_target="tpu_custom_call" | custom-call | flops 1024 | bytes 1024 | tf_op jit(solution)/shard_map/last_product/pallas_call | solution.py:493
  (89 shorter events, 19.9 us)
Async XLA Ops:
  0.6 86.5 %copy-start = (s32[512]{0:T(512)S(1)}, s32[512]{0:T(512)}, u32[]{:S(2)}) copy-start(s32[512]{0:T(512)} %param.9) | copy-start | bytes 6148
  0.6 18.5 %collective-permute-start.5 = (bf16[32,4,128,128]{3,2,1,0:T(8,128)(2,1)}, bf16[32,4,128,128]{3,2,1,0:T(8,128)(2,1)}, u32[]{:S(2)}, u32[]{:S(2)}) collective-permute-start(bf16[32,4,128,128]{3,2,1,0:T(8,128)(2,1)} %w_own.3), channel_id=1, source_target_pairs={{0,1},{1,0},{2,3},{3,2},{4,5},{5,4},{6,7},{7,6},{8,9},{9,8},{10,11... | collective-permute-start | bytes 12582920 | tf_op jit(solution)/shard_map/ppermute | solution.py:507
  1.2 14.8 %collective-permute-start.1 = (bf16[128,4096]{1,0:T(8,128)(2,1)}, bf16[128,4096]{1,0:T(8,128)(2,1)S(1)}, u32[]{:S(2)}, u32[]{:S(2)}) collective-permute-start(bf16[128,4096]{1,0:T(8,128)(2,1)} %x_own.1), channel_id=1, source_target_pairs={{0,1},{1,0},{2,3},{3,2},{4,5},{5,4},{6,7},{7,6},{8,9},{9,8},{10,11... | collective-permute-start | bytes 3145736 | tf_op jit(solution)/shard_map/ppermute | solution.py:507
  3.1 4.6 %collective-permute-start.2 = (f32[8,128]{1,0:T(8,128)S(1)}, f32[8,128]{1,0:T(8,128)S(1)}, u32[]{:S(2)}, u32[]{:S(2)}) collective-permute-start(f32[8,128]{1,0:T(8,128)S(1)} %teacher_stats.1.refs_0_), channel_id=1, source_target_pairs={{0,2},{1,3},{2,0},{3,1},{4,6},{5,7},{6,4},{7,5},{8,10},{9,11},{10,... | collective-permute-start | bytes 12296 | tf_op jit(solution)/shard_map/ppermute | solution.py:507
  7.7 4.7 %collective-permute-start.3 = (f32[8,128]{1,0:T(8,128)S(1)}, f32[8,128]{1,0:T(8,128)S(1)}, u32[]{:S(2)}, u32[]{:S(2)}) collective-permute-start(f32[8,128]{1,0:T(8,128)S(1)} %merge_stats.3.refs_0_), channel_id=1, source_target_pairs={{0,4},{1,5},{2,6},{3,7},{4,0},{5,1},{6,2},{7,3},{8,12},{9,13},{10,... | collective-permute-start | bytes 12296 | tf_op jit(solution)/shard_map/ppermute | solution.py:507
  11.7 1.2 collective-permute-start
  12.4 3.5 %collective-permute-start.4 = (f32[8,128]{1,0:T(8,128)S(1)}, f32[8,128]{1,0:T(8,128)S(1)}, u32[]{:S(2)}, u32[]{:S(2)}) collective-permute-start(f32[8,128]{1,0:T(8,128)S(1)} %merge_stats.4.refs_0_), channel_id=1, source_target_pairs={{0,1},{1,0},{2,3},{3,2},{4,5},{5,4},{6,7},{7,6},{8,9},{9,8},{10,11... | collective-permute-start | bytes 12296 | tf_op jit(solution)/shard_map/ppermute | solution.py:507
  24.3 26.8 %collective-permute-start.6 = (bf16[32,128,128]{2,1,0:T(8,128)(2,1)}, bf16[32,128,128]{2,1,0:T(8,128)(2,1)}, u32[]{:S(2)}, u32[]{:S(2)}) collective-permute-start(bf16[32,128,128]{2,1,0:T(8,128)(2,1)} %get-tuple-element.38), channel_id=1, source_target_pairs={{0,2},{1,3},{6,4},{7,5},{8,10},{9,11},{14,12},{15,13},{16,18},{17,... | collective-permute-start | bytes 3145736 | tf_op jit(solution)/shard_map/ppermute | solution.py:541
  28.3 22.8 %copy-start.13 = (bf16[32,128,128]{2,1,0:T(8,128)(2,1)S(1)}, bf16[32,128,128]{2,1,0:T(8,128)(2,1)}, u32[]{:S(2)}) copy-start(bf16[32,128,128]{2,1,0:T(8,128)(2,1)} %get-tuple-element.38) | copy-start | bytes 3145732
  28.3 26.7 %collective-permute-start.9 = (bf16[64,4608]{1,0:T(8,128)(2,1)S(1)}, bf16[64,4608]{1,0:T(8,128)(2,1)}, u32[]{:S(2)}, u32[]{:S(2)}) collective-permute-start(bf16[64,4608]{1,0:T(8,128)(2,1)S(1)} %constant_dynamic-slice_fusion), channel_id=1, source_target_pairs={{0,24},{8,16},{16,8},{24,0},{1,25},{9,17},{17,9},{25,1},{2,26},{10... | collective-permute-start | bytes 1769480 | tf_op jit(solution)/shard_map/ppermute | solution.py:507
  30.9 26.9 %collective-permute-start.8 = (bf16[64,4608]{1,0:T(8,128)(2,1)S(1)}, bf16[64,4608]{1,0:T(8,128)(2,1)}, u32[]{:S(2)}, u32[]{:S(2)}) collective-permute-start(bf16[64,4608]{1,0:T(8,128)(2,1)S(1)} %constant_dynamic-slice_fusion), channel_id=1, source_target_pairs={{0,16},{8,24},{16,0},{24,8},{1,17},{9,25},{17,1},{25,9},{2,18},{10... | collective-permute-start | bytes 1769480 | tf_op jit(solution)/shard_map/ppermute | solution.py:507
  31.4 26.5 %collective-permute-start.7 = (bf16[64,4608]{1,0:T(8,128)(2,1)S(1)}, bf16[64,4608]{1,0:T(8,128)(2,1)}, u32[]{:S(2)}, u32[]{:S(2)}) collective-permute-start(bf16[64,4608]{1,0:T(8,128)(2,1)S(1)} %constant_dynamic-slice_fusion), channel_id=1, source_target_pairs={{0,8},{8,0},{16,24},{24,16},{1,9},{9,1},{17,25},{25,17},{2,10},{10... | collective-permute-start | bytes 1769480 | tf_op jit(solution)/shard_map/ppermute | solution.py:507
  41.4 36.1 %collective-permute-start.13 = (bf16[32,128,128]{2,1,0:T(8,128)(2,1)}, bf16[32,128,128]{2,1,0:T(8,128)(2,1)}, u32[]{:S(2)}, u32[]{:S(2)}) collective-permute-start(bf16[32,128,128]{2,1,0:T(8,128)(2,1)} %get-tuple-element.50), channel_id=1, source_target_pairs={{0,2},{1,3},{6,4},{7,5},{8,10},{9,11},{14,12},{15,13},{16,18},{17,... | collective-permute-start | bytes 3145736 | tf_op jit(solution)/shard_map/ppermute | solution.py:541
  53.7 28.7 %collective-permute-start.14 = (bf16[32,128,128]{2,1,0:T(8,128)(2,1)}, bf16[32,128,128]{2,1,0:T(8,128)(2,1)}, u32[]{:S(2)}, u32[]{:S(2)}) collective-permute-start(bf16[32,128,128]{2,1,0:T(8,128)(2,1)} %add_convert_fusion.1), channel_id=1, source_target_pairs={{2,6},{3,7},{4,0},{5,1},{10,14},{11,15},{12,8},{13,9},{18,22},{19,... | collective-permute-start | bytes 3145736 | tf_op jit(solution)/shard_map/ppermute | solution.py:541
  57.8 2.2 %collective-permute-start.10 = (bf16[64,4608]{1,0:T(8,128)(2,1)}, bf16[64,4608]{1,0:T(8,128)(2,1)S(1)}, u32[]{:S(2)}, u32[]{:S(2)}) collective-permute-start(bf16[64,4608]{1,0:T(8,128)(2,1)} %collective-permute-done.7.refs_0_.refs_1_), channel_id=1, source_target_pairs={{0,1},{1,0},{2,3},{3,2},{4,5},{5,4},{6,7},{7,6},{8,9},{9,8},{10,11... | collective-permute-start | bytes 1769480 | tf_op jit(solution)/shard_map/ppermute | solution.py:507
  57.8 3.1 %collective-permute-start.11 = (bf16[64,4608]{1,0:T(8,128)(2,1)}, bf16[64,4608]{1,0:T(8,128)(2,1)S(1)}, u32[]{:S(2)}, u32[]{:S(2)}) collective-permute-start(bf16[64,4608]{1,0:T(8,128)(2,1)} %collective-permute-done.8.refs_1_.refs_2_), channel_id=1, source_target_pairs={{0,1},{1,0},{2,3},{3,2},{4,5},{5,4},{6,7},{7,6},{8,9},{9,8},{10,11... | collective-permute-start | bytes 1769480 | tf_op jit(solution)/shard_map/ppermute | solution.py:507
  58.4 3.4 %collective-permute-start.12 = (bf16[64,4608]{1,0:T(8,128)(2,1)}, bf16[64,4608]{1,0:T(8,128)(2,1)S(1)}, u32[]{:S(2)}, u32[]{:S(2)}) collective-permute-start(bf16[64,4608]{1,0:T(8,128)(2,1)} %collective-permute-done.9.refs_2_.refs_0_), channel_id=1, source_target_pairs={{0,1},{1,0},{2,3},{3,2},{4,5},{5,4},{6,7},{7,6},{8,9},{9,8},{10,11... | collective-permute-start | bytes 1769480 | tf_op jit(solution)/shard_map/ppermute | solution.py:507
  71.5 29.0 %all-to-all-start = ((f32[4,128,1024]{2,1,0:T(8,128)}), f32[4,128,1024]{2,1,0:T(8,128)S(1)}, u32[]{:S(2)}, u32[]{:S(2)}) async-start(f32[4,128,1024]{2,1,0:T(8,128)} %student_logits.1), calls=%async_computation | async-start | bytes 4194304 | tf_op jit(solution)/shard_map/all_to_all | solution.py:537
  75.1 35.8 %collective-permute-start.19 = (bf16[32,128,128]{2,1,0:T(8,128)(2,1)}, bf16[32,128,128]{2,1,0:T(8,128)(2,1)}, u32[]{:S(2)}, u32[]{:S(2)}) collective-permute-start(bf16[32,128,128]{2,1,0:T(8,128)(2,1)} %get-tuple-element.57), channel_id=1, source_target_pairs={{0,2},{1,3},{2,0},{3,1},{4,6},{5,7},{6,4},{7,5},{8,10},{9,11},{10,... | collective-permute-start | bytes 3145736 | tf_op jit(solution)/shard_map/ppermute | solution.py:507
  85.5 25.4 %collective-permute-start.20 = (bf16[32,128,128]{2,1,0:T(8,128)(2,1)}, bf16[32,128,128]{2,1,0:T(8,128)(2,1)}, u32[]{:S(2)}, u32[]{:S(2)}) collective-permute-start(bf16[32,128,128]{2,1,0:T(8,128)(2,1)} %add_convert_fusion), channel_id=1, source_target_pairs={{2,4},{3,5},{4,2},{5,3},{10,12},{11,13},{12,10},{13,11},{18,20},{1... | collective-permute-start | bytes 3145736 | tf_op jit(solution)/shard_map/ppermute | solution.py:541
  95.6 15.3 %copy-start.6 = (bf16[32,128,128]{2,1,0:T(8,128)(2,1)S(1)}, bf16[32,128,128]{2,1,0:T(8,128)(2,1)}, u32[]{:S(2)}) copy-start(bf16[32,128,128]{2,1,0:T(8,128)(2,1)} %get-tuple-element.56) | copy-start | bytes 3145732
  102.0 1.2 collective-permute-start.15
  103.2 5.6 %collective-permute-start.18 = (f32[8,128]{1,0:T(8,128)S(1)}, f32[8,128]{1,0:T(8,128)S(1)}, u32[]{:S(2)}, u32[]{:S(2)}) collective-permute-start(f32[8,128]{1,0:T(8,128)S(1)} %merge_stats.5.refs_0_), channel_id=1, source_target_pairs={{0,6},{1,7},{2,4},{3,5},{4,2},{5,3},{6,0},{7,1},{8,14},{9,15},{10,... | collective-permute-start | bytes 12296 | tf_op jit(solution)/shard_map/ppermute | solution.py:507
  106.2 4.5 %collective-permute-start.17 = (f32[8,128]{1,0:T(8,128)S(1)}, f32[8,128]{1,0:T(8,128)S(1)}, u32[]{:S(2)}, u32[]{:S(2)}) collective-permute-start(f32[8,128]{1,0:T(8,128)S(1)} %merge_stats.5.refs_0_), channel_id=1, source_target_pairs={{0,4},{1,5},{2,6},{3,7},{4,0},{5,1},{6,2},{7,3},{8,12},{9,13},{10,... | collective-permute-start | bytes 12296 | tf_op jit(solution)/shard_map/ppermute | solution.py:507
  107.1 3.7 %collective-permute-start.16 = (f32[8,128]{1,0:T(8,128)S(1)}, f32[8,128]{1,0:T(8,128)S(1)}, u32[]{:S(2)}, u32[]{:S(2)}) collective-permute-start(f32[8,128]{1,0:T(8,128)S(1)} %merge_stats.5.refs_0_), channel_id=1, source_target_pairs={{0,2},{1,3},{2,0},{3,1},{4,6},{5,7},{6,4},{7,5},{8,10},{9,11},{10,... | collective-permute-start | bytes 12296 | tf_op jit(solution)/shard_map/ppermute | solution.py:507
  110.7 11.8 %slice-start = ((s8[4718592]{0:T(1024)(128)(4,1)}), s8[4194304]{0:T(1024)(128)(4,1)S(1)}, s32[]{:S(2)}) async-start(s8[4718592]{0:T(1024)(128)(4,1)} %bitcast.12), calls=%async_computation.1 | async-start | bytes 8388608
  113.4 9.2 %collective-permute-start.23 = (bf16[128,1024]{1,0:T(8,128)(2,1)}, bf16[128,1024]{1,0:T(8,128)(2,1)S(1)}, u32[]{:S(2)}, u32[]{:S(2)}) collective-permute-start(bf16[128,1024]{1,0:T(8,128)(2,1)} %get-tuple-element.63), channel_id=1, source_target_pairs={{0,24},{8,16},{16,8},{24,0},{1,25},{9,17},{17,9},{25,1},{2,26},{10... | collective-permute-start | bytes 786440 | tf_op jit(solution)/shard_map/ppermute | solution.py:507
  119.7 8.8 %collective-permute-start.25 = (bf16[128,1024]{1,0:T(8,128)(2,1)}, bf16[128,1024]{1,0:T(8,128)(2,1)S(1)}, u32[]{:S(2)}, u32[]{:S(2)}) collective-permute-start(bf16[128,1024]{1,0:T(8,128)(2,1)} %get-tuple-element.66), channel_id=1, source_target_pairs={{0,8},{8,0},{16,24},{24,16},{1,9},{9,1},{17,25},{25,17},{2,10},{10... | collective-permute-start | bytes 786440 | tf_op jit(solution)/shard_map/ppermute | solution.py:507
  120.3 8.2 %collective-permute-start.26 = (bf16[128,1024]{1,0:T(8,128)(2,1)}, bf16[128,1024]{1,0:T(8,128)(2,1)S(1)}, u32[]{:S(2)}, u32[]{:S(2)}) collective-permute-start(bf16[128,1024]{1,0:T(8,128)(2,1)} %get-tuple-element.67), channel_id=1, source_target_pairs={{0,16},{8,24},{16,0},{24,8},{1,17},{9,25},{17,1},{25,9},{2,18},{10... | collective-permute-start | bytes 786440 | tf_op jit(solution)/shard_map/ppermute | solution.py:507
  120.9 1.1 collective-permute-start.21
  122.0 4.7 %collective-permute-start.22 = (f32[1,128]{1,0:T(1,128)S(1)}, f32[1,128]{1,0:T(1,128)S(1)}, u32[]{:S(2)}, u32[]{:S(2)}) collective-permute-start(f32[1,128]{1,0:T(1,128)S(1)} %add.88), channel_id=1, source_target_pairs={{0,2},{1,3},{2,0},{3,1},{4,6},{5,7},{6,4},{7,5},{8,10},{9,11},{10,... | collective-permute-start | bytes 1544 | tf_op jit(solution)/shard_map/ppermute | solution.py:507
  126.7 7.1 %collective-permute-start.24 = (f32[1,128]{1,0:T(1,128)S(1)}, f32[1,128]{1,0:T(1,128)S(1)}, u32[]{:S(2)}, u32[]{:S(2)}) collective-permute-start(f32[1,128]{1,0:T(1,128)S(1)} %add_add_fusion), channel_id=1, source_target_pairs={{0,4},{1,5},{2,6},{3,7},{4,0},{5,1},{6,2},{7,3},{8,12},{9,13},{10,... | collective-permute-start | bytes 1544 | tf_op jit(solution)/shard_map/ppermute | solution.py:507
  (12 other events, 68.1 us)

commit v7 on v6

--- a/solution.py
+++ b/solution.py
@@ -90,39 +90,48 @@
     return lax.shift_right_logical(x, n.bit_length() - 1) if n & (n - 1) == 0 else x // n
 
 
-def plan_kernel(own_ref, peer_ref, list_ref, count_ref):
-    lists = count_ref.shape[0]
-    entries = own_ref.shape[0]
-    for p in range(lists):
-        count_ref[p] = 0
-
-    def visit(i, carry):
-        for side, ref in enumerate((own_ref, peer_ref)):
-            code = ref[i]
-            row = lax.shift_right_logical(code, SLOT_BITS)
-            n = count_ref[row]
-            list_ref[row, n] = (side * entries + i) * SLOT_BASE + (code & (SLOT_BASE - 1))
-            count_ref[row] = n + 1
-        return carry
-
-    lax.fori_loop(0, entries, visit, 0, unroll=8)
-    for p in range(lists):
-        n = count_ref[p]
-        for k in range(BATCH - 1):
-            list_ref[p, n + k] = SLOT_BASE - 1
+def plan_kernel(own_ref, peer_ref, list_ref):
+    lists, room = list_ref.shape
+    codes = [own_ref[...], peer_ref[...]]
+    n = codes[0].shape[1]
+    rows = [lax.shift_right_logical(code, SLOT_BITS) for code in codes]
+    across = [jnp.broadcast_to(row.astype(F32), (n, n)) for row in rows]
+    down = [x.T for x in across]
+    before = lax.broadcasted_iota(jnp.int32, (n, n), 1) < lax.broadcasted_iota(jnp.int32, (n, n), 0)
+    count = lambda mask: jnp.sum(jnp.where(mask, 1.0, 0.0), axis=1, keepdims=True)
+    ranks = [count((down[0] == across[0]) & before)]
+    ranks.append(count((down[1] == across[1]) & before) + count(down[1] == across[0]))
+    place = lax.broadcasted_iota(jnp.int32, (n, room), 1).astype(F32)
+    entry = lax.broadcasted_iota(jnp.int32, (lists, n), 1).astype(F32)
+    entries = slots = jnp.zeros((lists, room), F32)
+    counts = jnp.zeros((lists, 1), F32)
+    for side, code in enumerate(codes):
+        member = jnp.broadcast_to(rows[side], (lists, n)) == lax.broadcasted_iota(jnp.int32, (lists, n), 0)
+        slot = jnp.broadcast_to(code & (SLOT_BASE - 1), (lists, n)).astype(F32)
+        here = jnp.where(place == ranks[side], 1.0, 0.0).astype(BF16)
+        pick = lambda x: jnp.dot(jnp.where(member, x, 0.0).astype(BF16), here, preferred_element_type=F32)
+        entries = entries + pick(entry + side * n)
+        slots = slots + pick(slot)
+        counts = counts + count(member)
+    column = lax.broadcasted_iota(jnp.int32, (lists, room), 1)
+    counts = counts.astype(jnp.int32)
+    items = entries.astype(jnp.int32) * SLOT_BASE + slots.astype(jnp.int32)
+    items = jnp.where(column < counts, items, SLOT_BASE - 1)
+    list_ref[...] = jnp.where(column == room - 1, counts, items)
 
 
 def plan(own_code, peer_code, lists):
-    room = 2 * own_code.size + BATCH
+    n = own_code.size
+    room = 3 * LANES
     return pl.pallas_call(
         plan_kernel,
-        in_specs=[SMEM_SPEC] * 2,
-        out_specs=[SMEM_SPEC] * 2,
-        out_shape=[jax.ShapeDtypeStruct((lists, room), jnp.int32), jax.ShapeDtypeStruct((lists,), jnp.int32)],
-        compiler_params=params(1),
+        in_specs=[VMEM_SPEC] * 2,
+        out_specs=VMEM_SPEC,
+        out_shape=jax.ShapeDtypeStruct((lists, room), jnp.int32),
+        compiler_params=params(4),
         cost_estimate=COST,
         name="entry_lists",
-    )(own_code, peer_code)
+    )(own_code.reshape(1, n), peer_code.reshape(1, n))
 
 
 def probs_kernel(x_own, x_peer, *refs):
@@ -140,7 +149,7 @@
             probs[side, j] = (raised * scale).astype(BF16)
 
 
-def sums_kernel(spot_ref, list_ref, count_ref, probs, w_own, w_peer, *refs, first, fan, pieces):
+def sums_kernel(spot_ref, list_ref, probs, w_own, w_peer, *refs, first, fan, pieces):
     outs, mass_ref, acc = refs[:-2], refs[-2], refs[-1]
     step = pl.program_id(0)
     slots, rows, _ = outs[0].shape
@@ -167,7 +176,7 @@
                 acc[jnp.minimum(slot, slots)] += part.astype(BF16).astype(F32)
             return carry
 
-        lax.fori_loop(0, divide(count_ref[piece] + BATCH - 1, BATCH), add, 0)
+        lax.fori_loop(0, divide(list_ref[piece, list_ref.shape[1] - 1] + BATCH - 1, BATCH), add, 0)
 
         def drain(i, mass):
             block = acc[i]
@@ -205,22 +214,22 @@
     return probs.reshape(2 * blocks, rows, LANES)
 
 
-def chip_sums(spot, lists, counts, probs, w_own, w_peer, first, n_out, steps, slots):
+def chip_sums(spot, lists, probs, w_own, w_peer, first, n_out, steps, slots):
     rows = probs.shape[1]
     fan = w_own.shape[1]
     whole = lambda shape: pl.BlockSpec(shape, lambda s: (0,) * len(shape))
     out = pltpu.HBM((steps * slots, rows, LANES), BF16)
     return pl.pallas_call(
-        functools.partial(sums_kernel, first=first, fan=fan, pieces=counts.shape[0] // 2),
+        functools.partial(sums_kernel, first=first, fan=fan, pieces=lists.shape[0] // 2),
         grid=(steps,),
-        in_specs=[SMEM_SPEC] * 3 + [VMEM_SPEC] * 3,
+        in_specs=[SMEM_SPEC] * 2 + [VMEM_SPEC] * 3,
         out_specs=[pl.BlockSpec((slots, rows, LANES), lambda s: (s, 0, 0))] * n_out + [whole((8, rows))],
         out_shape=[out] * n_out + [jax.ShapeDtypeStruct((8, rows), F32)],
         scratch_shapes=[pltpu.VMEM((slots + 1, rows, LANES), F32)],
         compiler_params=params(24),
         cost_estimate=COST,
         name="chip_sums",
-    )(spot, lists, counts, probs, w_own, w_peer)
+    )(spot, lists, probs, w_own, w_peer)
 
 
 def stack_rows(place_ref, own_ref, near, far, everyone):
@@ -572,18 +581,18 @@
     peer_code = swap(code, "vocab", 1)
     peer_weight = swap(map_weight, "vocab", 1)
     totals = butterfly(teacher_stats(teacher_logits))
-    lists, counts = plan(code, peer_code, 2 * n_z)
+    lists = plan(code, peer_code, 2 * n_z)
     probs = teacher_probs(teacher_logits, peer_logits, totals)
 
     half = lax.dynamic_slice_in_dim(hidden, spot[0] * (rows // 2), rows // 2)
     if in_line:
         inward, across, beyond = [(0, 1), (3, 2)], [(1, 2), (2, 1)], [(1, 3), (2, 0)]
-        far_outer, mass_a = chip_sums(spot, lists, counts, probs, map_weight, peer_weight, 0, 1, 1, slots)
+        far_outer, mass_a = chip_sums(spot, lists, probs, map_weight, peer_weight, 0, 1, 1, slots)
         first = send(far_outer, inward)
         half, probs, mass_a = lax.optimization_barrier((half, probs, mass_a))
         near = [swap(half, "tok", r) for r in range(1, n_tok)]
         far_inner, beside, own, mass_b = chip_sums(
-            spot, lists, counts, probs, map_weight, peer_weight, 1, 3, 1, slots
+            spot, lists, probs, map_weight, peer_weight, 1, 3, 1, slots
         )
         second = send(far_inner, inward)
         first, mass = lax.optimization_barrier((first, mass_a + mass_b))
@@ -592,7 +601,7 @@
         *near, waited, merged = lax.optimization_barrier((*near, beside, merged))
         third = swap(waited, "vocab", 2)
     else:
-        sums, mass = chip_sums(spot, lists, counts, probs, map_weight, peer_weight, 0, 1, n_z, slots)
+        sums, mass = chip_sums(spot, lists, probs, map_weight, peer_weight, 0, 1, n_z, slots)
         lines = [[2 * z + c for z in range(n_z)] for c in range(2)]
         sums = lax.all_to_all(
             sums.reshape(n_z, slots, rows, block),

time: 135 us -> 133 us (0.985)
  starting transfers between devices: 36.5 us -> 39.4 us
  waiting for transfers between devices: 31.2 us -> 28.3 us
  Pallas kernels: 51.7 us -> 49.3 us
    ppermute x4, waiting for transfers between devices: 12.3 us -> 8.67 us  [send(): lax.ppermute(x, 'vocab', [(2 * a + c, 2 * b + c) for a, b in hops for c i...]
    pallas_call x1, Pallas kernels: 2.99 us -> 0.35 us  [plan(): pl.pallas_call(plan_kernel, in_specs=[VMEM_SPEC] * 2, out_specs=VMEM_SPEC...]
    ppermute x23, starting transfers between devices: 23.7 us -> 25.4 us  [swap(): lax.ppermute(x, axis, [(i, i ^ mask) for i in range(lax.axis_size(axis))])]
  transfers between devices with their start and end apart: 28 -> 28, of which waited for: 15 -> 17; matrix products, arithmetic and copies ran while one was open for 5% -> 5% of each run, Pallas kernels for 33% -> 32%
where the time goes in v7:
time: 133 us; the launch traced here: 132 us
  Pallas kernels  49.3 us (37%)
  starting transfers between devices  39.4 us (30%)
  waiting for transfers between devices  28.3 us (21%)
  local copies, waits for them, and re-layouts  7.17 us (5%)
  other arithmetic  7.08 us (5%)
    ppermute x23, starting transfers between devices, swap(): lax.ppermute(x, axis, [(i, i ^ mask) for i in range(lax.axis_size(axis))])  25.4 us
    ppermute x23, waiting for transfers between devices, swap(): lax.ppermute(x, axis, [(i, i ^ mask) for i in range(lax.axis_size(axis))])  13.5 us
    pallas_call x2, Pallas kernels, chip_sums(): pl.pallas_call(functools.partial(sums_kernel, first=first, fan=fan, piece...  12.7 us
    ppermute x4, starting transfers between devices, send(): lax.ppermute(x, 'vocab', [(2 * a + c, 2 * b + c) for a, b in hops for c i...  10.4 us
    pallas_call x1, Pallas kernels, student_logits(): pl.pallas_call(logits_kernel, grid=(cols // tile,), in_specs=[SMEM_SPEC,...  9.69 us
    ppermute x4, waiting for transfers between devices, send(): lax.ppermute(x, 'vocab', [(2 * a + c, 2 * b + c) for a, b in hops for c i...  8.67 us
    unnamed x32, local copies, waits for them, and re-layouts  6.65 us
    pallas_call x2, Pallas kernels, grad_logits(): pl.pallas_call(functools.partial(grad_kernel, n_sums=len(sums), groups=gr...  6.5 us
  transfers between devices with their start and end apart: 28, of which 17 were waited for; matrix products, arithmetic and copies ran while one was open for 5% of the time, Pallas kernels for 32%

profile of v7, /device:TPU:0, one launch (start us, length us, event | category | flops | bytes accessed | tf_op | source)
XLA Modules:
  0.0 132.2 jit_solution(12181265716288953066)
XLA Ops:
  3.1 3.0 %collective-permute-start.2 = (f32[8,128]{1,0:T(8,128)S(1)}, f32[8,128]{1,0:T(8,128)S(1)}, u32[]{:S(2)}, u32[]{:S(2)}) collective-permute-start(f32[8,128]{1,0:T(8,128)S(1)} %teacher_stats.1.refs_0_), channel_id=1, source_target_pairs={{0,2},{1,3},{2,0},{3,1},{4,6},{5,7},{6,4},{7,5},{8,10},{9,11},{10,... | collective-permute-start | bytes 12296 | tf_op jit(solution)/shard_map/ppermute | solution.py:516
  6.1 1.6 %collective-permute-done.2.refs_1_ = f32[8,128]{1,0:T(8,128)S(1)} collective-permute-done((f32[8,128]{1,0:T(8,128)S(1)}, f32[8,128]{1,0:T(8,128)S(1)}, u32[]{:S(2)}, u32[]{:S(2)}) %collective-permute-start.2) | collective-permute-done | bytes 4128 | tf_op jit(solution)/shard_map/ppermute | solution.py:516
  7.7 3.1 %collective-permute-start.3 = (f32[8,128]{1,0:T(8,128)S(1)}, f32[8,128]{1,0:T(8,128)S(1)}, u32[]{:S(2)}, u32[]{:S(2)}) collective-permute-start(f32[8,128]{1,0:T(8,128)S(1)} %merge_stats.3.refs_0_), channel_id=1, source_target_pairs={{0,4},{1,5},{2,6},{3,7},{4,0},{5,1},{6,2},{7,3},{8,12},{9,13},{10,... | collective-permute-start | bytes 12296 | tf_op jit(solution)/shard_map/ppermute | solution.py:516
  13.6 3.3 %teacher_probs.1 = bf16[2,32,128,128]{3,2,1,0:T(8,128)(2,1)S(1)} custom-call(bf16[128,4096]{1,0:T(8,128)(2,1)} %x_own.1, bf16[128,4096]{1,0:T(8,128)(2,1)S(1)} %collective-permute-done.1.x_peer, f32[8,128]{1,0:T(8,128)S(1)} %merge_stats.4.refs_0_, f32[8,128]{1,0:T(8,128)S(1)} %collective-permute-done.4.refs_1_), custom_call_target="tpu_custom_call" | custom-call | flops 1024 | bytes 1024 | tf_op jit(solution)/shard_map/teacher_probs/pallas_call | solution.py:203
  16.9 4.3 %chip_sums.2 = (bf16[32,128,128]{2,1,0:T(8,128)(2,1)}, f32[8,128]{1,0:T(8,128)S(1)}) custom-call(s32[2]{0:T(128)S(1)} %pad_add_fusion.spot_ref, s32[8,384]{1,0:T(8,128)S(1)} %entry_lists.1.list_ref, bf16[64,128,128]{2,1,0:T(8,128)(2,1)S(1)} %bitcast.15, bf16[32,4,128,128]{3,2,1,0:T(8,128)(2,1)S(1)} %copy-done.2, ...), custom_call_target="tpu_custom_call" | custom-call | flops 1024 | bytes 1024 | tf_op jit(solution)/shard_map/chip_sums/pallas_call | solution.py:222
  21.2 5.2 %collective-permute-start.6 = (bf16[32,128,128]{2,1,0:T(8,128)(2,1)}, bf16[32,128,128]{2,1,0:T(8,128)(2,1)}, u32[]{:S(2)}, u32[]{:S(2)}) collective-permute-start(bf16[32,128,128]{2,1,0:T(8,128)(2,1)} %get-tuple-element.34), channel_id=1, source_target_pairs={{0,2},{1,3},{6,4},{7,5},{8,10},{9,11},{14,12},{15,13},{16,18},{17,... | collective-permute-start | bytes 3145736 | tf_op jit(solution)/shard_map/ppermute | solution.py:550
  26.5 2.5 %collective-permute-start.9 = (bf16[64,4608]{1,0:T(8,128)(2,1)S(1)}, bf16[64,4608]{1,0:T(8,128)(2,1)}, u32[]{:S(2)}, u32[]{:S(2)}) collective-permute-start(bf16[64,4608]{1,0:T(8,128)(2,1)S(1)} %constant_dynamic-slice_fusion), channel_id=1, source_target_pairs={{0,24},{8,16},{16,8},{24,0},{1,25},{9,17},{17,9},{25,1},{2,26},{10... | collective-permute-start | bytes 1769480 | tf_op jit(solution)/shard_map/ppermute | solution.py:516
  30.0 2.2 %copy-done.3 = bf16[32,4,128,128]{3,2,1,0:T(8,128)(2,1)S(1)} copy-done((bf16[32,4,128,128]{3,2,1,0:T(8,128)(2,1)S(1)}, bf16[32,4,128,128]{3,2,1,0:T(8,128)(2,1)}, u32[]{:S(2)}) %copy-start.3) | copy-done | bytes 4194328
  32.2 8.4 %chip_sums.3 = (bf16[32,128,128]{2,1,0:T(8,128)(2,1)}, bf16[32,128,128]{2,1,0:T(8,128)(2,1)}, bf16[32,128,128]{2,1,0:T(8,128)(2,1)}, f32[8,128]{1,0:T(8,128)S(1)}) custom-call(s32[2]{0:T(128)S(1)} %pad_add_fusion.spot_ref, s32[8,384]{1,0:T(8,128)S(1)} %entry_lists.1.list_ref, bf16[64,128,128]{2,1,0:T(8,128)(2,1)S(1)} %bitcast.16, ...), custom_call_target="tpu_custom_call" | custom-call | flops 1024 | bytes 1024 | tf_op jit(solution)/shard_map/chip_sums/pallas_call | solution.py:222
  40.6 2.3 %collective-permute-start.13 = (bf16[32,128,128]{2,1,0:T(8,128)(2,1)}, bf16[32,128,128]{2,1,0:T(8,128)(2,1)}, u32[]{:S(2)}, u32[]{:S(2)}) collective-permute-start(bf16[32,128,128]{2,1,0:T(8,128)(2,1)} %get-tuple-element.46), channel_id=1, source_target_pairs={{0,2},{1,3},{6,4},{7,5},{8,10},{9,11},{14,12},{15,13},{16,18},{17,... | collective-permute-start | bytes 3145736 | tf_op jit(solution)/shard_map/ppermute | solution.py:550
  42.9 6.4 %collective-permute-done.6 = bf16[32,128,128]{2,1,0:T(8,128)(2,1)} collective-permute-done((bf16[32,128,128]{2,1,0:T(8,128)(2,1)}, bf16[32,128,128]{2,1,0:T(8,128)(2,1)}, u32[]{:S(2)}, u32[]{:S(2)}) %collective-permute-start.6) | collective-permute-done | bytes 1048608 | tf_op jit(solution)/shard_map/ppermute | solution.py:550
  49.3 2.6 %add_convert_fusion.1 = bf16[32,128,128]{2,1,0:T(8,128)(2,1)} fusion(bf16[32,128,128]{2,1,0:T(8,128)(2,1)} %collective-permute-done.6, bf16[32,128,128]{2,1,0:T(8,128)(2,1)S(1)} %copy-done.13), kind=kLoop, calls=%fused_computation.1 | loop fusion | flops 2097152 | bytes 3145728 | tf_op jit(solution)/shard_map/convert_element_type | solution.py:542
  55.3 1.6 %collective-permute-done.10.refs_3_.refs_4_ = bf16[64,4608]{1,0:T(8,128)(2,1)S(1)} collective-permute-done((bf16[64,4608]{1,0:T(8,128)(2,1)}, bf16[64,4608]{1,0:T(8,128)(2,1)S(1)}, u32[]{:S(2)}, u32[]{:S(2)}) %collective-permute-start.10) | collective-permute-done | bytes 589856 | tf_op jit(solution)/shard_map/ppermute | solution.py:516
  58.7 9.7 %student_logits.1 = f32[4,128,1024]{2,1,0:T(8,128)} custom-call(s32[2]{0:T(128)S(1)} %pad_add_fusion.1.place_ref, f32[8,128]{1,0:T(8,128)S(1)} %add.84.after_ref.mass_ref, bf16[128,4608]{1,0:T(8,128)(2,1)S(1)} %copy-done.4, bf16[64,4608]{1,0:T(8,128)(2,1)} %collective-permute-done.7.refs_0_.refs_1_, bf16[64,4608]{1,0:T(8,128)(2,1)} %collective-permute-done.8.refs_1_.refs_2_, ...), custom_call_target="tpu_custom_call" | custom-call | flops 1024 | bytes 1024 | tf_op jit(solution)/shard_map/student_logits/pallas_call | solution.py:293
  68.4 3.6 %all-to-all-start = ((f32[4,128,1024]{2,1,0:T(8,128)}), f32[4,128,1024]{2,1,0:T(8,128)S(1)}, u32[]{:S(2)}, u32[]{:S(2)}) async-start(f32[4,128,1024]{2,1,0:T(8,128)} %student_logits.1), calls=%async_computation | async-start | bytes 4194304 | tf_op jit(solution)/shard_map/all_to_all | solution.py:546
  72.0 3.8 %collective-permute-start.19 = (bf16[32,128,128]{2,1,0:T(8,128)(2,1)}, bf16[32,128,128]{2,1,0:T(8,128)(2,1)}, u32[]{:S(2)}, u32[]{:S(2)}) collective-permute-start(bf16[32,128,128]{2,1,0:T(8,128)(2,1)} %get-tuple-element.53), channel_id=1, source_target_pairs={{0,2},{1,3},{2,0},{3,1},{4,6},{5,7},{6,4},{7,5},{8,10},{9,11},{10,... | collective-permute-start | bytes 3145736 | tf_op jit(solution)/shard_map/ppermute | solution.py:516
  75.8 2.2 %collective-permute-done.14 = bf16[32,128,128]{2,1,0:T(8,128)(2,1)} collective-permute-done((bf16[32,128,128]{2,1,0:T(8,128)(2,1)}, bf16[32,128,128]{2,1,0:T(8,128)(2,1)}, u32[]{:S(2)}, u32[]{:S(2)}) %collective-permute-start.14) | collective-permute-done | bytes 1048608 | tf_op jit(solution)/shard_map/ppermute | solution.py:550
  78.0 3.0 %add_convert_fusion = bf16[32,128,128]{2,1,0:T(8,128)(2,1)} fusion(bf16[32,128,128]{2,1,0:T(8,128)(2,1)} %collective-permute-done.13, bf16[32,128,128]{2,1,0:T(8,128)(2,1)} %get-tuple-element.46), kind=kLoop, calls=%fused_computation | loop fusion | flops 2097152 | bytes 3145728 | tf_op jit(solution)/shard_map/convert_element_type | solution.py:542
  81.1 1.6 %collective-permute-start.20 = (bf16[32,128,128]{2,1,0:T(8,128)(2,1)}, bf16[32,128,128]{2,1,0:T(8,128)(2,1)}, u32[]{:S(2)}, u32[]{:S(2)}) collective-permute-start(bf16[32,128,128]{2,1,0:T(8,128)(2,1)} %add_convert_fusion), channel_id=1, source_target_pairs={{2,4},{3,5},{4,2},{5,3},{10,12},{11,13},{12,10},{13,11},{18,20},{1... | collective-permute-start | bytes 3145736 | tf_op jit(solution)/shard_map/ppermute | solution.py:550
  86.1 5.1 %turned_rows.1.a_ref = bf16[4608,512]{1,0:T(8,128)(2,1)} custom-call(s32[2]{0:T(128)S(1)} %pad_add_fusion.1.place_ref, bf16[128,4608]{1,0:T(8,128)(2,1)S(1)} %copy-done.4, bf16[64,4608]{1,0:T(8,128)(2,1)} %collective-permute-done.9.refs_2_.refs_0_, bf16[64,4608]{1,0:T(8,128)(2,1)} %collective-permute-done.7.refs_0_.refs_1_, ...), custom_call_target="tpu_custom_call" | custom-call | flops 1024 | bytes 1024 | tf_op jit(solution)/shard_map/turned_rows/pallas_call | solution.py:273
  91.2 6.2 %all-to-all-done.logits_ref.refs_4_ = f32[4,128,1024]{2,1,0:T(8,128)S(1)} async-done(((f32[4,128,1024]{2,1,0:T(8,128)}), f32[4,128,1024]{2,1,0:T(8,128)S(1)}, u32[]{:S(2)}, u32[]{:S(2)}) %all-to-all-start) | async-done | bytes 2097184 | tf_op jit(solution)/shard_map/all_to_all | solution.py:546
  97.4 1.5 %student_stats.1.refs_0_ = f32[8,128]{1,0:T(8,128)S(1)} custom-call(s32[4]{0:T(128)S(1)} %add_multiply_fusion.base_ref, s32[128,1]{1,0:T(8,128)S(1)} %copy.15.labels_ref, f32[8,128]{1,0:T(8,128)S(1)} %add.84.after_ref.mass_ref, f32[4,128,1024]{2,1,0:T(8,128)S(1)} %all-to-all-done.logits_ref.refs_4_), custom_call_target="tpu_custom_call" | custom-call | flops 1024 | bytes 1024 | tf_op jit(solution)/shard_map/student_stats/pallas_call | solution.py:331
  100.1 3.0 %collective-permute-start.18 = (f32[8,128]{1,0:T(8,128)S(1)}, f32[8,128]{1,0:T(8,128)S(1)}, u32[]{:S(2)}, u32[]{:S(2)}) collective-permute-start(f32[8,128]{1,0:T(8,128)S(1)} %merge_stats.5.refs_0_), channel_id=1, source_target_pairs={{0,6},{1,7},{2,4},{3,5},{4,2},{5,3},{6,0},{7,1},{8,14},{9,15},{10,... | collective-permute-start | bytes 12296 | tf_op jit(solution)/shard_map/ppermute | solution.py:516
  103.1 2.2 %collective-permute-start.17 = (f32[8,128]{1,0:T(8,128)S(1)}, f32[8,128]{1,0:T(8,128)S(1)}, u32[]{:S(2)}, u32[]{:S(2)}) collective-permute-start(f32[8,128]{1,0:T(8,128)S(1)} %merge_stats.5.refs_0_), channel_id=1, source_target_pairs={{0,4},{1,5},{2,6},{3,7},{4,0},{5,1},{6,2},{7,3},{8,12},{9,13},{10,... | collective-permute-start | bytes 12296 | tf_op jit(solution)/shard_map/ppermute | solution.py:516
  105.6 2.0 %collective-permute-done.17.refs_2_ = f32[8,128]{1,0:T(8,128)S(1)} collective-permute-done((f32[8,128]{1,0:T(8,128)S(1)}, f32[8,128]{1,0:T(8,128)S(1)}, u32[]{:S(2)}, u32[]{:S(2)}) %collective-permute-start.17) | collective-permute-done | bytes 4128 | tf_op jit(solution)/shard_map/ppermute | solution.py:516
  109.1 2.4 %grad_logits.2 = (bf16[128,1024]{1,0:T(8,128)(2,1)}, f32[1,128]{1,0:T(1,128)S(1)}) custom-call(s32[1]{0:T(128)} %bitcast.5.tok_ref, s32[4]{0:T(128)S(1)} %add_multiply_fusion.base_ref, s32[128,1]{1,0:T(8,128)S(1)} %copy.15.labels_ref, f32[128,128]{1,0:T(8,128)S(1)} %get-tuple-element.51.columns, bf16[1,32,128,128]{3,2,1,0:T(8,128)(2,1)S(1)} %bitcast.17, ...), custom_call_target="tpu_custom_call" | custom-call | flops 1024 | bytes 1024 | tf_op jit(solution)/shard_map/grad_logits/pallas_call | solution.py:434
  111.5 1.4 %collective-permute-start.23 = (bf16[128,1024]{1,0:T(8,128)(2,1)}, bf16[128,1024]{1,0:T(8,128)(2,1)S(1)}, u32[]{:S(2)}, u32[]{:S(2)}) collective-permute-start(bf16[128,1024]{1,0:T(8,128)(2,1)} %get-tuple-element.59), channel_id=1, source_target_pairs={{0,24},{8,16},{16,8},{24,0},{1,25},{9,17},{17,9},{25,1},{2,26},{10... | collective-permute-start | bytes 786440 | tf_op jit(solution)/shard_map/ppermute | solution.py:516
  112.9 4.1 %grad_logits.3 = (bf16[128,1024]{1,0:T(8,128)(2,1)}, bf16[128,1024]{1,0:T(8,128)(2,1)}, bf16[128,1024]{1,0:T(8,128)(2,1)}, f32[1,128]{1,0:T(1,128)S(1)}) custom-call(s32[1]{0:T(128)} %bitcast.5.tok_ref, s32[4]{0:T(128)S(1)} %add_multiply_fusion.base_ref, s32[128,1]{1,0:T(8,128)S(1)} %copy.15.labels_ref, f32[128,128]{1,0:T(8,128)S(1)} %get-tuple-element.51.columns, ...), custom_call_target="tpu_custom_call" | custom-call | flops 1024 | bytes 1024 | tf_op jit(solution)/shard_map/grad_logits/pallas_call | solution.py:434
  117.0 1.5 %collective-permute-start.25 = (bf16[128,1024]{1,0:T(8,128)(2,1)}, bf16[128,1024]{1,0:T(8,128)(2,1)S(1)}, u32[]{:S(2)}, u32[]{:S(2)}) collective-permute-start(bf16[128,1024]{1,0:T(8,128)(2,1)} %get-tuple-element.62), channel_id=1, source_target_pairs={{0,8},{8,0},{16,24},{24,16},{1,9},{9,1},{17,25},{25,17},{2,10},{10... | collective-permute-start | bytes 786440 | tf_op jit(solution)/shard_map/ppermute | solution.py:516
  120.3 4.1 %first_product.1 = (f32[4608,1024]{1,0:T(8,128)S(1)}, f32[1,128]{1,0:T(1,128)S(1)}) custom-call(bf16[4608,512]{1,0:T(8,128)(2,1)S(1)} %bitcast.14, bf16[128,1024]{1,0:T(8,128)(2,1)} %get-tuple-element.58.refs_0_, bf16[128,1024]{1,0:T(8,128)(2,1)S(1)} %collective-permute-done.23.refs_1_), custom_call_target="tpu_custom_call" | custom-call | flops 1024 | bytes 1024 | tf_op jit(solution)/shard_map/first_product/pallas_call | solution.py:485
  124.4 1.9 %collective-permute-start.24 = (f32[1,128]{1,0:T(1,128)S(1)}, f32[1,128]{1,0:T(1,128)S(1)}, u32[]{:S(2)}, u32[]{:S(2)}) collective-permute-start(f32[1,128]{1,0:T(1,128)S(1)} %add_add_fusion), channel_id=1, source_target_pairs={{0,4},{1,5},{2,6},{3,7},{4,0},{5,1},{6,2},{7,3},{8,12},{9,13},{10,... | collective-permute-start | bytes 1544 | tf_op jit(solution)/shard_map/ppermute | solution.py:516
  126.3 5.3 %last_product.1 = (bf16[4608,1024]{1,0:T(8,128)(2,1)}, f32[1,128]{1,0:T(1,128)S(1)}) custom-call(bf16[4608,512]{1,0:T(8,128)(2,1)S(1)} %bitcast.14, f32[4608,1024]{1,0:T(8,128)S(1)} %get-tuple-element.61.acc_ref, bf16[128,1024]{1,0:T(8,128)(2,1)S(1)} %collective-permute-done.25.refs_0_, bf16[128,1024]{1,0:T(8,128)(2,1)S(1)} %collective-permute-done.26.refs_1_), custom_call_target="tpu_custom_call" | custom-call | flops 1024 | bytes 1024 | tf_op jit(solution)/shard_map/last_product/pallas_call | solution.py:502
  (90 shorter events, 20.0 us)
Async XLA Ops:
  0.6 82.1 %copy-start = (s32[512]{0:T(512)S(1)}, s32[512]{0:T(512)}, u32[]{:S(2)}) copy-start(s32[512]{0:T(512)} %param.9) | copy-start | bytes 6148
  0.6 16.3 %collective-permute-start.5 = (bf16[32,4,128,128]{3,2,1,0:T(8,128)(2,1)}, bf16[32,4,128,128]{3,2,1,0:T(8,128)(2,1)}, u32[]{:S(2)}, u32[]{:S(2)}) collective-permute-start(bf16[32,4,128,128]{3,2,1,0:T(8,128)(2,1)} %w_own.3), channel_id=1, source_target_pairs={{0,1},{1,0},{2,3},{3,2},{4,5},{5,4},{6,7},{7,6},{8,9},{9,8},{10,11... | collective-permute-start | bytes 12582920 | tf_op jit(solution)/shard_map/ppermute | solution.py:516
  1.2 12.5 %collective-permute-start.1 = (bf16[128,4096]{1,0:T(8,128)(2,1)}, bf16[128,4096]{1,0:T(8,128)(2,1)S(1)}, u32[]{:S(2)}, u32[]{:S(2)}) collective-permute-start(bf16[128,4096]{1,0:T(8,128)(2,1)} %x_own.1), channel_id=1, source_target_pairs={{0,1},{1,0},{2,3},{3,2},{4,5},{5,4},{6,7},{7,6},{8,9},{9,8},{10,11... | collective-permute-start | bytes 3145736 | tf_op jit(solution)/shard_map/ppermute | solution.py:516
  3.1 4.6 %collective-permute-start.2 = (f32[8,128]{1,0:T(8,128)S(1)}, f32[8,128]{1,0:T(8,128)S(1)}, u32[]{:S(2)}, u32[]{:S(2)}) collective-permute-start(f32[8,128]{1,0:T(8,128)S(1)} %teacher_stats.1.refs_0_), channel_id=1, source_target_pairs={{0,2},{1,3},{2,0},{3,1},{4,6},{5,7},{6,4},{7,5},{8,10},{9,11},{10,... | collective-permute-start | bytes 12296 | tf_op jit(solution)/shard_map/ppermute | solution.py:516
  7.7 4.7 %collective-permute-start.3 = (f32[8,128]{1,0:T(8,128)S(1)}, f32[8,128]{1,0:T(8,128)S(1)}, u32[]{:S(2)}, u32[]{:S(2)}) collective-permute-start(f32[8,128]{1,0:T(8,128)S(1)} %merge_stats.3.refs_0_), channel_id=1, source_target_pairs={{0,4},{1,5},{2,6},{3,7},{4,0},{5,1},{6,2},{7,3},{8,12},{9,13},{10,... | collective-permute-start | bytes 12296 | tf_op jit(solution)/shard_map/ppermute | solution.py:516
  11.7 1.2 collective-permute-start
  12.4 1.2 collective-permute-start.4
  21.2 28.1 %collective-permute-start.6 = (bf16[32,128,128]{2,1,0:T(8,128)(2,1)}, bf16[32,128,128]{2,1,0:T(8,128)(2,1)}, u32[]{:S(2)}, u32[]{:S(2)}) collective-permute-start(bf16[32,128,128]{2,1,0:T(8,128)(2,1)} %get-tuple-element.34), channel_id=1, source_target_pairs={{0,2},{1,3},{6,4},{7,5},{8,10},{9,11},{14,12},{15,13},{16,18},{17,... | collective-permute-start | bytes 3145736 | tf_op jit(solution)/shard_map/ppermute | solution.py:550
  26.4 22.9 %copy-start.13 = (bf16[32,128,128]{2,1,0:T(8,128)(2,1)S(1)}, bf16[32,128,128]{2,1,0:T(8,128)(2,1)}, u32[]{:S(2)}) copy-start(bf16[32,128,128]{2,1,0:T(8,128)(2,1)} %get-tuple-element.34) | copy-start | bytes 3145732
  26.5 26.8 %collective-permute-start.9 = (bf16[64,4608]{1,0:T(8,128)(2,1)S(1)}, bf16[64,4608]{1,0:T(8,128)(2,1)}, u32[]{:S(2)}, u32[]{:S(2)}) collective-permute-start(bf16[64,4608]{1,0:T(8,128)(2,1)S(1)} %constant_dynamic-slice_fusion), channel_id=1, source_target_pairs={{0,24},{8,16},{16,8},{24,0},{1,25},{9,17},{17,9},{25,1},{2,26},{10... | collective-permute-start | bytes 1769480 | tf_op jit(solution)/shard_map/ppermute | solution.py:516
  29.0 25.7 %collective-permute-start.8 = (bf16[64,4608]{1,0:T(8,128)(2,1)S(1)}, bf16[64,4608]{1,0:T(8,128)(2,1)}, u32[]{:S(2)}, u32[]{:S(2)}) collective-permute-start(bf16[64,4608]{1,0:T(8,128)(2,1)S(1)} %constant_dynamic-slice_fusion), channel_id=1, source_target_pairs={{0,16},{8,24},{16,0},{24,8},{1,17},{9,25},{17,1},{25,9},{2,18},{10... | collective-permute-start | bytes 1769480 | tf_op jit(solution)/shard_map/ppermute | solution.py:516
  29.5 25.3 %collective-permute-start.7 = (bf16[64,4608]{1,0:T(8,128)(2,1)S(1)}, bf16[64,4608]{1,0:T(8,128)(2,1)}, u32[]{:S(2)}, u32[]{:S(2)}) collective-permute-start(bf16[64,4608]{1,0:T(8,128)(2,1)S(1)} %constant_dynamic-slice_fusion), channel_id=1, source_target_pairs={{0,8},{8,0},{16,24},{24,16},{1,9},{9,1},{17,25},{25,17},{2,10},{10... | collective-permute-start | bytes 1769480 | tf_op jit(solution)/shard_map/ppermute | solution.py:516
  40.6 35.2 %collective-permute-start.13 = (bf16[32,128,128]{2,1,0:T(8,128)(2,1)}, bf16[32,128,128]{2,1,0:T(8,128)(2,1)}, u32[]{:S(2)}, u32[]{:S(2)}) collective-permute-start(bf16[32,128,128]{2,1,0:T(8,128)(2,1)} %get-tuple-element.46), channel_id=1, source_target_pairs={{0,2},{1,3},{6,4},{7,5},{8,10},{9,11},{14,12},{15,13},{16,18},{17,... | collective-permute-start | bytes 3145736 | tf_op jit(solution)/shard_map/ppermute | solution.py:550
  52.0 26.1 %collective-permute-start.14 = (bf16[32,128,128]{2,1,0:T(8,128)(2,1)}, bf16[32,128,128]{2,1,0:T(8,128)(2,1)}, u32[]{:S(2)}, u32[]{:S(2)}) collective-permute-start(bf16[32,128,128]{2,1,0:T(8,128)(2,1)} %add_convert_fusion.1), channel_id=1, source_target_pairs={{2,6},{3,7},{4,0},{5,1},{10,14},{11,15},{12,8},{13,9},{18,22},{19,... | collective-permute-start | bytes 3145736 | tf_op jit(solution)/shard_map/ppermute | solution.py:550
  54.8 2.2 %collective-permute-start.10 = (bf16[64,4608]{1,0:T(8,128)(2,1)}, bf16[64,4608]{1,0:T(8,128)(2,1)S(1)}, u32[]{:S(2)}, u32[]{:S(2)}) collective-permute-start(bf16[64,4608]{1,0:T(8,128)(2,1)} %collective-permute-done.7.refs_0_.refs_1_), channel_id=1, source_target_pairs={{0,1},{1,0},{2,3},{3,2},{4,5},{5,4},{6,7},{7,6},{8,9},{9,8},{10,11... | collective-permute-start | bytes 1769480 | tf_op jit(solution)/shard_map/ppermute | solution.py:516
  54.8 3.1 %collective-permute-start.11 = (bf16[64,4608]{1,0:T(8,128)(2,1)}, bf16[64,4608]{1,0:T(8,128)(2,1)S(1)}, u32[]{:S(2)}, u32[]{:S(2)}) collective-permute-start(bf16[64,4608]{1,0:T(8,128)(2,1)} %collective-permute-done.8.refs_1_.refs_2_), channel_id=1, source_target_pairs={{0,1},{1,0},{2,3},{3,2},{4,5},{5,4},{6,7},{7,6},{8,9},{9,8},{10,11... | collective-permute-start | bytes 1769480 | tf_op jit(solution)/shard_map/ppermute | solution.py:516
  55.3 3.4 %collective-permute-start.12 = (bf16[64,4608]{1,0:T(8,128)(2,1)}, bf16[64,4608]{1,0:T(8,128)(2,1)S(1)}, u32[]{:S(2)}, u32[]{:S(2)}) collective-permute-start(bf16[64,4608]{1,0:T(8,128)(2,1)} %collective-permute-done.9.refs_2_.refs_0_), channel_id=1, source_target_pairs={{0,1},{1,0},{2,3},{3,2},{4,5},{5,4},{6,7},{7,6},{8,9},{9,8},{10,11... | collective-permute-start | bytes 1769480 | tf_op jit(solution)/shard_map/ppermute | solution.py:516
  57.0 11.4 %copy-start.7 = (bf16[64,4608]{1,0:T(8,128)(2,1)}, bf16[64,4608]{1,0:T(8,128)(2,1)S(1)}, u32[]{:S(2)}) copy-start(bf16[64,4608]{1,0:T(8,128)(2,1)S(1)} %collective-permute-done.10.refs_3_.refs_4_) | copy-start | bytes 1769476
  68.4 29.0 %all-to-all-start = ((f32[4,128,1024]{2,1,0:T(8,128)}), f32[4,128,1024]{2,1,0:T(8,128)S(1)}, u32[]{:S(2)}, u32[]{:S(2)}) async-start(f32[4,128,1024]{2,1,0:T(8,128)} %student_logits.1), calls=%async_computation | async-start | bytes 4194304 | tf_op jit(solution)/shard_map/all_to_all | solution.py:546
  72.0 37.0 %collective-permute-start.19 = (bf16[32,128,128]{2,1,0:T(8,128)(2,1)}, bf16[32,128,128]{2,1,0:T(8,128)(2,1)}, u32[]{:S(2)}, u32[]{:S(2)}) collective-permute-start(bf16[32,128,128]{2,1,0:T(8,128)(2,1)} %get-tuple-element.53), channel_id=1, source_target_pairs={{0,2},{1,3},{2,0},{3,1},{4,6},{5,7},{6,4},{7,5},{8,10},{9,11},{10,... | collective-permute-start | bytes 3145736 | tf_op jit(solution)/shard_map/ppermute | solution.py:516
  81.1 28.0 %collective-permute-start.20 = (bf16[32,128,128]{2,1,0:T(8,128)(2,1)}, bf16[32,128,128]{2,1,0:T(8,128)(2,1)}, u32[]{:S(2)}, u32[]{:S(2)}) collective-permute-start(bf16[32,128,128]{2,1,0:T(8,128)(2,1)} %add_convert_fusion), channel_id=1, source_target_pairs={{2,4},{3,5},{4,2},{5,3},{10,12},{11,13},{12,10},{13,11},{18,20},{1... | collective-permute-start | bytes 3145736 | tf_op jit(solution)/shard_map/ppermute | solution.py:550
  91.2 17.8 %copy-start.6 = (bf16[32,128,128]{2,1,0:T(8,128)(2,1)S(1)}, bf16[32,128,128]{2,1,0:T(8,128)(2,1)}, u32[]{:S(2)}) copy-start(bf16[32,128,128]{2,1,0:T(8,128)(2,1)} %get-tuple-element.52) | copy-start | bytes 3145732
  98.9 1.2 collective-permute-start.15
  100.1 5.6 %collective-permute-start.18 = (f32[8,128]{1,0:T(8,128)S(1)}, f32[8,128]{1,0:T(8,128)S(1)}, u32[]{:S(2)}, u32[]{:S(2)}) collective-permute-start(f32[8,128]{1,0:T(8,128)S(1)} %merge_stats.5.refs_0_), channel_id=1, source_target_pairs={{0,6},{1,7},{2,4},{3,5},{4,2},{5,3},{6,0},{7,1},{8,14},{9,15},{10,... | collective-permute-start | bytes 12296 | tf_op jit(solution)/shard_map/ppermute | solution.py:516
  103.1 4.5 %collective-permute-start.17 = (f32[8,128]{1,0:T(8,128)S(1)}, f32[8,128]{1,0:T(8,128)S(1)}, u32[]{:S(2)}, u32[]{:S(2)}) collective-permute-start(f32[8,128]{1,0:T(8,128)S(1)} %merge_stats.5.refs_0_), channel_id=1, source_target_pairs={{0,4},{1,5},{2,6},{3,7},{4,0},{5,1},{6,2},{7,3},{8,12},{9,13},{10,... | collective-permute-start | bytes 12296 | tf_op jit(solution)/shard_map/ppermute | solution.py:516
  105.3 3.6 %collective-permute-start.16 = (f32[8,128]{1,0:T(8,128)S(1)}, f32[8,128]{1,0:T(8,128)S(1)}, u32[]{:S(2)}, u32[]{:S(2)}) collective-permute-start(f32[8,128]{1,0:T(8,128)S(1)} %merge_stats.5.refs_0_), channel_id=1, source_target_pairs={{0,2},{1,3},{2,0},{3,1},{4,6},{5,7},{6,4},{7,5},{8,10},{9,11},{10,... | collective-permute-start | bytes 12296 | tf_op jit(solution)/shard_map/ppermute | solution.py:516
  111.5 8.7 %collective-permute-start.23 = (bf16[128,1024]{1,0:T(8,128)(2,1)}, bf16[128,1024]{1,0:T(8,128)(2,1)S(1)}, u32[]{:S(2)}, u32[]{:S(2)}) collective-permute-start(bf16[128,1024]{1,0:T(8,128)(2,1)} %get-tuple-element.59), channel_id=1, source_target_pairs={{0,24},{8,16},{16,8},{24,0},{1,25},{9,17},{17,9},{25,1},{2,26},{10... | collective-permute-start | bytes 786440 | tf_op jit(solution)/shard_map/ppermute | solution.py:516
  117.0 9.3 %collective-permute-start.25 = (bf16[128,1024]{1,0:T(8,128)(2,1)}, bf16[128,1024]{1,0:T(8,128)(2,1)S(1)}, u32[]{:S(2)}, u32[]{:S(2)}) collective-permute-start(bf16[128,1024]{1,0:T(8,128)(2,1)} %get-tuple-element.62), channel_id=1, source_target_pairs={{0,8},{8,0},{16,24},{24,16},{1,9},{9,1},{17,25},{25,17},{2,10},{10... | collective-permute-start | bytes 786440 | tf_op jit(solution)/shard_map/ppermute | solution.py:516
  118.5 7.8 %collective-permute-start.26 = (bf16[128,1024]{1,0:T(8,128)(2,1)}, bf16[128,1024]{1,0:T(8,128)(2,1)S(1)}, u32[]{:S(2)}, u32[]{:S(2)}) collective-permute-start(bf16[128,1024]{1,0:T(8,128)(2,1)} %get-tuple-element.63), channel_id=1, source_target_pairs={{0,16},{8,24},{16,0},{24,8},{1,17},{9,25},{17,1},{25,9},{2,18},{10... | collective-permute-start | bytes 786440 | tf_op jit(solution)/shard_map/ppermute | solution.py:516
  119.1 1.1 collective-permute-start.21
  120.2 4.2 %collective-permute-start.22 = (f32[1,128]{1,0:T(1,128)S(1)}, f32[1,128]{1,0:T(1,128)S(1)}, u32[]{:S(2)}, u32[]{:S(2)}) collective-permute-start(f32[1,128]{1,0:T(1,128)S(1)} %add.88), channel_id=1, source_target_pairs={{0,2},{1,3},{2,0},{3,1},{4,6},{5,7},{6,4},{7,5},{8,10},{9,11},{10,... | collective-permute-start | bytes 1544 | tf_op jit(solution)/shard_map/ppermute | solution.py:516
  124.4 7.2 %collective-permute-start.24 = (f32[1,128]{1,0:T(1,128)S(1)}, f32[1,128]{1,0:T(1,128)S(1)}, u32[]{:S(2)}, u32[]{:S(2)}) collective-permute-start(f32[1,128]{1,0:T(1,128)S(1)} %add_add_fusion), channel_id=1, source_target_pairs={{0,4},{1,5},{2,6},{3,7},{4,0},{5,1},{6,2},{7,3},{8,12},{9,13},{10,... | collective-permute-start | bytes 1544 | tf_op jit(solution)/shard_map/ppermute | solution.py:516
  (12 other events, 68.4 us)

commit v8 on v7

--- a/solution.py
+++ b/solution.py
@@ -536,6 +536,24 @@
 
 def exchange_tok(x):
     return lax.all_to_all(x, "tok", split_axis=0, concat_axis=0, tiled=True)
+
+
+def merge_sums_kernel(a_ref, b_ref, o_ref):
+    o_ref[...] = (a_ref[...].astype(F32) + b_ref[...].astype(F32)).astype(BF16)
+
+
+def merge_sums(a, b):
+    spec = pl.BlockSpec((a.shape[0] // 2,) + a.shape[1:], lambda i: (i, 0, 0))
+    return pl.pallas_call(
+        merge_sums_kernel,
+        grid=(2,),
+        in_specs=[spec, spec],
+        out_specs=spec,
+        out_shape=pltpu.HBM(a.shape, BF16),
+        compiler_params=params(8),
+        cost_estimate=COST,
+        name="merge_sums",
+    )(in_hbm(a), b)
 
 
 def plus(a, b):
@@ -621,8 +639,8 @@
     label_column = lax.dynamic_slice_in_dim(labels, tok * rows, rows).reshape(rows, 1)
     scores = exchange_tok(logits)
     if in_line:
-        second, arrived, logits = lax.optimization_barrier((second, arrived, logits))
-        merged_inner = plus(far_inner, second)
+        second, logits = lax.optimization_barrier((second, logits))
+        merged_inner, arrived = lax.optimization_barrier((merge_sums(far_inner, second), arrived))
         crossed = send(merged_inner, across)
         where, merged_inner = lax.optimization_barrier((where, merged_inner))
         turned = turned_rows(where, hidden, near[-1:] + near[:-1], far[-1:] + far[:-1])

time: 133 us -> 138 us (1.038)
  waiting for transfers between devices: 28.3 us -> 31.4 us
  other arithmetic: 7.08 us -> 4.05 us
  Pallas kernels: 49.3 us -> 51.6 us
  starting transfers between devices: 39.4 us -> 41.6 us
    ppermute x4, waiting for transfers between devices: 8.67 us -> 14.4 us  [send(): lax.ppermute(x, 'vocab', [(2 * a + c, 2 * b + c) for a, b in hops for c i...]
    all_to_all x1, waiting for transfers between devices: 6.18 us -> 2 us  [exchange_tok(): return lax.all_to_all(x, 'tok', split_axis=0, concat_axis=0, tiled=True)]
    convert_element_type x2 -> x1, other arithmetic: 5.68 us -> 2.64 us  [plus(): return (a.astype(F32) + b.astype(F32)).astype(BF16)]
    ppermute x23, starting transfers between devices: 25.4 us -> 28.1 us  [swap(): lax.ppermute(x, axis, [(i, i ^ mask) for i in range(lax.axis_size(axis))])]
    pallas_call x0 -> x1, Pallas kernels: none -> 2.49 us  [merge_sums(): pl.pallas_call(merge_sums_kernel, grid=(2,), in_specs=[spec, spec], out_s...]
    ppermute x23, waiting for transfers between devices: 13.5 us -> 15 us  [swap(): lax.ppermute(x, axis, [(i, i ^ mask) for i in range(lax.axis_size(axis))])]
  transfers between devices with their start and end apart: 28 -> 28, of which waited for: 17 -> 13; matrix products, arithmetic and copies ran while one was open for 5% -> 3% of each run, Pallas kernels for 32% -> 33%
where the time goes in v8:
time: 138 us; the launch traced here: 137 us
  Pallas kernels  51.6 us (37%)
  starting transfers between devices  41.6 us (30%)
  waiting for transfers between devices  31.4 us (23%)
  local copies, waits for them, and re-layouts  7.17 us (5%)
  other arithmetic  4.05 us (3%)
    ppermute x23, starting transfers between devices, swap(): lax.ppermute(x, axis, [(i, i ^ mask) for i in range(lax.axis_size(axis))])  28.1 us
    ppermute x23, waiting for transfers between devices, swap(): lax.ppermute(x, axis, [(i, i ^ mask) for i in range(lax.axis_size(axis))])  15 us
    ppermute x4, waiting for transfers between devices, send(): lax.ppermute(x, 'vocab', [(2 * a + c, 2 * b + c) for a, b in hops for c i...  14.4 us
    pallas_call x2, Pallas kernels, chip_sums(): pl.pallas_call(functools.partial(sums_kernel, first=first, fan=fan, piece...  12.2 us
    pallas_call x1, Pallas kernels, student_logits(): pl.pallas_call(logits_kernel, grid=(cols // tile,), in_specs=[SMEM_SPEC,...  10.1 us
    ppermute x4, starting transfers between devices, send(): lax.ppermute(x, 'vocab', [(2 * a + c, 2 * b + c) for a, b in hops for c i...  9.87 us
    unnamed x32, local copies, waits for them, and re-layouts  6.65 us
    pallas_call x2, Pallas kernels, grad_logits(): pl.pallas_call(functools.partial(grad_kernel, n_sums=len(sums), groups=gr...  6.51 us
  transfers between devices with their start and end apart: 28, of which 13 were waited for; matrix products, arithmetic and copies ran while one was open for 3% of the time, Pallas kernels for 33%

profile of v8, /device:TPU:0, one launch (start us, length us, event | category | flops | bytes accessed | tf_op | source)
XLA Modules:
  0.0 136.8 jit_solution(16411724411425403990)
XLA Ops:
  3.1 3.0 %collective-permute-start.2 = (f32[8,128]{1,0:T(8,128)S(1)}, f32[8,128]{1,0:T(8,128)S(1)}, u32[]{:S(2)}, u32[]{:S(2)}) collective-permute-start(f32[8,128]{1,0:T(8,128)S(1)} %teacher_stats.1.refs_0_), channel_id=1, source_target_pairs={{0,2},{1,3},{2,0},{3,1},{4,6},{5,7},{6,4},{7,5},{8,10},{9,11},{10,... | collective-permute-start | bytes 12296 | tf_op jit(solution)/shard_map/ppermute | solution.py:516
  6.1 1.6 %collective-permute-done.2.refs_1_ = f32[8,128]{1,0:T(8,128)S(1)} collective-permute-done((f32[8,128]{1,0:T(8,128)S(1)}, f32[8,128]{1,0:T(8,128)S(1)}, u32[]{:S(2)}, u32[]{:S(2)}) %collective-permute-start.2) | collective-permute-done | bytes 4128 | tf_op jit(solution)/shard_map/ppermute | solution.py:516
  7.7 3.1 %collective-permute-start.3 = (f32[8,128]{1,0:T(8,128)S(1)}, f32[8,128]{1,0:T(8,128)S(1)}, u32[]{:S(2)}, u32[]{:S(2)}) collective-permute-start(f32[8,128]{1,0:T(8,128)S(1)} %merge_stats.3.refs_0_), channel_id=1, source_target_pairs={{0,4},{1,5},{2,6},{3,7},{4,0},{5,1},{6,2},{7,3},{8,12},{9,13},{10,... | collective-permute-start | bytes 12296 | tf_op jit(solution)/shard_map/ppermute | solution.py:516
  13.6 3.3 %teacher_probs.1 = bf16[2,32,128,128]{3,2,1,0:T(8,128)(2,1)S(1)} custom-call(bf16[128,4096]{1,0:T(8,128)(2,1)} %x_own.1, bf16[128,4096]{1,0:T(8,128)(2,1)S(1)} %collective-permute-done.1.x_peer, f32[8,128]{1,0:T(8,128)S(1)} %merge_stats.4.refs_0_, f32[8,128]{1,0:T(8,128)S(1)} %collective-permute-done.4.refs_1_), custom_call_target="tpu_custom_call" | custom-call | flops 1024 | bytes 1024 | tf_op jit(solution)/shard_map/teacher_probs/pallas_call | solution.py:203
  16.9 4.3 %chip_sums.2 = (bf16[32,128,128]{2,1,0:T(8,128)(2,1)}, f32[8,128]{1,0:T(8,128)S(1)}) custom-call(s32[2]{0:T(128)S(1)} %pad_add_fusion.spot_ref, s32[8,384]{1,0:T(8,128)S(1)} %entry_lists.1.list_ref, bf16[64,128,128]{2,1,0:T(8,128)(2,1)S(1)} %bitcast.15, bf16[32,4,128,128]{3,2,1,0:T(8,128)(2,1)S(1)} %copy-done.2, ...), custom_call_target="tpu_custom_call" | custom-call | flops 1024 | bytes 1024 | tf_op jit(solution)/shard_map/chip_sums/pallas_call | solution.py:222
  21.2 4.7 %collective-permute-start.6 = (bf16[32,128,128]{2,1,0:T(8,128)(2,1)}, bf16[32,128,128]{2,1,0:T(8,128)(2,1)}, u32[]{:S(2)}, u32[]{:S(2)}) collective-permute-start(bf16[32,128,128]{2,1,0:T(8,128)(2,1)} %get-tuple-element.35), channel_id=1, source_target_pairs={{0,2},{1,3},{6,4},{7,5},{8,10},{9,11},{14,12},{15,13},{16,18},{17,... | collective-permute-start | bytes 3145736 | tf_op jit(solution)/shard_map/ppermute | solution.py:568
  26.0 2.5 %collective-permute-start.9 = (bf16[64,4608]{1,0:T(8,128)(2,1)S(1)}, bf16[64,4608]{1,0:T(8,128)(2,1)}, u32[]{:S(2)}, u32[]{:S(2)}) collective-permute-start(bf16[64,4608]{1,0:T(8,128)(2,1)S(1)} %constant_dynamic-slice_fusion), channel_id=1, source_target_pairs={{0,24},{8,16},{16,8},{24,0},{1,25},{9,17},{17,9},{25,1},{2,26},{10... | collective-permute-start | bytes 1769480 | tf_op jit(solution)/shard_map/ppermute | solution.py:516
  29.5 2.2 %copy-done.3 = bf16[32,4,128,128]{3,2,1,0:T(8,128)(2,1)S(1)} copy-done((bf16[32,4,128,128]{3,2,1,0:T(8,128)(2,1)S(1)}, bf16[32,4,128,128]{3,2,1,0:T(8,128)(2,1)}, u32[]{:S(2)}) %copy-start.3) | copy-done | bytes 4194328
  31.7 7.9 %chip_sums.3 = (bf16[32,128,128]{2,1,0:T(8,128)(2,1)}, bf16[32,128,128]{2,1,0:T(8,128)(2,1)}, bf16[32,128,128]{2,1,0:T(8,128)(2,1)}, f32[8,128]{1,0:T(8,128)S(1)}) custom-call(s32[2]{0:T(128)S(1)} %pad_add_fusion.spot_ref, s32[8,384]{1,0:T(8,128)S(1)} %entry_lists.1.list_ref, bf16[64,128,128]{2,1,0:T(8,128)(2,1)S(1)} %bitcast.16, ...), custom_call_target="tpu_custom_call" | custom-call | flops 1024 | bytes 1024 | tf_op jit(solution)/shard_map/chip_sums/pallas_call | solution.py:222
  39.6 8.2 %collective-permute-done.6 = bf16[32,128,128]{2,1,0:T(8,128)(2,1)} collective-permute-done((bf16[32,128,128]{2,1,0:T(8,128)(2,1)}, bf16[32,128,128]{2,1,0:T(8,128)(2,1)}, u32[]{:S(2)}, u32[]{:S(2)}) %collective-permute-start.6) | collective-permute-done | bytes 1048608 | tf_op jit(solution)/shard_map/ppermute | solution.py:568
  47.8 2.6 %add_convert_fusion = bf16[32,128,128]{2,1,0:T(8,128)(2,1)} fusion(bf16[32,128,128]{2,1,0:T(8,128)(2,1)} %collective-permute-done.6, bf16[32,128,128]{2,1,0:T(8,128)(2,1)S(1)} %copy-done.13), kind=kLoop, calls=%fused_computation | loop fusion | flops 2097152 | bytes 3145728 | tf_op jit(solution)/shard_map/convert_element_type | solution.py:560
  50.4 4.2 %collective-permute-done.8.refs_1_.refs_2_ = bf16[64,4608]{1,0:T(8,128)(2,1)} collective-permute-done((bf16[64,4608]{1,0:T(8,128)(2,1)S(1)}, bf16[64,4608]{1,0:T(8,128)(2,1)}, u32[]{:S(2)}, u32[]{:S(2)}) %collective-permute-start.8) | collective-permute-done | bytes 589856 | tf_op jit(solution)/shard_map/ppermute | solution.py:516
  55.3 2.3 %collective-permute-start.13 = (bf16[32,128,128]{2,1,0:T(8,128)(2,1)}, bf16[32,128,128]{2,1,0:T(8,128)(2,1)}, u32[]{:S(2)}, u32[]{:S(2)}) collective-permute-start(bf16[32,128,128]{2,1,0:T(8,128)(2,1)} %get-tuple-element.47.a_ref), channel_id=1, source_target_pairs={{0,2},{1,3},{6,4},{7,5},{8,10},{9,11},{14,12},{15,13},{16,18},{17,... | collective-permute-start | bytes 3145736 | tf_op jit(solution)/shard_map/ppermute | solution.py:568
  58.9 10.1 %student_logits.1 = f32[4,128,1024]{2,1,0:T(8,128)} custom-call(s32[2]{0:T(128)S(1)} %pad_add_fusion.1.place_ref, f32[8,128]{1,0:T(8,128)S(1)} %add.81.after_ref.mass_ref, bf16[128,4608]{1,0:T(8,128)(2,1)S(1)} %copy-done.4, bf16[64,4608]{1,0:T(8,128)(2,1)} %collective-permute-done.7.refs_0_.refs_1_, bf16[64,4608]{1,0:T(8,128)(2,1)} %collective-permute-done.8.refs_1_.refs_2_, ...), custom_call_target="tpu_custom_call" | custom-call | flops 1024 | bytes 1024 | tf_op jit(solution)/shard_map/student_logits/pallas_call | solution.py:293
  69.0 3.6 %all-to-all-start = ((f32[4,128,1024]{2,1,0:T(8,128)}), f32[4,128,1024]{2,1,0:T(8,128)S(1)}, u32[]{:S(2)}, u32[]{:S(2)}) async-start(f32[4,128,1024]{2,1,0:T(8,128)} %student_logits.1), calls=%async_computation | async-start | bytes 4194304 | tf_op jit(solution)/shard_map/all_to_all | solution.py:564
  72.7 4.9 %collective-permute-start.19 = (bf16[32,128,128]{2,1,0:T(8,128)(2,1)}, bf16[32,128,128]{2,1,0:T(8,128)(2,1)}, u32[]{:S(2)}, u32[]{:S(2)}) collective-permute-start(bf16[32,128,128]{2,1,0:T(8,128)(2,1)} %get-tuple-element.55), channel_id=1, source_target_pairs={{0,2},{1,3},{2,0},{3,1},{4,6},{5,7},{6,4},{7,5},{8,10},{9,11},{10,... | collective-permute-start | bytes 3145736 | tf_op jit(solution)/shard_map/ppermute | solution.py:516
  77.6 2.8 %collective-permute-done.13.b_ref = bf16[32,128,128]{2,1,0:T(8,128)(2,1)} collective-permute-done((bf16[32,128,128]{2,1,0:T(8,128)(2,1)}, bf16[32,128,128]{2,1,0:T(8,128)(2,1)}, u32[]{:S(2)}, u32[]{:S(2)}) %collective-permute-start.13) | collective-permute-done | bytes 1048608 | tf_op jit(solution)/shard_map/ppermute | solution.py:568
  80.4 2.5 %merge_sums.1 = bf16[32,128,128]{2,1,0:T(8,128)(2,1)} custom-call(bf16[32,128,128]{2,1,0:T(8,128)(2,1)} %get-tuple-element.47.a_ref, bf16[32,128,128]{2,1,0:T(8,128)(2,1)} %collective-permute-done.13.b_ref), custom_call_target="tpu_custom_call" | custom-call | flops 1024 | bytes 1024 | tf_op jit(solution)/shard_map/merge_sums/pallas_call | solution.py:547
  82.9 3.4 %collective-permute-done.14 = bf16[32,128,128]{2,1,0:T(8,128)(2,1)} collective-permute-done((bf16[32,128,128]{2,1,0:T(8,128)(2,1)}, bf16[32,128,128]{2,1,0:T(8,128)(2,1)}, u32[]{:S(2)}, u32[]{:S(2)}) %collective-permute-start.14) | collective-permute-done | bytes 1048608 | tf_op jit(solution)/shard_map/ppermute | solution.py:568
  86.3 1.6 %collective-permute-start.20 = (bf16[32,128,128]{2,1,0:T(8,128)(2,1)}, bf16[32,128,128]{2,1,0:T(8,128)(2,1)}, u32[]{:S(2)}, u32[]{:S(2)}) collective-permute-start(bf16[32,128,128]{2,1,0:T(8,128)(2,1)} %merge_sums.1), channel_id=1, source_target_pairs={{2,4},{3,5},{4,2},{5,3},{10,12},{11,13},{12,10},{13,11},{18,20},{1... | collective-permute-start | bytes 3145736 | tf_op jit(solution)/shard_map/ppermute | solution.py:568
  91.3 5.1 %turned_rows.1.a_ref = bf16[4608,512]{1,0:T(8,128)(2,1)} custom-call(s32[2]{0:T(128)S(1)} %pad_add_fusion.1.place_ref, bf16[128,4608]{1,0:T(8,128)(2,1)S(1)} %copy-done.4, bf16[64,4608]{1,0:T(8,128)(2,1)} %collective-permute-done.9.refs_2_.refs_0_, bf16[64,4608]{1,0:T(8,128)(2,1)} %collective-permute-done.7.refs_0_.refs_1_, ...), custom_call_target="tpu_custom_call" | custom-call | flops 1024 | bytes 1024 | tf_op jit(solution)/shard_map/turned_rows/pallas_call | solution.py:273
  96.4 2.0 %all-to-all-done.logits_ref.refs_4_ = f32[4,128,1024]{2,1,0:T(8,128)S(1)} async-done(((f32[4,128,1024]{2,1,0:T(8,128)}), f32[4,128,1024]{2,1,0:T(8,128)S(1)}, u32[]{:S(2)}, u32[]{:S(2)}) %all-to-all-start) | async-done | bytes 2097184 | tf_op jit(solution)/shard_map/all_to_all | solution.py:564
  98.4 1.4 %student_stats.1.refs_0_ = f32[8,128]{1,0:T(8,128)S(1)} custom-call(s32[4]{0:T(128)S(1)} %add_multiply_fusion.base_ref, s32[128,1]{1,0:T(8,128)S(1)} %copy.15.labels_ref, f32[8,128]{1,0:T(8,128)S(1)} %add.81.after_ref.mass_ref, f32[4,128,1024]{2,1,0:T(8,128)S(1)} %all-to-all-done.logits_ref.refs_4_), custom_call_target="tpu_custom_call" | custom-call | flops 1024 | bytes 1024 | tf_op jit(solution)/shard_map/student_stats/pallas_call | solution.py:331
  101.1 2.8 %collective-permute-start.18 = (f32[8,128]{1,0:T(8,128)S(1)}, f32[8,128]{1,0:T(8,128)S(1)}, u32[]{:S(2)}, u32[]{:S(2)}) collective-permute-start(f32[8,128]{1,0:T(8,128)S(1)} %merge_stats.5.refs_0_), channel_id=1, source_target_pairs={{0,6},{1,7},{2,4},{3,5},{4,2},{5,3},{6,0},{7,1},{8,14},{9,15},{10,... | collective-permute-start | bytes 12296 | tf_op jit(solution)/shard_map/ppermute | solution.py:516
  103.9 3.3 %collective-permute-start.17 = (f32[8,128]{1,0:T(8,128)S(1)}, f32[8,128]{1,0:T(8,128)S(1)}, u32[]{:S(2)}, u32[]{:S(2)}) collective-permute-start(f32[8,128]{1,0:T(8,128)S(1)} %merge_stats.5.refs_0_), channel_id=1, source_target_pairs={{0,4},{1,5},{2,6},{3,7},{4,0},{5,1},{6,2},{7,3},{8,12},{9,13},{10,... | collective-permute-start | bytes 12296 | tf_op jit(solution)/shard_map/ppermute | solution.py:516
  107.2 5.6 %collective-permute-done.17.refs_2_ = f32[8,128]{1,0:T(8,128)S(1)} collective-permute-done((f32[8,128]{1,0:T(8,128)S(1)}, f32[8,128]{1,0:T(8,128)S(1)}, u32[]{:S(2)}, u32[]{:S(2)}) %collective-permute-start.17) | collective-permute-done | bytes 4128 | tf_op jit(solution)/shard_map/ppermute | solution.py:516
  113.0 2.4 %grad_logits.2 = (bf16[128,1024]{1,0:T(8,128)(2,1)}, f32[1,128]{1,0:T(1,128)S(1)}) custom-call(s32[1]{0:T(128)} %bitcast.5.tok_ref, s32[4]{0:T(128)S(1)} %add_multiply_fusion.base_ref, s32[128,1]{1,0:T(8,128)S(1)} %copy.15.labels_ref, f32[128,128]{1,0:T(8,128)S(1)} %get-tuple-element.53.columns, bf16[1,32,128,128]{3,2,1,0:T(8,128)(2,1)S(1)} %bitcast.17, ...), custom_call_target="tpu_custom_call" | custom-call | flops 1024 | bytes 1024 | tf_op jit(solution)/shard_map/grad_logits/pallas_call | solution.py:434
  115.4 1.6 %collective-permute-start.23 = (bf16[128,1024]{1,0:T(8,128)(2,1)}, bf16[128,1024]{1,0:T(8,128)(2,1)S(1)}, u32[]{:S(2)}, u32[]{:S(2)}) collective-permute-start(bf16[128,1024]{1,0:T(8,128)(2,1)} %get-tuple-element.61), channel_id=1, source_target_pairs={{0,24},{8,16},{16,8},{24,0},{1,25},{9,17},{17,9},{25,1},{2,26},{10... | collective-permute-start | bytes 786440 | tf_op jit(solution)/shard_map/ppermute | solution.py:516
  117.1 4.1 %grad_logits.3 = (bf16[128,1024]{1,0:T(8,128)(2,1)}, bf16[128,1024]{1,0:T(8,128)(2,1)}, bf16[128,1024]{1,0:T(8,128)(2,1)}, f32[1,128]{1,0:T(1,128)S(1)}) custom-call(s32[1]{0:T(128)} %bitcast.5.tok_ref, s32[4]{0:T(128)S(1)} %add_multiply_fusion.base_ref, s32[128,1]{1,0:T(8,128)S(1)} %copy.15.labels_ref, f32[128,128]{1,0:T(8,128)S(1)} %get-tuple-element.53.columns, ...), custom_call_target="tpu_custom_call" | custom-call | flops 1024 | bytes 1024 | tf_op jit(solution)/shard_map/grad_logits/pallas_call | solution.py:434
  124.7 4.1 %first_product.1 = (f32[4608,1024]{1,0:T(8,128)S(1)}, f32[1,128]{1,0:T(1,128)S(1)}) custom-call(bf16[4608,512]{1,0:T(8,128)(2,1)S(1)} %bitcast.14, bf16[128,1024]{1,0:T(8,128)(2,1)} %get-tuple-element.60.refs_0_, bf16[128,1024]{1,0:T(8,128)(2,1)S(1)} %collective-permute-done.23.refs_1_), custom_call_target="tpu_custom_call" | custom-call | flops 1024 | bytes 1024 | tf_op jit(solution)/shard_map/first_product/pallas_call | solution.py:485
  128.9 2.0 %collective-permute-start.24 = (f32[1,128]{1,0:T(1,128)S(1)}, f32[1,128]{1,0:T(1,128)S(1)}, u32[]{:S(2)}, u32[]{:S(2)}) collective-permute-start(f32[1,128]{1,0:T(1,128)S(1)} %add_add_fusion), channel_id=1, source_target_pairs={{0,4},{1,5},{2,6},{3,7},{4,0},{5,1},{6,2},{7,3},{8,12},{9,13},{10,... | collective-permute-start | bytes 1544 | tf_op jit(solution)/shard_map/ppermute | solution.py:516
  130.9 5.3 %last_product.1 = (bf16[4608,1024]{1,0:T(8,128)(2,1)}, f32[1,128]{1,0:T(1,128)S(1)}) custom-call(bf16[4608,512]{1,0:T(8,128)(2,1)S(1)} %bitcast.14, f32[4608,1024]{1,0:T(8,128)S(1)} %get-tuple-element.63.acc_ref, bf16[128,1024]{1,0:T(8,128)(2,1)S(1)} %collective-permute-done.25.refs_0_, bf16[128,1024]{1,0:T(8,128)(2,1)S(1)} %collective-permute-done.26.refs_1_), custom_call_target="tpu_custom_call" | custom-call | flops 1024 | bytes 1024 | tf_op jit(solution)/shard_map/last_product/pallas_call | solution.py:502
  (90 shorter events, 17.2 us)
Async XLA Ops:
  0.6 87.3 %copy-start = (s32[512]{0:T(512)S(1)}, s32[512]{0:T(512)}, u32[]{:S(2)}) copy-start(s32[512]{0:T(512)} %param.9) | copy-start | bytes 6148
  0.6 16.3 %collective-permute-start.5 = (bf16[32,4,128,128]{3,2,1,0:T(8,128)(2,1)}, bf16[32,4,128,128]{3,2,1,0:T(8,128)(2,1)}, u32[]{:S(2)}, u32[]{:S(2)}) collective-permute-start(bf16[32,4,128,128]{3,2,1,0:T(8,128)(2,1)} %w_own.3), channel_id=1, source_target_pairs={{0,1},{1,0},{2,3},{3,2},{4,5},{5,4},{6,7},{7,6},{8,9},{9,8},{10,11... | collective-permute-start | bytes 12582920 | tf_op jit(solution)/shard_map/ppermute | solution.py:516
  1.2 12.5 %collective-permute-start.1 = (bf16[128,4096]{1,0:T(8,128)(2,1)}, bf16[128,4096]{1,0:T(8,128)(2,1)S(1)}, u32[]{:S(2)}, u32[]{:S(2)}) collective-permute-start(bf16[128,4096]{1,0:T(8,128)(2,1)} %x_own.1), channel_id=1, source_target_pairs={{0,1},{1,0},{2,3},{3,2},{4,5},{5,4},{6,7},{7,6},{8,9},{9,8},{10,11... | collective-permute-start | bytes 3145736 | tf_op jit(solution)/shard_map/ppermute | solution.py:516
  3.1 4.6 %collective-permute-start.2 = (f32[8,128]{1,0:T(8,128)S(1)}, f32[8,128]{1,0:T(8,128)S(1)}, u32[]{:S(2)}, u32[]{:S(2)}) collective-permute-start(f32[8,128]{1,0:T(8,128)S(1)} %teacher_stats.1.refs_0_), channel_id=1, source_target_pairs={{0,2},{1,3},{2,0},{3,1},{4,6},{5,7},{6,4},{7,5},{8,10},{9,11},{10,... | collective-permute-start | bytes 12296 | tf_op jit(solution)/shard_map/ppermute | solution.py:516
  7.7 4.7 %collective-permute-start.3 = (f32[8,128]{1,0:T(8,128)S(1)}, f32[8,128]{1,0:T(8,128)S(1)}, u32[]{:S(2)}, u32[]{:S(2)}) collective-permute-start(f32[8,128]{1,0:T(8,128)S(1)} %merge_stats.3.refs_0_), channel_id=1, source_target_pairs={{0,4},{1,5},{2,6},{3,7},{4,0},{5,1},{6,2},{7,3},{8,12},{9,13},{10,... | collective-permute-start | bytes 12296 | tf_op jit(solution)/shard_map/ppermute | solution.py:516
  11.7 1.2 collective-permute-start
  12.4 1.2 collective-permute-start.4
  21.2 26.6 %collective-permute-start.6 = (bf16[32,128,128]{2,1,0:T(8,128)(2,1)}, bf16[32,128,128]{2,1,0:T(8,128)(2,1)}, u32[]{:S(2)}, u32[]{:S(2)}) collective-permute-start(bf16[32,128,128]{2,1,0:T(8,128)(2,1)} %get-tuple-element.35), channel_id=1, source_target_pairs={{0,2},{1,3},{6,4},{7,5},{8,10},{9,11},{14,12},{15,13},{16,18},{17,... | collective-permute-start | bytes 3145736 | tf_op jit(solution)/shard_map/ppermute | solution.py:568
  25.9 21.9 %copy-start.13 = (bf16[32,128,128]{2,1,0:T(8,128)(2,1)S(1)}, bf16[32,128,128]{2,1,0:T(8,128)(2,1)}, u32[]{:S(2)}) copy-start(bf16[32,128,128]{2,1,0:T(8,128)(2,1)} %get-tuple-element.35) | copy-start | bytes 3145732
  26.0 24.5 %collective-permute-start.9 = (bf16[64,4608]{1,0:T(8,128)(2,1)S(1)}, bf16[64,4608]{1,0:T(8,128)(2,1)}, u32[]{:S(2)}, u32[]{:S(2)}) collective-permute-start(bf16[64,4608]{1,0:T(8,128)(2,1)S(1)} %constant_dynamic-slice_fusion), channel_id=1, source_target_pairs={{0,24},{8,16},{16,8},{24,0},{1,25},{9,17},{17,9},{25,1},{2,26},{10... | collective-permute-start | bytes 1769480 | tf_op jit(solution)/shard_map/ppermute | solution.py:516
  28.5 26.2 %collective-permute-start.8 = (bf16[64,4608]{1,0:T(8,128)(2,1)S(1)}, bf16[64,4608]{1,0:T(8,128)(2,1)}, u32[]{:S(2)}, u32[]{:S(2)}) collective-permute-start(bf16[64,4608]{1,0:T(8,128)(2,1)S(1)} %constant_dynamic-slice_fusion), channel_id=1, source_target_pairs={{0,16},{8,24},{16,0},{24,8},{1,17},{9,25},{17,1},{25,9},{2,18},{10... | collective-permute-start | bytes 1769480 | tf_op jit(solution)/shard_map/ppermute | solution.py:516
  29.0 25.8 %collective-permute-start.7 = (bf16[64,4608]{1,0:T(8,128)(2,1)S(1)}, bf16[64,4608]{1,0:T(8,128)(2,1)}, u32[]{:S(2)}, u32[]{:S(2)}) collective-permute-start(bf16[64,4608]{1,0:T(8,128)(2,1)S(1)} %constant_dynamic-slice_fusion), channel_id=1, source_target_pairs={{0,8},{8,0},{16,24},{24,16},{1,9},{9,1},{17,25},{25,17},{2,10},{10... | collective-permute-start | bytes 1769480 | tf_op jit(solution)/shard_map/ppermute | solution.py:516
  54.7 4.1 %collective-permute-start.10 = (bf16[64,4608]{1,0:T(8,128)(2,1)}, bf16[64,4608]{1,0:T(8,128)(2,1)S(1)}, u32[]{:S(2)}, u32[]{:S(2)}) collective-permute-start(bf16[64,4608]{1,0:T(8,128)(2,1)} %collective-permute-done.7.refs_0_.refs_1_), channel_id=1, source_target_pairs={{0,1},{1,0},{2,3},{3,2},{4,5},{5,4},{6,7},{7,6},{8,9},{9,8},{10,11... | collective-permute-start | bytes 1769480 | tf_op jit(solution)/shard_map/ppermute | solution.py:516
  54.8 4.1 %collective-permute-start.11 = (bf16[64,4608]{1,0:T(8,128)(2,1)}, bf16[64,4608]{1,0:T(8,128)(2,1)S(1)}, u32[]{:S(2)}, u32[]{:S(2)}) collective-permute-start(bf16[64,4608]{1,0:T(8,128)(2,1)} %collective-permute-done.8.refs_1_.refs_2_), channel_id=1, source_target_pairs={{0,1},{1,0},{2,3},{3,2},{4,5},{5,4},{6,7},{7,6},{8,9},{9,8},{10,11... | collective-permute-start | bytes 1769480 | tf_op jit(solution)/shard_map/ppermute | solution.py:516
  55.3 3.6 %collective-permute-start.12 = (bf16[64,4608]{1,0:T(8,128)(2,1)}, bf16[64,4608]{1,0:T(8,128)(2,1)S(1)}, u32[]{:S(2)}, u32[]{:S(2)}) collective-permute-start(bf16[64,4608]{1,0:T(8,128)(2,1)} %collective-permute-done.9.refs_2_.refs_0_), channel_id=1, source_target_pairs={{0,1},{1,0},{2,3},{3,2},{4,5},{5,4},{6,7},{7,6},{8,9},{9,8},{10,11... | collective-permute-start | bytes 1769480 | tf_op jit(solution)/shard_map/ppermute | solution.py:516
  55.3 25.1 %collective-permute-start.13 = (bf16[32,128,128]{2,1,0:T(8,128)(2,1)}, bf16[32,128,128]{2,1,0:T(8,128)(2,1)}, u32[]{:S(2)}, u32[]{:S(2)}) collective-permute-start(bf16[32,128,128]{2,1,0:T(8,128)(2,1)} %get-tuple-element.47.a_ref), channel_id=1, source_target_pairs={{0,2},{1,3},{6,4},{7,5},{8,10},{9,11},{14,12},{15,13},{16,18},{17,... | collective-permute-start | bytes 3145736 | tf_op jit(solution)/shard_map/ppermute | solution.py:568
  57.5 28.8 %collective-permute-start.14 = (bf16[32,128,128]{2,1,0:T(8,128)(2,1)}, bf16[32,128,128]{2,1,0:T(8,128)(2,1)}, u32[]{:S(2)}, u32[]{:S(2)}) collective-permute-start(bf16[32,128,128]{2,1,0:T(8,128)(2,1)} %add_convert_fusion), channel_id=1, source_target_pairs={{2,6},{3,7},{4,0},{5,1},{10,14},{11,15},{12,8},{13,9},{18,22},{19,... | collective-permute-start | bytes 3145736 | tf_op jit(solution)/shard_map/ppermute | solution.py:568
  69.0 29.4 %all-to-all-start = ((f32[4,128,1024]{2,1,0:T(8,128)}), f32[4,128,1024]{2,1,0:T(8,128)S(1)}, u32[]{:S(2)}, u32[]{:S(2)}) async-start(f32[4,128,1024]{2,1,0:T(8,128)} %student_logits.1), calls=%async_computation | async-start | bytes 4194304 | tf_op jit(solution)/shard_map/all_to_all | solution.py:564
  72.7 40.3 %collective-permute-start.19 = (bf16[32,128,128]{2,1,0:T(8,128)(2,1)}, bf16[32,128,128]{2,1,0:T(8,128)(2,1)}, u32[]{:S(2)}, u32[]{:S(2)}) collective-permute-start(bf16[32,128,128]{2,1,0:T(8,128)(2,1)} %get-tuple-element.55), channel_id=1, source_target_pairs={{0,2},{1,3},{2,0},{3,1},{4,6},{5,7},{6,4},{7,5},{8,10},{9,11},{10,... | collective-permute-start | bytes 3145736 | tf_op jit(solution)/shard_map/ppermute | solution.py:516
  86.3 26.7 %collective-permute-start.20 = (bf16[32,128,128]{2,1,0:T(8,128)(2,1)}, bf16[32,128,128]{2,1,0:T(8,128)(2,1)}, u32[]{:S(2)}, u32[]{:S(2)}) collective-permute-start(bf16[32,128,128]{2,1,0:T(8,128)(2,1)} %merge_sums.1), channel_id=1, source_target_pairs={{2,4},{3,5},{4,2},{5,3},{10,12},{11,13},{12,10},{13,11},{18,20},{1... | collective-permute-start | bytes 3145736 | tf_op jit(solution)/shard_map/ppermute | solution.py:568
  96.4 16.5 %copy-start.6 = (bf16[32,128,128]{2,1,0:T(8,128)(2,1)S(1)}, bf16[32,128,128]{2,1,0:T(8,128)(2,1)}, u32[]{:S(2)}) copy-start(bf16[32,128,128]{2,1,0:T(8,128)(2,1)} %get-tuple-element.54) | copy-start | bytes 3145732
  99.9 1.2 collective-permute-start.15
  101.1 6.1 %collective-permute-start.18 = (f32[8,128]{1,0:T(8,128)S(1)}, f32[8,128]{1,0:T(8,128)S(1)}, u32[]{:S(2)}, u32[]{:S(2)}) collective-permute-start(f32[8,128]{1,0:T(8,128)S(1)} %merge_stats.5.refs_0_), channel_id=1, source_target_pairs={{0,6},{1,7},{2,4},{3,5},{4,2},{5,3},{6,0},{7,1},{8,14},{9,15},{10,... | collective-permute-start | bytes 12296 | tf_op jit(solution)/shard_map/ppermute | solution.py:516
  103.9 8.9 %collective-permute-start.17 = (f32[8,128]{1,0:T(8,128)S(1)}, f32[8,128]{1,0:T(8,128)S(1)}, u32[]{:S(2)}, u32[]{:S(2)}) collective-permute-start(f32[8,128]{1,0:T(8,128)S(1)} %merge_stats.5.refs_0_), channel_id=1, source_target_pairs={{0,4},{1,5},{2,6},{3,7},{4,0},{5,1},{6,2},{7,3},{8,12},{9,13},{10,... | collective-permute-start | bytes 12296 | tf_op jit(solution)/shard_map/ppermute | solution.py:516
  107.2 5.6 %collective-permute-start.16 = (f32[8,128]{1,0:T(8,128)S(1)}, f32[8,128]{1,0:T(8,128)S(1)}, u32[]{:S(2)}, u32[]{:S(2)}) collective-permute-start(f32[8,128]{1,0:T(8,128)S(1)} %merge_stats.5.refs_0_), channel_id=1, source_target_pairs={{0,2},{1,3},{2,0},{3,1},{4,6},{5,7},{6,4},{7,5},{8,10},{9,11},{10,... | collective-permute-start | bytes 12296 | tf_op jit(solution)/shard_map/ppermute | solution.py:516
  112.8 11.9 %slice-start = ((s8[4718592]{0:T(1024)(128)(4,1)}), s8[4194304]{0:T(1024)(128)(4,1)S(1)}, s32[]{:S(2)}) async-start(s8[4718592]{0:T(1024)(128)(4,1)} %bitcast.13), calls=%async_computation.1 | async-start | bytes 8388608
  115.4 9.3 %collective-permute-start.23 = (bf16[128,1024]{1,0:T(8,128)(2,1)}, bf16[128,1024]{1,0:T(8,128)(2,1)S(1)}, u32[]{:S(2)}, u32[]{:S(2)}) collective-permute-start(bf16[128,1024]{1,0:T(8,128)(2,1)} %get-tuple-element.61), channel_id=1, source_target_pairs={{0,24},{8,16},{16,8},{24,0},{1,25},{9,17},{17,9},{25,1},{2,26},{10... | collective-permute-start | bytes 786440 | tf_op jit(solution)/shard_map/ppermute | solution.py:516
  121.1 9.8 %collective-permute-start.25 = (bf16[128,1024]{1,0:T(8,128)(2,1)}, bf16[128,1024]{1,0:T(8,128)(2,1)S(1)}, u32[]{:S(2)}, u32[]{:S(2)}) collective-permute-start(bf16[128,1024]{1,0:T(8,128)(2,1)} %get-tuple-element.64), channel_id=1, source_target_pairs={{0,8},{8,0},{16,24},{24,16},{1,9},{9,1},{17,25},{25,17},{2,10},{10... | collective-permute-start | bytes 786440 | tf_op jit(solution)/shard_map/ppermute | solution.py:516
  122.4 8.6 %collective-permute-start.26 = (bf16[128,1024]{1,0:T(8,128)(2,1)}, bf16[128,1024]{1,0:T(8,128)(2,1)S(1)}, u32[]{:S(2)}, u32[]{:S(2)}) collective-permute-start(bf16[128,1024]{1,0:T(8,128)(2,1)} %get-tuple-element.65), channel_id=1, source_target_pairs={{0,16},{8,24},{16,0},{24,8},{1,17},{9,25},{17,1},{25,9},{2,18},{10... | collective-permute-start | bytes 786440 | tf_op jit(solution)/shard_map/ppermute | solution.py:516
  123.0 1.1 collective-permute-start.21
  124.1 4.8 %collective-permute-start.22 = (f32[1,128]{1,0:T(1,128)S(1)}, f32[1,128]{1,0:T(1,128)S(1)}, u32[]{:S(2)}, u32[]{:S(2)}) collective-permute-start(f32[1,128]{1,0:T(1,128)S(1)} %add.84), channel_id=1, source_target_pairs={{0,2},{1,3},{2,0},{3,1},{4,6},{5,7},{6,4},{7,5},{8,10},{9,11},{10,... | collective-permute-start | bytes 1544 | tf_op jit(solution)/shard_map/ppermute | solution.py:516
  128.9 7.4 %collective-permute-start.24 = (f32[1,128]{1,0:T(1,128)S(1)}, f32[1,128]{1,0:T(1,128)S(1)}, u32[]{:S(2)}, u32[]{:S(2)}) collective-permute-start(f32[1,128]{1,0:T(1,128)S(1)} %add_add_fusion), channel_id=1, source_target_pairs={{0,4},{1,5},{2,6},{3,7},{4,0},{5,1},{6,2},{7,3},{8,12},{9,13},{10,... | collective-permute-start | bytes 1544 | tf_op jit(solution)/shard_map/ppermute | solution.py:516
  (12 other events, 67.2 us)

commit v9 on v7

--- a/solution.py
+++ b/solution.py
@@ -598,8 +598,7 @@
         first, mass = lax.optimization_barrier((first, mass_a + mass_b))
         merged = plus(far_outer, first)
         arrived = send(merged, beyond)
-        *near, waited, merged = lax.optimization_barrier((*near, beside, merged))
-        third = swap(waited, "vocab", 2)
+        *near, merged = lax.optimization_barrier((*near, merged))
     else:
         sums, mass = chip_sums(spot, lists, probs, map_weight, peer_weight, 0, 1, n_z, slots)
         lines = [[2 * z + c for z in range(n_z)] for c in range(2)]
@@ -624,6 +623,8 @@
         second, arrived, logits = lax.optimization_barrier((second, arrived, logits))
         merged_inner = plus(far_inner, second)
         crossed = send(merged_inner, across)
+        waited, merged_inner = lax.optimization_barrier((beside, merged_inner))
+        third = swap(waited, "vocab", 2)
         where, merged_inner = lax.optimization_barrier((where, merged_inner))
         turned = turned_rows(where, hidden, near[-1:] + near[:-1], far[-1:] + far[:-1])
         scores, merged_inner, turned = lax.optimization_barrier((scores, merged_inner, turned))

time: 133 us -> 134 us (level)
  waiting for transfers between devices: 28.3 us -> 34.2 us
  starting transfers between devices: 39.4 us -> 35.6 us
    ppermute x4, waiting for transfers between devices: 8.67 us -> 13.3 us  [send(): lax.ppermute(x, 'vocab', [(2 * a + c, 2 * b + c) for a, b in hops for c i...]
    ppermute x23, starting transfers between devices: 25.4 us -> 21.6 us  [swap(): lax.ppermute(x, axis, [(i, i ^ mask) for i in range(lax.axis_size(axis))])]
    ppermute x23, waiting for transfers between devices: 13.5 us -> 15.4 us  [swap(): lax.ppermute(x, axis, [(i, i ^ mask) for i in range(lax.axis_size(axis))])]
  transfers between devices with their start and end apart: 28 -> 28, of which waited for: 17 -> 16; matrix products, arithmetic and copies ran while one was open for 5% -> 5% of each run, Pallas kernels for 32% -> 32%
where the time goes in v9:
time: 134 us
  Pallas kernels  48.9 us (36%)
  starting transfers between devices  35.6 us (27%)
  waiting for transfers between devices  34.2 us (26%)
  local copies, waits for them, and re-layouts  7.18 us (5%)
  other arithmetic  6.96 us (5%)
    ppermute x23, starting transfers between devices, swap(): lax.ppermute(x, axis, [(i, i ^ mask) for i in range(lax.axis_size(axis))])  21.6 us
    ppermute x23, waiting for transfers between devices, swap(): lax.ppermute(x, axis, [(i, i ^ mask) for i in range(lax.axis_size(axis))])  15.4 us
    ppermute x4, waiting for transfers between devices, send(): lax.ppermute(x, 'vocab', [(2 * a + c, 2 * b + c) for a, b in hops for c i...  13.3 us
    pallas_call x2, Pallas kernels, chip_sums(): pl.pallas_call(functools.partial(sums_kernel, first=first, fan=fan, piece...  12.4 us
    ppermute x4, starting transfers between devices, send(): lax.ppermute(x, 'vocab', [(2 * a + c, 2 * b + c) for a, b in hops for c i...  10.4 us
    pallas_call x1, Pallas kernels, student_logits(): pl.pallas_call(logits_kernel, grid=(cols // tile,), in_specs=[SMEM_SPEC,...  9.69 us
    unnamed x32, local copies, waits for them, and re-layouts  6.66 us
    pallas_call x2, Pallas kernels, grad_logits(): pl.pallas_call(functools.partial(grad_kernel, n_sums=len(sums), groups=gr...  6.5 us
  transfers between devices with their start and end apart: 28, of which 16 were waited for; matrix products, arithmetic and copies ran while one was open for 5% of the time, Pallas kernels for 32%

profile of v9, /device:TPU:0, one launch (start us, length us, event | category | flops | bytes accessed | tf_op | source)
XLA Modules:
  0.0 133.8 jit_solution(5705955855371069838)
XLA Ops:
  3.1 3.0 %collective-permute-start.2 = (f32[8,128]{1,0:T(8,128)S(1)}, f32[8,128]{1,0:T(8,128)S(1)}, u32[]{:S(2)}, u32[]{:S(2)}) collective-permute-start(f32[8,128]{1,0:T(8,128)S(1)} %teacher_stats.1.refs_0_), channel_id=1, source_target_pairs={{0,2},{1,3},{2,0},{3,1},{4,6},{5,7},{6,4},{7,5},{8,10},{9,11},{10,... | collective-permute-start | bytes 12296 | tf_op jit(solution)/shard_map/ppermute | solution.py:516
  6.1 1.6 %collective-permute-done.2.refs_1_ = f32[8,128]{1,0:T(8,128)S(1)} collective-permute-done((f32[8,128]{1,0:T(8,128)S(1)}, f32[8,128]{1,0:T(8,128)S(1)}, u32[]{:S(2)}, u32[]{:S(2)}) %collective-permute-start.2) | collective-permute-done | bytes 4128 | tf_op jit(solution)/shard_map/ppermute | solution.py:516
  7.7 3.1 %collective-permute-start.3 = (f32[8,128]{1,0:T(8,128)S(1)}, f32[8,128]{1,0:T(8,128)S(1)}, u32[]{:S(2)}, u32[]{:S(2)}) collective-permute-start(f32[8,128]{1,0:T(8,128)S(1)} %merge_stats.3.refs_0_), channel_id=1, source_target_pairs={{0,4},{1,5},{2,6},{3,7},{4,0},{5,1},{6,2},{7,3},{8,12},{9,13},{10,... | collective-permute-start | bytes 12296 | tf_op jit(solution)/shard_map/ppermute | solution.py:516
  13.6 3.3 %teacher_probs.1 = bf16[2,32,128,128]{3,2,1,0:T(8,128)(2,1)S(1)} custom-call(bf16[128,4096]{1,0:T(8,128)(2,1)} %x_own.1, bf16[128,4096]{1,0:T(8,128)(2,1)S(1)} %collective-permute-done.1.x_peer, f32[8,128]{1,0:T(8,128)S(1)} %merge_stats.4.refs_0_, f32[8,128]{1,0:T(8,128)S(1)} %collective-permute-done.4.refs_1_), custom_call_target="tpu_custom_call" | custom-call | flops 1024 | bytes 1024 | tf_op jit(solution)/shard_map/teacher_probs/pallas_call | solution.py:203
  16.9 4.3 %chip_sums.2 = (bf16[32,128,128]{2,1,0:T(8,128)(2,1)}, f32[8,128]{1,0:T(8,128)S(1)}) custom-call(s32[2]{0:T(128)S(1)} %pad_add_fusion.spot_ref, s32[8,384]{1,0:T(8,128)S(1)} %entry_lists.1.list_ref, bf16[64,128,128]{2,1,0:T(8,128)(2,1)S(1)} %bitcast.15, bf16[32,4,128,128]{3,2,1,0:T(8,128)(2,1)S(1)} %copy-done.2, ...), custom_call_target="tpu_custom_call" | custom-call | flops 1024 | bytes 1024 | tf_op jit(solution)/shard_map/chip_sums/pallas_call | solution.py:222
  21.2 5.2 %collective-permute-start.6 = (bf16[32,128,128]{2,1,0:T(8,128)(2,1)}, bf16[32,128,128]{2,1,0:T(8,128)(2,1)}, u32[]{:S(2)}, u32[]{:S(2)}) collective-permute-start(bf16[32,128,128]{2,1,0:T(8,128)(2,1)} %get-tuple-element.33), channel_id=1, source_target_pairs={{0,2},{1,3},{6,4},{7,5},{8,10},{9,11},{14,12},{15,13},{16,18},{17,... | collective-permute-start | bytes 3145736 | tf_op jit(solution)/shard_map/ppermute | solution.py:550
  26.5 2.5 %collective-permute-start.9 = (bf16[64,4608]{1,0:T(8,128)(2,1)S(1)}, bf16[64,4608]{1,0:T(8,128)(2,1)}, u32[]{:S(2)}, u32[]{:S(2)}) collective-permute-start(bf16[64,4608]{1,0:T(8,128)(2,1)S(1)} %constant_dynamic-slice_fusion), channel_id=1, source_target_pairs={{0,24},{8,16},{16,8},{24,0},{1,25},{9,17},{17,9},{25,1},{2,26},{10... | collective-permute-start | bytes 1769480 | tf_op jit(solution)/shard_map/ppermute | solution.py:516
  30.0 2.2 %copy-done.3 = bf16[32,4,128,128]{3,2,1,0:T(8,128)(2,1)S(1)} copy-done((bf16[32,4,128,128]{3,2,1,0:T(8,128)(2,1)S(1)}, bf16[32,4,128,128]{3,2,1,0:T(8,128)(2,1)}, u32[]{:S(2)}) %copy-start.3) | copy-done | bytes 4194328
  32.2 8.1 %chip_sums.3 = (bf16[32,128,128]{2,1,0:T(8,128)(2,1)}, bf16[32,128,128]{2,1,0:T(8,128)(2,1)}, bf16[32,128,128]{2,1,0:T(8,128)(2,1)}, f32[8,128]{1,0:T(8,128)S(1)}) custom-call(s32[2]{0:T(128)S(1)} %pad_add_fusion.spot_ref, s32[8,384]{1,0:T(8,128)S(1)} %entry_lists.1.list_ref, bf16[64,128,128]{2,1,0:T(8,128)(2,1)S(1)} %bitcast.16, ...), custom_call_target="tpu_custom_call" | custom-call | flops 1024 | bytes 1024 | tf_op jit(solution)/shard_map/chip_sums/pallas_call | solution.py:222
  40.4 2.3 %collective-permute-start.17 = (bf16[32,128,128]{2,1,0:T(8,128)(2,1)}, bf16[32,128,128]{2,1,0:T(8,128)(2,1)}, u32[]{:S(2)}, u32[]{:S(2)}) collective-permute-start(bf16[32,128,128]{2,1,0:T(8,128)(2,1)} %get-tuple-element.49), channel_id=1, source_target_pairs={{0,2},{1,3},{6,4},{7,5},{8,10},{9,11},{14,12},{15,13},{16,18},{17,... | collective-permute-start | bytes 3145736 | tf_op jit(solution)/shard_map/ppermute | solution.py:550
  42.7 6.6 %collective-permute-done.6 = bf16[32,128,128]{2,1,0:T(8,128)(2,1)} collective-permute-done((bf16[32,128,128]{2,1,0:T(8,128)(2,1)}, bf16[32,128,128]{2,1,0:T(8,128)(2,1)}, u32[]{:S(2)}, u32[]{:S(2)}) %collective-permute-start.6) | collective-permute-done | bytes 1048608 | tf_op jit(solution)/shard_map/ppermute | solution.py:550
  49.2 2.5 %add_convert_fusion.1 = bf16[32,128,128]{2,1,0:T(8,128)(2,1)} fusion(bf16[32,128,128]{2,1,0:T(8,128)(2,1)} %collective-permute-done.6, bf16[32,128,128]{2,1,0:T(8,128)(2,1)S(1)} %copy-done.13), kind=kLoop, calls=%fused_computation.1 | loop fusion | flops 2097152 | bytes 3145728 | tf_op jit(solution)/shard_map/convert_element_type | solution.py:542
  51.7 1.3 collective-permute-start.18
  53.0 2.4 %collective-permute-done.8.refs_1_.refs_2_ = bf16[64,4608]{1,0:T(8,128)(2,1)} collective-permute-done((bf16[64,4608]{1,0:T(8,128)(2,1)S(1)}, bf16[64,4608]{1,0:T(8,128)(2,1)}, u32[]{:S(2)}, u32[]{:S(2)}) %collective-permute-start.8) | collective-permute-done | bytes 589856 | tf_op jit(solution)/shard_map/ppermute | solution.py:516
  56.1 1.6 %collective-permute-done.10.refs_3_.refs_4_ = bf16[64,4608]{1,0:T(8,128)(2,1)S(1)} collective-permute-done((bf16[64,4608]{1,0:T(8,128)(2,1)}, bf16[64,4608]{1,0:T(8,128)(2,1)S(1)}, u32[]{:S(2)}, u32[]{:S(2)}) %collective-permute-start.10) | collective-permute-done | bytes 589856 | tf_op jit(solution)/shard_map/ppermute | solution.py:516
  59.4 9.7 %student_logits.1 = f32[4,128,1024]{2,1,0:T(8,128)} custom-call(s32[2]{0:T(128)S(1)} %pad_add_fusion.1.place_ref, f32[8,128]{1,0:T(8,128)S(1)} %add.84.after_ref.mass_ref, bf16[128,4608]{1,0:T(8,128)(2,1)S(1)} %copy-done.4, bf16[64,4608]{1,0:T(8,128)(2,1)} %collective-permute-done.7.refs_0_.refs_1_, bf16[64,4608]{1,0:T(8,128)(2,1)} %collective-permute-done.8.refs_1_.refs_2_, ...), custom_call_target="tpu_custom_call" | custom-call | flops 1024 | bytes 1024 | tf_op jit(solution)/shard_map/student_logits/pallas_call | solution.py:293
  69.1 3.6 %all-to-all-start = ((f32[4,128,1024]{2,1,0:T(8,128)}), f32[4,128,1024]{2,1,0:T(8,128)S(1)}, u32[]{:S(2)}, u32[]{:S(2)}) async-start(f32[4,128,1024]{2,1,0:T(8,128)} %student_logits.1), calls=%async_computation | async-start | bytes 4194304 | tf_op jit(solution)/shard_map/all_to_all | solution.py:546
  72.8 6.7 %collective-permute-done.18 = bf16[32,128,128]{2,1,0:T(8,128)(2,1)} collective-permute-done((bf16[32,128,128]{2,1,0:T(8,128)(2,1)}, bf16[32,128,128]{2,1,0:T(8,128)(2,1)}, u32[]{:S(2)}, u32[]{:S(2)}) %collective-permute-start.18) | collective-permute-done | bytes 1048608 | tf_op jit(solution)/shard_map/ppermute | solution.py:550
  79.5 3.0 %add_convert_fusion = bf16[32,128,128]{2,1,0:T(8,128)(2,1)} fusion(bf16[32,128,128]{2,1,0:T(8,128)(2,1)} %collective-permute-done.17, bf16[32,128,128]{2,1,0:T(8,128)(2,1)} %get-tuple-element.49), kind=kLoop, calls=%fused_computation | loop fusion | flops 2097152 | bytes 3145728 | tf_op jit(solution)/shard_map/convert_element_type | solution.py:542
  82.5 1.6 %collective-permute-start.20 = (bf16[32,128,128]{2,1,0:T(8,128)(2,1)}, bf16[32,128,128]{2,1,0:T(8,128)(2,1)}, u32[]{:S(2)}, u32[]{:S(2)}) collective-permute-start(bf16[32,128,128]{2,1,0:T(8,128)(2,1)} %add_convert_fusion), channel_id=1, source_target_pairs={{2,4},{3,5},{4,2},{5,3},{10,12},{11,13},{12,10},{13,11},{18,20},{1... | collective-permute-start | bytes 3145736 | tf_op jit(solution)/shard_map/ppermute | solution.py:550
  87.5 5.1 %turned_rows.1.a_ref = bf16[4608,512]{1,0:T(8,128)(2,1)} custom-call(s32[2]{0:T(128)S(1)} %pad_add_fusion.1.place_ref, bf16[128,4608]{1,0:T(8,128)(2,1)S(1)} %copy-done.4, bf16[64,4608]{1,0:T(8,128)(2,1)} %collective-permute-done.9.refs_2_.refs_0_, bf16[64,4608]{1,0:T(8,128)(2,1)} %collective-permute-done.7.refs_0_.refs_1_, ...), custom_call_target="tpu_custom_call" | custom-call | flops 1024 | bytes 1024 | tf_op jit(solution)/shard_map/turned_rows/pallas_call | solution.py:273
  92.7 5.5 %all-to-all-done.logits_ref.refs_4_ = f32[4,128,1024]{2,1,0:T(8,128)S(1)} async-done(((f32[4,128,1024]{2,1,0:T(8,128)}), f32[4,128,1024]{2,1,0:T(8,128)S(1)}, u32[]{:S(2)}, u32[]{:S(2)}) %all-to-all-start) | async-done | bytes 2097184 | tf_op jit(solution)/shard_map/all_to_all | solution.py:546
  98.2 1.5 %student_stats.1.refs_0_ = f32[8,128]{1,0:T(8,128)S(1)} custom-call(s32[4]{0:T(128)S(1)} %add_multiply_fusion.base_ref, s32[128,1]{1,0:T(8,128)S(1)} %copy.15.labels_ref, f32[8,128]{1,0:T(8,128)S(1)} %add.84.after_ref.mass_ref, f32[4,128,1024]{2,1,0:T(8,128)S(1)} %all-to-all-done.logits_ref.refs_4_), custom_call_target="tpu_custom_call" | custom-call | flops 1024 | bytes 1024 | tf_op jit(solution)/shard_map/student_stats/pallas_call | solution.py:331
  100.8 2.8 %collective-permute-start.16 = (f32[8,128]{1,0:T(8,128)S(1)}, f32[8,128]{1,0:T(8,128)S(1)}, u32[]{:S(2)}, u32[]{:S(2)}) collective-permute-start(f32[8,128]{1,0:T(8,128)S(1)} %merge_stats.5.refs_0_), channel_id=1, source_target_pairs={{0,6},{1,7},{2,4},{3,5},{4,2},{5,3},{6,0},{7,1},{8,14},{9,15},{10,... | collective-permute-start | bytes 12296 | tf_op jit(solution)/shard_map/ppermute | solution.py:516
  105.3 1.7 %collective-permute-done.16.refs_3_ = f32[8,128]{1,0:T(8,128)S(1)} collective-permute-done((f32[8,128]{1,0:T(8,128)S(1)}, f32[8,128]{1,0:T(8,128)S(1)}, u32[]{:S(2)}, u32[]{:S(2)}) %collective-permute-start.16) | collective-permute-done | bytes 4128 | tf_op jit(solution)/shard_map/ppermute | solution.py:516
  107.0 2.9 %collective-permute-done.15.refs_2_ = f32[8,128]{1,0:T(8,128)S(1)} collective-permute-done((f32[8,128]{1,0:T(8,128)S(1)}, f32[8,128]{1,0:T(8,128)S(1)}, u32[]{:S(2)}, u32[]{:S(2)}) %collective-permute-start.15) | collective-permute-done | bytes 4128 | tf_op jit(solution)/shard_map/ppermute | solution.py:516
  110.0 2.4 %grad_logits.2 = (bf16[128,1024]{1,0:T(8,128)(2,1)}, f32[1,128]{1,0:T(1,128)S(1)}) custom-call(s32[1]{0:T(128)} %bitcast.5.tok_ref, s32[4]{0:T(128)S(1)} %add_multiply_fusion.base_ref, s32[128,1]{1,0:T(8,128)S(1)} %copy.15.labels_ref, f32[128,128]{1,0:T(8,128)S(1)} %get-tuple-element.46.columns, bf16[1,32,128,128]{3,2,1,0:T(8,128)(2,1)S(1)} %bitcast.17, ...), custom_call_target="tpu_custom_call" | custom-call | flops 1024 | bytes 1024 | tf_op jit(solution)/shard_map/grad_logits/pallas_call | solution.py:434
  112.5 2.4 %collective-permute-start.23 = (bf16[128,1024]{1,0:T(8,128)(2,1)}, bf16[128,1024]{1,0:T(8,128)(2,1)S(1)}, u32[]{:S(2)}, u32[]{:S(2)}) collective-permute-start(bf16[128,1024]{1,0:T(8,128)(2,1)} %get-tuple-element.57), channel_id=1, source_target_pairs={{0,24},{8,16},{16,8},{24,0},{1,25},{9,17},{17,9},{25,1},{2,26},{10... | collective-permute-start | bytes 786440 | tf_op jit(solution)/shard_map/ppermute | solution.py:516
  114.9 4.1 %grad_logits.3 = (bf16[128,1024]{1,0:T(8,128)(2,1)}, bf16[128,1024]{1,0:T(8,128)(2,1)}, bf16[128,1024]{1,0:T(8,128)(2,1)}, f32[1,128]{1,0:T(1,128)S(1)}) custom-call(s32[1]{0:T(128)} %bitcast.5.tok_ref, s32[4]{0:T(128)S(1)} %add_multiply_fusion.base_ref, s32[128,1]{1,0:T(8,128)S(1)} %copy.15.labels_ref, f32[128,128]{1,0:T(8,128)S(1)} %get-tuple-element.46.columns, ...), custom_call_target="tpu_custom_call" | custom-call | flops 1024 | bytes 1024 | tf_op jit(solution)/shard_map/grad_logits/pallas_call | solution.py:434
  121.8 4.1 %first_product.1 = (f32[4608,1024]{1,0:T(8,128)S(1)}, f32[1,128]{1,0:T(1,128)S(1)}) custom-call(bf16[4608,512]{1,0:T(8,128)(2,1)S(1)} %bitcast.14, bf16[128,1024]{1,0:T(8,128)(2,1)} %get-tuple-element.56.refs_0_, bf16[128,1024]{1,0:T(8,128)(2,1)S(1)} %collective-permute-done.23.refs_1_), custom_call_target="tpu_custom_call" | custom-call | flops 1024 | bytes 1024 | tf_op jit(solution)/shard_map/first_product/pallas_call | solution.py:485
  125.9 2.1 %collective-permute-start.24 = (f32[1,128]{1,0:T(1,128)S(1)}, f32[1,128]{1,0:T(1,128)S(1)}, u32[]{:S(2)}, u32[]{:S(2)}) collective-permute-start(f32[1,128]{1,0:T(1,128)S(1)} %add_add_fusion), channel_id=1, source_target_pairs={{0,4},{1,5},{2,6},{3,7},{4,0},{5,1},{6,2},{7,3},{8,12},{9,13},{10,... | collective-permute-start | bytes 1544 | tf_op jit(solution)/shard_map/ppermute | solution.py:516
  128.0 5.2 %last_product.1 = (bf16[4608,1024]{1,0:T(8,128)(2,1)}, f32[1,128]{1,0:T(1,128)S(1)}) custom-call(bf16[4608,512]{1,0:T(8,128)(2,1)S(1)} %bitcast.14, f32[4608,1024]{1,0:T(8,128)S(1)} %get-tuple-element.59.acc_ref, bf16[128,1024]{1,0:T(8,128)(2,1)S(1)} %collective-permute-done.25.refs_0_, bf16[128,1024]{1,0:T(8,128)(2,1)S(1)} %collective-permute-done.26.refs_1_), custom_call_target="tpu_custom_call" | custom-call | flops 1024 | bytes 1024 | tf_op jit(solution)/shard_map/last_product/pallas_call | solution.py:502
  (90 shorter events, 18.4 us)
Async XLA Ops:
  0.6 83.5 %copy-start = (s32[512]{0:T(512)S(1)}, s32[512]{0:T(512)}, u32[]{:S(2)}) copy-start(s32[512]{0:T(512)} %param.9) | copy-start | bytes 6148
  0.6 16.3 %collective-permute-start.5 = (bf16[32,4,128,128]{3,2,1,0:T(8,128)(2,1)}, bf16[32,4,128,128]{3,2,1,0:T(8,128)(2,1)}, u32[]{:S(2)}, u32[]{:S(2)}) collective-permute-start(bf16[32,4,128,128]{3,2,1,0:T(8,128)(2,1)} %w_own.3), channel_id=1, source_target_pairs={{0,1},{1,0},{2,3},{3,2},{4,5},{5,4},{6,7},{7,6},{8,9},{9,8},{10,11... | collective-permute-start | bytes 12582920 | tf_op jit(solution)/shard_map/ppermute | solution.py:516
  1.2 12.5 %collective-permute-start.1 = (bf16[128,4096]{1,0:T(8,128)(2,1)}, bf16[128,4096]{1,0:T(8,128)(2,1)S(1)}, u32[]{:S(2)}, u32[]{:S(2)}) collective-permute-start(bf16[128,4096]{1,0:T(8,128)(2,1)} %x_own.1), channel_id=1, source_target_pairs={{0,1},{1,0},{2,3},{3,2},{4,5},{5,4},{6,7},{7,6},{8,9},{9,8},{10,11... | collective-permute-start | bytes 3145736 | tf_op jit(solution)/shard_map/ppermute | solution.py:516
  3.1 4.6 %collective-permute-start.2 = (f32[8,128]{1,0:T(8,128)S(1)}, f32[8,128]{1,0:T(8,128)S(1)}, u32[]{:S(2)}, u32[]{:S(2)}) collective-permute-start(f32[8,128]{1,0:T(8,128)S(1)} %teacher_stats.1.refs_0_), channel_id=1, source_target_pairs={{0,2},{1,3},{2,0},{3,1},{4,6},{5,7},{6,4},{7,5},{8,10},{9,11},{10,... | collective-permute-start | bytes 12296 | tf_op jit(solution)/shard_map/ppermute | solution.py:516
  7.7 4.7 %collective-permute-start.3 = (f32[8,128]{1,0:T(8,128)S(1)}, f32[8,128]{1,0:T(8,128)S(1)}, u32[]{:S(2)}, u32[]{:S(2)}) collective-permute-start(f32[8,128]{1,0:T(8,128)S(1)} %merge_stats.3.refs_0_), channel_id=1, source_target_pairs={{0,4},{1,5},{2,6},{3,7},{4,0},{5,1},{6,2},{7,3},{8,12},{9,13},{10,... | collective-permute-start | bytes 12296 | tf_op jit(solution)/shard_map/ppermute | solution.py:516
  11.7 1.2 collective-permute-start
  12.4 1.2 collective-permute-start.4
  21.2 28.0 %collective-permute-start.6 = (bf16[32,128,128]{2,1,0:T(8,128)(2,1)}, bf16[32,128,128]{2,1,0:T(8,128)(2,1)}, u32[]{:S(2)}, u32[]{:S(2)}) collective-permute-start(bf16[32,128,128]{2,1,0:T(8,128)(2,1)} %get-tuple-element.33), channel_id=1, source_target_pairs={{0,2},{1,3},{6,4},{7,5},{8,10},{9,11},{14,12},{15,13},{16,18},{17,... | collective-permute-start | bytes 3145736 | tf_op jit(solution)/shard_map/ppermute | solution.py:550
  26.4 22.8 %copy-start.13 = (bf16[32,128,128]{2,1,0:T(8,128)(2,1)S(1)}, bf16[32,128,128]{2,1,0:T(8,128)(2,1)}, u32[]{:S(2)}) copy-start(bf16[32,128,128]{2,1,0:T(8,128)(2,1)} %get-tuple-element.33) | copy-start | bytes 3145732
  26.5 26.5 %collective-permute-start.9 = (bf16[64,4608]{1,0:T(8,128)(2,1)S(1)}, bf16[64,4608]{1,0:T(8,128)(2,1)}, u32[]{:S(2)}, u32[]{:S(2)}) collective-permute-start(bf16[64,4608]{1,0:T(8,128)(2,1)S(1)} %constant_dynamic-slice_fusion), channel_id=1, source_target_pairs={{0,24},{8,16},{16,8},{24,0},{1,25},{9,17},{17,9},{25,1},{2,26},{10... | collective-permute-start | bytes 1769480 | tf_op jit(solution)/shard_map/ppermute | solution.py:516
  29.0 26.4 %collective-permute-start.8 = (bf16[64,4608]{1,0:T(8,128)(2,1)S(1)}, bf16[64,4608]{1,0:T(8,128)(2,1)}, u32[]{:S(2)}, u32[]{:S(2)}) collective-permute-start(bf16[64,4608]{1,0:T(8,128)(2,1)S(1)} %constant_dynamic-slice_fusion), channel_id=1, source_target_pairs={{0,16},{8,24},{16,0},{24,8},{1,17},{9,25},{17,1},{25,9},{2,18},{10... | collective-permute-start | bytes 1769480 | tf_op jit(solution)/shard_map/ppermute | solution.py:516
  29.5 26.0 %collective-permute-start.7 = (bf16[64,4608]{1,0:T(8,128)(2,1)S(1)}, bf16[64,4608]{1,0:T(8,128)(2,1)}, u32[]{:S(2)}, u32[]{:S(2)}) collective-permute-start(bf16[64,4608]{1,0:T(8,128)(2,1)S(1)} %constant_dynamic-slice_fusion), channel_id=1, source_target_pairs={{0,8},{8,0},{16,24},{24,16},{1,9},{9,1},{17,25},{25,17},{2,10},{10... | collective-permute-start | bytes 1769480 | tf_op jit(solution)/shard_map/ppermute | solution.py:516
  40.4 32.4 %collective-permute-start.17 = (bf16[32,128,128]{2,1,0:T(8,128)(2,1)}, bf16[32,128,128]{2,1,0:T(8,128)(2,1)}, u32[]{:S(2)}, u32[]{:S(2)}) collective-permute-start(bf16[32,128,128]{2,1,0:T(8,128)(2,1)} %get-tuple-element.49), channel_id=1, source_target_pairs={{0,2},{1,3},{6,4},{7,5},{8,10},{9,11},{14,12},{15,13},{16,18},{17,... | collective-permute-start | bytes 3145736 | tf_op jit(solution)/shard_map/ppermute | solution.py:550
  51.7 27.7 %collective-permute-start.18 = (bf16[32,128,128]{2,1,0:T(8,128)(2,1)}, bf16[32,128,128]{2,1,0:T(8,128)(2,1)}, u32[]{:S(2)}, u32[]{:S(2)}) collective-permute-start(bf16[32,128,128]{2,1,0:T(8,128)(2,1)} %add_convert_fusion.1), channel_id=1, source_target_pairs={{2,6},{3,7},{4,0},{5,1},{10,14},{11,15},{12,8},{13,9},{18,22},{19,... | collective-permute-start | bytes 3145736 | tf_op jit(solution)/shard_map/ppermute | solution.py:550
  55.5 2.2 %collective-permute-start.10 = (bf16[64,4608]{1,0:T(8,128)(2,1)}, bf16[64,4608]{1,0:T(8,128)(2,1)S(1)}, u32[]{:S(2)}, u32[]{:S(2)}) collective-permute-start(bf16[64,4608]{1,0:T(8,128)(2,1)} %collective-permute-done.7.refs_0_.refs_1_), channel_id=1, source_target_pairs={{0,1},{1,0},{2,3},{3,2},{4,5},{5,4},{6,7},{7,6},{8,9},{9,8},{10,11... | collective-permute-start | bytes 1769480 | tf_op jit(solution)/shard_map/ppermute | solution.py:516
  55.5 3.1 %collective-permute-start.11 = (bf16[64,4608]{1,0:T(8,128)(2,1)}, bf16[64,4608]{1,0:T(8,128)(2,1)S(1)}, u32[]{:S(2)}, u32[]{:S(2)}) collective-permute-start(bf16[64,4608]{1,0:T(8,128)(2,1)} %collective-permute-done.8.refs_1_.refs_2_), channel_id=1, source_target_pairs={{0,1},{1,0},{2,3},{3,2},{4,5},{5,4},{6,7},{7,6},{8,9},{9,8},{10,11... | collective-permute-start | bytes 1769480 | tf_op jit(solution)/shard_map/ppermute | solution.py:516
  56.0 3.4 %collective-permute-start.12 = (bf16[64,4608]{1,0:T(8,128)(2,1)}, bf16[64,4608]{1,0:T(8,128)(2,1)S(1)}, u32[]{:S(2)}, u32[]{:S(2)}) collective-permute-start(bf16[64,4608]{1,0:T(8,128)(2,1)} %collective-permute-done.9.refs_2_.refs_0_), channel_id=1, source_target_pairs={{0,1},{1,0},{2,3},{3,2},{4,5},{5,4},{6,7},{7,6},{8,9},{9,8},{10,11... | collective-permute-start | bytes 1769480 | tf_op jit(solution)/shard_map/ppermute | solution.py:516
  69.1 29.0 %all-to-all-start = ((f32[4,128,1024]{2,1,0:T(8,128)}), f32[4,128,1024]{2,1,0:T(8,128)S(1)}, u32[]{:S(2)}, u32[]{:S(2)}) async-start(f32[4,128,1024]{2,1,0:T(8,128)} %student_logits.1), calls=%async_computation | async-start | bytes 4194304 | tf_op jit(solution)/shard_map/all_to_all | solution.py:546
  82.5 27.5 %collective-permute-start.19 = (bf16[32,128,128]{2,1,0:T(8,128)(2,1)}, bf16[32,128,128]{2,1,0:T(8,128)(2,1)}, u32[]{:S(2)}, u32[]{:S(2)}) collective-permute-start(bf16[32,128,128]{2,1,0:T(8,128)(2,1)} %get-tuple-element.51), channel_id=1, source_target_pairs={{0,2},{1,3},{2,0},{3,1},{4,6},{5,7},{6,4},{7,5},{8,10},{9,11},{10,... | collective-permute-start | bytes 3145736 | tf_op jit(solution)/shard_map/ppermute | solution.py:516
  82.5 27.5 %collective-permute-start.20 = (bf16[32,128,128]{2,1,0:T(8,128)(2,1)}, bf16[32,128,128]{2,1,0:T(8,128)(2,1)}, u32[]{:S(2)}, u32[]{:S(2)}) collective-permute-start(bf16[32,128,128]{2,1,0:T(8,128)(2,1)} %add_convert_fusion), channel_id=1, source_target_pairs={{2,4},{3,5},{4,2},{5,3},{10,12},{11,13},{12,10},{13,11},{18,20},{1... | collective-permute-start | bytes 3145736 | tf_op jit(solution)/shard_map/ppermute | solution.py:550
  92.7 17.3 %copy-start.6 = (bf16[32,128,128]{2,1,0:T(8,128)(2,1)S(1)}, bf16[32,128,128]{2,1,0:T(8,128)(2,1)}, u32[]{:S(2)}) copy-start(bf16[32,128,128]{2,1,0:T(8,128)(2,1)} %get-tuple-element.47) | copy-start | bytes 3145732
  99.6 1.2 collective-permute-start.13
  100.8 6.1 %collective-permute-start.16 = (f32[8,128]{1,0:T(8,128)S(1)}, f32[8,128]{1,0:T(8,128)S(1)}, u32[]{:S(2)}, u32[]{:S(2)}) collective-permute-start(f32[8,128]{1,0:T(8,128)S(1)} %merge_stats.5.refs_0_), channel_id=1, source_target_pairs={{0,6},{1,7},{2,4},{3,5},{4,2},{5,3},{6,0},{7,1},{8,14},{9,15},{10,... | collective-permute-start | bytes 12296 | tf_op jit(solution)/shard_map/ppermute | solution.py:516
  103.6 6.2 %collective-permute-start.15 = (f32[8,128]{1,0:T(8,128)S(1)}, f32[8,128]{1,0:T(8,128)S(1)}, u32[]{:S(2)}, u32[]{:S(2)}) collective-permute-start(f32[8,128]{1,0:T(8,128)S(1)} %merge_stats.5.refs_0_), channel_id=1, source_target_pairs={{0,4},{1,5},{2,6},{3,7},{4,0},{5,1},{6,2},{7,3},{8,12},{9,13},{10,... | collective-permute-start | bytes 12296 | tf_op jit(solution)/shard_map/ppermute | solution.py:516
  104.5 5.3 %collective-permute-start.14 = (f32[8,128]{1,0:T(8,128)S(1)}, f32[8,128]{1,0:T(8,128)S(1)}, u32[]{:S(2)}, u32[]{:S(2)}) collective-permute-start(f32[8,128]{1,0:T(8,128)S(1)} %merge_stats.5.refs_0_), channel_id=1, source_target_pairs={{0,2},{1,3},{2,0},{3,1},{4,6},{5,7},{6,4},{7,5},{8,10},{9,11},{10,... | collective-permute-start | bytes 12296 | tf_op jit(solution)/shard_map/ppermute | solution.py:516
  109.9 11.9 %slice-start = ((s8[4718592]{0:T(1024)(128)(4,1)}), s8[4194304]{0:T(1024)(128)(4,1)S(1)}, s32[]{:S(2)}) async-start(s8[4718592]{0:T(1024)(128)(4,1)} %bitcast.13), calls=%async_computation.1 | async-start | bytes 8388608
  112.5 9.3 %collective-permute-start.23 = (bf16[128,1024]{1,0:T(8,128)(2,1)}, bf16[128,1024]{1,0:T(8,128)(2,1)S(1)}, u32[]{:S(2)}, u32[]{:S(2)}) collective-permute-start(bf16[128,1024]{1,0:T(8,128)(2,1)} %get-tuple-element.57), channel_id=1, source_target_pairs={{0,24},{8,16},{16,8},{24,0},{1,25},{9,17},{17,9},{25,1},{2,26},{10... | collective-permute-start | bytes 786440 | tf_op jit(solution)/shard_map/ppermute | solution.py:516
  119.0 9.0 %collective-permute-start.25 = (bf16[128,1024]{1,0:T(8,128)(2,1)}, bf16[128,1024]{1,0:T(8,128)(2,1)S(1)}, u32[]{:S(2)}, u32[]{:S(2)}) collective-permute-start(bf16[128,1024]{1,0:T(8,128)(2,1)} %get-tuple-element.60), channel_id=1, source_target_pairs={{0,8},{8,0},{16,24},{24,16},{1,9},{9,1},{17,25},{25,17},{2,10},{10... | collective-permute-start | bytes 786440 | tf_op jit(solution)/shard_map/ppermute | solution.py:516
  119.5 8.5 %collective-permute-start.26 = (bf16[128,1024]{1,0:T(8,128)(2,1)}, bf16[128,1024]{1,0:T(8,128)(2,1)S(1)}, u32[]{:S(2)}, u32[]{:S(2)}) collective-permute-start(bf16[128,1024]{1,0:T(8,128)(2,1)} %get-tuple-element.61), channel_id=1, source_target_pairs={{0,16},{8,24},{16,0},{24,8},{1,17},{9,25},{17,1},{25,9},{2,18},{10... | collective-permute-start | bytes 786440 | tf_op jit(solution)/shard_map/ppermute | solution.py:516
  120.0 1.1 collective-permute-start.21
  121.1 4.8 %collective-permute-start.22 = (f32[1,128]{1,0:T(1,128)S(1)}, f32[1,128]{1,0:T(1,128)S(1)}, u32[]{:S(2)}, u32[]{:S(2)}) collective-permute-start(f32[1,128]{1,0:T(1,128)S(1)} %add.88), channel_id=1, source_target_pairs={{0,2},{1,3},{2,0},{3,1},{4,6},{5,7},{6,4},{7,5},{8,10},{9,11},{10,... | collective-permute-start | bytes 1544 | tf_op jit(solution)/shard_map/ppermute | solution.py:516
  125.9 7.3 %collective-permute-start.24 = (f32[1,128]{1,0:T(1,128)S(1)}, f32[1,128]{1,0:T(1,128)S(1)}, u32[]{:S(2)}, u32[]{:S(2)}) collective-permute-start(f32[1,128]{1,0:T(1,128)S(1)} %add_add_fusion), channel_id=1, source_target_pairs={{0,4},{1,5},{2,6},{3,7},{4,0},{5,1},{6,2},{7,3},{8,12},{9,13},{10,... | collective-permute-start | bytes 1544 | tf_op jit(solution)/shard_map/ppermute | solution.py:516
  (12 other events, 68.9 us)

commit v10 on v9

--- a/solution.py
+++ b/solution.py
@@ -197,7 +197,7 @@
 
 def teacher_probs(x_own, x_peer, stats):
     rows, cols = x_own.shape
-    steps = 4
+    steps = 2
     blocks = cols // LANES
     part = pl.BlockSpec((rows, cols // steps), lambda i: (0, i))
     probs = pl.pallas_call(

time: 134 us -> 133 us (level)
  starting transfers between devices: 35.6 us -> 34.2 us
    ppermute x23, waiting for transfers between devices: 15.4 us -> 16.8 us  [swap(): lax.ppermute(x, axis, [(i, i ^ mask) for i in range(lax.axis_size(axis))])]
  transfers between devices with their start and end apart: 28 -> 28, of which waited for: 16 -> 16; matrix products, arithmetic and copies ran while one was open for 5% -> 5% of each run, Pallas kernels for 32% -> 31%
where the time goes in v10:
time: 133 us
  Pallas kernels  48.8 us (37%)
  waiting for transfers between devices  35.3 us (27%)
  starting transfers between devices  34.2 us (26%)
  local copies, waits for them, and re-layouts  7.18 us (5%)
  other arithmetic  6.96 us (5%)
    ppermute x23, starting transfers between devices, swap(): lax.ppermute(x, axis, [(i, i ^ mask) for i in range(lax.axis_size(axis))])  20.7 us
    ppermute x23, waiting for transfers between devices, swap(): lax.ppermute(x, axis, [(i, i ^ mask) for i in range(lax.axis_size(axis))])  16.8 us
    pallas_call x2, Pallas kernels, chip_sums(): pl.pallas_call(functools.partial(sums_kernel, first=first, fan=fan, piece...  12.9 us
    ppermute x4, waiting for transfers between devices, send(): lax.ppermute(x, 'vocab', [(2 * a + c, 2 * b + c) for a, b in hops for c i...  12.9 us
    ppermute x4, starting transfers between devices, send(): lax.ppermute(x, 'vocab', [(2 * a + c, 2 * b + c) for a, b in hops for c i...  9.89 us
    pallas_call x1, Pallas kernels, student_logits(): pl.pallas_call(logits_kernel, grid=(cols // tile,), in_specs=[SMEM_SPEC,...  9.69 us
    unnamed x32, local copies, waits for them, and re-layouts  6.66 us
    pallas_call x2, Pallas kernels, grad_logits(): pl.pallas_call(functools.partial(grad_kernel, n_sums=len(sums), groups=gr...  6.5 us
  transfers between devices with their start and end apart: 28, of which 16 were waited for; matrix products, arithmetic and copies ran while one was open for 5% of the time, Pallas kernels for 31%

profile of v10, /device:TPU:0, one launch (start us, length us, event | category | flops | bytes accessed | tf_op | source)
XLA Modules:
  0.0 133.4 jit_solution(16612162453797667589)
XLA Ops:
  3.1 3.0 %collective-permute-start.2 = (f32[8,128]{1,0:T(8,128)S(1)}, f32[8,128]{1,0:T(8,128)S(1)}, u32[]{:S(2)}, u32[]{:S(2)}) collective-permute-start(f32[8,128]{1,0:T(8,128)S(1)} %teacher_stats.1.refs_0_), channel_id=1, source_target_pairs={{0,2},{1,3},{2,0},{3,1},{4,6},{5,7},{6,4},{7,5},{8,10},{9,11},{10,... | collective-permute-start | bytes 12296 | tf_op jit(solution)/shard_map/ppermute | solution.py:516
  6.1 1.6 %collective-permute-done.2.refs_1_ = f32[8,128]{1,0:T(8,128)S(1)} collective-permute-done((f32[8,128]{1,0:T(8,128)S(1)}, f32[8,128]{1,0:T(8,128)S(1)}, u32[]{:S(2)}, u32[]{:S(2)}) %collective-permute-start.2) | collective-permute-done | bytes 4128 | tf_op jit(solution)/shard_map/ppermute | solution.py:516
  7.7 3.1 %collective-permute-start.3 = (f32[8,128]{1,0:T(8,128)S(1)}, f32[8,128]{1,0:T(8,128)S(1)}, u32[]{:S(2)}, u32[]{:S(2)}) collective-permute-start(f32[8,128]{1,0:T(8,128)S(1)} %merge_stats.3.refs_0_), channel_id=1, source_target_pairs={{0,4},{1,5},{2,6},{3,7},{4,0},{5,1},{6,2},{7,3},{8,12},{9,13},{10,... | collective-permute-start | bytes 12296 | tf_op jit(solution)/shard_map/ppermute | solution.py:516
  13.6 2.6 %teacher_probs.1 = bf16[2,32,128,128]{3,2,1,0:T(8,128)(2,1)S(1)} custom-call(bf16[128,4096]{1,0:T(8,128)(2,1)} %x_own.1, bf16[128,4096]{1,0:T(8,128)(2,1)S(1)} %collective-permute-done.1.x_peer, f32[8,128]{1,0:T(8,128)S(1)} %merge_stats.4.refs_0_, f32[8,128]{1,0:T(8,128)S(1)} %collective-permute-done.4.refs_1_), custom_call_target="tpu_custom_call" | custom-call | flops 1024 | bytes 1024 | tf_op jit(solution)/shard_map/teacher_probs/pallas_call | solution.py:203
  16.3 4.6 %chip_sums.2 = (bf16[32,128,128]{2,1,0:T(8,128)(2,1)}, f32[8,128]{1,0:T(8,128)S(1)}) custom-call(s32[2]{0:T(128)S(1)} %pad_add_fusion.spot_ref, s32[8,384]{1,0:T(8,128)S(1)} %entry_lists.1.list_ref, bf16[64,128,128]{2,1,0:T(8,128)(2,1)S(1)} %bitcast.15, bf16[32,4,128,128]{3,2,1,0:T(8,128)(2,1)S(1)} %copy-done.2, ...), custom_call_target="tpu_custom_call" | custom-call | flops 1024 | bytes 1024 | tf_op jit(solution)/shard_map/chip_sums/pallas_call | solution.py:222
  20.8 4.7 %collective-permute-start.6 = (bf16[32,128,128]{2,1,0:T(8,128)(2,1)}, bf16[32,128,128]{2,1,0:T(8,128)(2,1)}, u32[]{:S(2)}, u32[]{:S(2)}) collective-permute-start(bf16[32,128,128]{2,1,0:T(8,128)(2,1)} %get-tuple-element.33), channel_id=1, source_target_pairs={{0,2},{1,3},{6,4},{7,5},{8,10},{9,11},{14,12},{15,13},{16,18},{17,... | collective-permute-start | bytes 3145736 | tf_op jit(solution)/shard_map/ppermute | solution.py:550
  25.6 2.5 %collective-permute-start.9 = (bf16[64,4608]{1,0:T(8,128)(2,1)S(1)}, bf16[64,4608]{1,0:T(8,128)(2,1)}, u32[]{:S(2)}, u32[]{:S(2)}) collective-permute-start(bf16[64,4608]{1,0:T(8,128)(2,1)S(1)} %constant_dynamic-slice_fusion), channel_id=1, source_target_pairs={{0,24},{8,16},{16,8},{24,0},{1,25},{9,17},{17,9},{25,1},{2,26},{10... | collective-permute-start | bytes 1769480 | tf_op jit(solution)/shard_map/ppermute | solution.py:516
  29.1 2.2 %copy-done.3 = bf16[32,4,128,128]{3,2,1,0:T(8,128)(2,1)S(1)} copy-done((bf16[32,4,128,128]{3,2,1,0:T(8,128)(2,1)S(1)}, bf16[32,4,128,128]{3,2,1,0:T(8,128)(2,1)}, u32[]{:S(2)}) %copy-start.3) | copy-done | bytes 4194328
  31.3 8.4 %chip_sums.3 = (bf16[32,128,128]{2,1,0:T(8,128)(2,1)}, bf16[32,128,128]{2,1,0:T(8,128)(2,1)}, bf16[32,128,128]{2,1,0:T(8,128)(2,1)}, f32[8,128]{1,0:T(8,128)S(1)}) custom-call(s32[2]{0:T(128)S(1)} %pad_add_fusion.spot_ref, s32[8,384]{1,0:T(8,128)S(1)} %entry_lists.1.list_ref, bf16[64,128,128]{2,1,0:T(8,128)(2,1)S(1)} %bitcast.16, ...), custom_call_target="tpu_custom_call" | custom-call | flops 1024 | bytes 1024 | tf_op jit(solution)/shard_map/chip_sums/pallas_call | solution.py:222
  39.7 2.3 %collective-permute-start.17 = (bf16[32,128,128]{2,1,0:T(8,128)(2,1)}, bf16[32,128,128]{2,1,0:T(8,128)(2,1)}, u32[]{:S(2)}, u32[]{:S(2)}) collective-permute-start(bf16[32,128,128]{2,1,0:T(8,128)(2,1)} %get-tuple-element.49), channel_id=1, source_target_pairs={{0,2},{1,3},{6,4},{7,5},{8,10},{9,11},{14,12},{15,13},{16,18},{17,... | collective-permute-start | bytes 3145736 | tf_op jit(solution)/shard_map/ppermute | solution.py:550
  42.0 6.3 %collective-permute-done.6 = bf16[32,128,128]{2,1,0:T(8,128)(2,1)} collective-permute-done((bf16[32,128,128]{2,1,0:T(8,128)(2,1)}, bf16[32,128,128]{2,1,0:T(8,128)(2,1)}, u32[]{:S(2)}, u32[]{:S(2)}) %collective-permute-start.6) | collective-permute-done | bytes 1048608 | tf_op jit(solution)/shard_map/ppermute | solution.py:550
  48.3 2.5 %add_convert_fusion.1 = bf16[32,128,128]{2,1,0:T(8,128)(2,1)} fusion(bf16[32,128,128]{2,1,0:T(8,128)(2,1)} %collective-permute-done.6, bf16[32,128,128]{2,1,0:T(8,128)(2,1)S(1)} %copy-done.13), kind=kLoop, calls=%fused_computation.1 | loop fusion | flops 2097152 | bytes 3145728 | tf_op jit(solution)/shard_map/convert_element_type | solution.py:542
  50.8 1.3 collective-permute-start.18
  52.1 3.1 %collective-permute-done.8.refs_1_.refs_2_ = bf16[64,4608]{1,0:T(8,128)(2,1)} collective-permute-done((bf16[64,4608]{1,0:T(8,128)(2,1)S(1)}, bf16[64,4608]{1,0:T(8,128)(2,1)}, u32[]{:S(2)}, u32[]{:S(2)}) %collective-permute-start.8) | collective-permute-done | bytes 589856 | tf_op jit(solution)/shard_map/ppermute | solution.py:516
  56.0 1.6 %collective-permute-done.10.refs_3_.refs_4_ = bf16[64,4608]{1,0:T(8,128)(2,1)S(1)} collective-permute-done((bf16[64,4608]{1,0:T(8,128)(2,1)}, bf16[64,4608]{1,0:T(8,128)(2,1)S(1)}, u32[]{:S(2)}, u32[]{:S(2)}) %collective-permute-start.10) | collective-permute-done | bytes 589856 | tf_op jit(solution)/shard_map/ppermute | solution.py:516
  59.3 9.7 %student_logits.1 = f32[4,128,1024]{2,1,0:T(8,128)} custom-call(s32[2]{0:T(128)S(1)} %pad_add_fusion.1.place_ref, f32[8,128]{1,0:T(8,128)S(1)} %add.84.after_ref.mass_ref, bf16[128,4608]{1,0:T(8,128)(2,1)S(1)} %copy-done.4, bf16[64,4608]{1,0:T(8,128)(2,1)} %collective-permute-done.7.refs_0_.refs_1_, bf16[64,4608]{1,0:T(8,128)(2,1)} %collective-permute-done.8.refs_1_.refs_2_, ...), custom_call_target="tpu_custom_call" | custom-call | flops 1024 | bytes 1024 | tf_op jit(solution)/shard_map/student_logits/pallas_call | solution.py:293
  69.0 3.6 %all-to-all-start = ((f32[4,128,1024]{2,1,0:T(8,128)}), f32[4,128,1024]{2,1,0:T(8,128)S(1)}, u32[]{:S(2)}, u32[]{:S(2)}) async-start(f32[4,128,1024]{2,1,0:T(8,128)} %student_logits.1), calls=%async_computation | async-start | bytes 4194304 | tf_op jit(solution)/shard_map/all_to_all | solution.py:546
  72.6 6.6 %collective-permute-done.18 = bf16[32,128,128]{2,1,0:T(8,128)(2,1)} collective-permute-done((bf16[32,128,128]{2,1,0:T(8,128)(2,1)}, bf16[32,128,128]{2,1,0:T(8,128)(2,1)}, u32[]{:S(2)}, u32[]{:S(2)}) %collective-permute-start.18) | collective-permute-done | bytes 1048608 | tf_op jit(solution)/shard_map/ppermute | solution.py:550
  79.2 3.0 %add_convert_fusion = bf16[32,128,128]{2,1,0:T(8,128)(2,1)} fusion(bf16[32,128,128]{2,1,0:T(8,128)(2,1)} %collective-permute-done.17, bf16[32,128,128]{2,1,0:T(8,128)(2,1)} %get-tuple-element.49), kind=kLoop, calls=%fused_computation | loop fusion | flops 2097152 | bytes 3145728 | tf_op jit(solution)/shard_map/convert_element_type | solution.py:542
  82.2 1.6 %collective-permute-start.20 = (bf16[32,128,128]{2,1,0:T(8,128)(2,1)}, bf16[32,128,128]{2,1,0:T(8,128)(2,1)}, u32[]{:S(2)}, u32[]{:S(2)}) collective-permute-start(bf16[32,128,128]{2,1,0:T(8,128)(2,1)} %add_convert_fusion), channel_id=1, source_target_pairs={{2,4},{3,5},{4,2},{5,3},{10,12},{11,13},{12,10},{13,11},{18,20},{1... | collective-permute-start | bytes 3145736 | tf_op jit(solution)/shard_map/ppermute | solution.py:550
  87.3 5.1 %turned_rows.1.a_ref = bf16[4608,512]{1,0:T(8,128)(2,1)} custom-call(s32[2]{0:T(128)S(1)} %pad_add_fusion.1.place_ref, bf16[128,4608]{1,0:T(8,128)(2,1)S(1)} %copy-done.4, bf16[64,4608]{1,0:T(8,128)(2,1)} %collective-permute-done.9.refs_2_.refs_0_, bf16[64,4608]{1,0:T(8,128)(2,1)} %collective-permute-done.7.refs_0_.refs_1_, ...), custom_call_target="tpu_custom_call" | custom-call | flops 1024 | bytes 1024 | tf_op jit(solution)/shard_map/turned_rows/pallas_call | solution.py:273
  92.4 5.6 %all-to-all-done.logits_ref.refs_4_ = f32[4,128,1024]{2,1,0:T(8,128)S(1)} async-done(((f32[4,128,1024]{2,1,0:T(8,128)}), f32[4,128,1024]{2,1,0:T(8,128)S(1)}, u32[]{:S(2)}, u32[]{:S(2)}) %all-to-all-start) | async-done | bytes 2097184 | tf_op jit(solution)/shard_map/all_to_all | solution.py:546
  98.0 1.5 %student_stats.1.refs_0_ = f32[8,128]{1,0:T(8,128)S(1)} custom-call(s32[4]{0:T(128)S(1)} %add_multiply_fusion.base_ref, s32[128,1]{1,0:T(8,128)S(1)} %copy.15.labels_ref, f32[8,128]{1,0:T(8,128)S(1)} %add.84.after_ref.mass_ref, f32[4,128,1024]{2,1,0:T(8,128)S(1)} %all-to-all-done.logits_ref.refs_4_), custom_call_target="tpu_custom_call" | custom-call | flops 1024 | bytes 1024 | tf_op jit(solution)/shard_map/student_stats/pallas_call | solution.py:331
  100.7 1.5 %collective-permute-start.16 = (f32[8,128]{1,0:T(8,128)S(1)}, f32[8,128]{1,0:T(8,128)S(1)}, u32[]{:S(2)}, u32[]{:S(2)}) collective-permute-start(f32[8,128]{1,0:T(8,128)S(1)} %merge_stats.5.refs_0_), channel_id=1, source_target_pairs={{0,6},{1,7},{2,4},{3,5},{4,2},{5,3},{6,0},{7,1},{8,14},{9,15},{10,... | collective-permute-start | bytes 12296 | tf_op jit(solution)/shard_map/ppermute | solution.py:516
  102.2 1.5 %collective-permute-start.15 = (f32[8,128]{1,0:T(8,128)S(1)}, f32[8,128]{1,0:T(8,128)S(1)}, u32[]{:S(2)}, u32[]{:S(2)}) collective-permute-start(f32[8,128]{1,0:T(8,128)S(1)} %merge_stats.5.refs_0_), channel_id=1, source_target_pairs={{0,4},{1,5},{2,6},{3,7},{4,0},{5,1},{6,2},{7,3},{8,12},{9,13},{10,... | collective-permute-start | bytes 12296 | tf_op jit(solution)/shard_map/ppermute | solution.py:516
  103.7 1.4 %collective-permute-start.14 = (f32[8,128]{1,0:T(8,128)S(1)}, f32[8,128]{1,0:T(8,128)S(1)}, u32[]{:S(2)}, u32[]{:S(2)}) collective-permute-start(f32[8,128]{1,0:T(8,128)S(1)} %merge_stats.5.refs_0_), channel_id=1, source_target_pairs={{0,2},{1,3},{2,0},{3,1},{4,6},{5,7},{6,4},{7,5},{8,10},{9,11},{10,... | collective-permute-start | bytes 12296 | tf_op jit(solution)/shard_map/ppermute | solution.py:516
  106.3 4.1 %collective-permute-done.15.refs_2_ = f32[8,128]{1,0:T(8,128)S(1)} collective-permute-done((f32[8,128]{1,0:T(8,128)S(1)}, f32[8,128]{1,0:T(8,128)S(1)}, u32[]{:S(2)}, u32[]{:S(2)}) %collective-permute-start.15) | collective-permute-done | bytes 4128 | tf_op jit(solution)/shard_map/ppermute | solution.py:516
  110.5 2.4 %grad_logits.2 = (bf16[128,1024]{1,0:T(8,128)(2,1)}, f32[1,128]{1,0:T(1,128)S(1)}) custom-call(s32[1]{0:T(128)} %bitcast.5.tok_ref, s32[4]{0:T(128)S(1)} %add_multiply_fusion.base_ref, s32[128,1]{1,0:T(8,128)S(1)} %copy.15.labels_ref, f32[128,128]{1,0:T(8,128)S(1)} %get-tuple-element.46.columns, bf16[1,32,128,128]{3,2,1,0:T(8,128)(2,1)S(1)} %bitcast.17, ...), custom_call_target="tpu_custom_call" | custom-call | flops 1024 | bytes 1024 | tf_op jit(solution)/shard_map/grad_logits/pallas_call | solution.py:434
  112.9 2.5 %collective-permute-start.23 = (bf16[128,1024]{1,0:T(8,128)(2,1)}, bf16[128,1024]{1,0:T(8,128)(2,1)S(1)}, u32[]{:S(2)}, u32[]{:S(2)}) collective-permute-start(bf16[128,1024]{1,0:T(8,128)(2,1)} %get-tuple-element.57), channel_id=1, source_target_pairs={{0,24},{8,16},{16,8},{24,0},{1,25},{9,17},{17,9},{25,1},{2,26},{10... | collective-permute-start | bytes 786440 | tf_op jit(solution)/shard_map/ppermute | solution.py:516
  115.4 4.1 %grad_logits.3 = (bf16[128,1024]{1,0:T(8,128)(2,1)}, bf16[128,1024]{1,0:T(8,128)(2,1)}, bf16[128,1024]{1,0:T(8,128)(2,1)}, f32[1,128]{1,0:T(1,128)S(1)}) custom-call(s32[1]{0:T(128)} %bitcast.5.tok_ref, s32[4]{0:T(128)S(1)} %add_multiply_fusion.base_ref, s32[128,1]{1,0:T(8,128)S(1)} %copy.15.labels_ref, f32[128,128]{1,0:T(8,128)S(1)} %get-tuple-element.46.columns, ...), custom_call_target="tpu_custom_call" | custom-call | flops 1024 | bytes 1024 | tf_op jit(solution)/shard_map/grad_logits/pallas_call | solution.py:434
  122.2 4.1 %first_product.1 = (f32[4608,1024]{1,0:T(8,128)S(1)}, f32[1,128]{1,0:T(1,128)S(1)}) custom-call(bf16[4608,512]{1,0:T(8,128)(2,1)S(1)} %bitcast.14, bf16[128,1024]{1,0:T(8,128)(2,1)} %get-tuple-element.56.refs_0_, bf16[128,1024]{1,0:T(8,128)(2,1)S(1)} %collective-permute-done.23.refs_1_), custom_call_target="tpu_custom_call" | custom-call | flops 1024 | bytes 1024 | tf_op jit(solution)/shard_map/first_product/pallas_call | solution.py:485
  127.6 5.2 %last_product.1 = (bf16[4608,1024]{1,0:T(8,128)(2,1)}, f32[1,128]{1,0:T(1,128)S(1)}) custom-call(bf16[4608,512]{1,0:T(8,128)(2,1)S(1)} %bitcast.14, f32[4608,1024]{1,0:T(8,128)S(1)} %get-tuple-element.59.acc_ref, bf16[128,1024]{1,0:T(8,128)(2,1)S(1)} %collective-permute-done.25.refs_0_, bf16[128,1024]{1,0:T(8,128)(2,1)S(1)} %collective-permute-done.26.refs_1_), custom_call_target="tpu_custom_call" | custom-call | flops 1024 | bytes 1024 | tf_op jit(solution)/shard_map/last_product/pallas_call | solution.py:502
  (90 shorter events, 19.1 us)
Async XLA Ops:
  0.6 83.3 %copy-start = (s32[512]{0:T(512)S(1)}, s32[512]{0:T(512)}, u32[]{:S(2)}) copy-start(s32[512]{0:T(512)} %param.9) | copy-start | bytes 6148
  0.6 15.6 %collective-permute-start.5 = (bf16[32,4,128,128]{3,2,1,0:T(8,128)(2,1)}, bf16[32,4,128,128]{3,2,1,0:T(8,128)(2,1)}, u32[]{:S(2)}, u32[]{:S(2)}) collective-permute-start(bf16[32,4,128,128]{3,2,1,0:T(8,128)(2,1)} %w_own.3), channel_id=1, source_target_pairs={{0,1},{1,0},{2,3},{3,2},{4,5},{5,4},{6,7},{7,6},{8,9},{9,8},{10,11... | collective-permute-start | bytes 12582920 | tf_op jit(solution)/shard_map/ppermute | solution.py:516
  1.2 12.5 %collective-permute-start.1 = (bf16[128,4096]{1,0:T(8,128)(2,1)}, bf16[128,4096]{1,0:T(8,128)(2,1)S(1)}, u32[]{:S(2)}, u32[]{:S(2)}) collective-permute-start(bf16[128,4096]{1,0:T(8,128)(2,1)} %x_own.1), channel_id=1, source_target_pairs={{0,1},{1,0},{2,3},{3,2},{4,5},{5,4},{6,7},{7,6},{8,9},{9,8},{10,11... | collective-permute-start | bytes 3145736 | tf_op jit(solution)/shard_map/ppermute | solution.py:516
  3.1 4.6 %collective-permute-start.2 = (f32[8,128]{1,0:T(8,128)S(1)}, f32[8,128]{1,0:T(8,128)S(1)}, u32[]{:S(2)}, u32[]{:S(2)}) collective-permute-start(f32[8,128]{1,0:T(8,128)S(1)} %teacher_stats.1.refs_0_), channel_id=1, source_target_pairs={{0,2},{1,3},{2,0},{3,1},{4,6},{5,7},{6,4},{7,5},{8,10},{9,11},{10,... | collective-permute-start | bytes 12296 | tf_op jit(solution)/shard_map/ppermute | solution.py:516
  7.7 4.7 %collective-permute-start.3 = (f32[8,128]{1,0:T(8,128)S(1)}, f32[8,128]{1,0:T(8,128)S(1)}, u32[]{:S(2)}, u32[]{:S(2)}) collective-permute-start(f32[8,128]{1,0:T(8,128)S(1)} %merge_stats.3.refs_0_), channel_id=1, source_target_pairs={{0,4},{1,5},{2,6},{3,7},{4,0},{5,1},{6,2},{7,3},{8,12},{9,13},{10,... | collective-permute-start | bytes 12296 | tf_op jit(solution)/shard_map/ppermute | solution.py:516
  11.7 1.2 collective-permute-start
  12.4 1.2 collective-permute-start.4
  20.8 27.5 %collective-permute-start.6 = (bf16[32,128,128]{2,1,0:T(8,128)(2,1)}, bf16[32,128,128]{2,1,0:T(8,128)(2,1)}, u32[]{:S(2)}, u32[]{:S(2)}) collective-permute-start(bf16[32,128,128]{2,1,0:T(8,128)(2,1)} %get-tuple-element.33), channel_id=1, source_target_pairs={{0,2},{1,3},{6,4},{7,5},{8,10},{9,11},{14,12},{15,13},{16,18},{17,... | collective-permute-start | bytes 3145736 | tf_op jit(solution)/shard_map/ppermute | solution.py:550
  25.5 22.8 %copy-start.13 = (bf16[32,128,128]{2,1,0:T(8,128)(2,1)S(1)}, bf16[32,128,128]{2,1,0:T(8,128)(2,1)}, u32[]{:S(2)}) copy-start(bf16[32,128,128]{2,1,0:T(8,128)(2,1)} %get-tuple-element.33) | copy-start | bytes 3145732
  25.6 26.5 %collective-permute-start.9 = (bf16[64,4608]{1,0:T(8,128)(2,1)S(1)}, bf16[64,4608]{1,0:T(8,128)(2,1)}, u32[]{:S(2)}, u32[]{:S(2)}) collective-permute-start(bf16[64,4608]{1,0:T(8,128)(2,1)S(1)} %constant_dynamic-slice_fusion), channel_id=1, source_target_pairs={{0,24},{8,16},{16,8},{24,0},{1,25},{9,17},{17,9},{25,1},{2,26},{10... | collective-permute-start | bytes 1769480 | tf_op jit(solution)/shard_map/ppermute | solution.py:516
  28.1 27.2 %collective-permute-start.8 = (bf16[64,4608]{1,0:T(8,128)(2,1)S(1)}, bf16[64,4608]{1,0:T(8,128)(2,1)}, u32[]{:S(2)}, u32[]{:S(2)}) collective-permute-start(bf16[64,4608]{1,0:T(8,128)(2,1)S(1)} %constant_dynamic-slice_fusion), channel_id=1, source_target_pairs={{0,16},{8,24},{16,0},{24,8},{1,17},{9,25},{17,1},{25,9},{2,18},{10... | collective-permute-start | bytes 1769480 | tf_op jit(solution)/shard_map/ppermute | solution.py:516
  28.6 26.8 %collective-permute-start.7 = (bf16[64,4608]{1,0:T(8,128)(2,1)S(1)}, bf16[64,4608]{1,0:T(8,128)(2,1)}, u32[]{:S(2)}, u32[]{:S(2)}) collective-permute-start(bf16[64,4608]{1,0:T(8,128)(2,1)S(1)} %constant_dynamic-slice_fusion), channel_id=1, source_target_pairs={{0,8},{8,0},{16,24},{24,16},{1,9},{9,1},{17,25},{25,17},{2,10},{10... | collective-permute-start | bytes 1769480 | tf_op jit(solution)/shard_map/ppermute | solution.py:516
  39.7 32.9 %collective-permute-start.17 = (bf16[32,128,128]{2,1,0:T(8,128)(2,1)}, bf16[32,128,128]{2,1,0:T(8,128)(2,1)}, u32[]{:S(2)}, u32[]{:S(2)}) collective-permute-start(bf16[32,128,128]{2,1,0:T(8,128)(2,1)} %get-tuple-element.49), channel_id=1, source_target_pairs={{0,2},{1,3},{6,4},{7,5},{8,10},{9,11},{14,12},{15,13},{16,18},{17,... | collective-permute-start | bytes 3145736 | tf_op jit(solution)/shard_map/ppermute | solution.py:550
  50.8 28.4 %collective-permute-start.18 = (bf16[32,128,128]{2,1,0:T(8,128)(2,1)}, bf16[32,128,128]{2,1,0:T(8,128)(2,1)}, u32[]{:S(2)}, u32[]{:S(2)}) collective-permute-start(bf16[32,128,128]{2,1,0:T(8,128)(2,1)} %add_convert_fusion.1), channel_id=1, source_target_pairs={{2,6},{3,7},{4,0},{5,1},{10,14},{11,15},{12,8},{13,9},{18,22},{19,... | collective-permute-start | bytes 3145736 | tf_op jit(solution)/shard_map/ppermute | solution.py:550
  55.4 2.2 %collective-permute-start.10 = (bf16[64,4608]{1,0:T(8,128)(2,1)}, bf16[64,4608]{1,0:T(8,128)(2,1)S(1)}, u32[]{:S(2)}, u32[]{:S(2)}) collective-permute-start(bf16[64,4608]{1,0:T(8,128)(2,1)} %collective-permute-done.7.refs_0_.refs_1_), channel_id=1, source_target_pairs={{0,1},{1,0},{2,3},{3,2},{4,5},{5,4},{6,7},{7,6},{8,9},{9,8},{10,11... | collective-permute-start | bytes 1769480 | tf_op jit(solution)/shard_map/ppermute | solution.py:516
  55.4 3.1 %collective-permute-start.11 = (bf16[64,4608]{1,0:T(8,128)(2,1)}, bf16[64,4608]{1,0:T(8,128)(2,1)S(1)}, u32[]{:S(2)}, u32[]{:S(2)}) collective-permute-start(bf16[64,4608]{1,0:T(8,128)(2,1)} %collective-permute-done.8.refs_1_.refs_2_), channel_id=1, source_target_pairs={{0,1},{1,0},{2,3},{3,2},{4,5},{5,4},{6,7},{7,6},{8,9},{9,8},{10,11... | collective-permute-start | bytes 1769480 | tf_op jit(solution)/shard_map/ppermute | solution.py:516
  55.9 3.4 %collective-permute-start.12 = (bf16[64,4608]{1,0:T(8,128)(2,1)}, bf16[64,4608]{1,0:T(8,128)(2,1)S(1)}, u32[]{:S(2)}, u32[]{:S(2)}) collective-permute-start(bf16[64,4608]{1,0:T(8,128)(2,1)} %collective-permute-done.9.refs_2_.refs_0_), channel_id=1, source_target_pairs={{0,1},{1,0},{2,3},{3,2},{4,5},{5,4},{6,7},{7,6},{8,9},{9,8},{10,11... | collective-permute-start | bytes 1769480 | tf_op jit(solution)/shard_map/ppermute | solution.py:516
  69.0 29.0 %all-to-all-start = ((f32[4,128,1024]{2,1,0:T(8,128)}), f32[4,128,1024]{2,1,0:T(8,128)S(1)}, u32[]{:S(2)}, u32[]{:S(2)}) async-start(f32[4,128,1024]{2,1,0:T(8,128)} %student_logits.1), calls=%async_computation | async-start | bytes 4194304 | tf_op jit(solution)/shard_map/all_to_all | solution.py:546
  82.2 28.2 %collective-permute-start.19 = (bf16[32,128,128]{2,1,0:T(8,128)(2,1)}, bf16[32,128,128]{2,1,0:T(8,128)(2,1)}, u32[]{:S(2)}, u32[]{:S(2)}) collective-permute-start(bf16[32,128,128]{2,1,0:T(8,128)(2,1)} %get-tuple-element.51), channel_id=1, source_target_pairs={{0,2},{1,3},{2,0},{3,1},{4,6},{5,7},{6,4},{7,5},{8,10},{9,11},{10,... | collective-permute-start | bytes 3145736 | tf_op jit(solution)/shard_map/ppermute | solution.py:516
  82.2 28.2 %collective-permute-start.20 = (bf16[32,128,128]{2,1,0:T(8,128)(2,1)}, bf16[32,128,128]{2,1,0:T(8,128)(2,1)}, u32[]{:S(2)}, u32[]{:S(2)}) collective-permute-start(bf16[32,128,128]{2,1,0:T(8,128)(2,1)} %add_convert_fusion), channel_id=1, source_target_pairs={{2,4},{3,5},{4,2},{5,3},{10,12},{11,13},{12,10},{13,11},{18,20},{1... | collective-permute-start | bytes 3145736 | tf_op jit(solution)/shard_map/ppermute | solution.py:550
  92.4 18.1 %copy-start.6 = (bf16[32,128,128]{2,1,0:T(8,128)(2,1)S(1)}, bf16[32,128,128]{2,1,0:T(8,128)(2,1)}, u32[]{:S(2)}) copy-start(bf16[32,128,128]{2,1,0:T(8,128)(2,1)} %get-tuple-element.47) | copy-start | bytes 3145732
  99.5 1.2 collective-permute-start.13
  100.7 5.6 %collective-permute-start.16 = (f32[8,128]{1,0:T(8,128)S(1)}, f32[8,128]{1,0:T(8,128)S(1)}, u32[]{:S(2)}, u32[]{:S(2)}) collective-permute-start(f32[8,128]{1,0:T(8,128)S(1)} %merge_stats.5.refs_0_), channel_id=1, source_target_pairs={{0,6},{1,7},{2,4},{3,5},{4,2},{5,3},{6,0},{7,1},{8,14},{9,15},{10,... | collective-permute-start | bytes 12296 | tf_op jit(solution)/shard_map/ppermute | solution.py:516
  102.2 8.1 %collective-permute-start.15 = (f32[8,128]{1,0:T(8,128)S(1)}, f32[8,128]{1,0:T(8,128)S(1)}, u32[]{:S(2)}, u32[]{:S(2)}) collective-permute-start(f32[8,128]{1,0:T(8,128)S(1)} %merge_stats.5.refs_0_), channel_id=1, source_target_pairs={{0,4},{1,5},{2,6},{3,7},{4,0},{5,1},{6,2},{7,3},{8,12},{9,13},{10,... | collective-permute-start | bytes 12296 | tf_op jit(solution)/shard_map/ppermute | solution.py:516
  103.7 6.6 %collective-permute-start.14 = (f32[8,128]{1,0:T(8,128)S(1)}, f32[8,128]{1,0:T(8,128)S(1)}, u32[]{:S(2)}, u32[]{:S(2)}) collective-permute-start(f32[8,128]{1,0:T(8,128)S(1)} %merge_stats.5.refs_0_), channel_id=1, source_target_pairs={{0,2},{1,3},{2,0},{3,1},{4,6},{5,7},{6,4},{7,5},{8,10},{9,11},{10,... | collective-permute-start | bytes 12296 | tf_op jit(solution)/shard_map/ppermute | solution.py:516
  110.3 11.9 %slice-start = ((s8[4718592]{0:T(1024)(128)(4,1)}), s8[4194304]{0:T(1024)(128)(4,1)S(1)}, s32[]{:S(2)}) async-start(s8[4718592]{0:T(1024)(128)(4,1)} %bitcast.13), calls=%async_computation.1 | async-start | bytes 8388608
  112.9 9.3 %collective-permute-start.23 = (bf16[128,1024]{1,0:T(8,128)(2,1)}, bf16[128,1024]{1,0:T(8,128)(2,1)S(1)}, u32[]{:S(2)}, u32[]{:S(2)}) collective-permute-start(bf16[128,1024]{1,0:T(8,128)(2,1)} %get-tuple-element.57), channel_id=1, source_target_pairs={{0,24},{8,16},{16,8},{24,0},{1,25},{9,17},{17,9},{25,1},{2,26},{10... | collective-permute-start | bytes 786440 | tf_op jit(solution)/shard_map/ppermute | solution.py:516
  119.5 8.2 %collective-permute-start.25 = (bf16[128,1024]{1,0:T(8,128)(2,1)}, bf16[128,1024]{1,0:T(8,128)(2,1)S(1)}, u32[]{:S(2)}, u32[]{:S(2)}) collective-permute-start(bf16[128,1024]{1,0:T(8,128)(2,1)} %get-tuple-element.60), channel_id=1, source_target_pairs={{0,8},{8,0},{16,24},{24,16},{1,9},{9,1},{17,25},{25,17},{2,10},{10... | collective-permute-start | bytes 786440 | tf_op jit(solution)/shard_map/ppermute | solution.py:516
  120.0 7.7 %collective-permute-start.26 = (bf16[128,1024]{1,0:T(8,128)(2,1)}, bf16[128,1024]{1,0:T(8,128)(2,1)S(1)}, u32[]{:S(2)}, u32[]{:S(2)}) collective-permute-start(bf16[128,1024]{1,0:T(8,128)(2,1)} %get-tuple-element.61), channel_id=1, source_target_pairs={{0,16},{8,24},{16,0},{24,8},{1,17},{9,25},{17,1},{25,9},{2,18},{10... | collective-permute-start | bytes 786440 | tf_op jit(solution)/shard_map/ppermute | solution.py:516
  120.5 1.1 collective-permute-start.21
  121.6 4.8 %collective-permute-start.22 = (f32[1,128]{1,0:T(1,128)S(1)}, f32[1,128]{1,0:T(1,128)S(1)}, u32[]{:S(2)}, u32[]{:S(2)}) collective-permute-start(f32[1,128]{1,0:T(1,128)S(1)} %add.88), channel_id=1, source_target_pairs={{0,2},{1,3},{2,0},{3,1},{4,6},{5,7},{6,4},{7,5},{8,10},{9,11},{10,... | collective-permute-start | bytes 1544 | tf_op jit(solution)/shard_map/ppermute | solution.py:516
  126.4 6.5 %collective-permute-start.24 = (f32[1,128]{1,0:T(1,128)S(1)}, f32[1,128]{1,0:T(1,128)S(1)}, u32[]{:S(2)}, u32[]{:S(2)}) collective-permute-start(f32[1,128]{1,0:T(1,128)S(1)} %add_add_fusion), channel_id=1, source_target_pairs={{0,4},{1,5},{2,6},{3,7},{4,0},{5,1},{6,2},{7,3},{8,12},{9,13},{10,... | collective-permute-start | bytes 1544 | tf_op jit(solution)/shard_map/ppermute | solution.py:516
  (12 other events, 68.0 us)
